TPU v7x, 32 devices: a whole 2x2x4 slice. The times are simulated.
32 devices in a mesh: east: 16 (over z, y, core), north: 2 (over x).
Axes of the slice: x: 2, y: 2, z: 4, core: 2. Of those that a mesh axis runs over, the one named last changes fastest.
Arguments:
- features: bfloat16 [96, 128, 32, 8], P(None, 'east', 'north'), may hold values from -6 to 6
- brick_active: int32 [16, 4, 1], P('east', 'north'), may hold values 0 or 1
- voxel_occupancy: int32 [128, 32, 8], P('east', 'north'), may hold values 0 or 1
- first_weights: bfloat16 [27, 96, 96], replicated, may hold values from -0.125 to 0.125
- second_weights: bfloat16 [27, 96, 96], replicated, may hold values from -0.125 to 0.125
- head: bfloat16 [13, 96], replicated, may hold values from -0.625 to 0.625
- teacher: bfloat16 [13, 128, 32, 8], P(None, 'east', 'north'), may hold values from -6 to 6
Outputs:
- grad_features: bfloat16 [96, 128, 32, 8], P(None, 'east', 'north')
- grad_first: float32 [27, 96, 96], replicated
- grad_second: float32 [27, 96, 96], replicated
All inputs are finite; a program needn't handle non-finite values. No bound on the sum of `brick_active` or of `voxel_occupancy` on one device may be relied on, other than what follows from the above.
Results may differ from a plain program's by a relative error of at most 0.0058.
Values may be sent and summed in bfloat16 or wider, within the bound.
No kernel may reach another device: no remote copies, remote signals or barrier semaphores. Data moves between devices by JAX's collectives and lax.ppermute only.
A program may use at most 128 MiB of HBM per device.

v0:
```python
import functools
import math

import jax
import jax.numpy as jnp
from jax import lax
from jax.experimental import pallas as pl
from jax.experimental.pallas import tpu as pltpu
from jax.sharding import PartitionSpec as P

LANES = 128
HALO = 4
OFFSETS = 9
WIDE = OFFSETS * LANES
AXES = ("east", "north")
F32 = jnp.float32
BF16 = jnp.bfloat16


def halo_of(block, axis, dim, width):
    count = lax.axis_size(axis)
    size = block.shape[dim]
    if count == 1:
        empty = jnp.zeros_like(lax.slice_in_dim(block, 0, width, axis=dim))
        return empty, empty
    if count == 2:
        me = lax.axis_index(axis)
        mine = lax.dynamic_slice_in_dim(block, (1 - me) * (size - width), width, axis=dim)
        other = lax.ppermute(mine, axis, [(0, 1), (1, 0)])
        empty = jnp.zeros_like(other)
        return jnp.where(me == 1, other, empty), jnp.where(me == 0, other, empty)
    forward = [(i, i + 1) for i in range(count - 1)]
    backward = [(target, source) for source, target in forward]
    low = lax.ppermute(lax.slice_in_dim(block, size - width, size, axis=dim), axis, forward)
    high = lax.ppermute(lax.slice_in_dim(block, 0, width, axis=dim), axis, backward)
    return low, high


def lane_of(shape):
    return lax.broadcasted_iota(jnp.int32, shape, len(shape) - 1)


def put_stack(value, rows, upward, stack_ref, parity, index):
    cubes = value.reshape(rows // upward, upward, LANES)
    level = lax.broadcasted_iota(jnp.int32, cubes.shape, 1)
    below = jnp.where(level == 0, 0.0, pltpu.roll(cubes, 1, 1)).reshape(rows, LANES)
    above = jnp.where(level == upward - 1, 0.0, pltpu.roll(cubes, upward - 1, 1)).reshape(rows, LANES)
    start = index * rows
    for up, moved in enumerate((below, value, above)):
        shifts = (
            jnp.concatenate([moved[rows - upward :], moved[: rows - upward]], 0),
            moved,
            jnp.concatenate([moved[upward:], moved[:upward]], 0),
        )
        for north, shifted in enumerate(shifts):
            lane = (north * 3 + up) * LANES
            stack_ref[parity, pl.ds(start, rows), lane : lane + LANES] = shifted.astype(BF16)


def convolve(stack_ref, weight_ref, pairs, rows, acc_ref, transposed):
    dims = (((1,), (1,)), ((), ())) if transposed else (((1,), (0,)), ((), ()))
    total = None
    for p in range(4):
        first = (p // 2) * rows
        part = lax.dot_general(
            stack_ref[p % 2, first : first + pairs * rows, :],
            weight_ref[p],
            dims,
            preferred_element_type=F32,
        )
        total = part if total is None else total + part
    acc_ref[0 : pairs * rows, :] = total


def put_forward(weight_ref, w_ref, channels):
    weight_ref[...] = jnp.zeros_like(weight_ref)
    for p in range(4):
        for q in range(2):
            if 0 <= p - q <= 2:
                for j in range(OFFSETS):
                    weight_ref[p, q * LANES : q * LANES + channels, j * LANES : j * LANES + channels] = w_ref[
                        (p - q) * OFFSETS + j
                    ]


def put_backward(weight_ref, w_ref, channels):
    weight_ref[...] = jnp.zeros_like(weight_ref)
    for p in range(4):
        for q in range(2):
            if 0 <= p - q <= 2:
                for j in range(OFFSETS):
                    weight_ref[p, j * LANES : j * LANES + channels, q * LANES : q * LANES + channels] = w_ref[
                        (2 - (p - q)) * OFFSETS + 8 - j
                    ]


def put_turned(turned_ref, value, plane, east, channels):
    turned = value.T[0:channels].astype(BF16)
    size = value.shape[0]
    for d in range(3):
        e = plane + d - 1
        if 0 <= e < east:
            turned_ref[d * channels : (d + 1) * channels, e * size : (e + 1) * size] = turned


def kernel_sum(turned_ref, stack_ref, first, east, rows, low, size, channels, out_ref):
    total = None
    for i in range(east // 2):
        fields = []
        for e in (2 * i, 2 * i + 1):
            plane = e + first
            start = (plane // 2) * rows + low
            fields.append(stack_ref[plane % 2, start : start + size, :])
        part = jnp.dot(
            turned_ref[:, 2 * i * size : (2 * i + 2) * size],
            jnp.concatenate(fields, 0),
            preferred_element_type=F32,
        )
        total = part if total is None else total + part
    blocks = [
        total[d * channels : (d + 1) * channels, j * LANES : (j + 1) * LANES]
        for d in range(3)
        for j in range(OFFSETS)
    ]
    blocks.append(jnp.zeros_like(blocks[0]))
    lane = lane_of(blocks[0].shape)
    spare = LANES - channels
    row = 0
    for t in range(0, 28, 4):
        for r in range(3):
            tail = pltpu.roll(blocks[t + 3], channels - spare * r, 1)
            out_ref[row : row + channels, :] = jnp.where(lane < channels, blocks[t + r], tail).astype(BF16)
            row += channels
    if row < out_ref.shape[0]:
        out_ref[row:, :] = jnp.zeros((out_ref.shape[0] - row, LANES), BF16)


def whole_kernel(
    channels, classes, east, north, upward,
    x_ref, w1_ref, w2_ref, head_ref,
    out_ref, second_ref, first_ref,
    s0_ref, s1_ref, sg_ref, mask_ref, slope_ref, acc_ref, wt_ref, wb_ref, turned_ref,
):
    rows = (north + 2 * HALO) * upward
    low, size = HALO * upward, north * upward
    planes = east + 2 * HALO
    lane = lane_of((rows, LANES))

    put_forward(wt_ref, w1_ref, channels)

    def start(i, carry):
        for parity in range(2):
            x = x_ref[2 * i + parity].astype(F32)
            mask = jnp.broadcast_to(x[:, channels : channels + 1], (rows, LANES))
            mask_ref[2 * i + parity] = mask
            a0 = jnp.where((mask > 0) & (lane < channels), x, 0.0)
            put_stack(a0, rows, upward, s0_ref, parity, i)
        return carry

    lax.fori_loop(0, planes // 2, start, 0)
    convolve(s0_ref, wt_ref, (planes - 2) // 2, rows, acc_ref, True)
    put_forward(wt_ref, w2_ref, channels)

    def middle(i, carry):
        for parity in range(2):
            plane = 2 * i + parity
            mask = mask_ref[plane + 1]
            p1 = mask * acc_ref[pl.ds(i * rows, rows), parity * LANES : (parity + 1) * LANES]
            sig = jax.nn.sigmoid(p1)
            slope_ref[plane] = mask * (sig * (1.0 + p1 * (1.0 - sig)))
            put_stack(p1 * sig, rows, upward, s1_ref, parity, i)
        return carry

    lax.fori_loop(0, (planes - 2) // 2, middle, 0)
    convolve(s1_ref, wt_ref, (planes - 4) // 2, rows, acc_ref, True)
    put_backward(wb_ref, w2_ref, channels)

    head = head_ref[...]
    class_lane = (lane > channels) & (lane <= channels + classes)

    for i in range((planes - 4) // 2):
        for parity in range(2):
            plane = 2 * i + parity
            mask = mask_ref[plane + 2]
            p2 = mask * acc_ref[i * rows : (i + 1) * rows, parity * LANES : (parity + 1) * LANES]
            sig = jax.nn.sigmoid(p2)
            a2 = (p2 * sig).astype(BF16)
            logits = lax.dot_general(a2, head, (((1,), (1,)), ((), ())), preferred_element_type=F32)
            g_logits = jnp.where(class_lane, mask * (logits - x_ref[plane + 2].astype(F32)), 0.0)
            coarse = g_logits.astype(BF16)
            fine = (g_logits - coarse.astype(F32)).astype(BF16)
            g_a2 = jnp.dot(
                jnp.concatenate([coarse, fine], 1), jnp.concatenate([head, head], 0), preferred_element_type=F32
            )
            g_p2 = mask * g_a2 * (sig * (1.0 + p2 * (1.0 - sig)))
            put_stack(g_p2, rows, upward, sg_ref, parity, i)
            put_turned(turned_ref, g_p2[low : low + size], plane - 2, east, channels)

    kernel_sum(turned_ref, s1_ref, 3, east, rows, low, size, channels, second_ref)
    convolve(sg_ref, wb_ref, (planes - 6) // 2, rows, acc_ref, False)
    put_backward(wb_ref, w1_ref, channels)

    for i in range((planes - 6) // 2):
        for parity in range(2):
            plane = 2 * i + parity
            g_p1 = slope_ref[plane + 2] * acc_ref[i * rows : (i + 1) * rows, parity * LANES : (parity + 1) * LANES]
            put_stack(g_p1, rows, upward, sg_ref, parity, i)
            put_turned(turned_ref, g_p1[low : low + size], plane - 1, east, channels)

    kernel_sum(turned_ref, s0_ref, 4, east, rows, low, size, channels, first_ref)
    convolve(sg_ref, wb_ref, east // 2, rows, acc_ref, False)
    for i in range(east // 2):
        for parity in range(2):
            plane = 2 * i + parity
            value = acc_ref[i * rows + low : i * rows + low + size, parity * LANES : (parity + 1) * LANES]
            value = mask_ref[plane + HALO, low : low + size] * value
            out_ref[plane] = value[:, 0:channels].astype(BF16)


def unpack_kernel(channels, scale, second_in, first_in, first_out, second_out):
    spare = LANES - channels
    for source, target in ((first_in, first_out), (second_in, second_out)):
        for t in range(0, 27, 4):
            tiles = [
                source[(t // 4 * 3 + r) * channels : (t // 4 * 3 + r + 1) * channels, :].astype(F32) * scale
                for r in range(3)
            ]
            for r in range(3):
                target[t + r] = tiles[r][:, 0:channels]
            if t + 3 < 27:
                lane = lane_of(tiles[0].shape)
                parts = [pltpu.roll(tiles[r], (spare * r - channels) % LANES, 1) for r in range(3)]
                last = jnp.where(lane < spare, parts[0], jnp.where(lane < 2 * spare, parts[1], parts[2]))
                target[t + 3] = last[:, 0:channels]


def per_device(
    features, brick_active, voxel_occupancy, first_weights, second_weights, head, teacher
):
    channels = features.shape[0]
    east, north, upward = features.shape[1:]
    classes = teacher.shape[0]
    devices = lax.axis_size("east") * lax.axis_size("north")
    scale = 1.0 / math.sqrt(devices * east * north * upward)

    flags = jnp.repeat(brick_active, east // brick_active.shape[0], 0)
    flags = jnp.repeat(flags, north // brick_active.shape[1], 1)
    flags = jnp.repeat(flags, upward // brick_active.shape[2], 2)
    mask = (flags * voxel_occupancy).astype(BF16)
    x = jnp.concatenate(
        [
            features.transpose(1, 2, 3, 0),
            mask[..., None],
            teacher.transpose(1, 2, 3, 0),
            jnp.zeros((east, north, upward, LANES - channels - 1 - classes), BF16),
        ],
        -1,
    )
    low, high = halo_of(x, "north", 1, HALO)
    x = jnp.concatenate([low, x, high], 1)
    low, high = halo_of(x, "east", 0, HALO)
    x = jnp.concatenate([low, x, high], 0)

    planes = east + 2 * HALO
    rows = (north + 2 * HALO) * upward
    x = x.reshape(planes, rows, LANES)
    head_wide = jnp.pad(head, ((channels + 1, LANES - channels - 1 - classes), (0, LANES - channels)))

    chunk = -(-21 * channels // (devices * 16)) * 16
    packed = chunk * devices
    vmem = pl.BlockSpec(memory_space=pltpu.VMEM)
    grad_features, second, first = pl.pallas_call(
        functools.partial(whole_kernel, channels, classes, east, north, upward),
        out_shape=(
            jax.ShapeDtypeStruct((east, north * upward, channels), BF16),
            jax.ShapeDtypeStruct((packed, LANES), BF16),
            jax.ShapeDtypeStruct((packed, LANES), BF16),
        ),
        in_specs=[vmem] * 4,
        out_specs=(vmem, vmem, vmem),
        scratch_shapes=[
            pltpu.VMEM((2, planes // 2 * rows, WIDE), BF16),
            pltpu.VMEM((2, (planes - 2) // 2 * rows, WIDE), BF16),
            pltpu.VMEM((2, (planes - 4) // 2 * rows, WIDE), BF16),
            pltpu.VMEM((planes, rows, LANES), F32),
            pltpu.VMEM((planes - 2, rows, LANES), F32),
            pltpu.VMEM(((planes - 2) // 2 * rows, 2 * LANES), F32),
            pltpu.VMEM((4, 2 * LANES, WIDE), BF16),
            pltpu.VMEM((4, WIDE, 2 * LANES), BF16),
            pltpu.VMEM((3 * channels, east * north * upward), BF16),
        ],
        compiler_params=pltpu.CompilerParams(vmem_limit_bytes=56 * 1024 * 1024),
        name="fields",
    )(x, first_weights, second_weights, head_wide)

    both = jnp.concatenate(
        [second.reshape(devices, chunk, LANES), first.reshape(devices, chunk, LANES)], 1
    )
    parts = lax.all_to_all(both, AXES, 0, 0, tiled=True)
    mine = jnp.sum(parts.astype(F32), 0).astype(BF16)
    whole = lax.all_gather(mine, AXES, axis=0)
    second = whole[:, :chunk].reshape(packed, LANES)
    first = whole[:, chunk:].reshape(packed, LANES)

    grad_first, grad_second = pl.pallas_call(
        functools.partial(unpack_kernel, channels, scale),
        out_shape=(
            jax.ShapeDtypeStruct(first_weights.shape, F32),
            jax.ShapeDtypeStruct(second_weights.shape, F32),
        ),
        in_specs=[vmem] * 2,
        out_specs=(vmem, vmem),
        compiler_params=pltpu.CompilerParams(vmem_limit_bytes=32 * 1024 * 1024),
        name="unpack",
    )(second, first)
    grad_features = grad_features.reshape(east, north, upward, channels).transpose(3, 0, 1, 2)
    return (grad_features, grad_first, grad_second)


def solution(mesh):
    in_specs = (
        P(None, "east", "north", None),
        P("east", "north", None),
        P("east", "north", None),
        P(),
        P(),
        P(),
        P(None, "east", "north", None),
    )
    out_specs = (P(None, "east", "north", None), P(), P())
    return jax.shard_map(
        per_device, mesh=mesh, in_specs=in_specs, out_specs=out_specs, check_vma=False
    )
```

profile of v0, /device:TPU:0, one launch (start us, length us, event | category | flops | bytes accessed | tf_op | source)
XLA Modules:
  0.0 158.8 jit_solution(3784222480157013998)
XLA Ops:
  7.2 0.0 all-gather.3.cloned.1.call-start
  7.2 0.8 broadcast_in_dim.16
  8.0 0.1 broadcast_in_dim.17
  8.1 0.8 fusion.3
  8.8 0.5 copy.10
  9.3 1.4 copy.11
  10.8 1.0 fusion
  11.8 0.0 copy-start.1
  11.8 3.0 %collective-permute-start = (bf16[8,4,8,128]{3,2,1,0:T(8,128)(2,1)S(1)}, bf16[8,4,8,128]{3,2,1,0:T(8,128)(2,1)S(1)}, u32[]{:S(2)}, u32[]{:S(2)}) collective-permute-start(bf16[8,4,8,128]{3,2,1,0:T(8,128)(2,1)S(1)} %fusion), channel_id=1, source_target_pairs={{0,1},{1,0},{2,3},{3,2},{4,5},{5,4},{6,7},{7,6},{8,9},{9,8},{10,11... | collective-permute-start | bytes 196616 | tf_op jit(solution)/shard_map/ppermute | solution.py:29
  14.8 2.2 %collective-permute-done = bf16[8,4,8,128]{3,2,1,0:T(8,128)(2,1)S(1)} collective-permute-done((bf16[8,4,8,128]{3,2,1,0:T(8,128)(2,1)S(1)}, bf16[8,4,8,128]{3,2,1,0:T(8,128)(2,1)S(1)}, u32[]{:S(2)}, u32[]{:S(2)}) %collective-permute-start) | collective-permute-done | bytes 65568 | tf_op jit(solution)/shard_map/ppermute | solution.py:29
  17.1 0.4 pad_maximum_fusion.1
  17.4 1.3 collective-permute-start.1
  18.8 1.3 collective-permute-start.2
  20.1 0.6 pad.4.head_ref
  20.7 3.7 %collective-permute-done.2 = bf16[4,24,8,128]{3,2,1,0:T(8,128)(2,1)S(1)} collective-permute-done((bf16[4,24,8,128]{3,2,1,0:T(8,128)(2,1)S(1)}, bf16[4,24,8,128]{3,2,1,0:T(8,128)(2,1)S(1)}, u32[]{:S(2)}, u32[]{:S(2)}) %collective-permute-start.2) | collective-permute-done | bytes 196640 | tf_op jit(solution)/shard_map/ppermute | solution.py:35
  24.4 1.2 maximum_bitcast_fusion.x_ref
  25.6 32.6 %fields.1 = (bf16[8,128,96]{2,1,0:T(8,128)(2,1)}, bf16[2048,128]{1,0:T(8,128)(2,1)}, bf16[2048,128]{1,0:T(8,128)(2,1)}) custom-call(bf16[16,192,128]{2,1,0:T(8,128)(2,1)} %maximum_bitcast_fusion.x_ref, bf16[27,96,96]{2,1,0:T(8,128)(2,1)} %w1_ref.1, bf16[27,96,96]{2,1,0:T(8,128)(2,1)} %w2_ref.1, bf16[128,128]{1,0:T(8,128)(2,1)} %pad.4.head_ref), custom_call_target="tpu_custom_call" | custom-call | tf_op jit(solution)/shard_map/fields/pallas_call | solution.py:272
  58.2 1.3 pad_maximum_fusion
  59.5 35.5 %all_to_all.5 = bf16[32,128,128]{2,1,0:T(8,128)(2,1)S(1)} all-to-all(bf16[32,128,128]{2,1,0:T(8,128)(2,1)S(1)} %pad_maximum_fusion), channel_id=1, replica_groups=mesh['east'=16,'north'=2] {'east','north'}, dimensions={0} | all-to-all | bytes 2097152 | tf_op jit(solution)/shard_map/all_to_all | solution.py:299
  95.0 0.8 reduce_sum.12
  95.8 0.0 all-gather.3.cloned.1.call-update
  95.8 52.9 %all-gather.3.cloned.1.call-done = bf16[4096,128]{1,0:T(8,128)(2,1)} async-done(((bf16[128,128]{1,0:T(8,128)(2,1)}), bf16[4096,128]{1,0:T(8,128)(2,1)}) %all-gather.3.cloned.1.call-update) | async-done | bytes 1048592 | tf_op jit(solution)/shard_map/all_gather | solution.py:301
  148.7 1.3 fusion.4
  150.0 2.0 %unpack.1 = (f32[27,96,96]{2,1,0:T(8,128)}, f32[27,96,96]{2,1,0:T(8,128)}) custom-call(bf16[2048,128]{1,0:T(8,128)(2,1)S(1)} %bitcast.16, bf16[2048,128]{1,0:T(8,128)(2,1)S(1)} %bitcast.15), custom_call_target="tpu_custom_call" | custom-call | tf_op jit(solution)/shard_map/unpack/pallas_call | solution.py:305
  (7 shorter events, 0.1 us)
Async XLA Ops:
  7.2 9.9 %copy-start = (bf16[96,8,16,8]{0,3,2,1:T(8,128)(2,1)S(1)}, bf16[96,8,16,8]{0,3,2,1:T(8,128)(2,1)}, u32[]{:S(2)}) copy-start(bf16[96,8,16,8]{0,3,2,1:T(8,128)(2,1)} %param.7) | copy-start | bytes 589828
  7.2 141.5 %all-gather.3.cloned.1.call-start = ((), (), s32[]{:S(2)}) async-start(), calls=%async_computation.1 | async-start | bytes 1081344 | tf_op jit(solution)/shard_map/all_gather | solution.py:301
  11.8 8.3 %copy-start.1 = (bf16[13,96]{1,0:T(8,128)(2,1)S(1)}, bf16[13,96]{1,0:T(8,128)(2,1)}, u32[]{:S(2)}) copy-start(bf16[13,96]{1,0:T(8,128)(2,1)} %param.12) | copy-start | bytes 7492
  11.8 5.2 %collective-permute-start = (bf16[8,4,8,128]{3,2,1,0:T(8,128)(2,1)S(1)}, bf16[8,4,8,128]{3,2,1,0:T(8,128)(2,1)S(1)}, u32[]{:S(2)}, u32[]{:S(2)}) collective-permute-start(bf16[8,4,8,128]{3,2,1,0:T(8,128)(2,1)S(1)} %fusion), channel_id=1, source_target_pairs={{0,1},{1,0},{2,3},{3,2},{4,5},{5,4},{6,7},{7,6},{8,9},{9,8},{10,11... | collective-permute-start | bytes 196616 | tf_op jit(solution)/shard_map/ppermute | solution.py:29
  17.4 3.2 %collective-permute-start.1 = (bf16[4,24,8,128]{3,2,1,0:T(8,128)(2,1)S(1)}, bf16[4,24,8,128]{3,2,1,0:T(8,128)(2,1)S(1)}, u32[]{:S(2)}, u32[]{:S(2)}) collective-permute-start(bf16[4,24,8,128]{3,2,1,0:T(8,128)(2,1)S(1)} %get-tuple-element.15), channel_id=1, source_target_pairs={{0,2},{2,4},{4,6},{6,8},{8,10},{10,12},{12,14},{14,16},{16,18},{18... | collective-permute-start | bytes 589832 | tf_op jit(solution)/shard_map/ppermute | solution.py:34
  18.8 5.6 %collective-permute-start.2 = (bf16[4,24,8,128]{3,2,1,0:T(8,128)(2,1)S(1)}, bf16[4,24,8,128]{3,2,1,0:T(8,128)(2,1)S(1)}, u32[]{:S(2)}, u32[]{:S(2)}) collective-permute-start(bf16[4,24,8,128]{3,2,1,0:T(8,128)(2,1)S(1)} %get-tuple-element.16), channel_id=1, source_target_pairs={{2,0},{4,2},{6,4},{8,6},{10,8},{12,10},{14,12},{16,14},{18,16},{20... | collective-permute-start | bytes 589832 | tf_op jit(solution)/shard_map/ppermute | solution.py:35
Sparse Core Ops, SparseCore 0:
  95.9 52.7 all-gather.2
where the time goes:
time: 159 us
  waiting for transfers between devices  58.8 us (37%)
  blocking collectives  35.5 us (22%)
  Pallas kernels  34.5 us (22%)
  between operations  14.1 us (9%)
  starting transfers between devices  5.63 us (4%)
  other arithmetic  5.41 us (3%)
  local copies, waits for them, and re-layouts  4.7 us (3%)
    all_gather x1, waiting for transfers between devices, per_device(): whole = lax.all_gather(mine, AXES, axis=0)  52.9 us
    all_to_all x1, blocking collectives, per_device(): parts = lax.all_to_all(both, AXES, 0, 0, tiled=True)  35.5 us
    pallas_call x1, Pallas kernels, per_device(): pl.pallas_call(functools.partial(whole_kernel, channels, classes, east, n...  32.6 us
    ppermute x1, waiting for transfers between devices, halo_of(): lax.ppermute(lax.slice_in_dim(block, 0, width, axis=dim), axis, backward)  3.68 us
  transfers between devices with their start and end apart: 4, of which 3 were waited for; matrix products, arithmetic and copies ran while one was open for 0% of the time, Pallas kernels for 0%

commit v1 on v0

--- a/solution.py
+++ b/solution.py
@@ -12,7 +12,6 @@
 HALO = 4
 OFFSETS = 9
 WIDE = OFFSETS * LANES
-AXES = ("east", "north")
 F32 = jnp.float32
 BF16 = jnp.bfloat16
 
@@ -34,6 +33,51 @@
     low = lax.ppermute(lax.slice_in_dim(block, size - width, size, axis=dim), axis, forward)
     high = lax.ppermute(lax.slice_in_dim(block, 0, width, axis=dim), axis, backward)
     return low, high
+
+
+def exchange(value, axis, bit):
+    size = lax.axis_size(axis)
+    return lax.ppermute(value, axis, [(i, i ^ bit) for i in range(size)])
+
+
+def high_bit(axis, bit):
+    return (lax.axis_index(axis) // bit) % 2
+
+
+def bits_of(axis):
+    size = lax.axis_size(axis)
+    return [(axis, 1 << i) for i in range(size.bit_length() - 1)]
+
+
+def scatter_steps(values, orders):
+    for step in range(len(orders[0])):
+        sent = []
+        for value, order in zip(values, orders):
+            axis, bit = order[step]
+            half = value.shape[0] // 2
+            away = lax.dynamic_slice_in_dim(value, (1 - high_bit(axis, bit)) * half, half, 0)
+            sent.append(exchange(away.astype(BF16), axis, bit))
+        kept = []
+        for value, order, other in zip(values, orders, sent):
+            axis, bit = order[step]
+            half = value.shape[0] // 2
+            mine = lax.dynamic_slice_in_dim(value, high_bit(axis, bit) * half, half, 0)
+            kept.append(mine + other.astype(F32))
+        values = kept
+    return values
+
+
+def join(mine, other, axis, bit):
+    upper = high_bit(axis, bit) == 1
+    return jnp.concatenate([jnp.where(upper, other, mine), jnp.where(upper, mine, other)], 0)
+
+
+def gather_steps(values, orders):
+    for step in range(len(orders[0]) - 1, 0, -1):
+        others = [exchange(value, *order[step]) for value, order in zip(values, orders)]
+        values = [join(value, other, *order[step]) for value, other, order in zip(values, others, orders)]
+    others = [exchange(value, *order[0]) for value, order in zip(values, orders)]
+    return values, others
 
 
 def lane_of(shape):
@@ -129,10 +173,10 @@
     for t in range(0, 28, 4):
         for r in range(3):
             tail = pltpu.roll(blocks[t + 3], channels - spare * r, 1)
-            out_ref[row : row + channels, :] = jnp.where(lane < channels, blocks[t + r], tail).astype(BF16)
+            out_ref[row : row + channels, :] = jnp.where(lane < channels, blocks[t + r], tail)
             row += channels
     if row < out_ref.shape[0]:
-        out_ref[row:, :] = jnp.zeros((out_ref.shape[0] - row, LANES), BF16)
+        out_ref[row:, :] = jnp.zeros((out_ref.shape[0] - row, LANES), F32)
 
 
 def whole_kernel(
@@ -217,14 +261,25 @@
             out_ref[plane] = value[:, 0:channels].astype(BF16)
 
 
-def unpack_kernel(channels, scale, second_in, first_in, first_out, second_out):
+def unpack_kernel(channels, scale, upper_ref, second_mine, first_mine, second_other, first_other, first_out, second_out):
     spare = LANES - channels
-    for source, target in ((first_in, first_out), (second_in, second_out)):
+    half = first_mine.shape[0]
+    upper = upper_ref[0] == 1
+
+    def rows_of(mine, other, start):
+        pieces = []
+        for begin, stop in ((start, min(start + channels, half)), (max(start, half), start + channels)):
+            if begin < stop:
+                place = begin % half
+                picked = (mine[place : place + stop - begin, :], other[place : place + stop - begin, :])
+                if begin < half:
+                    picked = picked[::-1]
+                pieces.append(jnp.where(upper, *picked))
+        return (pieces[0] if len(pieces) == 1 else jnp.concatenate(pieces, 0)).astype(F32) * scale
+
+    for mine, other, target in ((first_mine, first_other, first_out), (second_mine, second_other, second_out)):
         for t in range(0, 27, 4):
-            tiles = [
-                source[(t // 4 * 3 + r) * channels : (t // 4 * 3 + r + 1) * channels, :].astype(F32) * scale
-                for r in range(3)
-            ]
+            tiles = [rows_of(mine, other, (t // 4 * 3 + r) * channels) for r in range(3)]
             for r in range(3):
                 target[t + r] = tiles[r][:, 0:channels]
             if t + 3 < 27:
@@ -273,8 +328,8 @@
         functools.partial(whole_kernel, channels, classes, east, north, upward),
         out_shape=(
             jax.ShapeDtypeStruct((east, north * upward, channels), BF16),
-            jax.ShapeDtypeStruct((packed, LANES), BF16),
-            jax.ShapeDtypeStruct((packed, LANES), BF16),
+            jax.ShapeDtypeStruct((packed, LANES), F32),
+            jax.ShapeDtypeStruct((packed, LANES), F32),
         ),
         in_specs=[vmem] * 4,
         out_specs=(vmem, vmem, vmem),
@@ -293,14 +348,14 @@
         name="fields",
     )(x, first_weights, second_weights, head_wide)
 
-    both = jnp.concatenate(
-        [second.reshape(devices, chunk, LANES), first.reshape(devices, chunk, LANES)], 1
+    east_bits, north_bits = bits_of("east"), bits_of("north")
+    orders = (
+        east_bits[:1] + north_bits + east_bits[1:],
+        east_bits[:2] + north_bits + east_bits[2:],
     )
-    parts = lax.all_to_all(both, AXES, 0, 0, tiled=True)
-    mine = jnp.sum(parts.astype(F32), 0).astype(BF16)
-    whole = lax.all_gather(mine, AXES, axis=0)
-    second = whole[:, :chunk].reshape(packed, LANES)
-    first = whole[:, chunk:].reshape(packed, LANES)
+    sums = scatter_steps((second, first), orders)
+    mine, others = gather_steps([total.astype(BF16) for total in sums], orders)
+    upper = high_bit(*east_bits[0]).reshape(1)
 
     grad_first, grad_second = pl.pallas_call(
         functools.partial(unpack_kernel, channels, scale),
@@ -308,11 +363,11 @@
             jax.ShapeDtypeStruct(first_weights.shape, F32),
             jax.ShapeDtypeStruct(second_weights.shape, F32),
         ),
-        in_specs=[vmem] * 2,
+        in_specs=[pl.BlockSpec(memory_space=pltpu.SMEM)] + [vmem] * 4,
         out_specs=(vmem, vmem),
         compiler_params=pltpu.CompilerParams(vmem_limit_bytes=32 * 1024 * 1024),
         name="unpack",
-    )(second, first)
+    )(upper, *mine, *others)
     grad_features = grad_features.reshape(east, north, upward, channels).transpose(3, 0, 1, 2)
     return (grad_features, grad_first, grad_second)
 

time: 159 us -> 105 us (0.66)
  waiting for transfers between devices: 58.8 us -> 20.6 us
  blocking collectives: 35.5 us -> 0 us
  starting transfers between devices: 5.63 us -> 39.2 us
  between operations: 14.1 us -> 0.96 us
    all_gather x1 -> x0, waiting for transfers between devices: 52.9 us -> none  [per_device(): whole = lax.all_gather(mine, AXES, axis=0)]
    all_to_all x1 -> x0, blocking collectives: 35.5 us -> none  [per_device(): parts = lax.all_to_all(both, AXES, 0, 0, tiled=True)]
    ppermute x0 -> x20, starting transfers between devices: none -> 33.6 us  [exchange(): return lax.ppermute(value, axis, [(i, i ^ bit) for i in range(size)])]
    ppermute x0 -> x20, waiting for transfers between devices: none -> 14.7 us  [exchange(): return lax.ppermute(value, axis, [(i, i ^ bit) for i in range(size)])]
    convert_element_type x0 -> x10, local copies, waits for them, and re-layouts: none -> 2.42 us  [scatter_steps(): sent.append(exchange(away.astype(BF16), axis, bit))]
  transfers between devices with their start and end apart: 4 -> 23, of which waited for: 3 -> 14; matrix products, arithmetic and copies ran while one was open for 0% -> 2% of each run, Pallas kernels for 0% -> 0%
where the time goes in v1:
time: 105 us
  starting transfers between devices  39.2 us (37%)
  Pallas kernels  34.6 us (33%)
  waiting for transfers between devices  20.6 us (20%)
  local copies, waits for them, and re-layouts  5.87 us (6%)
  other arithmetic  3.86 us (4%)
    ppermute x20, starting transfers between devices, exchange(): return lax.ppermute(value, axis, [(i, i ^ bit) for i in range(size)])  33.6 us
    pallas_call x1, Pallas kernels, per_device(): pl.pallas_call(functools.partial(whole_kernel, channels, classes, east, n...  32.6 us
    ppermute x20, waiting for transfers between devices, exchange(): return lax.ppermute(value, axis, [(i, i ^ bit) for i in range(size)])  14.7 us
    ppermute x1, waiting for transfers between devices, halo_of(): lax.ppermute(lax.slice_in_dim(block, 0, width, axis=dim), axis, backward)  3.66 us
    ppermute x1, starting transfers between devices, halo_of(): other = lax.ppermute(mine, axis, [(0, 1), (1, 0)])  3 us
    convert_element_type x10, local copies, waits for them, and re-layouts, scatter_steps(): sent.append(exchange(away.astype(BF16), axis, bit))  2.42 us
    ppermute x1, waiting for transfers between devices, halo_of(): other = lax.ppermute(mine, axis, [(0, 1), (1, 0)])  2.25 us
  transfers between devices with their start and end apart: 23, of which 14 were waited for; matrix products, arithmetic and copies ran while one was open for 2% of the time, Pallas kernels for 0%

profile of v1, /device:TPU:0, one launch (start us, length us, event | category | flops | bytes accessed | tf_op | source)
XLA Modules:
  0.0 105.1 jit_solution(15318941874624675535)
XLA Ops:
  5.2 3.0 %collective-permute-start = (bf16[8,4,8,128]{3,2,1,0:T(8,128)(2,1)S(1)}, bf16[8,4,8,128]{3,2,1,0:T(8,128)(2,1)S(1)}, u32[]{:S(2)}, u32[]{:S(2)}) collective-permute-start(bf16[8,4,8,128]{3,2,1,0:T(8,128)(2,1)S(1)} %fusion), channel_id=1, source_target_pairs={{0,1},{1,0},{2,3},{3,2},{4,5},{5,4},{6,7},{7,6},{8,9},{9,8},{10,11... | collective-permute-start | bytes 196616 | tf_op jit(solution)/shard_map/ppermute | solution.py:28
  8.2 2.2 %collective-permute-done = bf16[8,4,8,128]{3,2,1,0:T(8,128)(2,1)S(1)} collective-permute-done((bf16[8,4,8,128]{3,2,1,0:T(8,128)(2,1)S(1)}, bf16[8,4,8,128]{3,2,1,0:T(8,128)(2,1)S(1)}, u32[]{:S(2)}, u32[]{:S(2)}) %collective-permute-start) | collective-permute-done | bytes 65568 | tf_op jit(solution)/shard_map/ppermute | solution.py:28
  14.1 3.7 %collective-permute-done.2 = bf16[4,24,8,128]{3,2,1,0:T(8,128)(2,1)S(1)} collective-permute-done((bf16[4,24,8,128]{3,2,1,0:T(8,128)(2,1)S(1)}, bf16[4,24,8,128]{3,2,1,0:T(8,128)(2,1)S(1)}, u32[]{:S(2)}, u32[]{:S(2)}) %collective-permute-start.2) | collective-permute-done | bytes 196640 | tf_op jit(solution)/shard_map/ppermute | solution.py:34
  19.0 32.6 %fields.1 = (bf16[8,128,96]{2,1,0:T(8,128)(2,1)}, f32[2048,128]{1,0:T(8,128)}, f32[2048,128]{1,0:T(8,128)}) custom-call(bf16[16,192,128]{2,1,0:T(8,128)(2,1)} %maximum_bitcast_fusion.x_ref, bf16[27,96,96]{2,1,0:T(8,128)(2,1)} %w1_ref.1, bf16[27,96,96]{2,1,0:T(8,128)(2,1)} %w2_ref.1, bf16[128,128]{1,0:T(8,128)(2,1)} %pad.4.head_ref), custom_call_target="tpu_custom_call" | custom-call | tf_op jit(solution)/shard_map/fields/pallas_call | solution.py:327
  52.8 4.2 %collective-permute-start.12 = (bf16[1024,128]{1,0:T(8,128)(2,1)S(1)}, bf16[1024,128]{1,0:T(8,128)(2,1)S(1)}, u32[]{:S(2)}, u32[]{:S(2)}) collective-permute-start(bf16[1024,128]{1,0:T(8,128)(2,1)S(1)} %dynamic-slice_convert_fusion), channel_id=1, source_target_pairs={{0,2},{2,0},{4,6},{6,4},{8,10},{10,8},{12,14},{14,12},{16,18},{18,... | collective-permute-start | bytes 786440 | tf_op jit(solution)/shard_map/ppermute | solution.py:40
  58.4 2.5 %collective-permute-start.13 = (bf16[512,128]{1,0:T(8,128)(2,1)S(1)}, bf16[512,128]{1,0:T(8,128)(2,1)S(1)}, u32[]{:S(2)}, u32[]{:S(2)}) collective-permute-start(bf16[512,128]{1,0:T(8,128)(2,1)S(1)} %dynamic-slice_convert_fusion.2), channel_id=1, source_target_pairs={{0,4},{2,6},{4,0},{6,2},{8,12},{10,14},{12,8},{14,10},{16,20},{18,... | collective-permute-start | bytes 393224 | tf_op jit(solution)/shard_map/ppermute | solution.py:40
  61.0 1.6 %collective-permute-start.4 = (bf16[512,128]{1,0:T(8,128)(2,1)S(1)}, bf16[512,128]{1,0:T(8,128)(2,1)S(1)}, u32[]{:S(2)}, u32[]{:S(2)}) collective-permute-start(bf16[512,128]{1,0:T(8,128)(2,1)S(1)} %dynamic-slice_convert_fusion.3), channel_id=1, source_target_pairs={{0,1},{1,0},{2,3},{3,2},{4,5},{5,4},{6,7},{7,6},{8,9},{9,8},{10,11... | collective-permute-start | bytes 393224 | tf_op jit(solution)/shard_map/ppermute | solution.py:40
  62.6 2.3 %collective-permute-done.13 = bf16[512,128]{1,0:T(8,128)(2,1)S(1)} collective-permute-done((bf16[512,128]{1,0:T(8,128)(2,1)S(1)}, bf16[512,128]{1,0:T(8,128)(2,1)S(1)}, u32[]{:S(2)}, u32[]{:S(2)}) %collective-permute-start.13) | collective-permute-done | bytes 131104 | tf_op jit(solution)/shard_map/ppermute | solution.py:40
  65.0 1.6 %collective-permute-start.14 = (bf16[256,128]{1,0:T(8,128)(2,1)S(1)}, bf16[256,128]{1,0:T(8,128)(2,1)S(1)}, u32[]{:S(2)}, u32[]{:S(2)}) collective-permute-start(bf16[256,128]{1,0:T(8,128)(2,1)S(1)} %dynamic-slice_convert_fusion.4), channel_id=1, source_target_pairs={{0,1},{1,0},{2,3},{3,2},{4,5},{5,4},{6,7},{7,6},{8,9},{9,8},{10,11... | collective-permute-start | bytes 196616 | tf_op jit(solution)/shard_map/ppermute | solution.py:40
  66.6 1.8 %collective-permute-start.5 = (bf16[256,128]{1,0:T(8,128)(2,1)S(1)}, bf16[256,128]{1,0:T(8,128)(2,1)S(1)}, u32[]{:S(2)}, u32[]{:S(2)}) collective-permute-start(bf16[256,128]{1,0:T(8,128)(2,1)S(1)} %dynamic-slice_convert_fusion.5), channel_id=1, source_target_pairs={{0,4},{2,6},{4,0},{6,2},{8,12},{10,14},{12,8},{14,10},{16,20},{18,... | collective-permute-start | bytes 196616 | tf_op jit(solution)/shard_map/ppermute | solution.py:40
  69.4 1.6 %collective-permute-start.15 = (bf16[128,128]{1,0:T(8,128)(2,1)S(1)}, bf16[128,128]{1,0:T(8,128)(2,1)S(1)}, u32[]{:S(2)}, u32[]{:S(2)}) collective-permute-start(bf16[128,128]{1,0:T(8,128)(2,1)S(1)} %dynamic-slice_convert_fusion.6), channel_id=1, source_target_pairs={{0,8},{2,10},{4,12},{6,14},{8,0},{10,2},{12,4},{14,6},{16,24},{18,... | collective-permute-start | bytes 98312 | tf_op jit(solution)/shard_map/ppermute | solution.py:40
  71.0 1.6 %collective-permute-start.6 = (bf16[128,128]{1,0:T(8,128)(2,1)S(1)}, bf16[128,128]{1,0:T(8,128)(2,1)S(1)}, u32[]{:S(2)}, u32[]{:S(2)}) collective-permute-start(bf16[128,128]{1,0:T(8,128)(2,1)S(1)} %dynamic-slice_convert_fusion.7), channel_id=1, source_target_pairs={{0,8},{2,10},{4,12},{6,14},{8,0},{10,2},{12,4},{14,6},{16,24},{18,... | collective-permute-start | bytes 98312 | tf_op jit(solution)/shard_map/ppermute | solution.py:40
  73.4 2.7 %collective-permute-start.16 = (bf16[64,128]{1,0:T(8,128)(2,1)S(1)}, bf16[64,128]{1,0:T(8,128)(2,1)S(1)}, u32[]{:S(2)}, u32[]{:S(2)}) collective-permute-start(bf16[64,128]{1,0:T(8,128)(2,1)S(1)} %dynamic-slice_convert_fusion.8), channel_id=1, source_target_pairs={{0,16},{2,18},{4,20},{6,22},{8,24},{10,26},{12,28},{14,30},{16,0},... | collective-permute-start | bytes 49160 | tf_op jit(solution)/shard_map/ppermute | solution.py:40
  76.1 1.6 %collective-permute-start.7 = (bf16[64,128]{1,0:T(8,128)(2,1)S(1)}, bf16[64,128]{1,0:T(8,128)(2,1)S(1)}, u32[]{:S(2)}, u32[]{:S(2)}) collective-permute-start(bf16[64,128]{1,0:T(8,128)(2,1)S(1)} %dynamic-slice_convert_fusion.9), channel_id=1, source_target_pairs={{0,16},{2,18},{4,20},{6,22},{8,24},{10,26},{12,28},{14,30},{16,0},... | collective-permute-start | bytes 49160 | tf_op jit(solution)/shard_map/ppermute | solution.py:40
  78.1 2.7 %collective-permute-start.17 = (bf16[64,128]{1,0:T(8,128)(2,1)S(1)}, bf16[64,128]{1,0:T(8,128)(2,1)S(1)}, u32[]{:S(2)}, u32[]{:S(2)}) collective-permute-start(bf16[64,128]{1,0:T(8,128)(2,1)S(1)} %add_convert_fusion), channel_id=1, source_target_pairs={{0,16},{2,18},{4,20},{6,22},{8,24},{10,26},{12,28},{14,30},{16,0},... | collective-permute-start | bytes 49160 | tf_op jit(solution)/shard_map/ppermute | solution.py:40
  80.8 1.7 %collective-permute-start.8 = (bf16[64,128]{1,0:T(8,128)(2,1)S(1)}, bf16[64,128]{1,0:T(8,128)(2,1)S(1)}, u32[]{:S(2)}, u32[]{:S(2)}) collective-permute-start(bf16[64,128]{1,0:T(8,128)(2,1)S(1)} %add_convert_fusion.1), channel_id=1, source_target_pairs={{0,16},{2,18},{4,20},{6,22},{8,24},{10,26},{12,28},{14,30},{16,0},... | collective-permute-start | bytes 49160 | tf_op jit(solution)/shard_map/ppermute | solution.py:40
  82.8 1.6 %collective-permute-start.18 = (bf16[128,128]{1,0:T(8,128)(2,1)S(1)}, bf16[128,128]{1,0:T(8,128)(2,1)S(1)}, u32[]{:S(2)}, u32[]{:S(2)}) collective-permute-start(bf16[128,128]{1,0:T(8,128)(2,1)S(1)} %pad_maximum_fusion.8), channel_id=1, source_target_pairs={{0,8},{2,10},{4,12},{6,14},{8,0},{10,2},{12,4},{14,6},{16,24},{18,... | collective-permute-start | bytes 98312 | tf_op jit(solution)/shard_map/ppermute | solution.py:40
  86.8 2.7 %collective-permute-done.9 = bf16[128,128]{1,0:T(8,128)(2,1)S(1)} collective-permute-done((bf16[128,128]{1,0:T(8,128)(2,1)S(1)}, bf16[128,128]{1,0:T(8,128)(2,1)S(1)}, u32[]{:S(2)}, u32[]{:S(2)}) %collective-permute-start.9) | collective-permute-done | bytes 32800 | tf_op jit(solution)/shard_map/ppermute | solution.py:40
  89.5 2.2 %collective-permute-start.19 = (bf16[256,128]{1,0:T(8,128)(2,1)S(1)}, bf16[256,128]{1,0:T(8,128)(2,1)S(1)}, u32[]{:S(2)}, u32[]{:S(2)}) collective-permute-start(bf16[256,128]{1,0:T(8,128)(2,1)S(1)} %pad_maximum_fusion.6), channel_id=1, source_target_pairs={{0,1},{1,0},{2,3},{3,2},{4,5},{5,4},{6,7},{7,6},{8,9},{9,8},{10,11... | collective-permute-start | bytes 196616 | tf_op jit(solution)/shard_map/ppermute | solution.py:40
  94.0 2.3 %collective-permute-start.20 = (bf16[512,128]{1,0:T(8,128)(2,1)S(1)}, bf16[512,128]{1,0:T(8,128)(2,1)S(1)}, u32[]{:S(2)}, u32[]{:S(2)}) collective-permute-start(bf16[512,128]{1,0:T(8,128)(2,1)S(1)} %pad_maximum_fusion.4), channel_id=1, source_target_pairs={{0,4},{2,6},{4,0},{6,2},{8,12},{10,14},{12,8},{14,10},{16,20},{18,... | collective-permute-start | bytes 393224 | tf_op jit(solution)/shard_map/ppermute | solution.py:40
  97.5 1.7 %collective-permute-done.20 = bf16[512,128]{1,0:T(8,128)(2,1)S(1)} collective-permute-done((bf16[512,128]{1,0:T(8,128)(2,1)S(1)}, bf16[512,128]{1,0:T(8,128)(2,1)S(1)}, u32[]{:S(2)}, u32[]{:S(2)}) %collective-permute-start.20) | collective-permute-done | bytes 131104 | tf_op jit(solution)/shard_map/ppermute | solution.py:40
  99.4 2.0 %collective-permute-done.11 = bf16[512,128]{1,0:T(8,128)(2,1)S(1)} collective-permute-done((bf16[512,128]{1,0:T(8,128)(2,1)S(1)}, bf16[512,128]{1,0:T(8,128)(2,1)S(1)}, u32[]{:S(2)}, u32[]{:S(2)}) %collective-permute-start.11) | collective-permute-done | bytes 131104 | tf_op jit(solution)/shard_map/ppermute | solution.py:40
  101.5 1.5 %collective-permute-done.21.second_other = bf16[1024,128]{1,0:T(8,128)(2,1)S(1)} collective-permute-done((bf16[1024,128]{1,0:T(8,128)(2,1)S(1)}, bf16[1024,128]{1,0:T(8,128)(2,1)S(1)}, u32[]{:S(2)}, u32[]{:S(2)}) %collective-permute-start.21) | collective-permute-done | bytes 262176 | tf_op jit(solution)/shard_map/ppermute | solution.py:40
  103.1 2.0 %unpack.1 = (f32[27,96,96]{2,1,0:T(8,128)}, f32[27,96,96]{2,1,0:T(8,128)}) custom-call(s32[1]{0:T(128)} %bitcast.7.upper_ref, bf16[1024,128]{1,0:T(8,128)(2,1)S(1)} %pad_maximum_fusion.1.second_mine, bf16[1024,128]{1,0:T(8,128)(2,1)S(1)} %pad_maximum_fusion.2.first_mine, bf16[1024,128]{1,0:T(8,128)(2,1)S(1)} %collective-permute-done.21.second_other, ...), custom_call_target="tpu_custom_call" | custom-call | tf_op jit(solution)/shard_map/unpack/pallas_call | solution.py:360
  (79 shorter events, 20.9 us)
Async XLA Ops:
  0.6 9.8 %copy-start = (bf16[96,8,16,8]{0,3,2,1:T(8,128)(2,1)S(1)}, bf16[96,8,16,8]{0,3,2,1:T(8,128)(2,1)}, u32[]{:S(2)}) copy-start(bf16[96,8,16,8]{0,3,2,1:T(8,128)(2,1)} %param.7) | copy-start | bytes 589828
  5.2 5.2 %collective-permute-start = (bf16[8,4,8,128]{3,2,1,0:T(8,128)(2,1)S(1)}, bf16[8,4,8,128]{3,2,1,0:T(8,128)(2,1)S(1)}, u32[]{:S(2)}, u32[]{:S(2)}) collective-permute-start(bf16[8,4,8,128]{3,2,1,0:T(8,128)(2,1)S(1)} %fusion), channel_id=1, source_target_pairs={{0,1},{1,0},{2,3},{3,2},{4,5},{5,4},{6,7},{7,6},{8,9},{9,8},{10,11... | collective-permute-start | bytes 196616 | tf_op jit(solution)/shard_map/ppermute | solution.py:28
  10.9 3.3 %collective-permute-start.1 = (bf16[4,24,8,128]{3,2,1,0:T(8,128)(2,1)S(1)}, bf16[4,24,8,128]{3,2,1,0:T(8,128)(2,1)S(1)}, u32[]{:S(2)}, u32[]{:S(2)}) collective-permute-start(bf16[4,24,8,128]{3,2,1,0:T(8,128)(2,1)S(1)} %get-tuple-element.13), channel_id=1, source_target_pairs={{0,2},{2,4},{4,6},{6,8},{8,10},{10,12},{12,14},{14,16},{16,18},{18... | collective-permute-start | bytes 589832 | tf_op jit(solution)/shard_map/ppermute | solution.py:33
  12.2 5.6 %collective-permute-start.2 = (bf16[4,24,8,128]{3,2,1,0:T(8,128)(2,1)S(1)}, bf16[4,24,8,128]{3,2,1,0:T(8,128)(2,1)S(1)}, u32[]{:S(2)}, u32[]{:S(2)}) collective-permute-start(bf16[4,24,8,128]{3,2,1,0:T(8,128)(2,1)S(1)} %get-tuple-element.14), channel_id=1, source_target_pairs={{2,0},{4,2},{6,4},{8,6},{10,8},{12,10},{14,12},{16,14},{18,16},{20... | collective-permute-start | bytes 589832 | tf_op jit(solution)/shard_map/ppermute | solution.py:34
  52.8 5.5 %collective-permute-start.12 = (bf16[1024,128]{1,0:T(8,128)(2,1)S(1)}, bf16[1024,128]{1,0:T(8,128)(2,1)S(1)}, u32[]{:S(2)}, u32[]{:S(2)}) collective-permute-start(bf16[1024,128]{1,0:T(8,128)(2,1)S(1)} %dynamic-slice_convert_fusion), channel_id=1, source_target_pairs={{0,2},{2,0},{4,6},{6,4},{8,10},{10,8},{12,14},{14,12},{16,18},{18,... | collective-permute-start | bytes 786440 | tf_op jit(solution)/shard_map/ppermute | solution.py:40
  58.1 2.8 %collective-permute-start.3 = (bf16[1024,128]{1,0:T(8,128)(2,1)S(1)}, bf16[1024,128]{1,0:T(8,128)(2,1)S(1)}, u32[]{:S(2)}, u32[]{:S(2)}) collective-permute-start(bf16[1024,128]{1,0:T(8,128)(2,1)S(1)} %dynamic-slice_convert_fusion.1), channel_id=1, source_target_pairs={{0,2},{2,0},{4,6},{6,4},{8,10},{10,8},{12,14},{14,12},{16,18},{18,... | collective-permute-start | bytes 786440 | tf_op jit(solution)/shard_map/ppermute | solution.py:40
  58.4 6.5 %collective-permute-start.13 = (bf16[512,128]{1,0:T(8,128)(2,1)S(1)}, bf16[512,128]{1,0:T(8,128)(2,1)S(1)}, u32[]{:S(2)}, u32[]{:S(2)}) collective-permute-start(bf16[512,128]{1,0:T(8,128)(2,1)S(1)} %dynamic-slice_convert_fusion.2), channel_id=1, source_target_pairs={{0,4},{2,6},{4,0},{6,2},{8,12},{10,14},{12,8},{14,10},{16,20},{18,... | collective-permute-start | bytes 393224 | tf_op jit(solution)/shard_map/ppermute | solution.py:40
  61.0 5.5 %collective-permute-start.4 = (bf16[512,128]{1,0:T(8,128)(2,1)S(1)}, bf16[512,128]{1,0:T(8,128)(2,1)S(1)}, u32[]{:S(2)}, u32[]{:S(2)}) collective-permute-start(bf16[512,128]{1,0:T(8,128)(2,1)S(1)} %dynamic-slice_convert_fusion.3), channel_id=1, source_target_pairs={{0,1},{1,0},{2,3},{3,2},{4,5},{5,4},{6,7},{7,6},{8,9},{9,8},{10,11... | collective-permute-start | bytes 393224 | tf_op jit(solution)/shard_map/ppermute | solution.py:40
  65.0 4.3 %collective-permute-start.14 = (bf16[256,128]{1,0:T(8,128)(2,1)S(1)}, bf16[256,128]{1,0:T(8,128)(2,1)S(1)}, u32[]{:S(2)}, u32[]{:S(2)}) collective-permute-start(bf16[256,128]{1,0:T(8,128)(2,1)S(1)} %dynamic-slice_convert_fusion.4), channel_id=1, source_target_pairs={{0,1},{1,0},{2,3},{3,2},{4,5},{5,4},{6,7},{7,6},{8,9},{9,8},{10,11... | collective-permute-start | bytes 196616 | tf_op jit(solution)/shard_map/ppermute | solution.py:40
  66.6 4.4 %collective-permute-start.5 = (bf16[256,128]{1,0:T(8,128)(2,1)S(1)}, bf16[256,128]{1,0:T(8,128)(2,1)S(1)}, u32[]{:S(2)}, u32[]{:S(2)}) collective-permute-start(bf16[256,128]{1,0:T(8,128)(2,1)S(1)} %dynamic-slice_convert_fusion.5), channel_id=1, source_target_pairs={{0,4},{2,6},{4,0},{6,2},{8,12},{10,14},{12,8},{14,10},{16,20},{18,... | collective-permute-start | bytes 196616 | tf_op jit(solution)/shard_map/ppermute | solution.py:40
  69.4 4.0 %collective-permute-start.15 = (bf16[128,128]{1,0:T(8,128)(2,1)S(1)}, bf16[128,128]{1,0:T(8,128)(2,1)S(1)}, u32[]{:S(2)}, u32[]{:S(2)}) collective-permute-start(bf16[128,128]{1,0:T(8,128)(2,1)S(1)} %dynamic-slice_convert_fusion.6), channel_id=1, source_target_pairs={{0,8},{2,10},{4,12},{6,14},{8,0},{10,2},{12,4},{14,6},{16,24},{18,... | collective-permute-start | bytes 98312 | tf_op jit(solution)/shard_map/ppermute | solution.py:40
  71.0 5.0 %collective-permute-start.6 = (bf16[128,128]{1,0:T(8,128)(2,1)S(1)}, bf16[128,128]{1,0:T(8,128)(2,1)S(1)}, u32[]{:S(2)}, u32[]{:S(2)}) collective-permute-start(bf16[128,128]{1,0:T(8,128)(2,1)S(1)} %dynamic-slice_convert_fusion.7), channel_id=1, source_target_pairs={{0,8},{2,10},{4,12},{6,14},{8,0},{10,2},{12,4},{14,6},{16,24},{18,... | collective-permute-start | bytes 98312 | tf_op jit(solution)/shard_map/ppermute | solution.py:40
  73.4 4.7 %collective-permute-start.16 = (bf16[64,128]{1,0:T(8,128)(2,1)S(1)}, bf16[64,128]{1,0:T(8,128)(2,1)S(1)}, u32[]{:S(2)}, u32[]{:S(2)}) collective-permute-start(bf16[64,128]{1,0:T(8,128)(2,1)S(1)} %dynamic-slice_convert_fusion.8), channel_id=1, source_target_pairs={{0,16},{2,18},{4,20},{6,22},{8,24},{10,26},{12,28},{14,30},{16,0},... | collective-permute-start | bytes 49160 | tf_op jit(solution)/shard_map/ppermute | solution.py:40
  76.1 4.7 %collective-permute-start.7 = (bf16[64,128]{1,0:T(8,128)(2,1)S(1)}, bf16[64,128]{1,0:T(8,128)(2,1)S(1)}, u32[]{:S(2)}, u32[]{:S(2)}) collective-permute-start(bf16[64,128]{1,0:T(8,128)(2,1)S(1)} %dynamic-slice_convert_fusion.9), channel_id=1, source_target_pairs={{0,16},{2,18},{4,20},{6,22},{8,24},{10,26},{12,28},{14,30},{16,0},... | collective-permute-start | bytes 49160 | tf_op jit(solution)/shard_map/ppermute | solution.py:40
  78.1 4.7 %collective-permute-start.17 = (bf16[64,128]{1,0:T(8,128)(2,1)S(1)}, bf16[64,128]{1,0:T(8,128)(2,1)S(1)}, u32[]{:S(2)}, u32[]{:S(2)}) collective-permute-start(bf16[64,128]{1,0:T(8,128)(2,1)S(1)} %add_convert_fusion), channel_id=1, source_target_pairs={{0,16},{2,18},{4,20},{6,22},{8,24},{10,26},{12,28},{14,30},{16,0},... | collective-permute-start | bytes 49160 | tf_op jit(solution)/shard_map/ppermute | solution.py:40
  80.8 4.7 %collective-permute-start.8 = (bf16[64,128]{1,0:T(8,128)(2,1)S(1)}, bf16[64,128]{1,0:T(8,128)(2,1)S(1)}, u32[]{:S(2)}, u32[]{:S(2)}) collective-permute-start(bf16[64,128]{1,0:T(8,128)(2,1)S(1)} %add_convert_fusion.1), channel_id=1, source_target_pairs={{0,16},{2,18},{4,20},{6,22},{8,24},{10,26},{12,28},{14,30},{16,0},... | collective-permute-start | bytes 49160 | tf_op jit(solution)/shard_map/ppermute | solution.py:40
  82.8 4.0 %collective-permute-start.18 = (bf16[128,128]{1,0:T(8,128)(2,1)S(1)}, bf16[128,128]{1,0:T(8,128)(2,1)S(1)}, u32[]{:S(2)}, u32[]{:S(2)}) collective-permute-start(bf16[128,128]{1,0:T(8,128)(2,1)S(1)} %pad_maximum_fusion.8), channel_id=1, source_target_pairs={{0,8},{2,10},{4,12},{6,14},{8,0},{10,2},{12,4},{14,6},{16,24},{18,... | collective-permute-start | bytes 98312 | tf_op jit(solution)/shard_map/ppermute | solution.py:40
  85.5 4.0 %collective-permute-start.9 = (bf16[128,128]{1,0:T(8,128)(2,1)S(1)}, bf16[128,128]{1,0:T(8,128)(2,1)S(1)}, u32[]{:S(2)}, u32[]{:S(2)}) collective-permute-start(bf16[128,128]{1,0:T(8,128)(2,1)S(1)} %pad_maximum_fusion.7), channel_id=1, source_target_pairs={{0,8},{2,10},{4,12},{6,14},{8,0},{10,2},{12,4},{14,6},{16,24},{18,... | collective-permute-start | bytes 98312 | tf_op jit(solution)/shard_map/ppermute | solution.py:40
  89.5 4.5 %collective-permute-start.19 = (bf16[256,128]{1,0:T(8,128)(2,1)S(1)}, bf16[256,128]{1,0:T(8,128)(2,1)S(1)}, u32[]{:S(2)}, u32[]{:S(2)}) collective-permute-start(bf16[256,128]{1,0:T(8,128)(2,1)S(1)} %pad_maximum_fusion.6), channel_id=1, source_target_pairs={{0,1},{1,0},{2,3},{3,2},{4,5},{5,4},{6,7},{7,6},{8,9},{9,8},{10,11... | collective-permute-start | bytes 196616 | tf_op jit(solution)/shard_map/ppermute | solution.py:40
  91.7 4.5 %collective-permute-start.10 = (bf16[256,128]{1,0:T(8,128)(2,1)S(1)}, bf16[256,128]{1,0:T(8,128)(2,1)S(1)}, u32[]{:S(2)}, u32[]{:S(2)}) collective-permute-start(bf16[256,128]{1,0:T(8,128)(2,1)S(1)} %pad_maximum_fusion.5), channel_id=1, source_target_pairs={{0,4},{2,6},{4,0},{6,2},{8,12},{10,14},{12,8},{14,10},{16,20},{18,... | collective-permute-start | bytes 196616 | tf_op jit(solution)/shard_map/ppermute | solution.py:40
  94.0 5.2 %collective-permute-start.20 = (bf16[512,128]{1,0:T(8,128)(2,1)S(1)}, bf16[512,128]{1,0:T(8,128)(2,1)S(1)}, u32[]{:S(2)}, u32[]{:S(2)}) collective-permute-start(bf16[512,128]{1,0:T(8,128)(2,1)S(1)} %pad_maximum_fusion.4), channel_id=1, source_target_pairs={{0,4},{2,6},{4,0},{6,2},{8,12},{10,14},{12,8},{14,10},{16,20},{18,... | collective-permute-start | bytes 393224 | tf_op jit(solution)/shard_map/ppermute | solution.py:40
  96.3 5.0 %collective-permute-start.11 = (bf16[512,128]{1,0:T(8,128)(2,1)S(1)}, bf16[512,128]{1,0:T(8,128)(2,1)S(1)}, u32[]{:S(2)}, u32[]{:S(2)}) collective-permute-start(bf16[512,128]{1,0:T(8,128)(2,1)S(1)} %pad_maximum_fusion.3), channel_id=1, source_target_pairs={{0,1},{1,0},{2,3},{3,2},{4,5},{5,4},{6,7},{7,6},{8,9},{9,8},{10,11... | collective-permute-start | bytes 393224 | tf_op jit(solution)/shard_map/ppermute | solution.py:40
  99.3 2.2 %collective-permute-start.22 = (bf16[1024,128]{1,0:T(8,128)(2,1)S(1)}, bf16[1024,128]{1,0:T(8,128)(2,1)S(1)}, u32[]{:S(2)}, u32[]{:S(2)}) collective-permute-start(bf16[1024,128]{1,0:T(8,128)(2,1)S(1)} %pad_maximum_fusion.2.first_mine), channel_id=1, source_target_pairs={{0,2},{2,0},{4,6},{6,4},{8,10},{10,8},{12,14},{14,12},{16,18},{18,... | collective-permute-start | bytes 786440 | tf_op jit(solution)/shard_map/ppermute | solution.py:40
  101.5 1.6 %collective-permute-start.21 = (bf16[1024,128]{1,0:T(8,128)(2,1)S(1)}, bf16[1024,128]{1,0:T(8,128)(2,1)S(1)}, u32[]{:S(2)}, u32[]{:S(2)}) collective-permute-start(bf16[1024,128]{1,0:T(8,128)(2,1)S(1)} %pad_maximum_fusion.1.second_mine), channel_id=1, source_target_pairs={{0,2},{2,0},{4,6},{6,4},{8,10},{10,8},{12,14},{14,12},{16,18},{18,... | collective-permute-start | bytes 786440 | tf_op jit(solution)/shard_map/ppermute | solution.py:40
  (3 other events, 24.4 us)

commit v2 on v0

--- a/solution.py
+++ b/solution.py
@@ -12,7 +12,6 @@
 HALO = 4
 OFFSETS = 9
 WIDE = OFFSETS * LANES
-AXES = ("east", "north")
 F32 = jnp.float32
 BF16 = jnp.bfloat16
 
@@ -36,6 +35,39 @@
     return low, high
 
 
+def exchange(value, axis, bit):
+    size = lax.axis_size(axis)
+    return lax.ppermute(value, axis, [(i, i ^ bit) for i in range(size)])
+
+
+def high_bit(axis, bit):
+    return (lax.axis_index(axis) // bit) % 2
+
+
+def bits_of(axis):
+    size = lax.axis_size(axis)
+    return [(axis, 1 << i) for i in range(size.bit_length() - 1)]
+
+
+def scatter_steps(kept, sent, order):
+    for step, (axis, bit) in enumerate(order):
+        total = kept + exchange(sent, axis, bit).astype(F32)
+        if step + 1 < len(order):
+            upper = high_bit(*order[step + 1])
+            half = total.shape[0] // 2
+            sent = lax.dynamic_slice_in_dim(total, (1 - upper) * half, half, 0).astype(BF16)
+            kept = lax.dynamic_slice_in_dim(total, upper * half, half, 0)
+    return total
+
+
+def gather_steps(mine, order):
+    for axis, bit in order[:0:-1]:
+        other = exchange(mine, axis, bit)
+        upper = high_bit(axis, bit) == 1
+        mine = jnp.concatenate([jnp.where(upper, other, mine), jnp.where(upper, mine, other)], 0)
+    return mine, exchange(mine, *order[0])
+
+
 def lane_of(shape):
     return lax.broadcasted_iota(jnp.int32, shape, len(shape) - 1)
 
@@ -103,7 +135,7 @@
             turned_ref[d * channels : (d + 1) * channels, e * size : (e + 1) * size] = turned
 
 
-def kernel_sum(turned_ref, stack_ref, first, east, rows, low, size, channels, out_ref):
+def kernel_sum(turned_ref, stack_ref, first, east, rows, low, size, channels):
     total = None
     for i in range(east // 2):
         fields = []
@@ -125,20 +157,18 @@
     blocks.append(jnp.zeros_like(blocks[0]))
     lane = lane_of(blocks[0].shape)
     spare = LANES - channels
-    row = 0
+    tiles = []
     for t in range(0, 28, 4):
         for r in range(3):
             tail = pltpu.roll(blocks[t + 3], channels - spare * r, 1)
-            out_ref[row : row + channels, :] = jnp.where(lane < channels, blocks[t + r], tail).astype(BF16)
-            row += channels
-    if row < out_ref.shape[0]:
-        out_ref[row:, :] = jnp.zeros((out_ref.shape[0] - row, LANES), BF16)
+            tiles.append(jnp.where(lane < channels, blocks[t + r], tail))
+    return tiles
 
 
 def whole_kernel(
     channels, classes, east, north, upward,
-    x_ref, w1_ref, w2_ref, head_ref,
-    out_ref, second_ref, first_ref,
+    upper_ref, x_ref, w1_ref, w2_ref, head_ref,
+    grad_ref, kept_ref, sent_ref,
     s0_ref, s1_ref, sg_ref, mask_ref, slope_ref, acc_ref, wt_ref, wb_ref, turned_ref,
 ):
     rows = (north + 2 * HALO) * upward
@@ -196,35 +226,60 @@
             put_stack(g_p2, rows, upward, sg_ref, parity, i)
             put_turned(turned_ref, g_p2[low : low + size], plane - 2, east, channels)
 
-    kernel_sum(turned_ref, s1_ref, 3, east, rows, low, size, channels, second_ref)
+    upper = upper_ref[0] == 1
+    for t, tile in enumerate(kernel_sum(turned_ref, s1_ref, 3, east, rows, low, size, channels)):
+        kept_ref[t * channels : (t + 1) * channels, :] = tile
     convolve(sg_ref, wb_ref, (planes - 6) // 2, rows, acc_ref, False)
-    put_backward(wb_ref, w1_ref, channels)
 
     for i in range((planes - 6) // 2):
         for parity in range(2):
             plane = 2 * i + parity
             g_p1 = slope_ref[plane + 2] * acc_ref[i * rows : (i + 1) * rows, parity * LANES : (parity + 1) * LANES]
-            put_stack(g_p1, rows, upward, sg_ref, parity, i)
+            grad_ref[plane] = g_p1.astype(BF16)
             put_turned(turned_ref, g_p1[low : low + size], plane - 1, east, channels)
 
-    kernel_sum(turned_ref, s0_ref, 4, east, rows, low, size, channels, first_ref)
-    convolve(sg_ref, wb_ref, east // 2, rows, acc_ref, False)
+    tiles = kernel_sum(turned_ref, s0_ref, 4, east, rows, low, size, channels)
+    for t, first in enumerate(tiles):
+        place = slice(t * channels, (t + 1) * channels)
+        second = kept_ref[place, :]
+        sent_ref[place, :] = jnp.where(upper, second, first).astype(BF16)
+        kept_ref[place, :] = jnp.where(upper, first, second)
+    filled = len(tiles) * channels
+    if filled < kept_ref.shape[0]:
+        kept_ref[filled:, :] = jnp.zeros((kept_ref.shape[0] - filled, LANES), F32)
+        sent_ref[filled:, :] = jnp.zeros((kept_ref.shape[0] - filled, LANES), BF16)
+
+
+def last_kernel(channels, east, north, upward, x_ref, grad_ref, w1_ref, out_ref, stack_ref, wb_ref, acc_ref):
+    rows = (north + 2 * HALO) * upward
+    low, size = HALO * upward, north * upward
+    put_backward(wb_ref, w1_ref, channels)
+
+    def start(i, carry):
+        for parity in range(2):
+            put_stack(grad_ref[2 * i + parity].astype(F32), rows, upward, stack_ref, parity, i)
+        return carry
+
+    lax.fori_loop(0, east // 2 + 1, start, 0)
+    convolve(stack_ref, wb_ref, east // 2, rows, acc_ref, False)
     for i in range(east // 2):
         for parity in range(2):
             plane = 2 * i + parity
             value = acc_ref[i * rows + low : i * rows + low + size, parity * LANES : (parity + 1) * LANES]
-            value = mask_ref[plane + HALO, low : low + size] * value
-            out_ref[plane] = value[:, 0:channels].astype(BF16)
-
-
-def unpack_kernel(channels, scale, second_in, first_in, first_out, second_out):
+            mask = x_ref[plane + HALO, low : low + size, channels : channels + 1].astype(F32)
+            out_ref[plane] = (mask * value)[:, 0:channels].astype(BF16)
+
+
+def unpack_kernel(channels, scale, upper_ref, mine_ref, other_ref, first_out, second_out):
     spare = LANES - channels
-    for source, target in ((first_in, first_out), (second_in, second_out)):
+    upper = upper_ref[0] == 1
+    for target, here in ((first_out, upper), (second_out, jnp.logical_not(upper))):
         for t in range(0, 27, 4):
-            tiles = [
-                source[(t // 4 * 3 + r) * channels : (t // 4 * 3 + r + 1) * channels, :].astype(F32) * scale
-                for r in range(3)
-            ]
+            tiles = []
+            for r in range(3):
+                start = (t // 4 * 3 + r) * channels
+                place = slice(start, start + channels)
+                tiles.append(jnp.where(here, mine_ref[place, :], other_ref[place, :]).astype(F32) * scale)
             for r in range(3):
                 target[t + r] = tiles[r][:, 0:channels]
             if t + 3 < 27:
@@ -266,17 +321,21 @@
     x = x.reshape(planes, rows, LANES)
     head_wide = jnp.pad(head, ((channels + 1, LANES - channels - 1 - classes), (0, LANES - channels)))
 
-    chunk = -(-21 * channels // (devices * 16)) * 16
-    packed = chunk * devices
+    east_bits, north_bits = bits_of("east"), bits_of("north")
+    order = east_bits[:1] + north_bits + east_bits[1:]
+    upper = high_bit(*order[0]).reshape(1)
+    unit = devices // 2 * 16
+    packed = -(-21 * channels // unit) * unit
     vmem = pl.BlockSpec(memory_space=pltpu.VMEM)
-    grad_features, second, first = pl.pallas_call(
+    smem = pl.BlockSpec(memory_space=pltpu.SMEM)
+    grad, kept, sent = pl.pallas_call(
         functools.partial(whole_kernel, channels, classes, east, north, upward),
         out_shape=(
-            jax.ShapeDtypeStruct((east, north * upward, channels), BF16),
-            jax.ShapeDtypeStruct((packed, LANES), BF16),
+            jax.ShapeDtypeStruct((east + 2, rows, LANES), BF16),
+            jax.ShapeDtypeStruct((packed, LANES), F32),
             jax.ShapeDtypeStruct((packed, LANES), BF16),
         ),
-        in_specs=[vmem] * 4,
+        in_specs=[smem] + [vmem] * 4,
         out_specs=(vmem, vmem, vmem),
         scratch_shapes=[
             pltpu.VMEM((2, planes // 2 * rows, WIDE), BF16),
@@ -291,28 +350,35 @@
         ],
         compiler_params=pltpu.CompilerParams(vmem_limit_bytes=56 * 1024 * 1024),
         name="fields",
-    )(x, first_weights, second_weights, head_wide)
-
-    both = jnp.concatenate(
-        [second.reshape(devices, chunk, LANES), first.reshape(devices, chunk, LANES)], 1
-    )
-    parts = lax.all_to_all(both, AXES, 0, 0, tiled=True)
-    mine = jnp.sum(parts.astype(F32), 0).astype(BF16)
-    whole = lax.all_gather(mine, AXES, axis=0)
-    second = whole[:, :chunk].reshape(packed, LANES)
-    first = whole[:, chunk:].reshape(packed, LANES)
-
+    )(upper, x, first_weights, second_weights, head_wide)
+
+    grad_features = pl.pallas_call(
+        functools.partial(last_kernel, channels, east, north, upward),
+        out_shape=jax.ShapeDtypeStruct((east, north * upward, channels), BF16),
+        in_specs=[vmem] * 3,
+        out_specs=vmem,
+        scratch_shapes=[
+            pltpu.VMEM((2, (east + 2) // 2 * rows, WIDE), BF16),
+            pltpu.VMEM((4, WIDE, 2 * LANES), BF16),
+            pltpu.VMEM((east // 2 * rows, 2 * LANES), F32),
+        ],
+        compiler_params=pltpu.CompilerParams(vmem_limit_bytes=32 * 1024 * 1024),
+        name="features",
+    )(x, grad, first_weights)
+
+    total = scatter_steps(kept, sent, order)
+    mine, other = gather_steps(total.astype(BF16), order)
     grad_first, grad_second = pl.pallas_call(
         functools.partial(unpack_kernel, channels, scale),
         out_shape=(
             jax.ShapeDtypeStruct(first_weights.shape, F32),
             jax.ShapeDtypeStruct(second_weights.shape, F32),
         ),
-        in_specs=[vmem] * 2,
+        in_specs=[smem] + [vmem] * 2,
         out_specs=(vmem, vmem),
         compiler_params=pltpu.CompilerParams(vmem_limit_bytes=32 * 1024 * 1024),
         name="unpack",
-    )(second, first)
+    )(upper, mine, other)
     grad_features = grad_features.reshape(east, north, upward, channels).transpose(3, 0, 1, 2)
     return (grad_features, grad_first, grad_second)
 

time: 159 us -> 105 us (0.66)
  blocking collectives: 35.5 us -> 0 us
  waiting for transfers between devices: 58.8 us -> 35.3 us
  starting transfers between devices: 5.63 us -> 26.5 us
  between operations: 14.1 us -> 0.9 us
    all_gather x1 -> x0, waiting for transfers between devices: 52.9 us -> none  [per_device(): whole = lax.all_gather(mine, AXES, axis=0)]
    all_to_all x1 -> x0, blocking collectives: 35.5 us -> none  [per_device(): parts = lax.all_to_all(both, AXES, 0, 0, tiled=True)]
    ppermute x0 -> x10, waiting for transfers between devices: none -> 29.3 us  [exchange(): return lax.ppermute(value, axis, [(i, i ^ bit) for i in range(size)])]
    ppermute x0 -> x10, starting transfers between devices: none -> 20.9 us  [exchange(): return lax.ppermute(value, axis, [(i, i ^ bit) for i in range(size)])]
    pallas_call x1, Pallas kernels: 32.6 us -> 27.2 us  [per_device(): pl.pallas_call(functools.partial(whole_kernel, channels, classes, east, n...]
    pallas_call x0 -> x1, Pallas kernels: none -> 3.81 us  [per_device(): pl.pallas_call(functools.partial(last_kernel, channels, east, north, upwa...]
  transfers between devices with their start and end apart: 4 -> 13, of which waited for: 3 -> 11; matrix products, arithmetic and copies ran while one was open for 0% -> 1% of each run, Pallas kernels for 0% -> 4%
where the time goes in v2:
time: 105 us; the launch traced here: 104 us
  waiting for transfers between devices  35.3 us (34%)
  Pallas kernels  33 us (31%)
  starting transfers between devices  26.5 us (25%)
  other arithmetic  5.03 us (5%)
  local copies, waits for them, and re-layouts  3.56 us (3%)
    ppermute x10, waiting for transfers between devices, exchange(): return lax.ppermute(value, axis, [(i, i ^ bit) for i in range(size)])  29.3 us
    pallas_call x1, Pallas kernels, per_device(): pl.pallas_call(functools.partial(whole_kernel, channels, classes, east, n...  27.2 us
    ppermute x10, starting transfers between devices, exchange(): return lax.ppermute(value, axis, [(i, i ^ bit) for i in range(size)])  20.9 us
    pallas_call x1, Pallas kernels, per_device(): pl.pallas_call(functools.partial(last_kernel, channels, east, north, upwa...  3.81 us
    ppermute x1, waiting for transfers between devices, halo_of(): lax.ppermute(lax.slice_in_dim(block, 0, width, axis=dim), axis, backward)  3.66 us
    ppermute x1, starting transfers between devices, halo_of(): other = lax.ppermute(mine, axis, [(0, 1), (1, 0)])  3 us
    ppermute x1, waiting for transfers between devices, halo_of(): other = lax.ppermute(mine, axis, [(0, 1), (1, 0)])  2.25 us
  transfers between devices with their start and end apart: 13, of which 11 were waited for; matrix products, arithmetic and copies ran while one was open for 1% of the time, Pallas kernels for 4%

profile of v2, /device:TPU:0, one launch (start us, length us, event | category | flops | bytes accessed | tf_op | source)
XLA Modules:
  0.0 104.3 jit_solution(10308250347881400516)
XLA Ops:
  5.2 3.0 %collective-permute-start = (bf16[8,4,8,128]{3,2,1,0:T(8,128)(2,1)S(1)}, bf16[8,4,8,128]{3,2,1,0:T(8,128)(2,1)S(1)}, u32[]{:S(2)}, u32[]{:S(2)}) collective-permute-start(bf16[8,4,8,128]{3,2,1,0:T(8,128)(2,1)S(1)} %fusion), channel_id=1, source_target_pairs={{0,1},{1,0},{2,3},{3,2},{4,5},{5,4},{6,7},{7,6},{8,9},{9,8},{10,11... | collective-permute-start | bytes 196616 | tf_op jit(solution)/shard_map/ppermute | solution.py:28
  8.2 2.2 %collective-permute-done = bf16[8,4,8,128]{3,2,1,0:T(8,128)(2,1)S(1)} collective-permute-done((bf16[8,4,8,128]{3,2,1,0:T(8,128)(2,1)S(1)}, bf16[8,4,8,128]{3,2,1,0:T(8,128)(2,1)S(1)}, u32[]{:S(2)}, u32[]{:S(2)}) %collective-permute-start) | collective-permute-done | bytes 65568 | tf_op jit(solution)/shard_map/ppermute | solution.py:28
  14.1 3.7 %collective-permute-done.2 = bf16[4,24,8,128]{3,2,1,0:T(8,128)(2,1)S(1)} collective-permute-done((bf16[4,24,8,128]{3,2,1,0:T(8,128)(2,1)S(1)}, bf16[4,24,8,128]{3,2,1,0:T(8,128)(2,1)S(1)}, u32[]{:S(2)}, u32[]{:S(2)}) %collective-permute-start.2) | collective-permute-done | bytes 196640 | tf_op jit(solution)/shard_map/ppermute | solution.py:34
  19.0 27.2 %fields.1 = (bf16[10,192,128]{2,1,0:T(8,128)(2,1)}, f32[2048,128]{1,0:T(8,128)}, bf16[2048,128]{1,0:T(8,128)(2,1)}) custom-call(s32[1]{0:T(128)} %bitcast.5.upper_ref, bf16[16,192,128]{2,1,0:T(8,128)(2,1)} %maximum_bitcast_fusion.x_ref, bf16[27,96,96]{2,1,0:T(8,128)(2,1)} %w1_ref.3, bf16[27,96,96]{2,1,0:T(8,128)(2,1)} %w2_ref.1, bf16[128,128]{1,0:T(8,128)(2,1)} %pad.4.head_ref), custom_call_target="tpu_custom_call" | custom-call | tf_op jit(solution)/shard_map/fields/pallas_call | solution.py:331
  46.2 4.2 %collective-permute-start.3 = (bf16[2048,128]{1,0:T(8,128)(2,1)}, bf16[2048,128]{1,0:T(8,128)(2,1)S(1)}, u32[]{:S(2)}, u32[]{:S(2)}) collective-permute-start(bf16[2048,128]{1,0:T(8,128)(2,1)} %get-tuple-element.10), channel_id=1, source_target_pairs={{0,2},{2,0},{4,6},{6,4},{8,10},{10,8},{12,14},{14,12},{16,18},{18,... | collective-permute-start | bytes 1572872 | tf_op jit(solution)/shard_map/ppermute | solution.py:40
  50.4 1.7 %collective-permute-done.3 = bf16[2048,128]{1,0:T(8,128)(2,1)S(1)} collective-permute-done((bf16[2048,128]{1,0:T(8,128)(2,1)}, bf16[2048,128]{1,0:T(8,128)(2,1)S(1)}, u32[]{:S(2)}, u32[]{:S(2)}) %collective-permute-start.3) | collective-permute-done | bytes 524320 | tf_op jit(solution)/shard_map/ppermute | solution.py:40
  53.5 1.6 %collective-permute-start.4 = (bf16[1024,128]{1,0:T(8,128)(2,1)S(1)}, bf16[1024,128]{1,0:T(8,128)(2,1)S(1)}, u32[]{:S(2)}, u32[]{:S(2)}) collective-permute-start(bf16[1024,128]{1,0:T(8,128)(2,1)S(1)} %dynamic-slice_convert_fusion), channel_id=1, source_target_pairs={{0,1},{1,0},{2,3},{3,2},{4,5},{5,4},{6,7},{7,6},{8,9},{9,8},{10,11... | collective-permute-start | bytes 786440 | tf_op jit(solution)/shard_map/ppermute | solution.py:40
  55.0 7.1 %collective-permute-done.4 = bf16[1024,128]{1,0:T(8,128)(2,1)S(1)} collective-permute-done((bf16[1024,128]{1,0:T(8,128)(2,1)S(1)}, bf16[1024,128]{1,0:T(8,128)(2,1)S(1)}, u32[]{:S(2)}, u32[]{:S(2)}) %collective-permute-start.4) | collective-permute-done | bytes 262176 | tf_op jit(solution)/shard_map/ppermute | solution.py:40
  62.2 2.5 %collective-permute-start.5 = (bf16[512,128]{1,0:T(8,128)(2,1)S(1)}, bf16[512,128]{1,0:T(8,128)(2,1)S(1)}, u32[]{:S(2)}, u32[]{:S(2)}) collective-permute-start(bf16[512,128]{1,0:T(8,128)(2,1)S(1)} %dynamic-slice_convert_fusion.1), channel_id=1, source_target_pairs={{0,4},{2,6},{4,0},{6,2},{8,12},{10,14},{12,8},{14,10},{16,20},{18,... | collective-permute-start | bytes 393224 | tf_op jit(solution)/shard_map/ppermute | solution.py:40
  64.7 3.2 %collective-permute-done.5 = bf16[512,128]{1,0:T(8,128)(2,1)S(1)} collective-permute-done((bf16[512,128]{1,0:T(8,128)(2,1)S(1)}, bf16[512,128]{1,0:T(8,128)(2,1)S(1)}, u32[]{:S(2)}, u32[]{:S(2)}) %collective-permute-start.5) | collective-permute-done | bytes 131104 | tf_op jit(solution)/shard_map/ppermute | solution.py:40
  68.0 1.6 %collective-permute-start.6 = (bf16[256,128]{1,0:T(8,128)(2,1)S(1)}, bf16[256,128]{1,0:T(8,128)(2,1)S(1)}, u32[]{:S(2)}, u32[]{:S(2)}) collective-permute-start(bf16[256,128]{1,0:T(8,128)(2,1)S(1)} %dynamic-slice_convert_fusion.2), channel_id=1, source_target_pairs={{0,8},{2,10},{4,12},{6,14},{8,0},{10,2},{12,4},{14,6},{16,24},{18,... | collective-permute-start | bytes 196616 | tf_op jit(solution)/shard_map/ppermute | solution.py:40
  69.6 2.7 %collective-permute-done.6 = bf16[256,128]{1,0:T(8,128)(2,1)S(1)} collective-permute-done((bf16[256,128]{1,0:T(8,128)(2,1)S(1)}, bf16[256,128]{1,0:T(8,128)(2,1)S(1)}, u32[]{:S(2)}, u32[]{:S(2)}) %collective-permute-start.6) | collective-permute-done | bytes 65568 | tf_op jit(solution)/shard_map/ppermute | solution.py:40
  72.3 2.6 %collective-permute-start.7 = (bf16[128,128]{1,0:T(8,128)(2,1)S(1)}, bf16[128,128]{1,0:T(8,128)(2,1)S(1)}, u32[]{:S(2)}, u32[]{:S(2)}) collective-permute-start(bf16[128,128]{1,0:T(8,128)(2,1)S(1)} %dynamic-slice_convert_fusion.3), channel_id=1, source_target_pairs={{0,16},{2,18},{4,20},{6,22},{8,24},{10,26},{12,28},{14,30},{16,0},... | collective-permute-start | bytes 98312 | tf_op jit(solution)/shard_map/ppermute | solution.py:40
  75.0 2.2 %collective-permute-done.7 = bf16[128,128]{1,0:T(8,128)(2,1)S(1)} collective-permute-done((bf16[128,128]{1,0:T(8,128)(2,1)S(1)}, bf16[128,128]{1,0:T(8,128)(2,1)S(1)}, u32[]{:S(2)}, u32[]{:S(2)}) %collective-permute-start.7) | collective-permute-done | bytes 32800 | tf_op jit(solution)/shard_map/ppermute | solution.py:40
  77.2 2.8 %collective-permute-start.8 = (bf16[128,128]{1,0:T(8,128)(2,1)S(1)}, bf16[128,128]{1,0:T(8,128)(2,1)S(1)}, u32[]{:S(2)}, u32[]{:S(2)}) collective-permute-start(bf16[128,128]{1,0:T(8,128)(2,1)S(1)} %add_convert_fusion), channel_id=1, source_target_pairs={{0,16},{2,18},{4,20},{6,22},{8,24},{10,26},{12,28},{14,30},{16,0},... | collective-permute-start | bytes 98312 | tf_op jit(solution)/shard_map/ppermute | solution.py:40
  80.0 2.1 %collective-permute-done.8 = bf16[128,128]{1,0:T(8,128)(2,1)S(1)} collective-permute-done((bf16[128,128]{1,0:T(8,128)(2,1)S(1)}, bf16[128,128]{1,0:T(8,128)(2,1)S(1)}, u32[]{:S(2)}, u32[]{:S(2)}) %collective-permute-start.8) | collective-permute-done | bytes 32800 | tf_op jit(solution)/shard_map/ppermute | solution.py:40
  82.1 1.9 %collective-permute-start.9 = (bf16[256,128]{1,0:T(8,128)(2,1)S(1)}, bf16[256,128]{1,0:T(8,128)(2,1)S(1)}, u32[]{:S(2)}, u32[]{:S(2)}) collective-permute-start(bf16[256,128]{1,0:T(8,128)(2,1)S(1)} %pad_maximum_fusion.4), channel_id=1, source_target_pairs={{0,8},{2,10},{4,12},{6,14},{8,0},{10,2},{12,4},{14,6},{16,24},{18,... | collective-permute-start | bytes 196616 | tf_op jit(solution)/shard_map/ppermute | solution.py:40
  84.0 2.4 %collective-permute-done.9 = bf16[256,128]{1,0:T(8,128)(2,1)S(1)} collective-permute-done((bf16[256,128]{1,0:T(8,128)(2,1)S(1)}, bf16[256,128]{1,0:T(8,128)(2,1)S(1)}, u32[]{:S(2)}, u32[]{:S(2)}) %collective-permute-start.9) | collective-permute-done | bytes 65568 | tf_op jit(solution)/shard_map/ppermute | solution.py:40
  86.5 2.1 %collective-permute-start.10 = (bf16[512,128]{1,0:T(8,128)(2,1)S(1)}, bf16[512,128]{1,0:T(8,128)(2,1)S(1)}, u32[]{:S(2)}, u32[]{:S(2)}) collective-permute-start(bf16[512,128]{1,0:T(8,128)(2,1)S(1)} %pad_maximum_fusion.3), channel_id=1, source_target_pairs={{0,4},{2,6},{4,0},{6,2},{8,12},{10,14},{12,8},{14,10},{16,20},{18,... | collective-permute-start | bytes 393224 | tf_op jit(solution)/shard_map/ppermute | solution.py:40
  88.7 2.9 %collective-permute-done.10 = bf16[512,128]{1,0:T(8,128)(2,1)S(1)} collective-permute-done((bf16[512,128]{1,0:T(8,128)(2,1)S(1)}, bf16[512,128]{1,0:T(8,128)(2,1)S(1)}, u32[]{:S(2)}, u32[]{:S(2)}) %collective-permute-start.10) | collective-permute-done | bytes 131104 | tf_op jit(solution)/shard_map/ppermute | solution.py:40
  91.7 1.6 %collective-permute-start.11 = (bf16[1024,128]{1,0:T(8,128)(2,1)S(1)}, bf16[1024,128]{1,0:T(8,128)(2,1)S(1)}, u32[]{:S(2)}, u32[]{:S(2)}) collective-permute-start(bf16[1024,128]{1,0:T(8,128)(2,1)S(1)} %pad_maximum_fusion.2), channel_id=1, source_target_pairs={{0,1},{1,0},{2,3},{3,2},{4,5},{5,4},{6,7},{7,6},{8,9},{9,8},{10,11... | collective-permute-start | bytes 786440 | tf_op jit(solution)/shard_map/ppermute | solution.py:40
  93.3 4.9 %collective-permute-done.11 = bf16[1024,128]{1,0:T(8,128)(2,1)S(1)} collective-permute-done((bf16[1024,128]{1,0:T(8,128)(2,1)S(1)}, bf16[1024,128]{1,0:T(8,128)(2,1)S(1)}, u32[]{:S(2)}, u32[]{:S(2)}) %collective-permute-start.11) | collective-permute-done | bytes 262176 | tf_op jit(solution)/shard_map/ppermute | solution.py:40
  98.4 3.8 %features.1 = bf16[8,128,96]{2,1,0:T(8,128)(2,1)} custom-call(bf16[16,192,128]{2,1,0:T(8,128)(2,1)S(1)} %copy-done, bf16[10,192,128]{2,1,0:T(8,128)(2,1)S(1)} %copy-done.2, bf16[27,96,96]{2,1,0:T(8,128)(2,1)S(1)} %copy-done.1), custom_call_target="tpu_custom_call" | custom-call | tf_op jit(solution)/shard_map/features/pallas_call | solution.py:355
  102.2 2.0 %unpack.1 = (f32[27,96,96]{2,1,0:T(8,128)}, f32[27,96,96]{2,1,0:T(8,128)}) custom-call(s32[1]{0:T(128)} %bitcast.5.upper_ref, bf16[2048,128]{1,0:T(8,128)(2,1)S(1)} %pad_maximum_fusion.mine_ref, bf16[2048,128]{1,0:T(8,128)(2,1)S(1)} %collective-permute-done.12.other_ref), custom_call_target="tpu_custom_call" | custom-call | tf_op jit(solution)/shard_map/unpack/pallas_call | solution.py:371
  (44 shorter events, 11.3 us)
Async XLA Ops:
  0.6 9.8 %copy-start.3 = (bf16[96,8,16,8]{0,3,2,1:T(8,128)(2,1)S(1)}, bf16[96,8,16,8]{0,3,2,1:T(8,128)(2,1)}, u32[]{:S(2)}) copy-start(bf16[96,8,16,8]{0,3,2,1:T(8,128)(2,1)} %param.7) | copy-start | bytes 589828
  5.2 8.3 %copy-start.4 = (bf16[13,96]{1,0:T(8,128)(2,1)S(1)}, bf16[13,96]{1,0:T(8,128)(2,1)}, u32[]{:S(2)}) copy-start(bf16[13,96]{1,0:T(8,128)(2,1)} %param.12) | copy-start | bytes 7492
  5.2 5.2 %collective-permute-start = (bf16[8,4,8,128]{3,2,1,0:T(8,128)(2,1)S(1)}, bf16[8,4,8,128]{3,2,1,0:T(8,128)(2,1)S(1)}, u32[]{:S(2)}, u32[]{:S(2)}) collective-permute-start(bf16[8,4,8,128]{3,2,1,0:T(8,128)(2,1)S(1)} %fusion), channel_id=1, source_target_pairs={{0,1},{1,0},{2,3},{3,2},{4,5},{5,4},{6,7},{7,6},{8,9},{9,8},{10,11... | collective-permute-start | bytes 196616 | tf_op jit(solution)/shard_map/ppermute | solution.py:28
  10.9 3.3 %collective-permute-start.1 = (bf16[4,24,8,128]{3,2,1,0:T(8,128)(2,1)S(1)}, bf16[4,24,8,128]{3,2,1,0:T(8,128)(2,1)S(1)}, u32[]{:S(2)}, u32[]{:S(2)}) collective-permute-start(bf16[4,24,8,128]{3,2,1,0:T(8,128)(2,1)S(1)} %get-tuple-element.15), channel_id=1, source_target_pairs={{0,2},{2,4},{4,6},{6,8},{8,10},{10,12},{12,14},{14,16},{16,18},{18... | collective-permute-start | bytes 589832 | tf_op jit(solution)/shard_map/ppermute | solution.py:33
  12.2 5.6 %collective-permute-start.2 = (bf16[4,24,8,128]{3,2,1,0:T(8,128)(2,1)S(1)}, bf16[4,24,8,128]{3,2,1,0:T(8,128)(2,1)S(1)}, u32[]{:S(2)}, u32[]{:S(2)}) collective-permute-start(bf16[4,24,8,128]{3,2,1,0:T(8,128)(2,1)S(1)} %get-tuple-element.16), channel_id=1, source_target_pairs={{2,0},{4,2},{6,4},{8,6},{10,8},{12,10},{14,12},{16,14},{18,16},{20... | collective-permute-start | bytes 589832 | tf_op jit(solution)/shard_map/ppermute | solution.py:34
  46.2 5.9 %collective-permute-start.3 = (bf16[2048,128]{1,0:T(8,128)(2,1)}, bf16[2048,128]{1,0:T(8,128)(2,1)S(1)}, u32[]{:S(2)}, u32[]{:S(2)}) collective-permute-start(bf16[2048,128]{1,0:T(8,128)(2,1)} %get-tuple-element.10), channel_id=1, source_target_pairs={{0,2},{2,0},{4,6},{6,4},{8,10},{10,8},{12,14},{14,12},{16,18},{18,... | collective-permute-start | bytes 1572872 | tf_op jit(solution)/shard_map/ppermute | solution.py:40
  53.5 8.7 %collective-permute-start.4 = (bf16[1024,128]{1,0:T(8,128)(2,1)S(1)}, bf16[1024,128]{1,0:T(8,128)(2,1)S(1)}, u32[]{:S(2)}, u32[]{:S(2)}) collective-permute-start(bf16[1024,128]{1,0:T(8,128)(2,1)S(1)} %dynamic-slice_convert_fusion), channel_id=1, source_target_pairs={{0,1},{1,0},{2,3},{3,2},{4,5},{5,4},{6,7},{7,6},{8,9},{9,8},{10,11... | collective-permute-start | bytes 786440 | tf_op jit(solution)/shard_map/ppermute | solution.py:40
  62.2 5.7 %collective-permute-start.5 = (bf16[512,128]{1,0:T(8,128)(2,1)S(1)}, bf16[512,128]{1,0:T(8,128)(2,1)S(1)}, u32[]{:S(2)}, u32[]{:S(2)}) collective-permute-start(bf16[512,128]{1,0:T(8,128)(2,1)S(1)} %dynamic-slice_convert_fusion.1), channel_id=1, source_target_pairs={{0,4},{2,6},{4,0},{6,2},{8,12},{10,14},{12,8},{14,10},{16,20},{18,... | collective-permute-start | bytes 393224 | tf_op jit(solution)/shard_map/ppermute | solution.py:40
  68.0 4.3 %collective-permute-start.6 = (bf16[256,128]{1,0:T(8,128)(2,1)S(1)}, bf16[256,128]{1,0:T(8,128)(2,1)S(1)}, u32[]{:S(2)}, u32[]{:S(2)}) collective-permute-start(bf16[256,128]{1,0:T(8,128)(2,1)S(1)} %dynamic-slice_convert_fusion.2), channel_id=1, source_target_pairs={{0,8},{2,10},{4,12},{6,14},{8,0},{10,2},{12,4},{14,6},{16,24},{18,... | collective-permute-start | bytes 196616 | tf_op jit(solution)/shard_map/ppermute | solution.py:40
  72.3 4.9 %collective-permute-start.7 = (bf16[128,128]{1,0:T(8,128)(2,1)S(1)}, bf16[128,128]{1,0:T(8,128)(2,1)S(1)}, u32[]{:S(2)}, u32[]{:S(2)}) collective-permute-start(bf16[128,128]{1,0:T(8,128)(2,1)S(1)} %dynamic-slice_convert_fusion.3), channel_id=1, source_target_pairs={{0,16},{2,18},{4,20},{6,22},{8,24},{10,26},{12,28},{14,30},{16,0},... | collective-permute-start | bytes 98312 | tf_op jit(solution)/shard_map/ppermute | solution.py:40
  77.2 4.9 %collective-permute-start.8 = (bf16[128,128]{1,0:T(8,128)(2,1)S(1)}, bf16[128,128]{1,0:T(8,128)(2,1)S(1)}, u32[]{:S(2)}, u32[]{:S(2)}) collective-permute-start(bf16[128,128]{1,0:T(8,128)(2,1)S(1)} %add_convert_fusion), channel_id=1, source_target_pairs={{0,16},{2,18},{4,20},{6,22},{8,24},{10,26},{12,28},{14,30},{16,0},... | collective-permute-start | bytes 98312 | tf_op jit(solution)/shard_map/ppermute | solution.py:40
  82.1 4.3 %collective-permute-start.9 = (bf16[256,128]{1,0:T(8,128)(2,1)S(1)}, bf16[256,128]{1,0:T(8,128)(2,1)S(1)}, u32[]{:S(2)}, u32[]{:S(2)}) collective-permute-start(bf16[256,128]{1,0:T(8,128)(2,1)S(1)} %pad_maximum_fusion.4), channel_id=1, source_target_pairs={{0,8},{2,10},{4,12},{6,14},{8,0},{10,2},{12,4},{14,6},{16,24},{18,... | collective-permute-start | bytes 196616 | tf_op jit(solution)/shard_map/ppermute | solution.py:40
  86.5 5.1 %collective-permute-start.10 = (bf16[512,128]{1,0:T(8,128)(2,1)S(1)}, bf16[512,128]{1,0:T(8,128)(2,1)S(1)}, u32[]{:S(2)}, u32[]{:S(2)}) collective-permute-start(bf16[512,128]{1,0:T(8,128)(2,1)S(1)} %pad_maximum_fusion.3), channel_id=1, source_target_pairs={{0,4},{2,6},{4,0},{6,2},{8,12},{10,14},{12,8},{14,10},{16,20},{18,... | collective-permute-start | bytes 393224 | tf_op jit(solution)/shard_map/ppermute | solution.py:40
  91.7 6.7 %copy-start = (bf16[16,192,128]{2,1,0:T(8,128)(2,1)S(1)}, bf16[16,192,128]{2,1,0:T(8,128)(2,1)}, u32[]{:S(2)}) copy-start(bf16[16,192,128]{2,1,0:T(8,128)(2,1)} %maximum_bitcast_fusion.x_ref) | copy-start | bytes 2359300
  91.7 6.7 %copy-start.1 = (bf16[27,96,96]{2,1,0:T(8,128)(2,1)S(1)}, bf16[27,96,96]{2,1,0:T(8,128)(2,1)}, u32[]{:S(2)}) copy-start(bf16[27,96,96]{2,1,0:T(8,128)(2,1)} %w1_ref.3) | copy-start | bytes 1492996
  91.7 6.7 %copy-start.2 = (bf16[10,192,128]{2,1,0:T(8,128)(2,1)S(1)}, bf16[10,192,128]{2,1,0:T(8,128)(2,1)}, u32[]{:S(2)}) copy-start(bf16[10,192,128]{2,1,0:T(8,128)(2,1)} %get-tuple-element.8.grad_ref) | copy-start | bytes 1474564
  91.7 6.4 %collective-permute-start.11 = (bf16[1024,128]{1,0:T(8,128)(2,1)S(1)}, bf16[1024,128]{1,0:T(8,128)(2,1)S(1)}, u32[]{:S(2)}, u32[]{:S(2)}) collective-permute-start(bf16[1024,128]{1,0:T(8,128)(2,1)S(1)} %pad_maximum_fusion.2), channel_id=1, source_target_pairs={{0,1},{1,0},{2,3},{3,2},{4,5},{5,4},{6,7},{7,6},{8,9},{9,8},{10,11... | collective-permute-start | bytes 786440 | tf_op jit(solution)/shard_map/ppermute | solution.py:40
  98.3 3.9 %collective-permute-start.12 = (bf16[2048,128]{1,0:T(8,128)(2,1)S(1)}, bf16[2048,128]{1,0:T(8,128)(2,1)S(1)}, u32[]{:S(2)}, u32[]{:S(2)}) collective-permute-start(bf16[2048,128]{1,0:T(8,128)(2,1)S(1)} %pad_maximum_fusion.mine_ref), channel_id=1, source_target_pairs={{0,2},{2,0},{4,6},{6,4},{8,10},{10,8},{12,14},{14,12},{16,18},{18,... | collective-permute-start | bytes 1572872 | tf_op jit(solution)/shard_map/ppermute | solution.py:40

commit v3 on v0

--- a/solution.py
+++ b/solution.py
@@ -12,7 +12,6 @@
 HALO = 4
 OFFSETS = 9
 WIDE = OFFSETS * LANES
-AXES = ("east", "north")
 F32 = jnp.float32
 BF16 = jnp.bfloat16
 
@@ -36,6 +35,53 @@
     return low, high
 
 
+def high_bit(axis, bit):
+    return (lax.axis_index(axis) // bit) % 2
+
+
+def bits_of(axis):
+    size = lax.axis_size(axis)
+    return [(axis, 1 << i) for i in range(size.bit_length() - 1)]
+
+
+def swap(value, axis, bit):
+    north = lax.axis_size("north")
+    pairs = []
+    for e in range(1, lax.axis_size("east"), 2):
+        for n in range(north):
+            partner = (e ^ bit, n) if axis == "east" else (e, n ^ bit)
+            pairs.append((e * north + n, partner[0] * north + partner[1]))
+    return lax.ppermute(value, ("east", "north"), pairs)
+
+
+def halves(total, axis, bit):
+    upper = high_bit(axis, bit)
+    half = total.shape[0] // 2
+    sent = lax.dynamic_slice_in_dim(total, (1 - upper) * half, half, 0).astype(BF16)
+    return sent, lax.dynamic_slice_in_dim(total, upper * half, half, 0)
+
+
+def scatter_steps(totals, orders, beside):
+    for step in range(len(orders[0])):
+        sent, kept = zip(*[halves(total, *order[step]) for total, order in zip(totals, orders)])
+        if step == 0:
+            kept = beside(*kept)
+        others = [swap(value, *order[step]) for value, order in zip(sent, orders)]
+        totals = [mine + other.astype(F32) for mine, other in zip(kept, others)]
+    return totals
+
+
+def gather_steps(values, orders):
+    for step in range(len(orders[0]) - 1, 0, -1):
+        others = [swap(value, *order[step]) for value, order in zip(values, orders)]
+        joined = []
+        for mine, other, order in zip(values, others, orders):
+            upper = high_bit(*order[step]) == 1
+            joined.append(jnp.concatenate([jnp.where(upper, other, mine), jnp.where(upper, mine, other)], 0))
+        values = joined
+    return values, [swap(value, *order[0]) for value, order in zip(values, orders)]
+
+
 def lane_of(shape):
     return lax.broadcasted_iota(jnp.int32, shape, len(shape) - 1)
 
@@ -103,7 +149,7 @@
             turned_ref[d * channels : (d + 1) * channels, e * size : (e + 1) * size] = turned
 
 
-def kernel_sum(turned_ref, stack_ref, first, east, rows, low, size, channels, out_ref):
+def kernel_sum(turned_ref, stack_ref, first, east, rows, low, size, channels):
     total = None
     for i in range(east // 2):
         fields = []
@@ -125,20 +171,26 @@
     blocks.append(jnp.zeros_like(blocks[0]))
     lane = lane_of(blocks[0].shape)
     spare = LANES - channels
-    row = 0
+    tiles = []
     for t in range(0, 28, 4):
         for r in range(3):
             tail = pltpu.roll(blocks[t + 3], channels - spare * r, 1)
-            out_ref[row : row + channels, :] = jnp.where(lane < channels, blocks[t + r], tail).astype(BF16)
-            row += channels
-    if row < out_ref.shape[0]:
-        out_ref[row:, :] = jnp.zeros((out_ref.shape[0] - row, LANES), BF16)
+            tiles.append(jnp.where(lane < channels, blocks[t + r], tail))
+    return tiles
+
+
+def put_tiles(out_ref, tiles, channels):
+    for t, tile in enumerate(tiles):
+        out_ref[t * channels : (t + 1) * channels, :] = tile.astype(BF16)
+    filled = len(tiles) * channels
+    if filled < out_ref.shape[0]:
+        out_ref[filled:, :] = jnp.zeros((out_ref.shape[0] - filled, LANES), BF16)
 
 
 def whole_kernel(
     channels, classes, east, north, upward,
     x_ref, w1_ref, w2_ref, head_ref,
-    out_ref, second_ref, first_ref,
+    grad_ref, second_ref, first_ref,
     s0_ref, s1_ref, sg_ref, mask_ref, slope_ref, acc_ref, wt_ref, wb_ref, turned_ref,
 ):
     rows = (north + 2 * HALO) * upward
@@ -196,35 +248,71 @@
             put_stack(g_p2, rows, upward, sg_ref, parity, i)
             put_turned(turned_ref, g_p2[low : low + size], plane - 2, east, channels)
 
-    kernel_sum(turned_ref, s1_ref, 3, east, rows, low, size, channels, second_ref)
+    put_tiles(second_ref, kernel_sum(turned_ref, s1_ref, 3, east, rows, low, size, channels), channels)
     convolve(sg_ref, wb_ref, (planes - 6) // 2, rows, acc_ref, False)
-    put_backward(wb_ref, w1_ref, channels)
 
     for i in range((planes - 6) // 2):
         for parity in range(2):
             plane = 2 * i + parity
             g_p1 = slope_ref[plane + 2] * acc_ref[i * rows : (i + 1) * rows, parity * LANES : (parity + 1) * LANES]
-            put_stack(g_p1, rows, upward, sg_ref, parity, i)
+            grad_ref[plane] = g_p1.astype(BF16)
             put_turned(turned_ref, g_p1[low : low + size], plane - 1, east, channels)
 
-    kernel_sum(turned_ref, s0_ref, 4, east, rows, low, size, channels, first_ref)
-    convolve(sg_ref, wb_ref, east // 2, rows, acc_ref, False)
+    put_tiles(first_ref, kernel_sum(turned_ref, s0_ref, 4, east, rows, low, size, channels), channels)
+
+
+def last_kernel(
+    channels, east, north, upward,
+    x_ref, grad_ref, w1_ref, second_in, first_in,
+    out_ref, second_out, first_out,
+    stack_ref, wb_ref, acc_ref,
+):
+    rows = (north + 2 * HALO) * upward
+    low, size = HALO * upward, north * upward
+    put_backward(wb_ref, w1_ref, channels)
+
+    def start(i, carry):
+        for parity in range(2):
+            put_stack(grad_ref[2 * i + parity].astype(F32), rows, upward, stack_ref, parity, i)
+        return carry
+
+    lax.fori_loop(0, east // 2 + 1, start, 0)
+    convolve(stack_ref, wb_ref, east // 2, rows, acc_ref, False)
     for i in range(east // 2):
         for parity in range(2):
             plane = 2 * i + parity
             value = acc_ref[i * rows + low : i * rows + low + size, parity * LANES : (parity + 1) * LANES]
-            value = mask_ref[plane + HALO, low : low + size] * value
-            out_ref[plane] = value[:, 0:channels].astype(BF16)
-
-
-def unpack_kernel(channels, scale, second_in, first_in, first_out, second_out):
+            mask = x_ref[plane + HALO, low : low + size, channels : channels + 1].astype(F32)
+            out_ref[plane] = (mask * value)[:, 0:channels].astype(BF16)
+
+
+def unpack_kernel(
+    channels, scale, flags_ref, second_mine, first_mine, second_other, first_other, near_ref, far_ref, first_out, second_out
+):
     spare = LANES - channels
-    for source, target in ((first_in, first_out), (second_in, second_out)):
+    half = second_mine.shape[0]
+    odd = flags_ref[0] == 1
+    streams = (
+        (flags_ref[1] == 1, second_mine, second_other, 0, second_out),
+        (flags_ref[2] == 1, first_mine, first_other, half, first_out),
+    )
+
+    def rows_of(upper, mine_ref, other_ref, base, start, stop):
+        here = slice(start % half, start % half + stop - start)
+        there = slice(base + start % half, base + start % half + stop - start)
+        mine = jnp.where(odd, mine_ref[here, :], near_ref[there, :])
+        other = jnp.where(odd, other_ref[here, :], far_ref[there, :])
+        return jnp.where(upper, other, mine) if start < half else jnp.where(upper, mine, other)
+
+    for upper, mine_ref, other_ref, base, target in streams:
         for t in range(0, 27, 4):
-            tiles = [
-                source[(t // 4 * 3 + r) * channels : (t // 4 * 3 + r + 1) * channels, :].astype(F32) * scale
-                for r in range(3)
-            ]
+            tiles = []
+            for r in range(3):
+                start = (t // 4 * 3 + r) * channels
+                edges = sorted({start, start + channels, min(max(half, start), start + channels)})
+                pieces = [rows_of(upper, mine_ref, other_ref, base, *pair) for pair in zip(edges, edges[1:])]
+                tile = pieces[0] if len(pieces) == 1 else jnp.concatenate(pieces, 0)
+                tiles.append(tile.astype(F32) * scale)
             for r in range(3):
                 target[t + r] = tiles[r][:, 0:channels]
             if t + 3 < 27:
@@ -266,13 +354,16 @@
     x = x.reshape(planes, rows, LANES)
     head_wide = jnp.pad(head, ((channels + 1, LANES - channels - 1 - classes), (0, LANES - channels)))
 
-    chunk = -(-21 * channels // (devices * 16)) * 16
-    packed = chunk * devices
+    east_bits, north_bits = bits_of("east"), bits_of("north")
+    orders = (north_bits + east_bits[1:], east_bits[1:2] + north_bits + east_bits[2:])
+    unit = devices // 2 * 16
+    packed = -(-21 * channels // unit) * unit
     vmem = pl.BlockSpec(memory_space=pltpu.VMEM)
-    grad_features, second, first = pl.pallas_call(
+    smem = pl.BlockSpec(memory_space=pltpu.SMEM)
+    grad, second, first = pl.pallas_call(
         functools.partial(whole_kernel, channels, classes, east, north, upward),
         out_shape=(
-            jax.ShapeDtypeStruct((east, north * upward, channels), BF16),
+            jax.ShapeDtypeStruct((east + 2, rows, LANES), BF16),
             jax.ShapeDtypeStruct((packed, LANES), BF16),
             jax.ShapeDtypeStruct((packed, LANES), BF16),
         ),
@@ -293,26 +384,51 @@
         name="fields",
     )(x, first_weights, second_weights, head_wide)
 
-    both = jnp.concatenate(
-        [second.reshape(devices, chunk, LANES), first.reshape(devices, chunk, LANES)], 1
-    )
-    parts = lax.all_to_all(both, AXES, 0, 0, tiled=True)
-    mine = jnp.sum(parts.astype(F32), 0).astype(BF16)
-    whole = lax.all_gather(mine, AXES, axis=0)
-    second = whole[:, :chunk].reshape(packed, LANES)
-    first = whole[:, chunk:].reshape(packed, LANES)
-
+    anywhere = pl.BlockSpec(memory_space=pl.ANY)
+    features_out = []
+
+    def beside(second_kept, first_kept):
+        out, second_kept, first_kept = pl.pallas_call(
+            functools.partial(last_kernel, channels, east, north, upward),
+            out_shape=(
+                jax.ShapeDtypeStruct((east, north * upward, channels), BF16),
+                jax.ShapeDtypeStruct(second_kept.shape, F32),
+                jax.ShapeDtypeStruct(first_kept.shape, F32),
+            ),
+            in_specs=[vmem] * 3 + [anywhere] * 2,
+            out_specs=(vmem, anywhere, anywhere),
+            input_output_aliases={3: 1, 4: 2},
+            scratch_shapes=[
+                pltpu.VMEM((2, (east + 2) // 2 * rows, WIDE), BF16),
+                pltpu.VMEM((4, WIDE, 2 * LANES), BF16),
+                pltpu.VMEM((east // 2 * rows, 2 * LANES), F32),
+            ],
+            compiler_params=pltpu.CompilerParams(vmem_limit_bytes=32 * 1024 * 1024),
+            name="features",
+        )(x, grad, first_weights, second_kept, first_kept)
+        features_out.append(out)
+        return second_kept, first_kept
+
+    to_odd = [(e, e + 1) for e in range(0, lax.axis_size("east"), 2)]
+    to_even = [(e + 1, e) for e in range(0, lax.axis_size("east"), 2)]
+    sums = [value.astype(F32) + lax.ppermute(value, "east", to_odd).astype(F32) for value in (second, first)]
+    sums = scatter_steps(sums, orders, beside)
+    mine, other = gather_steps([total.astype(BF16) for total in sums], orders)
+    near = lax.ppermute(jnp.concatenate(mine, 0), "east", to_even)
+    far = lax.ppermute(jnp.concatenate(other, 0), "east", to_even)
+    flags = jnp.stack([high_bit("east", 1)] + [high_bit(*order[0]) for order in orders])
     grad_first, grad_second = pl.pallas_call(
         functools.partial(unpack_kernel, channels, scale),
         out_shape=(
             jax.ShapeDtypeStruct(first_weights.shape, F32),
             jax.ShapeDtypeStruct(second_weights.shape, F32),
         ),
-        in_specs=[vmem] * 2,
+        in_specs=[smem] + [vmem] * 6,
         out_specs=(vmem, vmem),
         compiler_params=pltpu.CompilerParams(vmem_limit_bytes=32 * 1024 * 1024),
         name="unpack",
-    )(second, first)
+    )(flags, *mine, *other, near, far)
+    (grad_features,) = features_out
     grad_features = grad_features.reshape(east, north, upward, channels).transpose(3, 0, 1, 2)
     return (grad_features, grad_first, grad_second)
 

time: 159 us -> 121 us (0.76)
  blocking collectives: 35.5 us -> 0 us
  starting transfers between devices: 5.63 us -> 26.5 us
  between operations: 14.1 us -> 1.48 us
  waiting for transfers between devices: 58.8 us -> 49.1 us
    all_gather x1 -> x0, waiting for transfers between devices: 52.9 us -> none  [per_device(): whole = lax.all_gather(mine, AXES, axis=0)]
    ppermute x0 -> x20, waiting for transfers between devices: none -> 43.2 us  [the longest x1 39 us: per_device(): near = lax.ppermute(jnp.concatenate(mine, 0), 'east', to_even)]
    all_to_all x1 -> x0, blocking collectives: 35.5 us -> none  [per_device(): parts = lax.all_to_all(both, AXES, 0, 0, tiled=True)]
    ppermute x0 -> x20, starting transfers between devices: none -> 20.9 us  [the longest x16 10.8 us: swap(): return lax.ppermute(value, ('east', 'north'), pairs)]
    pallas_call x1, Pallas kernels: 32.6 us -> 26.8 us  [per_device(): pl.pallas_call(functools.partial(whole_kernel, channels, classes, east, n...]
    pallas_call x0 -> x1, Pallas kernels: none -> 3.81 us  [beside(): pl.pallas_call(functools.partial(last_kernel, channels, east, north, upwa...]
  transfers between devices with their start and end apart: 4 -> 23, of which waited for: 3 -> 5; matrix products, arithmetic and copies ran while one was open for 0% -> 2% of each run, Pallas kernels for 0% -> 3%
where the time goes in v3:
time: 121 us; the launch traced here: 120 us
  waiting for transfers between devices  49.1 us (41%)
  Pallas kernels  33.2 us (27%)
  starting transfers between devices  26.5 us (22%)
  other arithmetic  5.25 us (4%)
  local copies, waits for them, and re-layouts  4.21 us (3%)
  between operations  1.48 us (1%)
    ppermute x1, waiting for transfers between devices, per_device(): near = lax.ppermute(jnp.concatenate(mine, 0), 'east', to_even)  39 us
    pallas_call x1, Pallas kernels, per_device(): pl.pallas_call(functools.partial(whole_kernel, channels, classes, east, n...  26.8 us
    ppermute x16, starting transfers between devices, swap(): return lax.ppermute(value, ('east', 'north'), pairs)  10.8 us
    ppermute x2, starting transfers between devices, per_device(): lax.ppermute(value, 'east', to_odd).astype(F32)  7.52 us
    ppermute x1, waiting for transfers between devices, per_device(): far = lax.ppermute(jnp.concatenate(other, 0), 'east', to_even)  4.09 us
    pallas_call x1, Pallas kernels, beside(): pl.pallas_call(functools.partial(last_kernel, channels, east, north, upwa...  3.81 us
    ppermute x1, waiting for transfers between devices, halo_of(): lax.ppermute(lax.slice_in_dim(block, 0, width, axis=dim), axis, backward)  3.67 us
    ppermute x1, starting transfers between devices, halo_of(): other = lax.ppermute(mine, axis, [(0, 1), (1, 0)])  3 us
  transfers between devices with their start and end apart: 23, of which 5 were waited for; matrix products, arithmetic and copies ran while one was open for 2% of the time, Pallas kernels for 3%

profile of v3, /device:TPU:0, one launch (start us, length us, event | category | flops | bytes accessed | tf_op | source)
XLA Modules:
  0.0 119.8 jit_solution(8592364049151720778)
XLA Ops:
  0.6 0.8 broadcast_in_dim.16
  1.5 0.8 fusion.3
  2.7 1.4 %copy.13 = bf16[8,16,8,13]{3,2,1,0:T(8,128)(2,1)S(1)} copy(bf16[8,16,8,13]{1,2,0,3:T(8,128)(2,1)} %bitcast.16) | data formatting | bytes 53248 | tf_op jit(solution)/shard_map/transpose | solution.py:342
  4.2 1.0 fusion
  5.2 3.0 %collective-permute-start = (bf16[8,4,8,128]{3,2,1,0:T(8,128)(2,1)S(1)}, bf16[8,4,8,128]{3,2,1,0:T(8,128)(2,1)S(1)}, u32[]{:S(2)}, u32[]{:S(2)}) collective-permute-start(bf16[8,4,8,128]{3,2,1,0:T(8,128)(2,1)S(1)} %fusion), channel_id=1, source_target_pairs={{0,1},{1,0},{2,3},{3,2},{4,5},{5,4},{6,7},{7,6},{8,9},{9,8},{10,11... | collective-permute-start | bytes 196616 | tf_op jit(solution)/shard_map/ppermute | solution.py:28
  8.2 2.2 %collective-permute-done = bf16[8,4,8,128]{3,2,1,0:T(8,128)(2,1)S(1)} collective-permute-done((bf16[8,4,8,128]{3,2,1,0:T(8,128)(2,1)S(1)}, bf16[8,4,8,128]{3,2,1,0:T(8,128)(2,1)S(1)}, u32[]{:S(2)}, u32[]{:S(2)}) %collective-permute-start) | collective-permute-done | bytes 65568 | tf_op jit(solution)/shard_map/ppermute | solution.py:28
  10.9 1.3 %collective-permute-start.1 = (bf16[4,24,8,128]{3,2,1,0:T(8,128)(2,1)S(1)}, bf16[4,24,8,128]{3,2,1,0:T(8,128)(2,1)S(1)}, u32[]{:S(2)}, u32[]{:S(2)}) collective-permute-start(bf16[4,24,8,128]{3,2,1,0:T(8,128)(2,1)S(1)} %get-tuple-element.19), channel_id=1, source_target_pairs={{0,2},{2,4},{4,6},{6,8},{8,10},{10,12},{12,14},{14,16},{16,18},{18... | collective-permute-start | bytes 589832 | tf_op jit(solution)/shard_map/ppermute | solution.py:33
  12.2 1.3 %collective-permute-start.2 = (bf16[4,24,8,128]{3,2,1,0:T(8,128)(2,1)S(1)}, bf16[4,24,8,128]{3,2,1,0:T(8,128)(2,1)S(1)}, u32[]{:S(2)}, u32[]{:S(2)}) collective-permute-start(bf16[4,24,8,128]{3,2,1,0:T(8,128)(2,1)S(1)} %get-tuple-element.20), channel_id=1, source_target_pairs={{2,0},{4,2},{6,4},{8,6},{10,8},{12,10},{14,12},{16,14},{18,16},{20... | collective-permute-start | bytes 589832 | tf_op jit(solution)/shard_map/ppermute | solution.py:34
  14.1 3.7 %collective-permute-done.2 = bf16[4,24,8,128]{3,2,1,0:T(8,128)(2,1)S(1)} collective-permute-done((bf16[4,24,8,128]{3,2,1,0:T(8,128)(2,1)S(1)}, bf16[4,24,8,128]{3,2,1,0:T(8,128)(2,1)S(1)}, u32[]{:S(2)}, u32[]{:S(2)}) %collective-permute-start.2) | collective-permute-done | bytes 196640 | tf_op jit(solution)/shard_map/ppermute | solution.py:34
  17.8 1.2 %maximum_bitcast_fusion.x_ref = bf16[16,192,128]{2,1,0:T(8,128)(2,1)} fusion(bf16[4,24,8,128]{3,2,1,0:T(8,128)(2,1)S(1)} %collective-permute-done.2, bf16[8,4,8,128]{3,2,1,0:T(8,128)(2,1)S(1)} %get-tuple-element.34, bf16[8,16,8,18]{3,2,1,0:T(8,128)(2,1)S(1)} %broadcast_in_dim.19, bf16[8,16,8,13]{3,2,1,0:T(8,128)(2,1)S(1)} %copy.13, ...), kind=kLoop, calls=%fused_computation.2 | loop fusion | flops 6291456 | bytes 1572864 | tf_op jit(solution)/shard_map/reshape | solution.py:354
  19.0 26.8 %fields.1 = (bf16[10,192,128]{2,1,0:T(8,128)(2,1)}, bf16[2048,128]{1,0:T(8,128)(2,1)}, bf16[2048,128]{1,0:T(8,128)(2,1)}) custom-call(bf16[16,192,128]{2,1,0:T(8,128)(2,1)} %maximum_bitcast_fusion.x_ref, bf16[27,96,96]{2,1,0:T(8,128)(2,1)} %w1_ref.3, bf16[27,96,96]{2,1,0:T(8,128)(2,1)} %w2_ref.1, bf16[128,128]{1,0:T(8,128)(2,1)} %pad.4.head_ref), custom_call_target="tpu_custom_call" | custom-call | tf_op jit(solution)/shard_map/fields/pallas_call | solution.py:363
  45.8 6.1 %collective-permute-start.3 = (bf16[2048,128]{1,0:T(8,128)(2,1)}, bf16[2048,128]{1,0:T(8,128)(2,1)S(1)}, u32[]{:S(2)}, u32[]{:S(2)}) collective-permute-start(bf16[2048,128]{1,0:T(8,128)(2,1)} %get-tuple-element.12), channel_id=1, source_target_pairs={{0,2},{4,6},{8,10},{12,14},{16,18},{20,22},{24,26},{28,30},{1,3},{... | collective-permute-start | bytes 1572872 | tf_op jit(solution)/shard_map/ppermute | solution.py:414
  52.1 1.5 %collective-permute-start.4 = (bf16[2048,128]{1,0:T(8,128)(2,1)}, bf16[2048,128]{1,0:T(8,128)(2,1)S(1)}, u32[]{:S(2)}, u32[]{:S(2)}) collective-permute-start(bf16[2048,128]{1,0:T(8,128)(2,1)} %get-tuple-element.13), channel_id=1, source_target_pairs={{0,2},{4,6},{8,10},{12,14},{16,18},{20,22},{24,26},{28,30},{1,3},{... | collective-permute-start | bytes 1572872 | tf_op jit(solution)/shard_map/ppermute | solution.py:414
  53.6 1.1 convert_add_fusion.1
  54.8 0.7 collective-permute-start.5
  55.7 0.8 collective-permute-start.12
  57.1 3.8 %features.1 = (bf16[8,128,96]{2,1,0:T(8,128)(2,1)}, f32[1024,128]{1,0:T(8,128)S(1)}, f32[1024,128]{1,0:T(8,128)S(1)}) custom-call(bf16[16,192,128]{2,1,0:T(8,128)(2,1)S(1)} %copy-done, bf16[10,192,128]{2,1,0:T(8,128)(2,1)S(1)} %copy-done.2, bf16[27,96,96]{2,1,0:T(8,128)(2,1)S(1)} %copy-done.1, ...), custom_call_target="tpu_custom_call", output_to_operand_aliasing={{1}: (3, {}), {2}: (4, {})} | custom-call | tf_op jit(solution)/shard_map/features/pallas_call | solution.py:391
  69.8 0.7 collective-permute-start.19
  70.6 0.7 collective-permute-start.20
  71.3 1.3 %collective-permute-start.21 = (bf16[2048,128]{1,0:T(8,128)(2,1)S(1)}, bf16[2048,128]{1,0:T(8,128)(2,1)S(1)}, u32[]{:S(2)}, u32[]{:S(2)}) collective-permute-start(bf16[2048,128]{1,0:T(8,128)(2,1)S(1)} %pad_maximum_fusion), channel_id=1, source_target_pairs={{2,0},{6,4},{10,8},{14,12},{18,16},{22,20},{26,24},{30,28},{3,1},{... | collective-permute-start | bytes 1572872 | tf_op jit(solution)/shard_map/ppermute | solution.py:417
  72.7 1.3 %collective-permute-start.22 = (bf16[2048,128]{1,0:T(8,128)(2,1)S(1)}, bf16[2048,128]{1,0:T(8,128)(2,1)S(1)}, u32[]{:S(2)}, u32[]{:S(2)}) collective-permute-start(bf16[2048,128]{1,0:T(8,128)(2,1)S(1)} %pad_maximum_fusion.1), channel_id=1, source_target_pairs={{2,0},{6,4},{10,8},{14,12},{18,16},{22,20},{26,24},{30,28},{3,1},{... | collective-permute-start | bytes 1572872 | tf_op jit(solution)/shard_map/ppermute | solution.py:418
  74.1 39.0 %collective-permute-done.21.near_ref = bf16[2048,128]{1,0:T(8,128)(2,1)S(1)} collective-permute-done((bf16[2048,128]{1,0:T(8,128)(2,1)S(1)}, bf16[2048,128]{1,0:T(8,128)(2,1)S(1)}, u32[]{:S(2)}, u32[]{:S(2)}) %collective-permute-start.21) | collective-permute-done | bytes 524320 | tf_op jit(solution)/shard_map/ppermute | solution.py:417
  113.1 4.1 %collective-permute-done.22.far_ref = bf16[2048,128]{1,0:T(8,128)(2,1)S(1)} collective-permute-done((bf16[2048,128]{1,0:T(8,128)(2,1)S(1)}, bf16[2048,128]{1,0:T(8,128)(2,1)S(1)}, u32[]{:S(2)}, u32[]{:S(2)}) %collective-permute-start.22) | collective-permute-done | bytes 524320 | tf_op jit(solution)/shard_map/ppermute | solution.py:418
  117.2 2.7 %unpack.1 = (f32[27,96,96]{2,1,0:T(8,128)}, f32[27,96,96]{2,1,0:T(8,128)}) custom-call(s32[3]{0:T(128)S(1)} %pad_add_fusion.flags_ref, bf16[1024,128]{1,0:T(8,128)(2,1)S(1)} %pad_maximum_fusion.3.second_mine, bf16[1024,128]{1,0:T(8,128)(2,1)S(1)} %pad_maximum_fusion.4.first_mine, bf16[1024,128]{1,0:T(8,128)(2,1)S(1)} %collective-permute-done.19.second_other, ...), custom_call_target="tpu_custom_call" | custom-call | tf_op jit(solution)/shard_map/unpack/pallas_call | solution.py:420
  (83 shorter events, 11.2 us)
Async XLA Ops:
  0.6 9.8 %copy-start.3 = (bf16[96,8,16,8]{0,3,2,1:T(8,128)(2,1)S(1)}, bf16[96,8,16,8]{0,3,2,1:T(8,128)(2,1)}, u32[]{:S(2)}) copy-start(bf16[96,8,16,8]{0,3,2,1:T(8,128)(2,1)} %param.7) | copy-start | bytes 589828
  5.2 5.2 %collective-permute-start = (bf16[8,4,8,128]{3,2,1,0:T(8,128)(2,1)S(1)}, bf16[8,4,8,128]{3,2,1,0:T(8,128)(2,1)S(1)}, u32[]{:S(2)}, u32[]{:S(2)}) collective-permute-start(bf16[8,4,8,128]{3,2,1,0:T(8,128)(2,1)S(1)} %fusion), channel_id=1, source_target_pairs={{0,1},{1,0},{2,3},{3,2},{4,5},{5,4},{6,7},{7,6},{8,9},{9,8},{10,11... | collective-permute-start | bytes 196616 | tf_op jit(solution)/shard_map/ppermute | solution.py:28
  10.9 3.2 %collective-permute-start.1 = (bf16[4,24,8,128]{3,2,1,0:T(8,128)(2,1)S(1)}, bf16[4,24,8,128]{3,2,1,0:T(8,128)(2,1)S(1)}, u32[]{:S(2)}, u32[]{:S(2)}) collective-permute-start(bf16[4,24,8,128]{3,2,1,0:T(8,128)(2,1)S(1)} %get-tuple-element.19), channel_id=1, source_target_pairs={{0,2},{2,4},{4,6},{6,8},{8,10},{10,12},{12,14},{14,16},{16,18},{18... | collective-permute-start | bytes 589832 | tf_op jit(solution)/shard_map/ppermute | solution.py:33
  12.2 5.6 %collective-permute-start.2 = (bf16[4,24,8,128]{3,2,1,0:T(8,128)(2,1)S(1)}, bf16[4,24,8,128]{3,2,1,0:T(8,128)(2,1)S(1)}, u32[]{:S(2)}, u32[]{:S(2)}) collective-permute-start(bf16[4,24,8,128]{3,2,1,0:T(8,128)(2,1)S(1)} %get-tuple-element.20), channel_id=1, source_target_pairs={{2,0},{4,2},{6,4},{8,6},{10,8},{12,10},{14,12},{16,14},{18,16},{20... | collective-permute-start | bytes 589832 | tf_op jit(solution)/shard_map/ppermute | solution.py:34
  45.8 7.8 %collective-permute-start.3 = (bf16[2048,128]{1,0:T(8,128)(2,1)}, bf16[2048,128]{1,0:T(8,128)(2,1)S(1)}, u32[]{:S(2)}, u32[]{:S(2)}) collective-permute-start(bf16[2048,128]{1,0:T(8,128)(2,1)} %get-tuple-element.12), channel_id=1, source_target_pairs={{0,2},{4,6},{8,10},{12,14},{16,18},{20,22},{24,26},{28,30},{1,3},{... | collective-permute-start | bytes 1572872 | tf_op jit(solution)/shard_map/ppermute | solution.py:414
  52.1 3.4 %collective-permute-start.4 = (bf16[2048,128]{1,0:T(8,128)(2,1)}, bf16[2048,128]{1,0:T(8,128)(2,1)S(1)}, u32[]{:S(2)}, u32[]{:S(2)}) collective-permute-start(bf16[2048,128]{1,0:T(8,128)(2,1)} %get-tuple-element.13), channel_id=1, source_target_pairs={{0,2},{4,6},{8,10},{12,14},{16,18},{20,22},{24,26},{28,30},{1,3},{... | collective-permute-start | bytes 1572872 | tf_op jit(solution)/shard_map/ppermute | solution.py:414
  54.8 6.1 %collective-permute-start.5 = (bf16[1024,128]{1,0:T(8,128)(2,1)S(1)}, bf16[1024,128]{1,0:T(8,128)(2,1)S(1)}, u32[]{:S(2)}, u32[]{:S(2)}) collective-permute-start(bf16[1024,128]{1,0:T(8,128)(2,1)S(1)} %dynamic-slice_convert_fusion.1), channel_id=1, source_target_pairs={{2,3},{3,2},{6,7},{7,6},{10,11},{11,10},{14,15},{15,14},{18,19},{1... | collective-permute-start | bytes 786440 | tf_op jit(solution)/shard_map/ppermute | solution.py:54
  55.7 6.0 %collective-permute-start.12 = (bf16[1024,128]{1,0:T(8,128)(2,1)S(1)}, bf16[1024,128]{1,0:T(8,128)(2,1)S(1)}, u32[]{:S(2)}, u32[]{:S(2)}) collective-permute-start(bf16[1024,128]{1,0:T(8,128)(2,1)S(1)} %dynamic-slice_convert_fusion), channel_id=1, source_target_pairs={{2,6},{3,7},{6,2},{7,3},{10,14},{11,15},{14,10},{15,11},{18,22},{1... | collective-permute-start | bytes 786440 | tf_op jit(solution)/shard_map/ppermute | solution.py:54
  61.0 1.5 %collective-permute-start.6 = (bf16[512,128]{1,0:T(8,128)(2,1)S(1)}, bf16[512,128]{1,0:T(8,128)(2,1)S(1)}, u32[]{:S(2)}, u32[]{:S(2)}) collective-permute-start(bf16[512,128]{1,0:T(8,128)(2,1)S(1)} %dynamic-slice_convert_fusion.3), channel_id=1, source_target_pairs={{2,6},{3,7},{6,2},{7,3},{10,14},{11,15},{14,10},{15,11},{18,22},{1... | collective-permute-start | bytes 393224 | tf_op jit(solution)/shard_map/ppermute | solution.py:54
  61.7 1.4 %collective-permute-start.13 = (bf16[512,128]{1,0:T(8,128)(2,1)S(1)}, bf16[512,128]{1,0:T(8,128)(2,1)S(1)}, u32[]{:S(2)}, u32[]{:S(2)}) collective-permute-start(bf16[512,128]{1,0:T(8,128)(2,1)S(1)} %dynamic-slice_convert_fusion.2), channel_id=1, source_target_pairs={{2,3},{3,2},{6,7},{7,6},{10,11},{11,10},{14,15},{15,14},{18,19},{1... | collective-permute-start | bytes 393224 | tf_op jit(solution)/shard_map/ppermute | solution.py:54
  62.5 1.4 %collective-permute-start.7 = (bf16[256,128]{1,0:T(8,128)(2,1)S(1)}, bf16[256,128]{1,0:T(8,128)(2,1)S(1)}, u32[]{:S(2)}, u32[]{:S(2)}) collective-permute-start(bf16[256,128]{1,0:T(8,128)(2,1)S(1)} %dynamic-slice_convert_fusion.5), channel_id=1, source_target_pairs={{2,10},{3,11},{6,14},{7,15},{10,2},{11,3},{14,6},{15,7},{18,26},{1... | collective-permute-start | bytes 196616 | tf_op jit(solution)/shard_map/ppermute | solution.py:54
  63.2 1.4 %collective-permute-start.14 = (bf16[256,128]{1,0:T(8,128)(2,1)S(1)}, bf16[256,128]{1,0:T(8,128)(2,1)S(1)}, u32[]{:S(2)}, u32[]{:S(2)}) collective-permute-start(bf16[256,128]{1,0:T(8,128)(2,1)S(1)} %dynamic-slice_convert_fusion.4), channel_id=1, source_target_pairs={{2,10},{3,11},{6,14},{7,15},{10,2},{11,3},{14,6},{15,7},{18,26},{1... | collective-permute-start | bytes 196616 | tf_op jit(solution)/shard_map/ppermute | solution.py:54
  64.0 1.4 %collective-permute-start.8 = (bf16[128,128]{1,0:T(8,128)(2,1)S(1)}, bf16[128,128]{1,0:T(8,128)(2,1)S(1)}, u32[]{:S(2)}, u32[]{:S(2)}) collective-permute-start(bf16[128,128]{1,0:T(8,128)(2,1)S(1)} %dynamic-slice_convert_fusion.7), channel_id=1, source_target_pairs={{2,18},{3,19},{6,22},{7,23},{10,26},{11,27},{14,30},{15,31},{18,2}... | collective-permute-start | bytes 98312 | tf_op jit(solution)/shard_map/ppermute | solution.py:54
  64.7 1.4 %collective-permute-start.15 = (bf16[128,128]{1,0:T(8,128)(2,1)S(1)}, bf16[128,128]{1,0:T(8,128)(2,1)S(1)}, u32[]{:S(2)}, u32[]{:S(2)}) collective-permute-start(bf16[128,128]{1,0:T(8,128)(2,1)S(1)} %dynamic-slice_convert_fusion.6), channel_id=1, source_target_pairs={{2,18},{3,19},{6,22},{7,23},{10,26},{11,27},{14,30},{15,31},{18,2}... | collective-permute-start | bytes 98312 | tf_op jit(solution)/shard_map/ppermute | solution.py:54
  65.4 1.4 %collective-permute-start.9 = (bf16[128,128]{1,0:T(8,128)(2,1)S(1)}, bf16[128,128]{1,0:T(8,128)(2,1)S(1)}, u32[]{:S(2)}, u32[]{:S(2)}) collective-permute-start(bf16[128,128]{1,0:T(8,128)(2,1)S(1)} %add_convert_fusion.1), channel_id=1, source_target_pairs={{2,18},{3,19},{6,22},{7,23},{10,26},{11,27},{14,30},{15,31},{18,2}... | collective-permute-start | bytes 98312 | tf_op jit(solution)/shard_map/ppermute | solution.py:54
  66.1 1.4 %collective-permute-start.16 = (bf16[128,128]{1,0:T(8,128)(2,1)S(1)}, bf16[128,128]{1,0:T(8,128)(2,1)S(1)}, u32[]{:S(2)}, u32[]{:S(2)}) collective-permute-start(bf16[128,128]{1,0:T(8,128)(2,1)S(1)} %add_convert_fusion), channel_id=1, source_target_pairs={{2,18},{3,19},{6,22},{7,23},{10,26},{11,27},{14,30},{15,31},{18,2}... | collective-permute-start | bytes 98312 | tf_op jit(solution)/shard_map/ppermute | solution.py:54
  66.8 1.4 %collective-permute-start.10 = (bf16[256,128]{1,0:T(8,128)(2,1)S(1)}, bf16[256,128]{1,0:T(8,128)(2,1)S(1)}, u32[]{:S(2)}, u32[]{:S(2)}) collective-permute-start(bf16[256,128]{1,0:T(8,128)(2,1)S(1)} %pad_maximum_fusion.7), channel_id=1, source_target_pairs={{2,10},{3,11},{6,14},{7,15},{10,2},{11,3},{14,6},{15,7},{18,26},{1... | collective-permute-start | bytes 196616 | tf_op jit(solution)/shard_map/ppermute | solution.py:54
  67.6 0.7 collective-permute-start.17
  68.3 1.4 %collective-permute-start.11 = (bf16[512,128]{1,0:T(8,128)(2,1)S(1)}, bf16[512,128]{1,0:T(8,128)(2,1)S(1)}, u32[]{:S(2)}, u32[]{:S(2)}) collective-permute-start(bf16[512,128]{1,0:T(8,128)(2,1)S(1)} %pad_maximum_fusion.5), channel_id=1, source_target_pairs={{2,6},{3,7},{6,2},{7,3},{10,14},{11,15},{14,10},{15,11},{18,22},{1... | collective-permute-start | bytes 393224 | tf_op jit(solution)/shard_map/ppermute | solution.py:54
  69.0 1.5 %collective-permute-start.18 = (bf16[512,128]{1,0:T(8,128)(2,1)S(1)}, bf16[512,128]{1,0:T(8,128)(2,1)S(1)}, u32[]{:S(2)}, u32[]{:S(2)}) collective-permute-start(bf16[512,128]{1,0:T(8,128)(2,1)S(1)} %pad_maximum_fusion.6), channel_id=1, source_target_pairs={{2,3},{3,2},{6,7},{7,6},{10,11},{11,10},{14,15},{15,14},{18,19},{1... | collective-permute-start | bytes 393224 | tf_op jit(solution)/shard_map/ppermute | solution.py:54
  69.8 2.8 %collective-permute-start.19 = (bf16[1024,128]{1,0:T(8,128)(2,1)S(1)}, bf16[1024,128]{1,0:T(8,128)(2,1)S(1)}, u32[]{:S(2)}, u32[]{:S(2)}) collective-permute-start(bf16[1024,128]{1,0:T(8,128)(2,1)S(1)} %pad_maximum_fusion.3.second_mine), channel_id=1, source_target_pairs={{2,3},{3,2},{6,7},{7,6},{10,11},{11,10},{14,15},{15,14},{18,19},{1... | collective-permute-start | bytes 786440 | tf_op jit(solution)/shard_map/ppermute | solution.py:54
  70.6 2.0 %collective-permute-start.20 = (bf16[1024,128]{1,0:T(8,128)(2,1)S(1)}, bf16[1024,128]{1,0:T(8,128)(2,1)S(1)}, u32[]{:S(2)}, u32[]{:S(2)}) collective-permute-start(bf16[1024,128]{1,0:T(8,128)(2,1)S(1)} %pad_maximum_fusion.4.first_mine), channel_id=1, source_target_pairs={{2,6},{3,7},{6,2},{7,3},{10,14},{11,15},{14,10},{15,11},{18,22},{1... | collective-permute-start | bytes 786440 | tf_op jit(solution)/shard_map/ppermute | solution.py:54
  71.3 41.8 %collective-permute-start.21 = (bf16[2048,128]{1,0:T(8,128)(2,1)S(1)}, bf16[2048,128]{1,0:T(8,128)(2,1)S(1)}, u32[]{:S(2)}, u32[]{:S(2)}) collective-permute-start(bf16[2048,128]{1,0:T(8,128)(2,1)S(1)} %pad_maximum_fusion), channel_id=1, source_target_pairs={{2,0},{6,4},{10,8},{14,12},{18,16},{22,20},{26,24},{30,28},{3,1},{... | collective-permute-start | bytes 1572872 | tf_op jit(solution)/shard_map/ppermute | solution.py:417
  72.7 44.5 %collective-permute-start.22 = (bf16[2048,128]{1,0:T(8,128)(2,1)S(1)}, bf16[2048,128]{1,0:T(8,128)(2,1)S(1)}, u32[]{:S(2)}, u32[]{:S(2)}) collective-permute-start(bf16[2048,128]{1,0:T(8,128)(2,1)S(1)} %pad_maximum_fusion.1), channel_id=1, source_target_pairs={{2,0},{6,4},{10,8},{14,12},{18,16},{22,20},{26,24},{30,28},{3,1},{... | collective-permute-start | bytes 1572872 | tf_op jit(solution)/shard_map/ppermute | solution.py:418
  (5 other events, 15.7 us)

commit v4 on v3

--- a/solution.py
+++ b/solution.py
@@ -16,22 +16,27 @@
 BF16 = jnp.bfloat16
 
 
+def neighbours(count, first):
+    pairs = [(i, i) for i in range(first)]
+    for i in range(first, count, 2):
+        pairs += [(i, i + 1), (i + 1, i)] if i + 1 < count else [(i, i)]
+    return pairs
+
+
 def halo_of(block, axis, dim, width):
     count = lax.axis_size(axis)
     size = block.shape[dim]
-    if count == 1:
-        empty = jnp.zeros_like(lax.slice_in_dim(block, 0, width, axis=dim))
-        return empty, empty
+    me = lax.axis_index(axis)
+    odd = me % 2
+    start = (1 - odd) * (size - width)
+    other = lax.ppermute(lax.dynamic_slice_in_dim(block, start, width, axis=dim), axis, neighbours(count, 0))
+    empty = jnp.zeros_like(other)
     if count == 2:
-        me = lax.axis_index(axis)
-        mine = lax.dynamic_slice_in_dim(block, (1 - me) * (size - width), width, axis=dim)
-        other = lax.ppermute(mine, axis, [(0, 1), (1, 0)])
-        empty = jnp.zeros_like(other)
-        return jnp.where(me == 1, other, empty), jnp.where(me == 0, other, empty)
-    forward = [(i, i + 1) for i in range(count - 1)]
-    backward = [(target, source) for source, target in forward]
-    low = lax.ppermute(lax.slice_in_dim(block, size - width, size, axis=dim), axis, forward)
-    high = lax.ppermute(lax.slice_in_dim(block, 0, width, axis=dim), axis, backward)
+        return jnp.where(odd == 1, other, empty), jnp.where(odd == 0, other, empty)
+    start = odd * (size - width)
+    next_other = lax.ppermute(lax.dynamic_slice_in_dim(block, start, width, axis=dim), axis, neighbours(count, 1))
+    low = jnp.where(me == 0, empty, jnp.where(odd == 1, other, next_other))
+    high = jnp.where(me == count - 1, empty, jnp.where(odd == 1, next_other, other))
     return low, high
 
 
@@ -47,9 +52,11 @@
 def swap(value, axis, bit):
     north = lax.axis_size("north")
     pairs = []
-    for e in range(1, lax.axis_size("east"), 2):
+    for e in range(lax.axis_size("east")):
         for n in range(north):
             partner = (e ^ bit, n) if axis == "east" else (e, n ^ bit)
+            if e % 2 == 0:
+                partner = (e, n)
             pairs.append((e * north + n, partner[0] * north + partner[1]))
     return lax.ppermute(value, ("east", "north"), pairs)
 
@@ -409,13 +416,12 @@
         features_out.append(out)
         return second_kept, first_kept
 
-    to_odd = [(e, e + 1) for e in range(0, lax.axis_size("east"), 2)]
-    to_even = [(e + 1, e) for e in range(0, lax.axis_size("east"), 2)]
-    sums = [value.astype(F32) + lax.ppermute(value, "east", to_odd).astype(F32) for value in (second, first)]
+    cores = neighbours(lax.axis_size("east"), 0)
+    sums = [value.astype(F32) + lax.ppermute(value, "east", cores).astype(F32) for value in (second, first)]
     sums = scatter_steps(sums, orders, beside)
     mine, other = gather_steps([total.astype(BF16) for total in sums], orders)
-    near = lax.ppermute(jnp.concatenate(mine, 0), "east", to_even)
-    far = lax.ppermute(jnp.concatenate(other, 0), "east", to_even)
+    near = lax.ppermute(jnp.concatenate(mine, 0), "east", cores)
+    far = lax.ppermute(jnp.concatenate(other, 0), "east", cores)
     flags = jnp.stack([high_bit("east", 1)] + [high_bit(*order[0]) for order in orders])
     grad_first, grad_second = pl.pallas_call(
         functools.partial(unpack_kernel, channels, scale),

time: 121 us -> 116 us (0.959)
  waiting for transfers between devices: 49.1 us -> 5.59 us
  starting transfers between devices: 26.5 us -> 65.5 us
    ppermute x7, waiting for transfers between devices: 49.1 us -> 5.55 us  [the longest x3 2.35 us: halo_of(): lax.ppermute(lax.dynamic_slice_in_dim(block, start, width, axis=dim), axi...]
    ppermute x7, starting transfers between devices: 15.7 us -> 54.7 us  [the longest x1 39.8 us: per_device(): near = lax.ppermute(jnp.concatenate(mine, 0), 'east', cores)]
  transfers between devices with their start and end apart: 23 -> 23, of which waited for: 5 -> 4; matrix products, arithmetic and copies ran while one was open for 2% -> 2% of each run, Pallas kernels for 3% -> 3%
where the time goes in v4:
time: 116 us; the launch traced here: 115 us
  starting transfers between devices  65.5 us (56%)
  Pallas kernels  33.2 us (29%)
  waiting for transfers between devices  5.59 us (5%)
  other arithmetic  5.28 us (5%)
  local copies, waits for them, and re-layouts  4.21 us (4%)
  between operations  1.29 us (1%)
    ppermute x1, starting transfers between devices, per_device(): near = lax.ppermute(jnp.concatenate(mine, 0), 'east', cores)  39.8 us
    pallas_call x1, Pallas kernels, per_device(): pl.pallas_call(functools.partial(whole_kernel, channels, classes, east, n...  26.8 us
    ppermute x16, starting transfers between devices, swap(): return lax.ppermute(value, ('east', 'north'), pairs)  10.8 us
    ppermute x2, starting transfers between devices, per_device(): lax.ppermute(value, 'east', cores).astype(F32)  7.35 us
    pallas_call x1, Pallas kernels, beside(): pl.pallas_call(functools.partial(last_kernel, channels, east, north, upwa...  3.81 us
    ppermute x1, starting transfers between devices, per_device(): far = lax.ppermute(jnp.concatenate(other, 0), 'east', cores)  3.77 us
    ppermute x3, starting transfers between devices, halo_of(): lax.ppermute(lax.dynamic_slice_in_dim(block, start, width, axis=dim), axi...  3.75 us
    pallas_call x1, Pallas kernels, per_device(): pl.pallas_call(functools.partial(unpack_kernel, channels, scale), out_sha...  2.67 us
  transfers between devices with their start and end apart: 23, of which 4 were waited for; matrix products, arithmetic and copies ran while one was open for 2% of the time, Pallas kernels for 3%

profile of v4, /device:TPU:0, one launch (start us, length us, event | category | flops | bytes accessed | tf_op | source)
XLA Modules:
  0.0 115.1 jit_solution(5810340983496556359)
XLA Ops:
  0.7 0.8 broadcast_in_dim.20
  1.5 0.8 fusion.3
  2.7 1.4 %copy.13 = bf16[8,16,8,13]{3,2,1,0:T(8,128)(2,1)S(1)} copy(bf16[8,16,8,13]{1,2,0,3:T(8,128)(2,1)} %bitcast.16) | data formatting | bytes 53248 | tf_op jit(solution)/shard_map/transpose | solution.py:349
  4.2 1.0 fusion
  5.2 3.0 %collective-permute-start = (bf16[8,4,8,128]{3,2,1,0:T(8,128)(2,1)S(1)}, bf16[8,4,8,128]{3,2,1,0:T(8,128)(2,1)S(1)}, u32[]{:S(2)}, u32[]{:S(2)}) collective-permute-start(bf16[8,4,8,128]{3,2,1,0:T(8,128)(2,1)S(1)} %fusion), channel_id=1, source_target_pairs={{0,1},{1,0},{2,3},{3,2},{4,5},{5,4},{6,7},{7,6},{8,9},{9,8},{10,11... | collective-permute-start | bytes 196616 | tf_op jit(solution)/shard_map/ppermute | solution.py:32
  8.2 2.2 %collective-permute-done = bf16[8,4,8,128]{3,2,1,0:T(8,128)(2,1)S(1)} collective-permute-done((bf16[8,4,8,128]{3,2,1,0:T(8,128)(2,1)S(1)}, bf16[8,4,8,128]{3,2,1,0:T(8,128)(2,1)S(1)}, u32[]{:S(2)}, u32[]{:S(2)}) %collective-permute-start) | collective-permute-done | bytes 65568 | tf_op jit(solution)/shard_map/ppermute | solution.py:32
  11.0 0.7 collective-permute-start.2
  12.4 1.3 %maximum_bitcast_fusion.x_ref = bf16[16,192,128]{2,1,0:T(8,128)(2,1)} fusion(bf16[4,24,8,128]{3,2,1,0:T(8,128)(2,1)S(1)} %get-tuple-element.20, bf16[8,4,8,128]{3,2,1,0:T(8,128)(2,1)S(1)} %get-tuple-element.36, bf16[8,16,8,18]{3,2,1,0:T(8,128)(2,1)S(1)} %broadcast_in_dim.23, bf16[8,16,8,13]{3,2,1,0:T(8,128)(2,1)S(1)} %copy.13, ...), kind=kLoop, calls=%fused_computation.2 | loop fusion | flops 6291456 | bytes 1572864 | tf_op jit(solution)/shard_map/reshape | solution.py:361
  13.7 26.8 %fields.1 = (bf16[10,192,128]{2,1,0:T(8,128)(2,1)}, bf16[2048,128]{1,0:T(8,128)(2,1)}, bf16[2048,128]{1,0:T(8,128)(2,1)}) custom-call(bf16[16,192,128]{2,1,0:T(8,128)(2,1)} %maximum_bitcast_fusion.x_ref, bf16[27,96,96]{2,1,0:T(8,128)(2,1)} %w1_ref.3, bf16[27,96,96]{2,1,0:T(8,128)(2,1)} %w2_ref.1, bf16[128,128]{1,0:T(8,128)(2,1)} %pad.4.head_ref), custom_call_target="tpu_custom_call" | custom-call | tf_op jit(solution)/shard_map/fields/pallas_call | solution.py:370
  40.5 7.3 %collective-permute-start.3 = (bf16[2048,128]{1,0:T(8,128)(2,1)}, bf16[2048,128]{1,0:T(8,128)(2,1)S(1)}, u32[]{:S(2)}, u32[]{:S(2)}) collective-permute-start(bf16[2048,128]{1,0:T(8,128)(2,1)} %get-tuple-element.12), channel_id=1, source_target_pairs={{0,2},{2,0},{4,6},{6,4},{8,10},{10,8},{12,14},{14,12},{16,18},{18,... | collective-permute-start | bytes 1572872 | tf_op jit(solution)/shard_map/ppermute | solution.py:420
  47.8 1.7 %collective-permute-done.3 = bf16[2048,128]{1,0:T(8,128)(2,1)S(1)} collective-permute-done((bf16[2048,128]{1,0:T(8,128)(2,1)}, bf16[2048,128]{1,0:T(8,128)(2,1)S(1)}, u32[]{:S(2)}, u32[]{:S(2)}) %collective-permute-start.3) | collective-permute-done | bytes 524320 | tf_op jit(solution)/shard_map/ppermute | solution.py:420
  49.6 1.1 convert_add_fusion.1
  50.8 0.7 collective-permute-start.5
  51.7 0.8 collective-permute-start.12
  53.1 3.8 %features.1 = (bf16[8,128,96]{2,1,0:T(8,128)(2,1)}, f32[1024,128]{1,0:T(8,128)S(1)}, f32[1024,128]{1,0:T(8,128)S(1)}) custom-call(bf16[16,192,128]{2,1,0:T(8,128)(2,1)S(1)} %copy-done, bf16[10,192,128]{2,1,0:T(8,128)(2,1)S(1)} %copy-done.2, bf16[27,96,96]{2,1,0:T(8,128)(2,1)S(1)} %copy-done.1, ...), custom_call_target="tpu_custom_call", output_to_operand_aliasing={{1}: (3, {}), {2}: (4, {})} | custom-call | tf_op jit(solution)/shard_map/features/pallas_call | solution.py:398
  56.9 0.7 collective-permute-start.6
  57.7 0.7 collective-permute-start.13
  65.0 0.7 collective-permute-start.18
  65.8 0.7 collective-permute-start.19
  66.6 0.7 collective-permute-start.20
  67.3 39.8 %collective-permute-start.21 = (bf16[2048,128]{1,0:T(8,128)(2,1)S(1)}, bf16[2048,128]{1,0:T(8,128)(2,1)S(1)}, u32[]{:S(2)}, u32[]{:S(2)}) collective-permute-start(bf16[2048,128]{1,0:T(8,128)(2,1)S(1)} %pad_maximum_fusion), channel_id=1, source_target_pairs={{0,2},{2,0},{4,6},{6,4},{8,10},{10,8},{12,14},{14,12},{16,18},{18,... | collective-permute-start | bytes 1572872 | tf_op jit(solution)/shard_map/ppermute | solution.py:423
  107.1 3.8 %collective-permute-start.22 = (bf16[2048,128]{1,0:T(8,128)(2,1)S(1)}, bf16[2048,128]{1,0:T(8,128)(2,1)S(1)}, u32[]{:S(2)}, u32[]{:S(2)}) collective-permute-start(bf16[2048,128]{1,0:T(8,128)(2,1)S(1)} %pad_maximum_fusion.1), channel_id=1, source_target_pairs={{0,2},{2,0},{4,6},{6,4},{8,10},{10,8},{12,14},{14,12},{16,18},{18,... | collective-permute-start | bytes 1572872 | tf_op jit(solution)/shard_map/ppermute | solution.py:424
  111.0 1.5 %collective-permute-done.22.far_ref = bf16[2048,128]{1,0:T(8,128)(2,1)S(1)} collective-permute-done((bf16[2048,128]{1,0:T(8,128)(2,1)S(1)}, bf16[2048,128]{1,0:T(8,128)(2,1)S(1)}, u32[]{:S(2)}, u32[]{:S(2)}) %collective-permute-start.22) | collective-permute-done | bytes 524320 | tf_op jit(solution)/shard_map/ppermute | solution.py:424
  112.4 2.7 %unpack.1 = (f32[27,96,96]{2,1,0:T(8,128)}, f32[27,96,96]{2,1,0:T(8,128)}) custom-call(s32[3]{0:T(128)S(1)} %pad_add_fusion.flags_ref, bf16[1024,128]{1,0:T(8,128)(2,1)S(1)} %pad_maximum_fusion.3.second_mine, bf16[1024,128]{1,0:T(8,128)(2,1)S(1)} %pad_maximum_fusion.4.first_mine, bf16[1024,128]{1,0:T(8,128)(2,1)S(1)} %collective-permute-done.19.second_other, ...), custom_call_target="tpu_custom_call" | custom-call | tf_op jit(solution)/shard_map/unpack/pallas_call | solution.py:426
  (84 shorter events, 9.4 us)
Async XLA Ops:
  0.6 9.9 %copy-start.3 = (bf16[96,8,16,8]{0,3,2,1:T(8,128)(2,1)S(1)}, bf16[96,8,16,8]{0,3,2,1:T(8,128)(2,1)}, u32[]{:S(2)}) copy-start(bf16[96,8,16,8]{0,3,2,1:T(8,128)(2,1)} %param.7) | copy-start | bytes 589828
  5.2 5.2 %collective-permute-start = (bf16[8,4,8,128]{3,2,1,0:T(8,128)(2,1)S(1)}, bf16[8,4,8,128]{3,2,1,0:T(8,128)(2,1)S(1)}, u32[]{:S(2)}, u32[]{:S(2)}) collective-permute-start(bf16[8,4,8,128]{3,2,1,0:T(8,128)(2,1)S(1)} %fusion), channel_id=1, source_target_pairs={{0,1},{1,0},{2,3},{3,2},{4,5},{5,4},{6,7},{7,6},{8,9},{9,8},{10,11... | collective-permute-start | bytes 196616 | tf_op jit(solution)/shard_map/ppermute | solution.py:32
  10.9 1.5 %collective-permute-start.1 = (bf16[4,24,8,128]{3,2,1,0:T(8,128)(2,1)S(1)}, bf16[4,24,8,128]{3,2,1,0:T(8,128)(2,1)S(1)}, u32[]{:S(2)}, u32[]{:S(2)}) collective-permute-start(bf16[4,24,8,128]{3,2,1,0:T(8,128)(2,1)S(1)} %get-tuple-element.21), channel_id=1, source_target_pairs={{0,2},{2,0},{4,6},{6,4},{8,10},{10,8},{12,14},{14,12},{16,18},{18,... | collective-permute-start | bytes 589832 | tf_op jit(solution)/shard_map/ppermute | solution.py:32
  11.0 1.4 %collective-permute-start.2 = (bf16[4,24,8,128]{3,2,1,0:T(8,128)(2,1)S(1)}, bf16[4,24,8,128]{3,2,1,0:T(8,128)(2,1)S(1)}, u32[]{:S(2)}, u32[]{:S(2)}) collective-permute-start(bf16[4,24,8,128]{3,2,1,0:T(8,128)(2,1)S(1)} %get-tuple-element.22), channel_id=1, source_target_pairs={{0,0},{2,4},{4,2},{6,8},{8,6},{10,12},{12,10},{14,16},{16,14},{18,... | collective-permute-start | bytes 589832 | tf_op jit(solution)/shard_map/ppermute | solution.py:37
  40.5 9.1 %collective-permute-start.3 = (bf16[2048,128]{1,0:T(8,128)(2,1)}, bf16[2048,128]{1,0:T(8,128)(2,1)S(1)}, u32[]{:S(2)}, u32[]{:S(2)}) collective-permute-start(bf16[2048,128]{1,0:T(8,128)(2,1)} %get-tuple-element.12), channel_id=1, source_target_pairs={{0,2},{2,0},{4,6},{6,4},{8,10},{10,8},{12,14},{14,12},{16,18},{18,... | collective-permute-start | bytes 1572872 | tf_op jit(solution)/shard_map/ppermute | solution.py:420
  47.8 3.6 %collective-permute-start.4 = (bf16[2048,128]{1,0:T(8,128)(2,1)}, bf16[2048,128]{1,0:T(8,128)(2,1)S(1)}, u32[]{:S(2)}, u32[]{:S(2)}) collective-permute-start(bf16[2048,128]{1,0:T(8,128)(2,1)} %get-tuple-element.13), channel_id=1, source_target_pairs={{0,2},{2,0},{4,6},{6,4},{8,10},{10,8},{12,14},{14,12},{16,18},{18,... | collective-permute-start | bytes 1572872 | tf_op jit(solution)/shard_map/ppermute | solution.py:420
  50.8 6.1 %collective-permute-start.5 = (bf16[1024,128]{1,0:T(8,128)(2,1)S(1)}, bf16[1024,128]{1,0:T(8,128)(2,1)S(1)}, u32[]{:S(2)}, u32[]{:S(2)}) collective-permute-start(bf16[1024,128]{1,0:T(8,128)(2,1)S(1)} %dynamic-slice_convert_fusion.1), channel_id=1, source_target_pairs={{0,0},{1,1},{2,3},{3,2},{4,4},{5,5},{6,7},{7,6},{8,8},{9,9},{10,11... | collective-permute-start | bytes 786440 | tf_op jit(solution)/shard_map/ppermute | solution.py:61
  51.7 6.0 %collective-permute-start.12 = (bf16[1024,128]{1,0:T(8,128)(2,1)S(1)}, bf16[1024,128]{1,0:T(8,128)(2,1)S(1)}, u32[]{:S(2)}, u32[]{:S(2)}) collective-permute-start(bf16[1024,128]{1,0:T(8,128)(2,1)S(1)} %dynamic-slice_convert_fusion), channel_id=1, source_target_pairs={{0,0},{1,1},{2,6},{3,7},{4,4},{5,5},{6,2},{7,3},{8,8},{9,9},{10,14... | collective-permute-start | bytes 786440 | tf_op jit(solution)/shard_map/ppermute | solution.py:61
  56.9 1.5 %collective-permute-start.6 = (bf16[512,128]{1,0:T(8,128)(2,1)S(1)}, bf16[512,128]{1,0:T(8,128)(2,1)S(1)}, u32[]{:S(2)}, u32[]{:S(2)}) collective-permute-start(bf16[512,128]{1,0:T(8,128)(2,1)S(1)} %dynamic-slice_convert_fusion.3), channel_id=1, source_target_pairs={{0,0},{1,1},{2,6},{3,7},{4,4},{5,5},{6,2},{7,3},{8,8},{9,9},{10,14... | collective-permute-start | bytes 393224 | tf_op jit(solution)/shard_map/ppermute | solution.py:61
  57.7 1.4 %collective-permute-start.13 = (bf16[512,128]{1,0:T(8,128)(2,1)S(1)}, bf16[512,128]{1,0:T(8,128)(2,1)S(1)}, u32[]{:S(2)}, u32[]{:S(2)}) collective-permute-start(bf16[512,128]{1,0:T(8,128)(2,1)S(1)} %dynamic-slice_convert_fusion.2), channel_id=1, source_target_pairs={{0,0},{1,1},{2,3},{3,2},{4,4},{5,5},{6,7},{7,6},{8,8},{9,9},{10,11... | collective-permute-start | bytes 393224 | tf_op jit(solution)/shard_map/ppermute | solution.py:61
  58.5 1.4 %collective-permute-start.7 = (bf16[256,128]{1,0:T(8,128)(2,1)S(1)}, bf16[256,128]{1,0:T(8,128)(2,1)S(1)}, u32[]{:S(2)}, u32[]{:S(2)}) collective-permute-start(bf16[256,128]{1,0:T(8,128)(2,1)S(1)} %dynamic-slice_convert_fusion.5), channel_id=1, source_target_pairs={{0,0},{1,1},{2,10},{3,11},{4,4},{5,5},{6,14},{7,15},{8,8},{9,9},{1... | collective-permute-start | bytes 196616 | tf_op jit(solution)/shard_map/ppermute | solution.py:61
  59.2 1.4 %collective-permute-start.14 = (bf16[256,128]{1,0:T(8,128)(2,1)S(1)}, bf16[256,128]{1,0:T(8,128)(2,1)S(1)}, u32[]{:S(2)}, u32[]{:S(2)}) collective-permute-start(bf16[256,128]{1,0:T(8,128)(2,1)S(1)} %dynamic-slice_convert_fusion.4), channel_id=1, source_target_pairs={{0,0},{1,1},{2,10},{3,11},{4,4},{5,5},{6,14},{7,15},{8,8},{9,9},{1... | collective-permute-start | bytes 196616 | tf_op jit(solution)/shard_map/ppermute | solution.py:61
  59.9 1.4 %collective-permute-start.8 = (bf16[128,128]{1,0:T(8,128)(2,1)S(1)}, bf16[128,128]{1,0:T(8,128)(2,1)S(1)}, u32[]{:S(2)}, u32[]{:S(2)}) collective-permute-start(bf16[128,128]{1,0:T(8,128)(2,1)S(1)} %dynamic-slice_convert_fusion.7), channel_id=1, source_target_pairs={{0,0},{1,1},{2,18},{3,19},{4,4},{5,5},{6,22},{7,23},{8,8},{9,9},{1... | collective-permute-start | bytes 98312 | tf_op jit(solution)/shard_map/ppermute | solution.py:61
  60.7 1.4 %collective-permute-start.15 = (bf16[128,128]{1,0:T(8,128)(2,1)S(1)}, bf16[128,128]{1,0:T(8,128)(2,1)S(1)}, u32[]{:S(2)}, u32[]{:S(2)}) collective-permute-start(bf16[128,128]{1,0:T(8,128)(2,1)S(1)} %dynamic-slice_convert_fusion.6), channel_id=1, source_target_pairs={{0,0},{1,1},{2,18},{3,19},{4,4},{5,5},{6,22},{7,23},{8,8},{9,9},{1... | collective-permute-start | bytes 98312 | tf_op jit(solution)/shard_map/ppermute | solution.py:61
  61.4 1.4 %collective-permute-start.9 = (bf16[128,128]{1,0:T(8,128)(2,1)S(1)}, bf16[128,128]{1,0:T(8,128)(2,1)S(1)}, u32[]{:S(2)}, u32[]{:S(2)}) collective-permute-start(bf16[128,128]{1,0:T(8,128)(2,1)S(1)} %add_convert_fusion.1), channel_id=1, source_target_pairs={{0,0},{1,1},{2,18},{3,19},{4,4},{5,5},{6,22},{7,23},{8,8},{9,9},{1... | collective-permute-start | bytes 98312 | tf_op jit(solution)/shard_map/ppermute | solution.py:61
  62.1 1.4 %collective-permute-start.16 = (bf16[128,128]{1,0:T(8,128)(2,1)S(1)}, bf16[128,128]{1,0:T(8,128)(2,1)S(1)}, u32[]{:S(2)}, u32[]{:S(2)}) collective-permute-start(bf16[128,128]{1,0:T(8,128)(2,1)S(1)} %add_convert_fusion), channel_id=1, source_target_pairs={{0,0},{1,1},{2,18},{3,19},{4,4},{5,5},{6,22},{7,23},{8,8},{9,9},{1... | collective-permute-start | bytes 98312 | tf_op jit(solution)/shard_map/ppermute | solution.py:61
  62.8 1.4 %collective-permute-start.10 = (bf16[256,128]{1,0:T(8,128)(2,1)S(1)}, bf16[256,128]{1,0:T(8,128)(2,1)S(1)}, u32[]{:S(2)}, u32[]{:S(2)}) collective-permute-start(bf16[256,128]{1,0:T(8,128)(2,1)S(1)} %pad_maximum_fusion.7), channel_id=1, source_target_pairs={{0,0},{1,1},{2,10},{3,11},{4,4},{5,5},{6,14},{7,15},{8,8},{9,9},{1... | collective-permute-start | bytes 196616 | tf_op jit(solution)/shard_map/ppermute | solution.py:61
  63.5 0.7 collective-permute-start.17
  64.3 1.4 %collective-permute-start.11 = (bf16[512,128]{1,0:T(8,128)(2,1)S(1)}, bf16[512,128]{1,0:T(8,128)(2,1)S(1)}, u32[]{:S(2)}, u32[]{:S(2)}) collective-permute-start(bf16[512,128]{1,0:T(8,128)(2,1)S(1)} %pad_maximum_fusion.5), channel_id=1, source_target_pairs={{0,0},{1,1},{2,6},{3,7},{4,4},{5,5},{6,2},{7,3},{8,8},{9,9},{10,14... | collective-permute-start | bytes 393224 | tf_op jit(solution)/shard_map/ppermute | solution.py:61
  65.0 1.5 %collective-permute-start.18 = (bf16[512,128]{1,0:T(8,128)(2,1)S(1)}, bf16[512,128]{1,0:T(8,128)(2,1)S(1)}, u32[]{:S(2)}, u32[]{:S(2)}) collective-permute-start(bf16[512,128]{1,0:T(8,128)(2,1)S(1)} %pad_maximum_fusion.6), channel_id=1, source_target_pairs={{0,0},{1,1},{2,3},{3,2},{4,4},{5,5},{6,7},{7,6},{8,8},{9,9},{10,11... | collective-permute-start | bytes 393224 | tf_op jit(solution)/shard_map/ppermute | solution.py:61
  65.8 41.3 %collective-permute-start.19 = (bf16[1024,128]{1,0:T(8,128)(2,1)S(1)}, bf16[1024,128]{1,0:T(8,128)(2,1)S(1)}, u32[]{:S(2)}, u32[]{:S(2)}) collective-permute-start(bf16[1024,128]{1,0:T(8,128)(2,1)S(1)} %pad_maximum_fusion.3.second_mine), channel_id=1, source_target_pairs={{0,0},{1,1},{2,3},{3,2},{4,4},{5,5},{6,7},{7,6},{8,8},{9,9},{10,11... | collective-permute-start | bytes 786440 | tf_op jit(solution)/shard_map/ppermute | solution.py:61
  66.6 40.5 %collective-permute-start.20 = (bf16[1024,128]{1,0:T(8,128)(2,1)S(1)}, bf16[1024,128]{1,0:T(8,128)(2,1)S(1)}, u32[]{:S(2)}, u32[]{:S(2)}) collective-permute-start(bf16[1024,128]{1,0:T(8,128)(2,1)S(1)} %pad_maximum_fusion.4.first_mine), channel_id=1, source_target_pairs={{0,0},{1,1},{2,6},{3,7},{4,4},{5,5},{6,2},{7,3},{8,8},{9,9},{10,14... | collective-permute-start | bytes 786440 | tf_op jit(solution)/shard_map/ppermute | solution.py:61
  67.3 43.7 %collective-permute-start.21 = (bf16[2048,128]{1,0:T(8,128)(2,1)S(1)}, bf16[2048,128]{1,0:T(8,128)(2,1)S(1)}, u32[]{:S(2)}, u32[]{:S(2)}) collective-permute-start(bf16[2048,128]{1,0:T(8,128)(2,1)S(1)} %pad_maximum_fusion), channel_id=1, source_target_pairs={{0,2},{2,0},{4,6},{6,4},{8,10},{10,8},{12,14},{14,12},{16,18},{18,... | collective-permute-start | bytes 1572872 | tf_op jit(solution)/shard_map/ppermute | solution.py:423
  107.1 5.3 %collective-permute-start.22 = (bf16[2048,128]{1,0:T(8,128)(2,1)S(1)}, bf16[2048,128]{1,0:T(8,128)(2,1)S(1)}, u32[]{:S(2)}, u32[]{:S(2)}) collective-permute-start(bf16[2048,128]{1,0:T(8,128)(2,1)S(1)} %pad_maximum_fusion.1), channel_id=1, source_target_pairs={{0,2},{2,0},{4,6},{6,4},{8,10},{10,8},{12,14},{14,12},{16,18},{18,... | collective-permute-start | bytes 1572872 | tf_op jit(solution)/shard_map/ppermute | solution.py:424
  (5 other events, 14.0 us)

commit v5 on v2

--- a/solution.py
+++ b/solution.py
@@ -16,28 +16,26 @@
 BF16 = jnp.bfloat16
 
 
-def halo_of(block, axis, dim, width):
+def rounds_of(axis):
     count = lax.axis_size(axis)
-    size = block.shape[dim]
-    if count == 1:
-        empty = jnp.zeros_like(lax.slice_in_dim(block, 0, width, axis=dim))
-        return empty, empty
-    if count == 2:
-        me = lax.axis_index(axis)
-        mine = lax.dynamic_slice_in_dim(block, (1 - me) * (size - width), width, axis=dim)
-        other = lax.ppermute(mine, axis, [(0, 1), (1, 0)])
-        empty = jnp.zeros_like(other)
-        return jnp.where(me == 1, other, empty), jnp.where(me == 0, other, empty)
-    forward = [(i, i + 1) for i in range(count - 1)]
-    backward = [(target, source) for source, target in forward]
-    low = lax.ppermute(lax.slice_in_dim(block, size - width, size, axis=dim), axis, forward)
-    high = lax.ppermute(lax.slice_in_dim(block, 0, width, axis=dim), axis, backward)
-    return low, high
-
-
-def exchange(value, axis, bit):
-    size = lax.axis_size(axis)
-    return lax.ppermute(value, axis, [(i, i ^ bit) for i in range(size)])
+    me = lax.axis_index(axis)
+    rounds = [(neighbours(count, 0), me % 2, jnp.int32(1))]
+    if count > 2:
+        inside = ((me > 0) & (me < count - 1)).astype(jnp.int32)
+        rounds.append((neighbours(count, 1), (me + 1) % 2, inside))
+    return rounds
+
+
+def neighbours(count, first):
+    pairs = []
+    for i in range(first, count, 2):
+        pairs += [(i, (i + 1) % count), ((i + 1) % count, i)]
+    return pairs
+
+
+def jointly(east_pairs, north_pairs):
+    north = lax.axis_size("north")
+    return [(e * north + n, f * north + m) for e, f in east_pairs for n, m in north_pairs]
 
 
 def high_bit(axis, bit):
@@ -49,23 +47,50 @@
     return [(axis, 1 << i) for i in range(size.bit_length() - 1)]
 
 
-def scatter_steps(kept, sent, order):
-    for step, (axis, bit) in enumerate(order):
-        total = kept + exchange(sent, axis, bit).astype(F32)
-        if step + 1 < len(order):
-            upper = high_bit(*order[step + 1])
-            half = total.shape[0] // 2
-            sent = lax.dynamic_slice_in_dim(total, (1 - upper) * half, half, 0).astype(BF16)
-            kept = lax.dynamic_slice_in_dim(total, upper * half, half, 0)
+def place_in(group):
+    return sum(high_bit(axis, bit) << i for i, (axis, bit) in enumerate(group))
+
+
+def swap(value, group, change):
+    masks = {"east": 0, "north": 0}
+    for i, (axis, bit) in enumerate(group):
+        if change >> i & 1:
+            masks[axis] |= bit
+    pairs = [[(i, i ^ masks[axis]) for i in range(lax.axis_size(axis))] for axis in ("east", "north")]
+    return lax.ppermute(value, ("east", "north"), jointly(*pairs))
+
+
+def scatter_sums(total, groups, beside):
+    for number, group in enumerate(groups):
+        ways = 1 << len(group)
+        part = total.shape[0] // ways
+        place = place_in(group)
+        sent = [
+            lax.dynamic_slice_in_dim(total, (place ^ change) * part, part, 0).astype(BF16)
+            for change in range(1, ways)
+        ]
+        kept = lax.dynamic_slice_in_dim(total, place * part, part, 0)
+        if number == 0:
+            kept = beside(kept)
+        for change in range(1, ways):
+            kept = kept + swap(sent[change - 1], group, change).astype(F32)
+        total = kept
     return total
 
 
-def gather_steps(mine, order):
-    for axis, bit in order[:0:-1]:
-        other = exchange(mine, axis, bit)
-        upper = high_bit(axis, bit) == 1
-        mine = jnp.concatenate([jnp.where(upper, other, mine), jnp.where(upper, mine, other)], 0)
-    return mine, exchange(mine, *order[0])
+def gather_parts(mine, groups):
+    for group in reversed(groups):
+        ways = 1 << len(group)
+        place = place_in(group)
+        parts = [mine] + [swap(mine, group, change) for change in range(1, ways)]
+        joined = []
+        for row in range(ways):
+            piece = parts[0]
+            for change in range(1, ways):
+                piece = jnp.where((place ^ row) == change, parts[change], piece)
+            joined.append(piece)
+        mine = jnp.concatenate(joined, 0)
+    return mine
 
 
 def lane_of(shape):
@@ -165,17 +190,87 @@
     return tiles
 
 
-def whole_kernel(
-    channels, classes, east, north, upward,
-    upper_ref, x_ref, w1_ref, w2_ref, head_ref,
-    grad_ref, kept_ref, sent_ref,
-    s0_ref, s1_ref, sg_ref, mask_ref, slope_ref, acc_ref, wt_ref, wb_ref, turned_ref,
+def prepare_kernel(
+    channels, upward, edge, east_rounds, north_rounds,
+    flags_ref, active_ref, features_ref, occupied_ref, teacher_ref,
+    center_ref, *edge_refs,
 ):
+    east, size, _ = center_ref.shape
+    north = size // upward
+    classes = teacher_ref.shape[0]
+    wide = (classes + 1) * upward
+    row = lax.broadcasted_iota(jnp.int32, (size, north), 0) // upward
+    spread = (row == lax.broadcasted_iota(jnp.int32, (size, north), 1)).astype(BF16)
+    level = lax.broadcasted_iota(jnp.int32, (size, wide), 0) % upward
+    same = level == lax.broadcasted_iota(jnp.int32, (size, wide), 1) % upward
+    target = lax.broadcasted_iota(jnp.int32, (wide, LANES), 0) // upward + channels
+    gather = (target == lax.broadcasted_iota(jnp.int32, (wide, LANES), 1)).astype(BF16)
+    bricks = active_ref.shape
+    up = lax.broadcasted_iota(jnp.int32, (upward, north), 0) // (upward // bricks[2])
+    along = lax.broadcasted_iota(jnp.int32, (upward, north), 1) // (north // bricks[1])
+    for e in range(east):
+        mask = jnp.zeros((upward, north), jnp.int32)
+        for b in range(bricks[1]):
+            for c in range(bricks[2]):
+                inside = (along == b) & (up == c)
+                mask = jnp.where(inside, active_ref[e // (east // bricks[0]), b, c], mask)
+        mask = (mask * occupied_ref[e]).astype(F32)
+        field = jnp.concatenate([mask] + [teacher_ref[c, e].astype(F32) for c in range(classes)], 0).astype(BF16)
+        everywhere = lax.dot_general(spread, field, (((1,), (1,)), ((), ())), preferred_element_type=F32)
+        own = jnp.where(same, everywhere, 0.0).astype(BF16)
+        tail = jnp.dot(own, gather, preferred_element_type=F32).astype(BF16)
+        center_ref[e, :, 0:channels] = features_ref[e]
+        center_ref[e, :, channels:LANES] = tail[:, channels:LANES]
+    east_starts = [(1 - flags_ref[r]) * (east - HALO) for r in range(east_rounds)]
+    north_starts = [
+        pl.multiple_of((1 - flags_ref[2 * east_rounds + r]) * (size - edge), edge) for r in range(north_rounds)
+    ]
+    edge_refs = iter(edge_refs)
+    for e in east_starts:
+        next(edge_refs)[...] = center_ref[pl.ds(e, HALO)]
+    for n in north_starts:
+        next(edge_refs)[...] = center_ref[:, pl.ds(n, edge), :]
+    for e in east_starts:
+        for n in north_starts:
+            next(edge_refs)[...] = center_ref[pl.ds(e, HALO), pl.ds(n, edge), :]
+
+
+def place_edges(flags_ref, center_ref, edge_refs, east_rounds, north_rounds, edge, x_ref):
+    east, size, _ = center_ref.shape
+    x_ref[...] = jnp.zeros_like(x_ref)
+    x_ref[HALO : HALO + east, edge : edge + size, :] = center_ref[...]
+    edge_refs = iter(edge_refs)
+    easts = [(flags_ref[r], flags_ref[east_rounds + r]) for r in range(east_rounds)]
+    base = 2 * east_rounds
+    norths = [(flags_ref[base + r], flags_ref[base + north_rounds + r]) for r in range(north_rounds)]
+    middle_east, middle_north = pl.ds(HALO, east), pl.ds(edge, size)
+    east_places = [(pl.ds((1 - side) * (east + HALO), HALO), inside) for side, inside in easts]
+    north_places = [
+        (pl.ds(pl.multiple_of((1 - side) * (size + edge), edge), edge), inside) for side, inside in norths
+    ]
+    spots = [(e, middle_north, inside) for e, inside in east_places]
+    spots += [(middle_east, n, inside) for n, inside in north_places]
+    spots += [(e, n, a * b) for e, a in east_places for n, b in north_places]
+    for e, n, inside in spots:
+        ref = next(edge_refs)
+
+        @pl.when(inside == 1)
+        def _(ref=ref, e=e, n=n):
+            x_ref[e, n, :] = ref[...]
+
+
+def whole_kernel(channels, classes, east, north, upward, east_rounds, north_rounds, flags_ref, w1_ref, w2_ref, head_ref, center_ref, *refs):
+    edges = east_rounds + north_rounds + east_rounds * north_rounds
+    (
+        grad_ref, kept_ref, sent_ref,
+        x_ref, s0_ref, s1_ref, sg_ref, mask_ref, slope_ref, acc_ref, wt_ref, wb_ref, turned_ref,
+    ) = refs[edges:]
     rows = (north + 2 * HALO) * upward
     low, size = HALO * upward, north * upward
     planes = east + 2 * HALO
     lane = lane_of((rows, LANES))
 
+    place_edges(flags_ref, center_ref, refs[:edges], east_rounds, north_rounds, low, x_ref)
     put_forward(wt_ref, w1_ref, channels)
 
     def start(i, carry):
@@ -226,9 +321,9 @@
             put_stack(g_p2, rows, upward, sg_ref, parity, i)
             put_turned(turned_ref, g_p2[low : low + size], plane - 2, east, channels)
 
-    upper = upper_ref[0] == 1
+    upper = flags_ref[2 * (east_rounds + north_rounds)] == 1
     for t, tile in enumerate(kernel_sum(turned_ref, s1_ref, 3, east, rows, low, size, channels)):
-        kept_ref[t * channels : (t + 1) * channels, :] = tile
+        kept_ref[t * channels : (t + 1) * channels, :] = tile.astype(BF16)
     convolve(sg_ref, wb_ref, (planes - 6) // 2, rows, acc_ref, False)
 
     for i in range((planes - 6) // 2):
@@ -239,18 +334,23 @@
             put_turned(turned_ref, g_p1[low : low + size], plane - 1, east, channels)
 
     tiles = kernel_sum(turned_ref, s0_ref, 4, east, rows, low, size, channels)
-    for t, first in enumerate(tiles):
+    for t, tile in enumerate(tiles):
         place = slice(t * channels, (t + 1) * channels)
-        second = kept_ref[place, :]
-        sent_ref[place, :] = jnp.where(upper, second, first).astype(BF16)
+        first, second = tile.astype(BF16), kept_ref[place, :]
+        sent_ref[place, :] = jnp.where(upper, second, first)
         kept_ref[place, :] = jnp.where(upper, first, second)
     filled = len(tiles) * channels
     if filled < kept_ref.shape[0]:
-        kept_ref[filled:, :] = jnp.zeros((kept_ref.shape[0] - filled, LANES), F32)
+        kept_ref[filled:, :] = jnp.zeros((kept_ref.shape[0] - filled, LANES), BF16)
         sent_ref[filled:, :] = jnp.zeros((kept_ref.shape[0] - filled, LANES), BF16)
 
 
-def last_kernel(channels, east, north, upward, x_ref, grad_ref, w1_ref, out_ref, stack_ref, wb_ref, acc_ref):
+def last_kernel(
+    channels, east, north, upward,
+    center_ref, grad_ref, w1_ref, kept_in,
+    out_ref, kept_out,
+    stack_ref, wb_ref, acc_ref,
+):
     rows = (north + 2 * HALO) * upward
     low, size = HALO * upward, north * upward
     put_backward(wb_ref, w1_ref, channels)
@@ -266,7 +366,7 @@
         for parity in range(2):
             plane = 2 * i + parity
             value = acc_ref[i * rows + low : i * rows + low + size, parity * LANES : (parity + 1) * LANES]
-            mask = x_ref[plane + HALO, low : low + size, channels : channels + 1].astype(F32)
+            mask = center_ref[plane, :, channels : channels + 1].astype(F32)
             out_ref[plane] = (mask * value)[:, 0:channels].astype(BF16)
 
 
@@ -297,47 +397,57 @@
     classes = teacher.shape[0]
     devices = lax.axis_size("east") * lax.axis_size("north")
     scale = 1.0 / math.sqrt(devices * east * north * upward)
-
-    flags = jnp.repeat(brick_active, east // brick_active.shape[0], 0)
-    flags = jnp.repeat(flags, north // brick_active.shape[1], 1)
-    flags = jnp.repeat(flags, upward // brick_active.shape[2], 2)
-    mask = (flags * voxel_occupancy).astype(BF16)
-    x = jnp.concatenate(
-        [
-            features.transpose(1, 2, 3, 0),
-            mask[..., None],
-            teacher.transpose(1, 2, 3, 0),
-            jnp.zeros((east, north, upward, LANES - channels - 1 - classes), BF16),
-        ],
-        -1,
-    )
-    low, high = halo_of(x, "north", 1, HALO)
-    x = jnp.concatenate([low, x, high], 1)
-    low, high = halo_of(x, "east", 0, HALO)
-    x = jnp.concatenate([low, x, high], 0)
-
     planes = east + 2 * HALO
     rows = (north + 2 * HALO) * upward
-    x = x.reshape(planes, rows, LANES)
+    edge, size = HALO * upward, north * upward
+    vmem = pl.BlockSpec(memory_space=pltpu.VMEM)
+    smem = pl.BlockSpec(memory_space=pltpu.SMEM)
+    anywhere = pl.BlockSpec(memory_space=pl.ANY)
+
+    east_bits, north_bits = bits_of("east"), bits_of("north")
+    rest = north_bits + east_bits[1:]
+    groups = [rest[i : i + 2] for i in range(0, len(rest), 2)]
+    upper = high_bit(*east_bits[0])
+    easts, norths = rounds_of("east"), rounds_of("north")
+    counts = (len(easts), len(norths))
+    flags = [side for _, side, _ in easts] + [inside for _, _, inside in easts]
+    flags += [side for _, side, _ in norths] + [inside for _, _, inside in norths] + [upper]
+    flags = jnp.stack(flags).astype(jnp.int32)
+
+    shapes = [(HALO, size, LANES)] * counts[0] + [(east, edge, LANES)] * counts[1]
+    shapes += [(HALO, edge, LANES)] * (counts[0] * counts[1])
+    center, *edges = pl.pallas_call(
+        functools.partial(prepare_kernel, channels, upward, edge, *counts),
+        out_shape=[jax.ShapeDtypeStruct(shape, BF16) for shape in [(east, size, LANES)] + shapes],
+        in_specs=[smem] * 2 + [vmem] * 3,
+        out_specs=[vmem] * (1 + len(shapes)),
+        compiler_params=pltpu.CompilerParams(vmem_limit_bytes=32 * 1024 * 1024),
+        name="prepare",
+    )(
+        flags,
+        brick_active,
+        features.transpose(1, 2, 3, 0).reshape(east, size, channels),
+        voxel_occupancy.transpose(0, 2, 1),
+        teacher.transpose(0, 1, 3, 2),
+    )
+    routes = [("east", pairs) for pairs, _, _ in easts] + [("north", pairs) for pairs, _, _ in norths]
+    routes += [(("east", "north"), jointly(a, b)) for a, _, _ in easts for b, _, _ in norths]
+    edges = [lax.ppermute(value, *route) for value, route in zip(edges, routes)]
+
     head_wide = jnp.pad(head, ((channels + 1, LANES - channels - 1 - classes), (0, LANES - channels)))
-
-    east_bits, north_bits = bits_of("east"), bits_of("north")
-    order = east_bits[:1] + north_bits + east_bits[1:]
-    upper = high_bit(*order[0]).reshape(1)
     unit = devices // 2 * 16
     packed = -(-21 * channels // unit) * unit
-    vmem = pl.BlockSpec(memory_space=pltpu.VMEM)
-    smem = pl.BlockSpec(memory_space=pltpu.SMEM)
     grad, kept, sent = pl.pallas_call(
-        functools.partial(whole_kernel, channels, classes, east, north, upward),
+        functools.partial(whole_kernel, channels, classes, east, north, upward, *counts),
         out_shape=(
             jax.ShapeDtypeStruct((east + 2, rows, LANES), BF16),
-            jax.ShapeDtypeStruct((packed, LANES), F32),
+            jax.ShapeDtypeStruct((packed, LANES), BF16),
             jax.ShapeDtypeStruct((packed, LANES), BF16),
         ),
-        in_specs=[smem] + [vmem] * 4,
+        in_specs=[smem] + [vmem] * (4 + len(edges)),
         out_specs=(vmem, vmem, vmem),
         scratch_shapes=[
+            pltpu.VMEM((planes, rows, LANES), BF16),
             pltpu.VMEM((2, planes // 2 * rows, WIDE), BF16),
             pltpu.VMEM((2, (planes - 2) // 2 * rows, WIDE), BF16),
             pltpu.VMEM((2, (planes - 4) // 2 * rows, WIDE), BF16),
@@ -346,28 +456,39 @@
             pltpu.VMEM(((planes - 2) // 2 * rows, 2 * LANES), F32),
             pltpu.VMEM((4, 2 * LANES, WIDE), BF16),
             pltpu.VMEM((4, WIDE, 2 * LANES), BF16),
-            pltpu.VMEM((3 * channels, east * north * upward), BF16),
+            pltpu.VMEM((3 * channels, east * size), BF16),
         ],
         compiler_params=pltpu.CompilerParams(vmem_limit_bytes=56 * 1024 * 1024),
         name="fields",
-    )(upper, x, first_weights, second_weights, head_wide)
-
-    grad_features = pl.pallas_call(
-        functools.partial(last_kernel, channels, east, north, upward),
-        out_shape=jax.ShapeDtypeStruct((east, north * upward, channels), BF16),
-        in_specs=[vmem] * 3,
-        out_specs=vmem,
-        scratch_shapes=[
-            pltpu.VMEM((2, (east + 2) // 2 * rows, WIDE), BF16),
-            pltpu.VMEM((4, WIDE, 2 * LANES), BF16),
-            pltpu.VMEM((east // 2 * rows, 2 * LANES), F32),
-        ],
-        compiler_params=pltpu.CompilerParams(vmem_limit_bytes=32 * 1024 * 1024),
-        name="features",
-    )(x, grad, first_weights)
-
-    total = scatter_steps(kept, sent, order)
-    mine, other = gather_steps(total.astype(BF16), order)
+    )(flags, first_weights, second_weights, head_wide, center, *edges)
+
+    features_out = []
+
+    def beside(kept):
+        out, kept = pl.pallas_call(
+            functools.partial(last_kernel, channels, east, north, upward),
+            out_shape=(
+                jax.ShapeDtypeStruct((east, size, channels), BF16),
+                jax.ShapeDtypeStruct(kept.shape, F32),
+            ),
+            in_specs=[vmem] * 3 + [anywhere],
+            out_specs=(vmem, anywhere),
+            input_output_aliases={3: 1},
+            scratch_shapes=[
+                pltpu.VMEM((2, (east + 2) // 2 * rows, WIDE), BF16),
+                pltpu.VMEM((4, WIDE, 2 * LANES), BF16),
+                pltpu.VMEM((east // 2 * rows, 2 * LANES), F32),
+            ],
+            compiler_params=pltpu.CompilerParams(vmem_limit_bytes=32 * 1024 * 1024),
+            name="features",
+        )(center, grad, first_weights, kept)
+        features_out.append(out)
+        return kept
+
+    total = kept.astype(F32) + swap(sent, east_bits[:1], 1).astype(F32)
+    total = scatter_sums(total, groups, beside)
+    mine = gather_parts(total.astype(BF16), groups)
+    other = swap(mine, east_bits[:1], 1)
     grad_first, grad_second = pl.pallas_call(
         functools.partial(unpack_kernel, channels, scale),
         out_shape=(
@@ -378,7 +499,8 @@
         out_specs=(vmem, vmem),
         compiler_params=pltpu.CompilerParams(vmem_limit_bytes=32 * 1024 * 1024),
         name="unpack",
-    )(upper, mine, other)
+    )(upper.reshape(1).astype(jnp.int32), mine, other)
+    (grad_features,) = features_out
     grad_features = grad_features.reshape(east, north, upward, channels).transpose(3, 0, 1, 2)
     return (grad_features, grad_first, grad_second)
 

time: 105 us -> 90.2 us (0.86)
  waiting for transfers between devices: 35.3 us -> 21.7 us
  other arithmetic: 5.03 us -> 1.64 us
  local copies, waits for them, and re-layouts: 3.56 us -> 6.29 us
  Pallas kernels: 33 us -> 35 us
  starting transfers between devices: 26.5 us -> 24.5 us
    ppermute x13 -> x19, waiting for transfers between devices: 35.3 us -> 21.7 us  [the longest x14 17.7 us: swap(): return lax.ppermute(value, ('east', 'north'), jointly(*pairs))]
    unnamed x10 -> x27, local copies, waits for them, and re-layouts: 0.03 us -> 4.79 us
    ppermute x13 -> x19, starting transfers between devices: 26.5 us -> 24.5 us  [the longest x14 15.2 us: swap(): return lax.ppermute(value, ('east', 'north'), jointly(*pairs))]
    pallas_call x1 -> x2, Pallas kernels: 3.81 us -> 5.8 us  [the longest x1 4.03 us: beside(): pl.pallas_call(functools.partial(last_kernel, channels, east, north, upwa...]
    transpose x1 -> x0, local copies, waits for them, and re-layouts: 1.42 us -> none  [per_device(): teacher.transpose(1, 2, 3, 0)]
    broadcast_in_dim x4 -> x0, local copies, waits for them, and re-layouts: 1.36 us -> none  [the longest x2 0.85 us: per_device(): flags = jnp.repeat(flags, north // brick_active.shape[1], 1)]
    concatenate x6 -> x2, other arithmetic: 1.41 us -> 0.05 us  [gather_parts(): mine = jnp.concatenate(joined, 0)]
    reshape x1 -> x0, other arithmetic: 1.25 us -> none  [per_device(): x = x.reshape(planes, rows, LANES)]
  transfers between devices with their start and end apart: 13 -> 19, of which waited for: 11 -> 13; matrix products, arithmetic and copies ran while one was open for 1% -> 1% of each run, Pallas kernels for 4% -> 4%
where the time goes in v5:
time: 90.2 us; the launch traced here: 89.9 us
  Pallas kernels  35 us (39%)
  starting transfers between devices  24.5 us (27%)
  waiting for transfers between devices  21.7 us (24%)
  local copies, waits for them, and re-layouts  6.29 us (7%)
  other arithmetic  1.64 us (2%)
    pallas_call x1, Pallas kernels, per_device(): pl.pallas_call(functools.partial(whole_kernel, channels, classes, east, n...  27.1 us
    ppermute x14, waiting for transfers between devices, swap(): return lax.ppermute(value, ('east', 'north'), jointly(*pairs))  17.7 us
    ppermute x14, starting transfers between devices, swap(): return lax.ppermute(value, ('east', 'north'), jointly(*pairs))  15.2 us
    ppermute x5, starting transfers between devices, per_device(): edges = [lax.ppermute(value, *route) for value, route in zip(edges, routes)]  9.3 us
    unnamed x27, local copies, waits for them, and re-layouts  4.79 us
    pallas_call x1, Pallas kernels, beside(): pl.pallas_call(functools.partial(last_kernel, channels, east, north, upwa...  4.03 us
    ppermute x5, waiting for transfers between devices, per_device(): edges = [lax.ppermute(value, *route) for value, route in zip(edges, routes)]  3.95 us
    pallas_call x1, Pallas kernels, per_device(): pl.pallas_call(functools.partial(unpack_kernel, channels, scale), out_sha...  2.02 us
  transfers between devices with their start and end apart: 19, of which 13 were waited for; matrix products, arithmetic and copies ran while one was open for 1% of the time, Pallas kernels for 4%

profile of v5, /device:TPU:0, one launch (start us, length us, event | category | flops | bytes accessed | tf_op | source)
XLA Modules:
  0.0 89.9 jit_solution(9987547722120330400)
XLA Ops:
  4.1 1.8 %prepare.1 = (bf16[8,128,128]{2,1,0:T(8,128)(2,1)S(1)}, bf16[4,128,128]{2,1,0:T(8,128)(2,1)S(1)}, bf16[4,128,128]{2,1,0:T(8,128)(2,1)S(1)}, bf16[8,32,128]{2,1,0...) custom-call(s32[7]{0:T(128)S(1)} %stack.24.flags_ref, ...), custom_call_target="tpu_custom_call" | custom-call | tf_op jit(solution)/shard_map/prepare/pallas_call | solution.py:419
  7.1 5.7 %collective-permute-start.1 = (bf16[4,128,128]{2,1,0:T(8,128)(2,1)S(1)}, bf16[4,128,128]{2,1,0:T(8,128)(2,1)S(1)}, u32[]{:S(2)}, u32[]{:S(2)}) collective-permute-start(bf16[4,128,128]{2,1,0:T(8,128)(2,1)S(1)} %get-tuple-element.18), channel_id=1, source_target_pairs={{2,4},{4,2},{6,8},{8,6},{10,12},{12,10},{14,16},{16,14},{18,20},{2... | collective-permute-start | bytes 393224 | tf_op jit(solution)/shard_map/ppermute | solution.py:435
  12.7 1.5 %collective-permute-start.2 = (bf16[8,32,128]{2,1,0:T(8,128)(2,1)S(1)}, bf16[8,32,128]{2,1,0:T(8,128)(2,1)S(1)}, u32[]{:S(2)}, u32[]{:S(2)}) collective-permute-start(bf16[8,32,128]{2,1,0:T(8,128)(2,1)S(1)} %get-tuple-element.19), channel_id=1, source_target_pairs={{0,1},{1,0},{2,3},{3,2},{4,5},{5,4},{6,7},{7,6},{8,9},{9,8},{10,11... | collective-permute-start | bytes 196616 | tf_op jit(solution)/shard_map/ppermute | solution.py:435
  14.2 1.7 %collective-permute-start.4 = (bf16[4,32,128]{2,1,0:T(8,128)(2,1)S(1)}, bf16[4,32,128]{2,1,0:T(8,128)(2,1)S(1)}, u32[]{:S(2)}, u32[]{:S(2)}) collective-permute-start(bf16[4,32,128]{2,1,0:T(8,128)(2,1)S(1)} %get-tuple-element.21), channel_id=1, source_target_pairs={{2,5},{3,4},{4,3},{5,2},{6,9},{7,8},{8,7},{9,6},{10,13},{11,12},{1... | collective-permute-start | bytes 98312 | tf_op jit(solution)/shard_map/ppermute | solution.py:435
  15.9 1.3 %pad.4.head_ref = bf16[128,128]{1,0:T(8,128)(2,1)} pad(bf16[13,96]{1,0:T(8,128)(2,1)} %param.12, bf16[]{:T(256)} %constant.119.clone.1), padding=97_18x0_32 | pad | bytes 35266 | tf_op jit(solution)/shard_map/jit(_pad)/pad | solution.py:437
  17.7 3.5 %collective-permute-done.4.refs_4_ = bf16[4,32,128]{2,1,0:T(8,128)(2,1)S(1)} collective-permute-done((bf16[4,32,128]{2,1,0:T(8,128)(2,1)S(1)}, bf16[4,32,128]{2,1,0:T(8,128)(2,1)S(1)}, u32[]{:S(2)}, u32[]{:S(2)}) %collective-permute-start.4) | collective-permute-done | bytes 32800 | tf_op jit(solution)/shard_map/ppermute | solution.py:435
  21.9 27.1 %fields.1 = (bf16[10,192,128]{2,1,0:T(8,128)(2,1)}, bf16[2048,128]{1,0:T(8,128)(2,1)}, bf16[2048,128]{1,0:T(8,128)(2,1)}) custom-call(s32[7]{0:T(128)} %copy-done.7, bf16[27,96,96]{2,1,0:T(8,128)(2,1)} %w1_ref.3, bf16[27,96,96]{2,1,0:T(8,128)(2,1)} %w2_ref.1, bf16[128,128]{1,0:T(8,128)(2,1)} %pad.4.head_ref, bf16[8,128,128]{2,1,0:T(8,128)(2,1)} %copy-done.1, ...), custom_call_target="tpu_custom_call" | custom-call | tf_op jit(solution)/shard_map/fields/pallas_call | solution.py:440
  49.1 2.1 %collective-permute-done.5 = bf16[2048,128]{1,0:T(8,128)(2,1)S(1)} collective-permute-done((bf16[2048,128]{1,0:T(8,128)(2,1)}, bf16[2048,128]{1,0:T(8,128)(2,1)S(1)}, u32[]{:S(2)}, u32[]{:S(2)}) %collective-permute-start.5) | collective-permute-done | bytes 524320 | tf_op jit(solution)/shard_map/ppermute | solution.py:60
  51.2 1.3 %convert_add_fusion = f32[2048,128]{1,0:T(8,128)S(1)} fusion(bf16[2048,128]{1,0:T(8,128)(2,1)S(1)} %collective-permute-done.5, bf16[2048,128]{1,0:T(8,128)(2,1)} %get-tuple-element.23), kind=kLoop, calls=%fused_computation | loop fusion | flops 786432 | bytes 2097152 | tf_op jit(solution)/shard_map/add | solution.py:488
  53.1 3.0 %collective-permute-start.7 = (bf16[512,128]{1,0:T(8,128)(2,1)S(1)}, bf16[512,128]{1,0:T(8,128)(2,1)S(1)}, u32[]{:S(2)}, u32[]{:S(2)}) collective-permute-start(bf16[512,128]{1,0:T(8,128)(2,1)S(1)} %get-tuple-element.31), channel_id=1, source_target_pairs={{0,4},{1,5},{2,6},{3,7},{4,0},{5,1},{6,2},{7,3},{8,12},{9,13},{10,... | collective-permute-start | bytes 393224 | tf_op jit(solution)/shard_map/ppermute | solution.py:60
  56.1 4.0 %features.1 = (bf16[8,128,96]{2,1,0:T(8,128)(2,1)}, f32[512,128]{1,0:T(8,128)S(1)}) custom-call(bf16[8,128,128]{2,1,0:T(8,128)(2,1)S(1)} %copy-done.2, bf16[10,192,128]{2,1,0:T(8,128)(2,1)S(1)} %copy-done.3, bf16[27,96,96]{2,1,0:T(8,128)(2,1)S(1)} %copy-done, f32[512,128]{1,0:T(8,128)S(1)} %constant_dynamic-slice_fusion.kept_in), custom_call_target="tpu_custom_call", output_to_operand_aliasing={{1}: (3, {})} | custom-call | tf_op jit(solution)/shard_map/features/pallas_call | solution.py:468
  60.2 1.9 %collective-permute-done.7 = bf16[512,128]{1,0:T(8,128)(2,1)S(1)} collective-permute-done((bf16[512,128]{1,0:T(8,128)(2,1)S(1)}, bf16[512,128]{1,0:T(8,128)(2,1)S(1)}, u32[]{:S(2)}, u32[]{:S(2)}) %collective-permute-start.7) | collective-permute-done | bytes 131104 | tf_op jit(solution)/shard_map/ppermute | solution.py:60
  62.3 1.4 %collective-permute-start.11 = (bf16[128,128]{1,0:T(8,128)(2,1)S(1)}, bf16[128,128]{1,0:T(8,128)(2,1)S(1)}, u32[]{:S(2)}, u32[]{:S(2)}) collective-permute-start(bf16[128,128]{1,0:T(8,128)(2,1)S(1)} %get-tuple-element.37), channel_id=1, source_target_pairs={{0,24},{1,25},{2,26},{3,27},{4,28},{5,29},{6,30},{7,31},{8,16},{9,... | collective-permute-start | bytes 98312 | tf_op jit(solution)/shard_map/ppermute | solution.py:60
  63.7 2.1 %collective-permute-start.10 = (bf16[128,128]{1,0:T(8,128)(2,1)S(1)}, bf16[128,128]{1,0:T(8,128)(2,1)S(1)}, u32[]{:S(2)}, u32[]{:S(2)}) collective-permute-start(bf16[128,128]{1,0:T(8,128)(2,1)S(1)} %get-tuple-element.38), channel_id=1, source_target_pairs={{0,16},{1,17},{2,18},{3,19},{4,20},{5,21},{6,22},{7,23},{8,24},{9,... | collective-permute-start | bytes 98312 | tf_op jit(solution)/shard_map/ppermute | solution.py:60
  66.2 1.9 %collective-permute-done.11 = bf16[128,128]{1,0:T(8,128)(2,1)S(1)} collective-permute-done((bf16[128,128]{1,0:T(8,128)(2,1)S(1)}, bf16[128,128]{1,0:T(8,128)(2,1)S(1)}, u32[]{:S(2)}, u32[]{:S(2)}) %collective-permute-start.11) | collective-permute-done | bytes 32800 | tf_op jit(solution)/shard_map/ppermute | solution.py:60
  69.6 2.0 %collective-permute-start.13 = (bf16[128,128]{1,0:T(8,128)(2,1)S(1)}, bf16[128,128]{1,0:T(8,128)(2,1)S(1)}, u32[]{:S(2)}, u32[]{:S(2)}) collective-permute-start(bf16[128,128]{1,0:T(8,128)(2,1)S(1)} %add_convert_fusion), channel_id=1, source_target_pairs={{0,16},{1,17},{2,18},{3,19},{4,20},{5,21},{6,22},{7,23},{8,24},{9,... | collective-permute-start | bytes 98312 | tf_op jit(solution)/shard_map/ppermute | solution.py:60
  71.6 1.4 %collective-permute-start.12 = (bf16[128,128]{1,0:T(8,128)(2,1)S(1)}, bf16[128,128]{1,0:T(8,128)(2,1)S(1)}, u32[]{:S(2)}, u32[]{:S(2)}) collective-permute-start(bf16[128,128]{1,0:T(8,128)(2,1)S(1)} %add_convert_fusion), channel_id=1, source_target_pairs={{0,24},{1,25},{2,26},{3,27},{4,28},{5,29},{6,30},{7,31},{8,16},{9,... | collective-permute-start | bytes 98312 | tf_op jit(solution)/shard_map/ppermute | solution.py:60
  73.0 1.5 %collective-permute-done.13 = bf16[128,128]{1,0:T(8,128)(2,1)S(1)} collective-permute-done((bf16[128,128]{1,0:T(8,128)(2,1)S(1)}, bf16[128,128]{1,0:T(8,128)(2,1)S(1)}, u32[]{:S(2)}, u32[]{:S(2)}) %collective-permute-start.13) | collective-permute-done | bytes 32800 | tf_op jit(solution)/shard_map/ppermute | solution.py:60
  74.4 2.9 %collective-permute-done.12 = bf16[128,128]{1,0:T(8,128)(2,1)S(1)} collective-permute-done((bf16[128,128]{1,0:T(8,128)(2,1)S(1)}, bf16[128,128]{1,0:T(8,128)(2,1)S(1)}, u32[]{:S(2)}, u32[]{:S(2)}) %collective-permute-start.12) | collective-permute-done | bytes 32800 | tf_op jit(solution)/shard_map/ppermute | solution.py:60
  78.1 1.7 %collective-permute-start.16 = (bf16[512,128]{1,0:T(8,128)(2,1)S(1)}, bf16[512,128]{1,0:T(8,128)(2,1)S(1)}, u32[]{:S(2)}, u32[]{:S(2)}) collective-permute-start(bf16[512,128]{1,0:T(8,128)(2,1)S(1)} %pad_maximum_fusion.1), channel_id=1, source_target_pairs={{0,4},{1,5},{2,6},{3,7},{4,0},{5,1},{6,2},{7,3},{8,12},{9,13},{10,... | collective-permute-start | bytes 393224 | tf_op jit(solution)/shard_map/ppermute | solution.py:60
  80.9 1.5 %collective-permute-done.17 = bf16[512,128]{1,0:T(8,128)(2,1)S(1)} collective-permute-done((bf16[512,128]{1,0:T(8,128)(2,1)S(1)}, bf16[512,128]{1,0:T(8,128)(2,1)S(1)}, u32[]{:S(2)}, u32[]{:S(2)}) %collective-permute-start.17) | collective-permute-done | bytes 131104 | tf_op jit(solution)/shard_map/ppermute | solution.py:60
  83.0 2.6 %collective-permute-done.15 = bf16[512,128]{1,0:T(8,128)(2,1)S(1)} collective-permute-done((bf16[512,128]{1,0:T(8,128)(2,1)S(1)}, bf16[512,128]{1,0:T(8,128)(2,1)S(1)}, u32[]{:S(2)}, u32[]{:S(2)}) %collective-permute-start.15) | collective-permute-done | bytes 131104 | tf_op jit(solution)/shard_map/ppermute | solution.py:60
  86.0 1.9 %collective-permute-done.18.other_ref = bf16[2048,128]{1,0:T(8,128)(2,1)S(1)} collective-permute-done((bf16[2048,128]{1,0:T(8,128)(2,1)S(1)}, bf16[2048,128]{1,0:T(8,128)(2,1)S(1)}, u32[]{:S(2)}, u32[]{:S(2)}) %collective-permute-start.18) | collective-permute-done | bytes 524320 | tf_op jit(solution)/shard_map/ppermute | solution.py:60
  87.9 2.0 %unpack.1 = (f32[27,96,96]{2,1,0:T(8,128)}, f32[27,96,96]{2,1,0:T(8,128)}) custom-call(s32[1]{0:T(128)} %bitcast.upper_ref, bf16[2048,128]{1,0:T(8,128)(2,1)S(1)} %pad_maximum_fusion.mine_ref, bf16[2048,128]{1,0:T(8,128)(2,1)S(1)} %collective-permute-done.18.other_ref), custom_call_target="tpu_custom_call" | custom-call | tf_op jit(solution)/shard_map/unpack/pallas_call | solution.py:492
  (58 shorter events, 11.4 us)
Async XLA Ops:
  1.5 19.7 %copy-start.7 = (s32[7]{0:T(128)}, s32[7]{0:T(128)S(1)}, u32[]{:S(2)}) copy-start(s32[7]{0:T(128)S(1)} %stack.24.flags_ref) | copy-start | bytes 88
  6.6 14.6 %collective-permute-start = (bf16[4,128,128]{2,1,0:T(8,128)(2,1)S(1)}, bf16[4,128,128]{2,1,0:T(8,128)(2,1)S(1)}, u32[]{:S(2)}, u32[]{:S(2)}) collective-permute-start(bf16[4,128,128]{2,1,0:T(8,128)(2,1)S(1)} %get-tuple-element.17), channel_id=1, source_target_pairs={{0,2},{2,0},{4,6},{6,4},{8,10},{10,8},{12,14},{14,12},{16,18},{18,... | collective-permute-start | bytes 393224 | tf_op jit(solution)/shard_map/ppermute | solution.py:435
  7.1 14.1 %collective-permute-start.1 = (bf16[4,128,128]{2,1,0:T(8,128)(2,1)S(1)}, bf16[4,128,128]{2,1,0:T(8,128)(2,1)S(1)}, u32[]{:S(2)}, u32[]{:S(2)}) collective-permute-start(bf16[4,128,128]{2,1,0:T(8,128)(2,1)S(1)} %get-tuple-element.18), channel_id=1, source_target_pairs={{2,4},{4,2},{6,8},{8,6},{10,12},{12,10},{14,16},{16,14},{18,20},{2... | collective-permute-start | bytes 393224 | tf_op jit(solution)/shard_map/ppermute | solution.py:435
  12.7 8.4 %collective-permute-start.2 = (bf16[8,32,128]{2,1,0:T(8,128)(2,1)S(1)}, bf16[8,32,128]{2,1,0:T(8,128)(2,1)S(1)}, u32[]{:S(2)}, u32[]{:S(2)}) collective-permute-start(bf16[8,32,128]{2,1,0:T(8,128)(2,1)S(1)} %get-tuple-element.19), channel_id=1, source_target_pairs={{0,1},{1,0},{2,3},{3,2},{4,5},{5,4},{6,7},{7,6},{8,9},{9,8},{10,11... | collective-permute-start | bytes 196616 | tf_op jit(solution)/shard_map/ppermute | solution.py:435
  14.2 3.5 %collective-permute-start.3 = (bf16[4,32,128]{2,1,0:T(8,128)(2,1)S(1)}, bf16[4,32,128]{2,1,0:T(8,128)(2,1)S(1)}, u32[]{:S(2)}, u32[]{:S(2)}) collective-permute-start(bf16[4,32,128]{2,1,0:T(8,128)(2,1)S(1)} %get-tuple-element.20), channel_id=1, source_target_pairs={{0,3},{1,2},{2,1},{3,0},{4,7},{5,6},{6,5},{7,4},{8,11},{9,10},{10,... | collective-permute-start | bytes 98312 | tf_op jit(solution)/shard_map/ppermute | solution.py:435
  14.2 6.9 %collective-permute-start.4 = (bf16[4,32,128]{2,1,0:T(8,128)(2,1)S(1)}, bf16[4,32,128]{2,1,0:T(8,128)(2,1)S(1)}, u32[]{:S(2)}, u32[]{:S(2)}) collective-permute-start(bf16[4,32,128]{2,1,0:T(8,128)(2,1)S(1)} %get-tuple-element.21), channel_id=1, source_target_pairs={{2,5},{3,4},{4,3},{5,2},{6,9},{7,8},{8,7},{9,6},{10,13},{11,12},{1... | collective-permute-start | bytes 98312 | tf_op jit(solution)/shard_map/ppermute | solution.py:435
  17.7 3.5 %copy-start.11 = (bf16[4,32,128]{2,1,0:T(8,128)(2,1)}, bf16[4,32,128]{2,1,0:T(8,128)(2,1)S(1)}, u32[]{:S(2)}) copy-start(bf16[4,32,128]{2,1,0:T(8,128)(2,1)S(1)} %collective-permute-done.3.refs_3_) | copy-start | bytes 98308
  49.1 2.1 %collective-permute-start.5 = (bf16[2048,128]{1,0:T(8,128)(2,1)}, bf16[2048,128]{1,0:T(8,128)(2,1)S(1)}, u32[]{:S(2)}, u32[]{:S(2)}) collective-permute-start(bf16[2048,128]{1,0:T(8,128)(2,1)} %get-tuple-element.24), channel_id=1, source_target_pairs={{0,2},{1,3},{2,0},{3,1},{4,6},{5,7},{6,4},{7,5},{8,10},{9,11},{10,... | collective-permute-start | bytes 1572872 | tf_op jit(solution)/shard_map/ppermute | solution.py:60
  51.2 4.9 %copy-start = (bf16[27,96,96]{2,1,0:T(8,128)(2,1)S(1)}, bf16[27,96,96]{2,1,0:T(8,128)(2,1)}, u32[]{:S(2)}) copy-start(bf16[27,96,96]{2,1,0:T(8,128)(2,1)} %w1_ref.3) | copy-start | bytes 1492996
  51.2 4.9 %copy-start.2 = (bf16[8,128,128]{2,1,0:T(8,128)(2,1)S(1)}, bf16[8,128,128]{2,1,0:T(8,128)(2,1)}, u32[]{:S(2)}) copy-start(bf16[8,128,128]{2,1,0:T(8,128)(2,1)} %copy-done.1) | copy-start | bytes 786436
  51.2 4.9 %copy-start.3 = (bf16[10,192,128]{2,1,0:T(8,128)(2,1)S(1)}, bf16[10,192,128]{2,1,0:T(8,128)(2,1)}, u32[]{:S(2)}) copy-start(bf16[10,192,128]{2,1,0:T(8,128)(2,1)} %get-tuple-element.22.grad_ref) | copy-start | bytes 1474564
  52.5 7.6 %collective-permute-start.6 = (bf16[512,128]{1,0:T(8,128)(2,1)S(1)}, bf16[512,128]{1,0:T(8,128)(2,1)S(1)}, u32[]{:S(2)}, u32[]{:S(2)}) collective-permute-start(bf16[512,128]{1,0:T(8,128)(2,1)S(1)} %get-tuple-element.29), channel_id=1, source_target_pairs={{0,1},{1,0},{2,3},{3,2},{4,5},{5,4},{6,7},{7,6},{8,9},{9,8},{10,11... | collective-permute-start | bytes 393224 | tf_op jit(solution)/shard_map/ppermute | solution.py:60
  53.1 7.0 %collective-permute-start.8 = (bf16[512,128]{1,0:T(8,128)(2,1)S(1)}, bf16[512,128]{1,0:T(8,128)(2,1)S(1)}, u32[]{:S(2)}, u32[]{:S(2)}) collective-permute-start(bf16[512,128]{1,0:T(8,128)(2,1)S(1)} %get-tuple-element.30), channel_id=1, source_target_pairs={{0,5},{1,4},{2,7},{3,6},{4,1},{5,0},{6,3},{7,2},{8,13},{9,12},{10,... | collective-permute-start | bytes 393224 | tf_op jit(solution)/shard_map/ppermute | solution.py:60
  53.1 9.0 %collective-permute-start.7 = (bf16[512,128]{1,0:T(8,128)(2,1)S(1)}, bf16[512,128]{1,0:T(8,128)(2,1)S(1)}, u32[]{:S(2)}, u32[]{:S(2)}) collective-permute-start(bf16[512,128]{1,0:T(8,128)(2,1)S(1)} %get-tuple-element.31), channel_id=1, source_target_pairs={{0,4},{1,5},{2,6},{3,7},{4,0},{5,1},{6,2},{7,3},{8,12},{9,13},{10,... | collective-permute-start | bytes 393224 | tf_op jit(solution)/shard_map/ppermute | solution.py:60
  62.2 4.0 %collective-permute-start.9 = (bf16[128,128]{1,0:T(8,128)(2,1)S(1)}, bf16[128,128]{1,0:T(8,128)(2,1)S(1)}, u32[]{:S(2)}, u32[]{:S(2)}) collective-permute-start(bf16[128,128]{1,0:T(8,128)(2,1)S(1)} %get-tuple-element.36), channel_id=1, source_target_pairs={{0,8},{1,9},{2,10},{3,11},{4,12},{5,13},{6,14},{7,15},{8,0},{9,1},... | collective-permute-start | bytes 98312 | tf_op jit(solution)/shard_map/ppermute | solution.py:60
  62.3 5.8 %collective-permute-start.11 = (bf16[128,128]{1,0:T(8,128)(2,1)S(1)}, bf16[128,128]{1,0:T(8,128)(2,1)S(1)}, u32[]{:S(2)}, u32[]{:S(2)}) collective-permute-start(bf16[128,128]{1,0:T(8,128)(2,1)S(1)} %get-tuple-element.37), channel_id=1, source_target_pairs={{0,24},{1,25},{2,26},{3,27},{4,28},{5,29},{6,30},{7,31},{8,16},{9,... | collective-permute-start | bytes 98312 | tf_op jit(solution)/shard_map/ppermute | solution.py:60
  63.7 4.8 %collective-permute-start.10 = (bf16[128,128]{1,0:T(8,128)(2,1)S(1)}, bf16[128,128]{1,0:T(8,128)(2,1)S(1)}, u32[]{:S(2)}, u32[]{:S(2)}) collective-permute-start(bf16[128,128]{1,0:T(8,128)(2,1)S(1)} %get-tuple-element.38), channel_id=1, source_target_pairs={{0,16},{1,17},{2,18},{3,19},{4,20},{5,21},{6,22},{7,23},{8,24},{9,... | collective-permute-start | bytes 98312 | tf_op jit(solution)/shard_map/ppermute | solution.py:60
  68.5 4.5 %collective-permute-start.14 = (bf16[128,128]{1,0:T(8,128)(2,1)S(1)}, bf16[128,128]{1,0:T(8,128)(2,1)S(1)}, u32[]{:S(2)}, u32[]{:S(2)}) collective-permute-start(bf16[128,128]{1,0:T(8,128)(2,1)S(1)} %add_convert_fusion), channel_id=1, source_target_pairs={{0,8},{1,9},{2,10},{3,11},{4,12},{5,13},{6,14},{7,15},{8,0},{9,1},... | collective-permute-start | bytes 98312 | tf_op jit(solution)/shard_map/ppermute | solution.py:60
  69.6 4.8 %collective-permute-start.13 = (bf16[128,128]{1,0:T(8,128)(2,1)S(1)}, bf16[128,128]{1,0:T(8,128)(2,1)S(1)}, u32[]{:S(2)}, u32[]{:S(2)}) collective-permute-start(bf16[128,128]{1,0:T(8,128)(2,1)S(1)} %add_convert_fusion), channel_id=1, source_target_pairs={{0,16},{1,17},{2,18},{3,19},{4,20},{5,21},{6,22},{7,23},{8,24},{9,... | collective-permute-start | bytes 98312 | tf_op jit(solution)/shard_map/ppermute | solution.py:60
  71.6 5.7 %collective-permute-start.12 = (bf16[128,128]{1,0:T(8,128)(2,1)S(1)}, bf16[128,128]{1,0:T(8,128)(2,1)S(1)}, u32[]{:S(2)}, u32[]{:S(2)}) collective-permute-start(bf16[128,128]{1,0:T(8,128)(2,1)S(1)} %add_convert_fusion), channel_id=1, source_target_pairs={{0,24},{1,25},{2,26},{3,27},{4,28},{5,29},{6,30},{7,31},{8,16},{9,... | collective-permute-start | bytes 98312 | tf_op jit(solution)/shard_map/ppermute | solution.py:60
  77.4 5.0 %collective-permute-start.17 = (bf16[512,128]{1,0:T(8,128)(2,1)S(1)}, bf16[512,128]{1,0:T(8,128)(2,1)S(1)}, u32[]{:S(2)}, u32[]{:S(2)}) collective-permute-start(bf16[512,128]{1,0:T(8,128)(2,1)S(1)} %pad_maximum_fusion.1), channel_id=1, source_target_pairs={{0,1},{1,0},{2,3},{3,2},{4,5},{5,4},{6,7},{7,6},{8,9},{9,8},{10,11... | collective-permute-start | bytes 393224 | tf_op jit(solution)/shard_map/ppermute | solution.py:60
  78.1 5.0 %collective-permute-start.16 = (bf16[512,128]{1,0:T(8,128)(2,1)S(1)}, bf16[512,128]{1,0:T(8,128)(2,1)S(1)}, u32[]{:S(2)}, u32[]{:S(2)}) collective-permute-start(bf16[512,128]{1,0:T(8,128)(2,1)S(1)} %pad_maximum_fusion.1), channel_id=1, source_target_pairs={{0,4},{1,5},{2,6},{3,7},{4,0},{5,1},{6,2},{7,3},{8,12},{9,13},{10,... | collective-permute-start | bytes 393224 | tf_op jit(solution)/shard_map/ppermute | solution.py:60
  79.8 5.9 %collective-permute-start.15 = (bf16[512,128]{1,0:T(8,128)(2,1)S(1)}, bf16[512,128]{1,0:T(8,128)(2,1)S(1)}, u32[]{:S(2)}, u32[]{:S(2)}) collective-permute-start(bf16[512,128]{1,0:T(8,128)(2,1)S(1)} %pad_maximum_fusion.1), channel_id=1, source_target_pairs={{0,5},{1,4},{2,7},{3,6},{4,1},{5,0},{6,3},{7,2},{8,13},{9,12},{10,... | collective-permute-start | bytes 393224 | tf_op jit(solution)/shard_map/ppermute | solution.py:60
  85.9 2.0 %collective-permute-start.18 = (bf16[2048,128]{1,0:T(8,128)(2,1)S(1)}, bf16[2048,128]{1,0:T(8,128)(2,1)S(1)}, u32[]{:S(2)}, u32[]{:S(2)}) collective-permute-start(bf16[2048,128]{1,0:T(8,128)(2,1)S(1)} %pad_maximum_fusion.mine_ref), channel_id=1, source_target_pairs={{0,2},{1,3},{2,0},{3,1},{4,6},{5,7},{6,4},{7,5},{8,10},{9,11},{10,... | collective-permute-start | bytes 1572872 | tf_op jit(solution)/shard_map/ppermute | solution.py:60
  (8 other events, 6.0 us)

commit v6 on v5

--- a/solution.py
+++ b/solution.py
@@ -60,8 +60,8 @@
     return lax.ppermute(value, ("east", "north"), jointly(*pairs))
 
 
-def scatter_sums(total, groups, beside):
-    for number, group in enumerate(groups):
+def scatter_sums(total, groups):
+    for group in groups:
         ways = 1 << len(group)
         part = total.shape[0] // ways
         place = place_in(group)
@@ -69,12 +69,9 @@
             lax.dynamic_slice_in_dim(total, (place ^ change) * part, part, 0).astype(BF16)
             for change in range(1, ways)
         ]
-        kept = lax.dynamic_slice_in_dim(total, place * part, part, 0)
-        if number == 0:
-            kept = beside(kept)
+        total = lax.dynamic_slice_in_dim(total, place * part, part, 0)
         for change in range(1, ways):
-            kept = kept + swap(sent[change - 1], group, change).astype(F32)
-        total = kept
+            total = total + swap(sent[change - 1], group, change).astype(F32)
     return total
 
 
@@ -97,21 +94,19 @@
     return lax.broadcasted_iota(jnp.int32, shape, len(shape) - 1)
 
 
-def put_stack(value, rows, upward, stack_ref, parity, index):
-    cubes = value.reshape(rows // upward, upward, LANES)
+def put_stack(value, upward, stack_ref, parity, index):
+    total = value.shape[0]
+    rows = total - 2 * upward
+    cubes = value.reshape(total // upward, upward, LANES)
     level = lax.broadcasted_iota(jnp.int32, cubes.shape, 1)
-    below = jnp.where(level == 0, 0.0, pltpu.roll(cubes, 1, 1)).reshape(rows, LANES)
-    above = jnp.where(level == upward - 1, 0.0, pltpu.roll(cubes, upward - 1, 1)).reshape(rows, LANES)
-    start = index * rows
+    below = jnp.where(level == 0, 0.0, pltpu.roll(cubes, 1, 1)).reshape(total, LANES)
+    above = jnp.where(level == upward - 1, 0.0, pltpu.roll(cubes, upward - 1, 1)).reshape(total, LANES)
     for up, moved in enumerate((below, value, above)):
-        shifts = (
-            jnp.concatenate([moved[rows - upward :], moved[: rows - upward]], 0),
-            moved,
-            jnp.concatenate([moved[upward:], moved[:upward]], 0),
-        )
+        even = moved.astype(BF16)
+        shifts = (even[0:rows], moved[upward : upward + rows].astype(BF16), even[2 * upward :])
         for north, shifted in enumerate(shifts):
             lane = (north * 3 + up) * LANES
-            stack_ref[parity, pl.ds(start, rows), lane : lane + LANES] = shifted.astype(BF16)
+            stack_ref[parity, pl.ds(index * rows, rows), lane : lane + LANES] = shifted
 
 
 def convolve(stack_ref, weight_ref, pairs, rows, acc_ref, transposed):
@@ -129,26 +124,35 @@
     acc_ref[0 : pairs * rows, :] = total
 
 
-def put_forward(weight_ref, w_ref, channels):
-    weight_ref[...] = jnp.zeros_like(weight_ref)
-    for p in range(4):
-        for q in range(2):
-            if 0 <= p - q <= 2:
-                for j in range(OFFSETS):
-                    weight_ref[p, q * LANES : q * LANES + channels, j * LANES : j * LANES + channels] = w_ref[
-                        (p - q) * OFFSETS + j
-                    ]
-
-
-def put_backward(weight_ref, w_ref, channels):
-    weight_ref[...] = jnp.zeros_like(weight_ref)
-    for p in range(4):
-        for q in range(2):
-            if 0 <= p - q <= 2:
-                for j in range(OFFSETS):
-                    weight_ref[p, j * LANES : j * LANES + channels, q * LANES : q * LANES + channels] = w_ref[
-                        (2 - (p - q)) * OFFSETS + 8 - j
-                    ]
+def weights_kernel(
+    channels, classes,
+    w1_in, w2_in, head_ref,
+    ahead1_ref, ahead2_ref, back1_ref, back2_ref, head_out,
+    w1_ref, w2_ref, arrived,
+):
+    copies = [
+        pltpu.make_async_copy(w1_in, w1_ref, arrived.at[0]),
+        pltpu.make_async_copy(w2_in, w2_ref, arrived.at[1]),
+    ]
+    for copy in copies:
+        copy.start()
+    for ref in (ahead1_ref, ahead2_ref, back1_ref, back2_ref):
+        ref[...] = jnp.zeros_like(ref)
+    for copy in copies:
+        copy.wait()
+    for w_ref, ahead_ref, back_ref in ((w1_ref, ahead1_ref, back1_ref), (w2_ref, ahead2_ref, back2_ref)):
+        for d in range(3):
+            for j in range(OFFSETS):
+                value = w_ref[d * OFFSETS + j]
+                for q in range(2):
+                    side = slice(q * LANES, q * LANES + channels)
+                    ahead_ref[d + q, side, j * LANES : j * LANES + channels] = value
+                    turn = (OFFSETS - 1 - j) * LANES
+                    back_ref[2 - d + q, turn : turn + channels, side] = value
+    row = lax.broadcasted_iota(jnp.int32, (LANES, classes), 0)
+    spread = (row == lax.broadcasted_iota(jnp.int32, (LANES, classes), 1) + channels + 1).astype(BF16)
+    head_out[...] = jnp.zeros_like(head_out)
+    head_out[:, 0:channels] = jnp.dot(spread, head_ref[...], preferred_element_type=F32).astype(BF16)
 
 
 def put_turned(turned_ref, value, plane, east, channels):
@@ -192,9 +196,20 @@
 
 def prepare_kernel(
     channels, upward, edge, east_rounds, north_rounds,
-    flags_ref, active_ref, features_ref, occupied_ref, teacher_ref,
+    flags_ref, active_ref, features_in, occupied_in, teacher_in,
     center_ref, *edge_refs,
 ):
+    *edge_refs, features_ref, occupied_ref, teacher_ref, arrived = edge_refs
+    copies = [
+        pltpu.make_async_copy(source, target, arrived.at[i])
+        for i, (source, target) in enumerate(
+            ((occupied_in, occupied_ref), (teacher_in, teacher_ref), (features_in, features_ref))
+        )
+    ]
+    for copy in copies:
+        copy.start()
+    for copy in copies:
+        copy.wait()
     east, size, _ = center_ref.shape
     north = size // upward
     classes = teacher_ref.shape[0]
@@ -259,19 +274,24 @@
             x_ref[e, n, :] = ref[...]
 
 
-def whole_kernel(channels, classes, east, north, upward, east_rounds, north_rounds, flags_ref, w1_ref, w2_ref, head_ref, center_ref, *refs):
+def whole_kernel(
+    channels, classes, east, north, upward, east_rounds, north_rounds,
+    flags_ref, ahead1_ref, ahead2_ref, back2_ref, head_ref, center_ref, *refs,
+):
     edges = east_rounds + north_rounds + east_rounds * north_rounds
     (
         grad_ref, kept_ref, sent_ref,
-        x_ref, s0_ref, s1_ref, sg_ref, mask_ref, slope_ref, acc_ref, wt_ref, wb_ref, turned_ref,
+        x_ref, s0_ref, s1_ref, sg_ref, mask_ref, slope_ref, acc_ref, turned_ref,
     ) = refs[edges:]
     rows = (north + 2 * HALO) * upward
     low, size = HALO * upward, north * upward
     planes = east + 2 * HALO
     lane = lane_of((rows, LANES))
+    rows1, rows2, rows3 = rows - 2 * upward, rows - 4 * upward, rows - 6 * upward
+    low1, low2, low3 = low - upward, low - 2 * upward, low - 3 * upward
 
     place_edges(flags_ref, center_ref, refs[:edges], east_rounds, north_rounds, low, x_ref)
-    put_forward(wt_ref, w1_ref, channels)
+    border = jnp.zeros((upward, LANES), F32)
 
     def start(i, carry):
         for parity in range(2):
@@ -279,12 +299,11 @@
             mask = jnp.broadcast_to(x[:, channels : channels + 1], (rows, LANES))
             mask_ref[2 * i + parity] = mask
             a0 = jnp.where((mask > 0) & (lane < channels), x, 0.0)
-            put_stack(a0, rows, upward, s0_ref, parity, i)
+            put_stack(jnp.concatenate([border, a0, border], 0), upward, s0_ref, parity, i)
         return carry
 
     lax.fori_loop(0, planes // 2, start, 0)
-    convolve(s0_ref, wt_ref, (planes - 2) // 2, rows, acc_ref, True)
-    put_forward(wt_ref, w2_ref, channels)
+    convolve(s0_ref, ahead1_ref, (planes - 2) // 2, rows, acc_ref, True)
 
     def middle(i, carry):
         for parity in range(2):
@@ -293,45 +312,48 @@
             p1 = mask * acc_ref[pl.ds(i * rows, rows), parity * LANES : (parity + 1) * LANES]
             sig = jax.nn.sigmoid(p1)
             slope_ref[plane] = mask * (sig * (1.0 + p1 * (1.0 - sig)))
-            put_stack(p1 * sig, rows, upward, s1_ref, parity, i)
+            put_stack((p1 * sig)[upward : upward + rows1], upward, s1_ref, parity, i)
         return carry
 
     lax.fori_loop(0, (planes - 2) // 2, middle, 0)
-    convolve(s1_ref, wt_ref, (planes - 4) // 2, rows, acc_ref, True)
-    put_backward(wb_ref, w2_ref, channels)
+    convolve(s1_ref, ahead2_ref, (planes - 4) // 2, rows2, acc_ref, True)
 
     head = head_ref[...]
-    class_lane = (lane > channels) & (lane <= channels + classes)
+    class_lane = (lane[0:rows2] > channels) & (lane[0:rows2] <= channels + classes)
+    here = slice(2 * upward, 2 * upward + rows2)
 
     for i in range((planes - 4) // 2):
         for parity in range(2):
             plane = 2 * i + parity
-            mask = mask_ref[plane + 2]
-            p2 = mask * acc_ref[i * rows : (i + 1) * rows, parity * LANES : (parity + 1) * LANES]
+            mask = mask_ref[plane + 2, here]
+            p2 = mask * acc_ref[i * rows2 : (i + 1) * rows2, parity * LANES : (parity + 1) * LANES]
             sig = jax.nn.sigmoid(p2)
             a2 = (p2 * sig).astype(BF16)
             logits = lax.dot_general(a2, head, (((1,), (1,)), ((), ())), preferred_element_type=F32)
-            g_logits = jnp.where(class_lane, mask * (logits - x_ref[plane + 2].astype(F32)), 0.0)
+            g_logits = jnp.where(class_lane, mask * (logits - x_ref[plane + 2, here].astype(F32)), 0.0)
             coarse = g_logits.astype(BF16)
             fine = (g_logits - coarse.astype(F32)).astype(BF16)
             g_a2 = jnp.dot(
                 jnp.concatenate([coarse, fine], 1), jnp.concatenate([head, head], 0), preferred_element_type=F32
             )
             g_p2 = mask * g_a2 * (sig * (1.0 + p2 * (1.0 - sig)))
-            put_stack(g_p2, rows, upward, sg_ref, parity, i)
-            put_turned(turned_ref, g_p2[low : low + size], plane - 2, east, channels)
+            put_stack(g_p2, upward, sg_ref, parity, i)
+            put_turned(turned_ref, g_p2[low2 : low2 + size], plane - 2, east, channels)
 
     upper = flags_ref[2 * (east_rounds + north_rounds)] == 1
-    for t, tile in enumerate(kernel_sum(turned_ref, s1_ref, 3, east, rows, low, size, channels)):
+    for t, tile in enumerate(kernel_sum(turned_ref, s1_ref, 3, east, rows2, low2, size, channels)):
         kept_ref[t * channels : (t + 1) * channels, :] = tile.astype(BF16)
-    convolve(sg_ref, wb_ref, (planes - 6) // 2, rows, acc_ref, False)
-
+    convolve(sg_ref, back2_ref, (planes - 6) // 2, rows3, acc_ref, False)
+
+    there = slice(2 * upward + upward, 2 * upward + upward + rows3)
     for i in range((planes - 6) // 2):
         for parity in range(2):
             plane = 2 * i + parity
-            g_p1 = slope_ref[plane + 2] * acc_ref[i * rows : (i + 1) * rows, parity * LANES : (parity + 1) * LANES]
+            g_p1 = slope_ref[plane + 2, there] * acc_ref[
+                i * rows3 : (i + 1) * rows3, parity * LANES : (parity + 1) * LANES
+            ]
             grad_ref[plane] = g_p1.astype(BF16)
-            put_turned(turned_ref, g_p1[low : low + size], plane - 1, east, channels)
+            put_turned(turned_ref, g_p1[low3 : low3 + size], plane - 1, east, channels)
 
     tiles = kernel_sum(turned_ref, s0_ref, 4, east, rows, low, size, channels)
     for t, tile in enumerate(tiles):
@@ -347,46 +369,68 @@
 
 def last_kernel(
     channels, east, north, upward,
-    center_ref, grad_ref, w1_ref, kept_in,
+    center_ref, grad_ref, back1_ref, kept_in,
     out_ref, kept_out,
-    stack_ref, wb_ref, acc_ref,
+    stack_ref, acc_ref,
 ):
-    rows = (north + 2 * HALO) * upward
-    low, size = HALO * upward, north * upward
-    put_backward(wb_ref, w1_ref, channels)
+    size = north * upward
 
     def start(i, carry):
         for parity in range(2):
-            put_stack(grad_ref[2 * i + parity].astype(F32), rows, upward, stack_ref, parity, i)
+            put_stack(grad_ref[2 * i + parity].astype(F32), upward, stack_ref, parity, i)
         return carry
 
     lax.fori_loop(0, east // 2 + 1, start, 0)
-    convolve(stack_ref, wb_ref, east // 2, rows, acc_ref, False)
+    convolve(stack_ref, back1_ref, east // 2, size, acc_ref, False)
     for i in range(east // 2):
         for parity in range(2):
             plane = 2 * i + parity
-            value = acc_ref[i * rows + low : i * rows + low + size, parity * LANES : (parity + 1) * LANES]
+            value = acc_ref[i * size : (i + 1) * size, parity * LANES : (parity + 1) * LANES]
             mask = center_ref[plane, :, channels : channels + 1].astype(F32)
             out_ref[plane] = (mask * value)[:, 0:channels].astype(BF16)
 
 
-def unpack_kernel(channels, scale, upper_ref, mine_ref, other_ref, first_out, second_out):
+def parts_kernel(place_ref, kept_ref, came_ref, total_ref, *sent_refs):
+    part = total_ref.shape[0]
+    for change, ref in enumerate((total_ref,) + sent_refs):
+        start = pl.multiple_of((place_ref[0] ^ change) * part, part)
+        rows = pl.ds(start, part)
+        ref[...] = (kept_ref[rows, :].astype(F32) + came_ref[rows, :].astype(F32)).astype(ref.dtype)
+
+
+def unpack_kernel(channels, scale, aliased, first_ref_flag, packed_ref, *refs):
+    first_out, second_out, whole_ref, done = refs[2:] if aliased else refs
     spare = LANES - channels
-    upper = upper_ref[0] == 1
-    for target, here in ((first_out, upper), (second_out, jnp.logical_not(upper))):
-        for t in range(0, 27, 4):
-            tiles = []
-            for r in range(3):
-                start = (t // 4 * 3 + r) * channels
-                place = slice(start, start + channels)
-                tiles.append(jnp.where(here, mine_ref[place, :], other_ref[place, :]).astype(F32) * scale)
-            for r in range(3):
-                target[t + r] = tiles[r][:, 0:channels]
-            if t + 3 < 27:
-                lane = lane_of(tiles[0].shape)
-                parts = [pltpu.roll(tiles[r], (spare * r - channels) % LANES, 1) for r in range(3)]
-                last = jnp.where(lane < spare, parts[0], jnp.where(lane < 2 * spare, parts[1], parts[2]))
-                target[t + 3] = last[:, 0:channels]
+    is_first = first_ref_flag[0] == 1
+    spans = [(t, min(t + 4, 27)) for t in range(0, 27, 4)]
+
+    def copy_of(target, i):
+        a, b = spans[i]
+        return pltpu.make_async_copy(whole_ref.at[a:b], target.at[a:b], done.at[i])
+
+    for i, (t, stop) in enumerate(spans):
+        tiles = []
+        for r in range(3):
+            start = (t // 4 * 3 + r) * channels
+            tiles.append(packed_ref[start : start + channels, :].astype(F32) * scale)
+        for r in range(3):
+            whole_ref[t + r] = tiles[r][:, 0:channels]
+        if stop - t == 4:
+            lane = lane_of(tiles[0].shape)
+            parts = [pltpu.roll(tiles[r], (spare * r - channels) % LANES, 1) for r in range(3)]
+            last = jnp.where(lane < spare, parts[0], jnp.where(lane < 2 * spare, parts[1], parts[2]))
+            whole_ref[t + 3] = last[:, 0:channels]
+
+        @pl.when(is_first)
+        def _(i=i):
+            copy_of(first_out, i).start()
+
+        @pl.when(jnp.logical_not(is_first))
+        def _(i=i):
+            copy_of(second_out, i).start()
+
+    for i in range(len(spans)):
+        copy_of(first_out, i).wait()
 
 
 def per_device(
@@ -403,6 +447,7 @@
     vmem = pl.BlockSpec(memory_space=pltpu.VMEM)
     smem = pl.BlockSpec(memory_space=pltpu.SMEM)
     anywhere = pl.BlockSpec(memory_space=pl.ANY)
+    far = pl.BlockSpec(memory_space=pltpu.HBM)
 
     east_bits, north_bits = bits_of("east"), bits_of("north")
     rest = north_bits + east_bits[1:]
@@ -419,48 +464,70 @@
     center, *edges = pl.pallas_call(
         functools.partial(prepare_kernel, channels, upward, edge, *counts),
         out_shape=[jax.ShapeDtypeStruct(shape, BF16) for shape in [(east, size, LANES)] + shapes],
-        in_specs=[smem] * 2 + [vmem] * 3,
+        in_specs=[smem] * 2 + [far] * 3,
         out_specs=[vmem] * (1 + len(shapes)),
-        compiler_params=pltpu.CompilerParams(vmem_limit_bytes=32 * 1024 * 1024),
+        scratch_shapes=[
+            pltpu.VMEM((east, size, channels), BF16),
+            pltpu.VMEM((east, upward, north), jnp.int32),
+            pltpu.VMEM((classes, east, upward, north), BF16),
+            pltpu.SemaphoreType.DMA((3,)),
+        ],
+        compiler_params=pltpu.CompilerParams(vmem_limit_bytes=16 * 1024 * 1024),
         name="prepare",
     )(
         flags,
         brick_active,
-        features.transpose(1, 2, 3, 0).reshape(east, size, channels),
-        voxel_occupancy.transpose(0, 2, 1),
-        teacher.transpose(0, 1, 3, 2),
+        pltpu.with_memory_space_constraint(features.transpose(1, 2, 3, 0).reshape(east, size, channels), pltpu.HBM),
+        pltpu.with_memory_space_constraint(voxel_occupancy.transpose(0, 2, 1), pltpu.HBM),
+        pltpu.with_memory_space_constraint(teacher.transpose(0, 1, 3, 2), pltpu.HBM),
     )
     routes = [("east", pairs) for pairs, _, _ in easts] + [("north", pairs) for pairs, _, _ in norths]
     routes += [(("east", "north"), jointly(a, b)) for a, _, _ in easts for b, _, _ in norths]
     edges = [lax.ppermute(value, *route) for value, route in zip(edges, routes)]
 
-    head_wide = jnp.pad(head, ((channels + 1, LANES - channels - 1 - classes), (0, LANES - channels)))
     unit = devices // 2 * 16
     packed = -(-21 * channels // unit) * unit
+    wide = (4, 2 * LANES, WIDE)
+    tall = (4, WIDE, 2 * LANES)
+    ahead1, ahead2, back1, back2, head_wide = pl.pallas_call(
+        functools.partial(weights_kernel, channels, classes),
+        out_shape=[jax.ShapeDtypeStruct(shape, BF16) for shape in (wide, wide, tall, tall, (LANES, LANES))],
+        in_specs=[far, far, vmem],
+        out_specs=[vmem] * 5,
+        scratch_shapes=[
+            pltpu.VMEM(first_weights.shape, BF16),
+            pltpu.VMEM(second_weights.shape, BF16),
+            pltpu.SemaphoreType.DMA((2,)),
+        ],
+        compiler_params=pltpu.CompilerParams(vmem_limit_bytes=20 * 1024 * 1024),
+        name="weights",
+    )(
+        pltpu.with_memory_space_constraint(first_weights, pltpu.HBM),
+        pltpu.with_memory_space_constraint(second_weights, pltpu.HBM),
+        head,
+    )
     grad, kept, sent = pl.pallas_call(
         functools.partial(whole_kernel, channels, classes, east, north, upward, *counts),
         out_shape=(
-            jax.ShapeDtypeStruct((east + 2, rows, LANES), BF16),
+            jax.ShapeDtypeStruct((east + 2, rows - 6 * upward, LANES), BF16),
             jax.ShapeDtypeStruct((packed, LANES), BF16),
             jax.ShapeDtypeStruct((packed, LANES), BF16),
         ),
-        in_specs=[smem] + [vmem] * (4 + len(edges)),
+        in_specs=[smem] + [vmem] * (5 + len(edges)),
         out_specs=(vmem, vmem, vmem),
         scratch_shapes=[
             pltpu.VMEM((planes, rows, LANES), BF16),
             pltpu.VMEM((2, planes // 2 * rows, WIDE), BF16),
-            pltpu.VMEM((2, (planes - 2) // 2 * rows, WIDE), BF16),
-            pltpu.VMEM((2, (planes - 4) // 2 * rows, WIDE), BF16),
+            pltpu.VMEM((2, (planes - 2) // 2 * (rows - 4 * upward), WIDE), BF16),
+            pltpu.VMEM((2, (planes - 4) // 2 * (rows - 6 * upward), WIDE), BF16),
             pltpu.VMEM((planes, rows, LANES), F32),
             pltpu.VMEM((planes - 2, rows, LANES), F32),
             pltpu.VMEM(((planes - 2) // 2 * rows, 2 * LANES), F32),
-            pltpu.VMEM((4, 2 * LANES, WIDE), BF16),
-            pltpu.VMEM((4, WIDE, 2 * LANES), BF16),
             pltpu.VMEM((3 * channels, east * size), BF16),
         ],
-        compiler_params=pltpu.CompilerParams(vmem_limit_bytes=56 * 1024 * 1024),
+        compiler_params=pltpu.CompilerParams(vmem_limit_bytes=38 * 1024 * 1024),
         name="fields",
-    )(flags, first_weights, second_weights, head_wide, center, *edges)
+    )(flags, ahead1, ahead2, back2, head_wide, center, *edges)
 
     features_out = []
 
@@ -475,31 +542,50 @@
             out_specs=(vmem, anywhere),
             input_output_aliases={3: 1},
             scratch_shapes=[
-                pltpu.VMEM((2, (east + 2) // 2 * rows, WIDE), BF16),
-                pltpu.VMEM((4, WIDE, 2 * LANES), BF16),
-                pltpu.VMEM((east // 2 * rows, 2 * LANES), F32),
+                pltpu.VMEM((2, (east + 2) // 2 * size, WIDE), BF16),
+                pltpu.VMEM((east // 2 * size, 2 * LANES), F32),
             ],
-            compiler_params=pltpu.CompilerParams(vmem_limit_bytes=32 * 1024 * 1024),
+            compiler_params=pltpu.CompilerParams(vmem_limit_bytes=24 * 1024 * 1024),
             name="features",
-        )(center, grad, first_weights, kept)
+        )(center, grad, back1, kept)
         features_out.append(out)
         return kept
 
-    total = kept.astype(F32) + swap(sent, east_bits[:1], 1).astype(F32)
-    total = scatter_sums(total, groups, beside)
+    ways = 1 << len(groups[0])
+    part = packed // ways
+    total, *parts = pl.pallas_call(
+        parts_kernel,
+        out_shape=[jax.ShapeDtypeStruct((part, LANES), F32)]
+        + [jax.ShapeDtypeStruct((part, LANES), BF16)] * (ways - 1),
+        in_specs=[smem] + [vmem] * 2,
+        out_specs=[vmem] * ways,
+        compiler_params=pltpu.CompilerParams(vmem_limit_bytes=8 * 1024 * 1024),
+        name="parts",
+    )(place_in(groups[0]).reshape(1).astype(jnp.int32), kept, swap(sent, east_bits[:1], 1))
+    total = beside(total)
+    for change in range(1, ways):
+        total = total + swap(parts[change - 1], groups[0], change).astype(F32)
+    total = scatter_sums(total, groups[1:])
     mine = gather_parts(total.astype(BF16), groups)
     other = swap(mine, east_bits[:1], 1)
-    grad_first, grad_second = pl.pallas_call(
-        functools.partial(unpack_kernel, channels, scale),
-        out_shape=(
-            jax.ShapeDtypeStruct(first_weights.shape, F32),
-            jax.ShapeDtypeStruct(second_weights.shape, F32),
-        ),
-        in_specs=[smem] + [vmem] * 2,
-        out_specs=(vmem, vmem),
-        compiler_params=pltpu.CompilerParams(vmem_limit_bytes=32 * 1024 * 1024),
-        name="unpack",
-    )(upper.reshape(1).astype(jnp.int32), mine, other)
+
+    def unpack(is_first, value, *aliased):
+        return pl.pallas_call(
+            functools.partial(unpack_kernel, channels, scale, bool(aliased)),
+            out_shape=(
+                jax.ShapeDtypeStruct(first_weights.shape, F32),
+                jax.ShapeDtypeStruct(second_weights.shape, F32),
+            ),
+            in_specs=[smem, vmem] + [anywhere] * len(aliased),
+            out_specs=(anywhere, anywhere),
+            input_output_aliases={2: 0, 3: 1} if aliased else {},
+            scratch_shapes=[pltpu.VMEM(first_weights.shape, F32), pltpu.SemaphoreType.DMA((7,))],
+            compiler_params=pltpu.CompilerParams(vmem_limit_bytes=12 * 1024 * 1024),
+            name="unpack",
+        )(is_first.reshape(1).astype(jnp.int32), value, *aliased)
+
+    outputs = unpack(upper, mine)
+    grad_first, grad_second = unpack(1 - upper, other, *outputs)
     (grad_features,) = features_out
     grad_features = grad_features.reshape(east, north, upward, channels).transpose(3, 0, 1, 2)
     return (grad_features, grad_first, grad_second)

time: 90.2 us -> 81 us (0.90)
  waiting for transfers between devices: 21.7 us -> 16.5 us
  local copies, waits for them, and re-layouts: 6.29 us -> 3.26 us
  other arithmetic: 1.64 us -> 0.36 us
    pallas_call x1 -> x4, Pallas kernels: 2.02 us -> 6.27 us  [the longest x2 2.43 us: unpack(): pl.pallas_call(functools.partial(unpack_kernel, channels, scale, bool(ali...]
    pallas_call x1, Pallas kernels: 27.1 us -> 23.2 us  [per_device(): pl.pallas_call(functools.partial(whole_kernel, channels, classes, east, n...]
    ppermute x14, waiting for transfers between devices: 17.7 us -> 14 us  [swap(): return lax.ppermute(value, ('east', 'north'), jointly(*pairs))]
    unnamed x27 -> x7, local copies, waits for them, and re-layouts: 4.79 us -> 3.15 us
    ppermute x5, waiting for transfers between devices: 3.95 us -> 2.49 us  [per_device(): edges = [lax.ppermute(value, *route) for value, route in zip(edges, routes)]]
    pad x1 -> x0, local copies, waits for them, and re-layouts: 1.31 us -> none  [per_device(): jnp.pad(head, ((channels + 1, LANES - channels - 1 - classes), (0, LANES...]
    add x2 -> x1, other arithmetic: 1.33 us -> 0.06 us  [per_device(): total = total + swap(parts[change - 1], groups[0], change).astype(F32)]
    pallas_call x1, Pallas kernels: 4.03 us -> 2.81 us  [beside(): pl.pallas_call(functools.partial(last_kernel, channels, east, north, upwa...]
  transfers between devices with their start and end apart: 19 -> 19, of which waited for: 13 -> 12; matrix products, arithmetic and copies ran while one was open for 1% -> 0% of each run, Pallas kernels for 4% -> 8%
where the time goes in v6:
time: 81 us; the launch traced here: 80.7 us
  Pallas kernels  35.2 us (43%)
  starting transfers between devices  24.5 us (30%)
  waiting for transfers between devices  16.5 us (20%)
  local copies, waits for them, and re-layouts  3.26 us (4%)
  between operations  0.96 us (1%)
    pallas_call x1, Pallas kernels, per_device(): pl.pallas_call(functools.partial(whole_kernel, channels, classes, east, n...  23.2 us
    ppermute x14, starting transfers between devices, swap(): return lax.ppermute(value, ('east', 'north'), jointly(*pairs))  15.1 us
    ppermute x14, waiting for transfers between devices, swap(): return lax.ppermute(value, ('east', 'north'), jointly(*pairs))  14 us
    ppermute x5, starting transfers between devices, per_device(): edges = [lax.ppermute(value, *route) for value, route in zip(edges, routes)]  9.36 us
    unnamed x7, local copies, waits for them, and re-layouts  3.15 us
    pallas_call x1, Pallas kernels, per_device(): pl.pallas_call(functools.partial(prepare_kernel, channels, upward, edge,...  2.89 us
    pallas_call x1, Pallas kernels, beside(): pl.pallas_call(functools.partial(last_kernel, channels, east, north, upwa...  2.81 us
    ppermute x5, waiting for transfers between devices, per_device(): edges = [lax.ppermute(value, *route) for value, route in zip(edges, routes)]  2.49 us
  transfers between devices with their start and end apart: 19, of which 12 were waited for; matrix products, arithmetic and copies ran while one was open for 0% of the time, Pallas kernels for 8%

profile of v6, /device:TPU:0, one launch (start us, length us, event | category | flops | bytes accessed | tf_op | source)
XLA Modules:
  0.0 80.7 jit_solution(2681514603386239095)
XLA Ops:
  1.5 2.9 %prepare.1 = (bf16[8,128,128]{2,1,0:T(8,128)(2,1)S(1)}, bf16[4,128,128]{2,1,0:T(8,128)(2,1)S(1)}, bf16[4,128,128]{2,1,0:T(8,128)(2,1)S(1)}, bf16[8,32,128]{2,1,0...) custom-call(s32[7]{0:T(128)S(1)} %stack.24.flags_ref, ...), custom_call_target="tpu_custom_call" | custom-call | tf_op jit(solution)/shard_map/prepare/pallas_call | solution.py:464
  4.9 5.7 %collective-permute-start.1 = (bf16[4,128,128]{2,1,0:T(8,128)(2,1)S(1)}, bf16[4,128,128]{2,1,0:T(8,128)(2,1)S(1)}, u32[]{:S(2)}, u32[]{:S(2)}) collective-permute-start(bf16[4,128,128]{2,1,0:T(8,128)(2,1)S(1)} %get-tuple-element.33), channel_id=1, source_target_pairs={{2,4},{4,2},{6,8},{8,6},{10,12},{12,10},{14,16},{16,14},{18,20},{2... | collective-permute-start | bytes 393224 | tf_op jit(solution)/shard_map/ppermute | solution.py:486
  10.6 1.5 %collective-permute-start.2 = (bf16[8,32,128]{2,1,0:T(8,128)(2,1)S(1)}, bf16[8,32,128]{2,1,0:T(8,128)(2,1)S(1)}, u32[]{:S(2)}, u32[]{:S(2)}) collective-permute-start(bf16[8,32,128]{2,1,0:T(8,128)(2,1)S(1)} %get-tuple-element.34), channel_id=1, source_target_pairs={{0,1},{1,0},{2,3},{3,2},{4,5},{5,4},{6,7},{7,6},{8,9},{9,8},{10,11... | collective-permute-start | bytes 196616 | tf_op jit(solution)/shard_map/ppermute | solution.py:486
  12.1 1.7 %collective-permute-start.4 = (bf16[4,32,128]{2,1,0:T(8,128)(2,1)S(1)}, bf16[4,32,128]{2,1,0:T(8,128)(2,1)S(1)}, u32[]{:S(2)}, u32[]{:S(2)}) collective-permute-start(bf16[4,32,128]{2,1,0:T(8,128)(2,1)S(1)} %get-tuple-element.36), channel_id=1, source_target_pairs={{2,5},{3,4},{4,3},{5,2},{6,9},{7,8},{8,7},{9,6},{10,13},{11,12},{1... | collective-permute-start | bytes 98312 | tf_op jit(solution)/shard_map/ppermute | solution.py:486
  14.4 2.1 %weights.1 = (bf16[4,256,1152]{2,1,0:T(8,128)(2,1)S(1)}, bf16[4,256,1152]{2,1,0:T(8,128)(2,1)S(1)}, bf16[4,1152,256]{2,1,0:T(8,128)(2,1)S(1)}, bf16[4,1152,256]{2,1,0:T(8,128)(2,1)S(1)}, bf16[128,128]{1,0:T(8,128)(2,1)S(1)}) custom-call(bf16[27,96,96]{2,1,0:T(8,128)(2,1)} %w1_in.1, bf16[27,96,96]{2,1,0:T(8,128)(2,1)} %w2_in.1, bf16[13,96]{1,0:T(8,128)(2,1)S(1)} %copy-done.2), custom_call_target="tpu_custom_call" | custom-call | tf_op jit(solution)/shard_map/weights/pallas_call | solution.py:492
  16.5 2.5 %collective-permute-done.4.refs_4_ = bf16[4,32,128]{2,1,0:T(8,128)(2,1)S(1)} collective-permute-done((bf16[4,32,128]{2,1,0:T(8,128)(2,1)S(1)}, bf16[4,32,128]{2,1,0:T(8,128)(2,1)S(1)}, u32[]{:S(2)}, u32[]{:S(2)}) %collective-permute-start.4) | collective-permute-done | bytes 32800 | tf_op jit(solution)/shard_map/ppermute | solution.py:486
  19.0 23.2 %fields.1 = (bf16[10,144,128]{2,1,0:T(8,128)(2,1)S(1)}, bf16[2048,128]{1,0:T(8,128)(2,1)S(1)}, bf16[2048,128]{1,0:T(8,128)(2,1)}) custom-call(s32[7]{0:T(128)S(1)} %stack.24.flags_ref, bf16[4,256,1152]{2,1,0:T(8,128)(2,1)S(1)} %get-tuple-element.28.ahead1_ref, bf16[4,256,1152]{2,1,0:T(8,128)(2,1)S(1)} %get-tuple-element.29.ahead2_ref, ...), custom_call_target="tpu_custom_call" | custom-call | tf_op jit(solution)/shard_map/fields/pallas_call | solution.py:509
  43.0 2.2 %collective-permute-done.5.came_ref = bf16[2048,128]{1,0:T(8,128)(2,1)} collective-permute-done((bf16[2048,128]{1,0:T(8,128)(2,1)}, bf16[2048,128]{1,0:T(8,128)(2,1)}, u32[]{:S(2)}, u32[]{:S(2)}) %collective-permute-start.5) | collective-permute-done | bytes 524320 | tf_op jit(solution)/shard_map/ppermute | solution.py:60
  45.2 1.8 %parts.1 = (f32[512,128]{1,0:T(8,128)S(1)}, bf16[512,128]{1,0:T(8,128)(2,1)}, bf16[512,128]{1,0:T(8,128)(2,1)}, bf16[512,128]{1,0:T(8,128)(2,1)S(1)}) custom-call(s32[1]{0:T(128)} %bitcast.8.place_ref, bf16[2048,128]{1,0:T(8,128)(2,1)S(1)} %get-tuple-element.39.kept_ref, bf16[2048,128]{1,0:T(8,128)(2,1)} %collective-permute-done.5.came_ref), custom_call_target="tpu_custom_call" | custom-call | tf_op jit(solution)/shard_map/parts/pallas_call | solution.py:556
  47.5 3.0 %collective-permute-start.8 = (bf16[512,128]{1,0:T(8,128)(2,1)S(1)}, bf16[512,128]{1,0:T(8,128)(2,1)S(1)}, u32[]{:S(2)}, u32[]{:S(2)}) collective-permute-start(bf16[512,128]{1,0:T(8,128)(2,1)S(1)} %get-tuple-element.46), channel_id=1, source_target_pairs={{0,5},{1,4},{2,7},{3,6},{4,1},{5,0},{6,3},{7,2},{8,13},{9,12},{10,... | collective-permute-start | bytes 393224 | tf_op jit(solution)/shard_map/ppermute | solution.py:60
  51.5 2.8 %features.1 = (bf16[8,128,96]{2,1,0:T(8,128)(2,1)}, f32[512,128]{1,0:T(8,128)S(1)}) custom-call(bf16[8,128,128]{2,1,0:T(8,128)(2,1)S(1)} %get-tuple-element.27.center_ref, bf16[10,144,128]{2,1,0:T(8,128)(2,1)S(1)} %copy-done.1, bf16[4,1152,256]{2,1,0:T(8,128)(2,1)S(1)} %get-tuple-element.38.back1_ref, ...), custom_call_target="tpu_custom_call", output_to_operand_aliasing={{1}: (3, {})} | custom-call | tf_op jit(solution)/shard_map/features/pallas_call | solution.py:535
  54.3 1.5 %collective-permute-done.7 = bf16[512,128]{1,0:T(8,128)(2,1)S(1)} collective-permute-done((bf16[512,128]{1,0:T(8,128)(2,1)}, bf16[512,128]{1,0:T(8,128)(2,1)S(1)}, u32[]{:S(2)}, u32[]{:S(2)}) %collective-permute-start.7) | collective-permute-done | bytes 131104 | tf_op jit(solution)/shard_map/ppermute | solution.py:60
  56.8 2.6 %collective-permute-start.9 = (bf16[128,128]{1,0:T(8,128)(2,1)S(1)}, bf16[128,128]{1,0:T(8,128)(2,1)S(1)}, u32[]{:S(2)}, u32[]{:S(2)}) collective-permute-start(bf16[128,128]{1,0:T(8,128)(2,1)S(1)} %get-tuple-element.55), channel_id=1, source_target_pairs={{0,8},{1,9},{2,10},{3,11},{4,12},{5,13},{6,14},{7,15},{8,0},{9,1},... | collective-permute-start | bytes 98312 | tf_op jit(solution)/shard_map/ppermute | solution.py:60
  59.5 1.3 %collective-permute-done.10 = bf16[128,128]{1,0:T(8,128)(2,1)S(1)} collective-permute-done((bf16[128,128]{1,0:T(8,128)(2,1)S(1)}, bf16[128,128]{1,0:T(8,128)(2,1)S(1)}, u32[]{:S(2)}, u32[]{:S(2)}) %collective-permute-start.10) | collective-permute-done | bytes 32800 | tf_op jit(solution)/shard_map/ppermute | solution.py:60
  61.8 2.1 %collective-permute-start.12 = (bf16[128,128]{1,0:T(8,128)(2,1)S(1)}, bf16[128,128]{1,0:T(8,128)(2,1)S(1)}, u32[]{:S(2)}, u32[]{:S(2)}) collective-permute-start(bf16[128,128]{1,0:T(8,128)(2,1)S(1)} %add_convert_fusion), channel_id=1, source_target_pairs={{0,24},{1,25},{2,26},{3,27},{4,28},{5,29},{6,30},{7,31},{8,16},{9,... | collective-permute-start | bytes 98312 | tf_op jit(solution)/shard_map/ppermute | solution.py:60
  64.9 1.3 %collective-permute-start.14 = (bf16[128,128]{1,0:T(8,128)(2,1)S(1)}, bf16[128,128]{1,0:T(8,128)(2,1)S(1)}, u32[]{:S(2)}, u32[]{:S(2)}) collective-permute-start(bf16[128,128]{1,0:T(8,128)(2,1)S(1)} %add_convert_fusion), channel_id=1, source_target_pairs={{0,8},{1,9},{2,10},{3,11},{4,12},{5,13},{6,14},{7,15},{8,0},{9,1},... | collective-permute-start | bytes 98312 | tf_op jit(solution)/shard_map/ppermute | solution.py:60
  66.2 1.3 %collective-permute-done.12 = bf16[128,128]{1,0:T(8,128)(2,1)S(1)} collective-permute-done((bf16[128,128]{1,0:T(8,128)(2,1)S(1)}, bf16[128,128]{1,0:T(8,128)(2,1)S(1)}, u32[]{:S(2)}, u32[]{:S(2)}) %collective-permute-start.12) | collective-permute-done | bytes 32800 | tf_op jit(solution)/shard_map/ppermute | solution.py:60
  67.6 1.1 %collective-permute-done.13 = bf16[128,128]{1,0:T(8,128)(2,1)S(1)} collective-permute-done((bf16[128,128]{1,0:T(8,128)(2,1)S(1)}, bf16[128,128]{1,0:T(8,128)(2,1)S(1)}, u32[]{:S(2)}, u32[]{:S(2)}) %collective-permute-start.13) | collective-permute-done | bytes 32800 | tf_op jit(solution)/shard_map/ppermute | solution.py:60
  69.1 1.3 %collective-permute-start.15 = (bf16[512,128]{1,0:T(8,128)(2,1)S(1)}, bf16[512,128]{1,0:T(8,128)(2,1)S(1)}, u32[]{:S(2)}, u32[]{:S(2)}) collective-permute-start(bf16[512,128]{1,0:T(8,128)(2,1)S(1)} %pad_maximum_fusion.1), channel_id=1, source_target_pairs={{0,5},{1,4},{2,7},{3,6},{4,1},{5,0},{6,3},{7,2},{8,13},{9,12},{10,... | collective-permute-start | bytes 393224 | tf_op jit(solution)/shard_map/ppermute | solution.py:60
  70.4 1.7 %collective-permute-start.16 = (bf16[512,128]{1,0:T(8,128)(2,1)S(1)}, bf16[512,128]{1,0:T(8,128)(2,1)S(1)}, u32[]{:S(2)}, u32[]{:S(2)}) collective-permute-start(bf16[512,128]{1,0:T(8,128)(2,1)S(1)} %pad_maximum_fusion.1), channel_id=1, source_target_pairs={{0,4},{1,5},{2,6},{3,7},{4,0},{5,1},{6,2},{7,3},{8,12},{9,13},{10,... | collective-permute-start | bytes 393224 | tf_op jit(solution)/shard_map/ppermute | solution.py:60
  72.6 2.5 %collective-permute-done.15 = bf16[512,128]{1,0:T(8,128)(2,1)S(1)} collective-permute-done((bf16[512,128]{1,0:T(8,128)(2,1)S(1)}, bf16[512,128]{1,0:T(8,128)(2,1)S(1)}, u32[]{:S(2)}, u32[]{:S(2)}) %collective-permute-start.15) | collective-permute-done | bytes 131104 | tf_op jit(solution)/shard_map/ppermute | solution.py:60
  75.1 1.3 %collective-permute-done.16 = bf16[512,128]{1,0:T(8,128)(2,1)S(1)} collective-permute-done((bf16[512,128]{1,0:T(8,128)(2,1)S(1)}, bf16[512,128]{1,0:T(8,128)(2,1)S(1)}, u32[]{:S(2)}, u32[]{:S(2)}) %collective-permute-start.16) | collective-permute-done | bytes 131104 | tf_op jit(solution)/shard_map/ppermute | solution.py:60
  77.4 1.2 %unpack.2 = (f32[27,96,96]{2,1,0:T(8,128)}, f32[27,96,96]{2,1,0:T(8,128)}) custom-call(s32[1]{0:T(128)} %bitcast.first_ref_flag, bf16[2048,128]{1,0:T(8,128)(2,1)S(1)} %pad_maximum_fusion.packed_ref), custom_call_target="tpu_custom_call" | custom-call | tf_op jit(solution)/shard_map/unpack/pallas_call | solution.py:573
  79.3 1.2 %unpack.3 = (f32[27,96,96]{2,1,0:T(8,128)}, f32[27,96,96]{2,1,0:T(8,128)}) custom-call(s32[1]{0:T(128)} %bitcast.11.first_ref_flag, bf16[2048,128]{1,0:T(8,128)(2,1)S(1)} %collective-permute-done.18.packed_ref, f32[27,96,96]{2,1,0:T(8,128)} %get-tuple-element.47.refs_0_, ...), custom_call_target="tpu_custom_call", output_to_operand_aliasing={{0}: (2, {}), {1}: (3, {})} | custom-call | tf_op jit(solution)/shard_map/unpack/pallas_call | solution.py:573
  (37 shorter events, 9.9 us)
Async XLA Ops:
  4.4 14.6 %collective-permute-start = (bf16[4,128,128]{2,1,0:T(8,128)(2,1)S(1)}, bf16[4,128,128]{2,1,0:T(8,128)(2,1)S(1)}, u32[]{:S(2)}, u32[]{:S(2)}) collective-permute-start(bf16[4,128,128]{2,1,0:T(8,128)(2,1)S(1)} %get-tuple-element.32), channel_id=1, source_target_pairs={{0,2},{2,0},{4,6},{6,4},{8,10},{10,8},{12,14},{14,12},{16,18},{18,... | collective-permute-start | bytes 393224 | tf_op jit(solution)/shard_map/ppermute | solution.py:486
  4.9 14.1 %collective-permute-start.1 = (bf16[4,128,128]{2,1,0:T(8,128)(2,1)S(1)}, bf16[4,128,128]{2,1,0:T(8,128)(2,1)S(1)}, u32[]{:S(2)}, u32[]{:S(2)}) collective-permute-start(bf16[4,128,128]{2,1,0:T(8,128)(2,1)S(1)} %get-tuple-element.33), channel_id=1, source_target_pairs={{2,4},{4,2},{6,8},{8,6},{10,12},{12,10},{14,16},{16,14},{18,20},{2... | collective-permute-start | bytes 393224 | tf_op jit(solution)/shard_map/ppermute | solution.py:486
  10.6 8.4 %collective-permute-start.2 = (bf16[8,32,128]{2,1,0:T(8,128)(2,1)S(1)}, bf16[8,32,128]{2,1,0:T(8,128)(2,1)S(1)}, u32[]{:S(2)}, u32[]{:S(2)}) collective-permute-start(bf16[8,32,128]{2,1,0:T(8,128)(2,1)S(1)} %get-tuple-element.34), channel_id=1, source_target_pairs={{0,1},{1,0},{2,3},{3,2},{4,5},{5,4},{6,7},{7,6},{8,9},{9,8},{10,11... | collective-permute-start | bytes 196616 | tf_op jit(solution)/shard_map/ppermute | solution.py:486
  12.1 4.4 %collective-permute-start.3 = (bf16[4,32,128]{2,1,0:T(8,128)(2,1)S(1)}, bf16[4,32,128]{2,1,0:T(8,128)(2,1)S(1)}, u32[]{:S(2)}, u32[]{:S(2)}) collective-permute-start(bf16[4,32,128]{2,1,0:T(8,128)(2,1)S(1)} %get-tuple-element.35), channel_id=1, source_target_pairs={{0,3},{1,2},{2,1},{3,0},{4,7},{5,6},{6,5},{7,4},{8,11},{9,10},{10,... | collective-permute-start | bytes 98312 | tf_op jit(solution)/shard_map/ppermute | solution.py:486
  12.1 6.9 %collective-permute-start.4 = (bf16[4,32,128]{2,1,0:T(8,128)(2,1)S(1)}, bf16[4,32,128]{2,1,0:T(8,128)(2,1)S(1)}, u32[]{:S(2)}, u32[]{:S(2)}) collective-permute-start(bf16[4,32,128]{2,1,0:T(8,128)(2,1)S(1)} %get-tuple-element.36), channel_id=1, source_target_pairs={{2,5},{3,4},{4,3},{5,2},{6,9},{7,8},{8,7},{9,6},{10,13},{11,12},{1... | collective-permute-start | bytes 98312 | tf_op jit(solution)/shard_map/ppermute | solution.py:486
  13.7 0.7 copy-start.2
  42.2 0.7 copy-start
  43.0 2.3 %collective-permute-start.5 = (bf16[2048,128]{1,0:T(8,128)(2,1)}, bf16[2048,128]{1,0:T(8,128)(2,1)}, u32[]{:S(2)}, u32[]{:S(2)}) collective-permute-start(bf16[2048,128]{1,0:T(8,128)(2,1)} %get-tuple-element.40), channel_id=1, source_target_pairs={{0,2},{1,3},{2,0},{3,1},{4,6},{5,7},{6,4},{7,5},{8,10},{9,11},{10,... | collective-permute-start | bytes 1572872 | tf_op jit(solution)/shard_map/ppermute | solution.py:60
  47.0 7.3 %collective-permute-start.6 = (bf16[512,128]{1,0:T(8,128)(2,1)}, bf16[512,128]{1,0:T(8,128)(2,1)S(1)}, u32[]{:S(2)}, u32[]{:S(2)}) collective-permute-start(bf16[512,128]{1,0:T(8,128)(2,1)} %get-tuple-element.44), channel_id=1, source_target_pairs={{0,1},{1,0},{2,3},{3,2},{4,5},{5,4},{6,7},{7,6},{8,9},{9,8},{10,11... | collective-permute-start | bytes 393224 | tf_op jit(solution)/shard_map/ppermute | solution.py:60
  47.5 8.3 %collective-permute-start.7 = (bf16[512,128]{1,0:T(8,128)(2,1)}, bf16[512,128]{1,0:T(8,128)(2,1)S(1)}, u32[]{:S(2)}, u32[]{:S(2)}) collective-permute-start(bf16[512,128]{1,0:T(8,128)(2,1)} %get-tuple-element.45), channel_id=1, source_target_pairs={{0,4},{1,5},{2,6},{3,7},{4,0},{5,1},{6,2},{7,3},{8,12},{9,13},{10,... | collective-permute-start | bytes 393224 | tf_op jit(solution)/shard_map/ppermute | solution.py:60
  47.5 8.3 %collective-permute-start.8 = (bf16[512,128]{1,0:T(8,128)(2,1)S(1)}, bf16[512,128]{1,0:T(8,128)(2,1)S(1)}, u32[]{:S(2)}, u32[]{:S(2)}) collective-permute-start(bf16[512,128]{1,0:T(8,128)(2,1)S(1)} %get-tuple-element.46), channel_id=1, source_target_pairs={{0,5},{1,4},{2,7},{3,6},{4,1},{5,0},{6,3},{7,2},{8,13},{9,12},{10,... | collective-permute-start | bytes 393224 | tf_op jit(solution)/shard_map/ppermute | solution.py:60
  50.5 1.0 %copy-start.1 = (bf16[10,144,128]{2,1,0:T(8,128)(2,1)S(1)}, bf16[10,144,128]{2,1,0:T(8,128)(2,1)}, u32[]{:S(2)}) copy-start(bf16[10,144,128]{2,1,0:T(8,128)(2,1)} %copy-done) | copy-start | bytes 1105924
  55.9 4.9 %collective-permute-start.10 = (bf16[128,128]{1,0:T(8,128)(2,1)S(1)}, bf16[128,128]{1,0:T(8,128)(2,1)S(1)}, u32[]{:S(2)}, u32[]{:S(2)}) collective-permute-start(bf16[128,128]{1,0:T(8,128)(2,1)S(1)} %get-tuple-element.57), channel_id=1, source_target_pairs={{0,16},{1,17},{2,18},{3,19},{4,20},{5,21},{6,22},{7,23},{8,24},{9,... | collective-permute-start | bytes 98312 | tf_op jit(solution)/shard_map/ppermute | solution.py:60
  56.0 5.8 %collective-permute-start.11 = (bf16[128,128]{1,0:T(8,128)(2,1)S(1)}, bf16[128,128]{1,0:T(8,128)(2,1)S(1)}, u32[]{:S(2)}, u32[]{:S(2)}) collective-permute-start(bf16[128,128]{1,0:T(8,128)(2,1)S(1)} %get-tuple-element.56), channel_id=1, source_target_pairs={{0,24},{1,25},{2,26},{3,27},{4,28},{5,29},{6,30},{7,31},{8,16},{9,... | collective-permute-start | bytes 98312 | tf_op jit(solution)/shard_map/ppermute | solution.py:60
  56.8 4.9 %collective-permute-start.9 = (bf16[128,128]{1,0:T(8,128)(2,1)S(1)}, bf16[128,128]{1,0:T(8,128)(2,1)S(1)}, u32[]{:S(2)}, u32[]{:S(2)}) collective-permute-start(bf16[128,128]{1,0:T(8,128)(2,1)S(1)} %get-tuple-element.55), channel_id=1, source_target_pairs={{0,8},{1,9},{2,10},{3,11},{4,12},{5,13},{6,14},{7,15},{8,0},{9,1},... | collective-permute-start | bytes 98312 | tf_op jit(solution)/shard_map/ppermute | solution.py:60
  61.8 5.8 %collective-permute-start.12 = (bf16[128,128]{1,0:T(8,128)(2,1)S(1)}, bf16[128,128]{1,0:T(8,128)(2,1)S(1)}, u32[]{:S(2)}, u32[]{:S(2)}) collective-permute-start(bf16[128,128]{1,0:T(8,128)(2,1)S(1)} %add_convert_fusion), channel_id=1, source_target_pairs={{0,24},{1,25},{2,26},{3,27},{4,28},{5,29},{6,30},{7,31},{8,16},{9,... | collective-permute-start | bytes 98312 | tf_op jit(solution)/shard_map/ppermute | solution.py:60
  63.9 4.8 %collective-permute-start.13 = (bf16[128,128]{1,0:T(8,128)(2,1)S(1)}, bf16[128,128]{1,0:T(8,128)(2,1)S(1)}, u32[]{:S(2)}, u32[]{:S(2)}) collective-permute-start(bf16[128,128]{1,0:T(8,128)(2,1)S(1)} %add_convert_fusion), channel_id=1, source_target_pairs={{0,16},{1,17},{2,18},{3,19},{4,20},{5,21},{6,22},{7,23},{8,24},{9,... | collective-permute-start | bytes 98312 | tf_op jit(solution)/shard_map/ppermute | solution.py:60
  64.9 4.1 %collective-permute-start.14 = (bf16[128,128]{1,0:T(8,128)(2,1)S(1)}, bf16[128,128]{1,0:T(8,128)(2,1)S(1)}, u32[]{:S(2)}, u32[]{:S(2)}) collective-permute-start(bf16[128,128]{1,0:T(8,128)(2,1)S(1)} %add_convert_fusion), channel_id=1, source_target_pairs={{0,8},{1,9},{2,10},{3,11},{4,12},{5,13},{6,14},{7,15},{8,0},{9,1},... | collective-permute-start | bytes 98312 | tf_op jit(solution)/shard_map/ppermute | solution.py:60
  69.1 6.0 %collective-permute-start.15 = (bf16[512,128]{1,0:T(8,128)(2,1)S(1)}, bf16[512,128]{1,0:T(8,128)(2,1)S(1)}, u32[]{:S(2)}, u32[]{:S(2)}) collective-permute-start(bf16[512,128]{1,0:T(8,128)(2,1)S(1)} %pad_maximum_fusion.1), channel_id=1, source_target_pairs={{0,5},{1,4},{2,7},{3,6},{4,1},{5,0},{6,3},{7,2},{8,13},{9,12},{10,... | collective-permute-start | bytes 393224 | tf_op jit(solution)/shard_map/ppermute | solution.py:60
  70.4 6.1 %collective-permute-start.16 = (bf16[512,128]{1,0:T(8,128)(2,1)S(1)}, bf16[512,128]{1,0:T(8,128)(2,1)S(1)}, u32[]{:S(2)}, u32[]{:S(2)}) collective-permute-start(bf16[512,128]{1,0:T(8,128)(2,1)S(1)} %pad_maximum_fusion.1), channel_id=1, source_target_pairs={{0,4},{1,5},{2,6},{3,7},{4,0},{5,1},{6,2},{7,3},{8,12},{9,13},{10,... | collective-permute-start | bytes 393224 | tf_op jit(solution)/shard_map/ppermute | solution.py:60
  72.1 5.0 %collective-permute-start.17 = (bf16[512,128]{1,0:T(8,128)(2,1)S(1)}, bf16[512,128]{1,0:T(8,128)(2,1)S(1)}, u32[]{:S(2)}, u32[]{:S(2)}) collective-permute-start(bf16[512,128]{1,0:T(8,128)(2,1)S(1)} %pad_maximum_fusion.1), channel_id=1, source_target_pairs={{0,1},{1,0},{2,3},{3,2},{4,5},{5,4},{6,7},{7,6},{8,9},{9,8},{10,11... | collective-permute-start | bytes 393224 | tf_op jit(solution)/shard_map/ppermute | solution.py:60
  77.3 2.0 %collective-permute-start.18 = (bf16[2048,128]{1,0:T(8,128)(2,1)S(1)}, bf16[2048,128]{1,0:T(8,128)(2,1)S(1)}, u32[]{:S(2)}, u32[]{:S(2)}) collective-permute-start(bf16[2048,128]{1,0:T(8,128)(2,1)S(1)} %pad_maximum_fusion.packed_ref), channel_id=1, source_target_pairs={{0,2},{1,3},{2,0},{3,1},{4,6},{5,7},{6,4},{7,5},{8,10},{9,11},{10,... | collective-permute-start | bytes 1572872 | tf_op jit(solution)/shard_map/ppermute | solution.py:60

commit v7 on v6

--- a/solution.py
+++ b/solution.py
@@ -19,23 +19,26 @@
 def rounds_of(axis):
     count = lax.axis_size(axis)
     me = lax.axis_index(axis)
-    rounds = [(neighbours(count, 0), me % 2, jnp.int32(1))]
+    rounds = [([i ^ 1 for i in range(count)], me % 2, jnp.int32(1))]
     if count > 2:
         inside = ((me > 0) & (me < count - 1)).astype(jnp.int32)
-        rounds.append((neighbours(count, 1), (me + 1) % 2, inside))
+        partners = [0] + [((i - 1) ^ 1) + 1 for i in range(1, count - 1)] + [count - 1]
+        rounds.append((partners, (me + 1) % 2, inside))
     return rounds
 
 
-def neighbours(count, first):
-    pairs = []
-    for i in range(first, count, 2):
-        pairs += [(i, (i + 1) % count), ((i + 1) % count, i)]
-    return pairs
-
-
-def jointly(east_pairs, north_pairs):
-    north = lax.axis_size("north")
-    return [(e * north + n, f * north + m) for e, f in east_pairs for n, m in north_pairs]
+def exchange(value, east, north):
+    count = len(north)
+    target = {(e, n): (f, m) for e, f in enumerate(east) for n, m in enumerate(north)}
+    alone = [place for place, other in target.items() if place == other]
+    while alone:
+        e, n = alone.pop(0)
+        near = [place for place in ((e, n ^ 1), (e ^ 1, n)) if place in alone]
+        other = near[0] if near else alone[0]
+        alone.remove(other)
+        target[e, n], target[other] = other, (e, n)
+    pairs = [(e * count + n, f * count + m) for (e, n), (f, m) in target.items()]
+    return lax.ppermute(value, ("east", "north"), pairs)
 
 
 def high_bit(axis, bit):
@@ -56,8 +59,8 @@
     for i, (axis, bit) in enumerate(group):
         if change >> i & 1:
             masks[axis] |= bit
-    pairs = [[(i, i ^ masks[axis]) for i in range(lax.axis_size(axis))] for axis in ("east", "north")]
-    return lax.ppermute(value, ("east", "north"), jointly(*pairs))
+    partners = [[i ^ masks[axis] for i in range(lax.axis_size(axis))] for axis in ("east", "north")]
+    return exchange(value, *partners)
 
 
 def scatter_sums(total, groups):
@@ -109,49 +112,43 @@
             stack_ref[parity, pl.ds(index * rows, rows), lane : lane + LANES] = shifted
 
 
-def convolve(stack_ref, weight_ref, pairs, rows, acc_ref, transposed):
-    dims = (((1,), (1,)), ((), ())) if transposed else (((1,), (0,)), ((), ()))
-    total = None
-    for p in range(4):
-        first = (p // 2) * rows
-        part = lax.dot_general(
-            stack_ref[p % 2, first : first + pairs * rows, :],
-            weight_ref[p],
-            dims,
-            preferred_element_type=F32,
-        )
-        total = part if total is None else total + part
-    acc_ref[0 : pairs * rows, :] = total
+def convolve(stack_ref, weight_ref, pair, rows):
+    fields = [stack_ref[p % 2, (pair + p // 2) * rows : (pair + p // 2 + 1) * rows, :] for p in range(4)]
+    both = jnp.dot(jnp.concatenate(fields, 1), weight_ref[...], preferred_element_type=F32)
+    return both[:, 0:LANES], both[:, LANES:]
 
 
 def weights_kernel(
     channels, classes,
-    w1_in, w2_in, head_ref,
+    w1_in, w2_in, head_in,
     ahead1_ref, ahead2_ref, back1_ref, back2_ref, head_out,
-    w1_ref, w2_ref, arrived,
+    w1_ref, w2_ref, head_ref, arrived,
 ):
     copies = [
-        pltpu.make_async_copy(w1_in, w1_ref, arrived.at[0]),
-        pltpu.make_async_copy(w2_in, w2_ref, arrived.at[1]),
+        pltpu.make_async_copy(source, target, arrived.at[i])
+        for i, (source, target) in enumerate(((w1_in, w1_ref), (w2_in, w2_ref), (head_in, head_ref)))
     ]
     for copy in copies:
         copy.start()
-    for ref in (ahead1_ref, ahead2_ref, back1_ref, back2_ref):
+    for ref in (ahead1_ref, ahead2_ref, back1_ref, back2_ref, head_out):
         ref[...] = jnp.zeros_like(ref)
     for copy in copies:
         copy.wait()
+    row = lax.broadcasted_iota(jnp.int32, (channels, channels), 0)
+    unit = (row == lax.broadcasted_iota(jnp.int32, (channels, channels), 1)).astype(BF16)
     for w_ref, ahead_ref, back_ref in ((w1_ref, ahead1_ref, back1_ref), (w2_ref, ahead2_ref, back2_ref)):
         for d in range(3):
             for j in range(OFFSETS):
                 value = w_ref[d * OFFSETS + j]
+                turned = lax.dot_general(unit, value, (((1,), (1,)), ((), ())), preferred_element_type=F32).astype(BF16)
                 for q in range(2):
                     side = slice(q * LANES, q * LANES + channels)
-                    ahead_ref[d + q, side, j * LANES : j * LANES + channels] = value
-                    turn = (OFFSETS - 1 - j) * LANES
-                    back_ref[2 - d + q, turn : turn + channels, side] = value
+                    start = ((d + q) * OFFSETS + j) * LANES
+                    ahead_ref[start : start + channels, side] = turned
+                    start = ((2 - d + q) * OFFSETS + OFFSETS - 1 - j) * LANES
+                    back_ref[start : start + channels, side] = value
     row = lax.broadcasted_iota(jnp.int32, (LANES, classes), 0)
     spread = (row == lax.broadcasted_iota(jnp.int32, (LANES, classes), 1) + channels + 1).astype(BF16)
-    head_out[...] = jnp.zeros_like(head_out)
     head_out[:, 0:channels] = jnp.dot(spread, head_ref[...], preferred_element_type=F32).astype(BF16)
 
 
@@ -281,7 +278,7 @@
     edges = east_rounds + north_rounds + east_rounds * north_rounds
     (
         grad_ref, kept_ref, sent_ref,
-        x_ref, s0_ref, s1_ref, sg_ref, mask_ref, slope_ref, acc_ref, turned_ref,
+        x_ref, s0_ref, s1_ref, sg_ref, mask_ref, slope_ref, turned_ref,
     ) = refs[edges:]
     rows = (north + 2 * HALO) * upward
     low, size = HALO * upward, north * upward
@@ -293,40 +290,31 @@
     place_edges(flags_ref, center_ref, refs[:edges], east_rounds, north_rounds, low, x_ref)
     border = jnp.zeros((upward, LANES), F32)
 
-    def start(i, carry):
-        for parity in range(2):
-            x = x_ref[2 * i + parity].astype(F32)
-            mask = jnp.broadcast_to(x[:, channels : channels + 1], (rows, LANES))
-            mask_ref[2 * i + parity] = mask
-            a0 = jnp.where((mask > 0) & (lane < channels), x, 0.0)
-            put_stack(jnp.concatenate([border, a0, border], 0), upward, s0_ref, parity, i)
-        return carry
-
-    lax.fori_loop(0, planes // 2, start, 0)
-    convolve(s0_ref, ahead1_ref, (planes - 2) // 2, rows, acc_ref, True)
-
-    def middle(i, carry):
-        for parity in range(2):
+    for plane in range(planes):
+        x = x_ref[plane].astype(F32)
+        mask = jnp.broadcast_to(x[:, channels : channels + 1], (rows, LANES))
+        mask_ref[plane] = mask
+        a0 = jnp.where((mask > 0) & (lane < channels), x, 0.0)
+        put_stack(jnp.concatenate([border, a0, border], 0), upward, s0_ref, plane % 2, plane // 2)
+
+    for i in range((planes - 2) // 2):
+        for parity, value in enumerate(convolve(s0_ref, ahead1_ref, i, rows)):
             plane = 2 * i + parity
             mask = mask_ref[plane + 1]
-            p1 = mask * acc_ref[pl.ds(i * rows, rows), parity * LANES : (parity + 1) * LANES]
+            p1 = mask * value
             sig = jax.nn.sigmoid(p1)
             slope_ref[plane] = mask * (sig * (1.0 + p1 * (1.0 - sig)))
             put_stack((p1 * sig)[upward : upward + rows1], upward, s1_ref, parity, i)
-        return carry
-
-    lax.fori_loop(0, (planes - 2) // 2, middle, 0)
-    convolve(s1_ref, ahead2_ref, (planes - 4) // 2, rows2, acc_ref, True)
 
     head = head_ref[...]
     class_lane = (lane[0:rows2] > channels) & (lane[0:rows2] <= channels + classes)
     here = slice(2 * upward, 2 * upward + rows2)
 
     for i in range((planes - 4) // 2):
-        for parity in range(2):
+        for parity, value in enumerate(convolve(s1_ref, ahead2_ref, i, rows2)):
             plane = 2 * i + parity
             mask = mask_ref[plane + 2, here]
-            p2 = mask * acc_ref[i * rows2 : (i + 1) * rows2, parity * LANES : (parity + 1) * LANES]
+            p2 = mask * value
             sig = jax.nn.sigmoid(p2)
             a2 = (p2 * sig).astype(BF16)
             logits = lax.dot_general(a2, head, (((1,), (1,)), ((), ())), preferred_element_type=F32)
@@ -343,15 +331,12 @@
     upper = flags_ref[2 * (east_rounds + north_rounds)] == 1
     for t, tile in enumerate(kernel_sum(turned_ref, s1_ref, 3, east, rows2, low2, size, channels)):
         kept_ref[t * channels : (t + 1) * channels, :] = tile.astype(BF16)
-    convolve(sg_ref, back2_ref, (planes - 6) // 2, rows3, acc_ref, False)
 
     there = slice(2 * upward + upward, 2 * upward + upward + rows3)
     for i in range((planes - 6) // 2):
-        for parity in range(2):
+        for parity, value in enumerate(convolve(sg_ref, back2_ref, i, rows3)):
             plane = 2 * i + parity
-            g_p1 = slope_ref[plane + 2, there] * acc_ref[
-                i * rows3 : (i + 1) * rows3, parity * LANES : (parity + 1) * LANES
-            ]
+            g_p1 = slope_ref[plane + 2, there] * value
             grad_ref[plane] = g_p1.astype(BF16)
             put_turned(turned_ref, g_p1[low3 : low3 + size], plane - 1, east, channels)
 
@@ -371,21 +356,14 @@
     channels, east, north, upward,
     center_ref, grad_ref, back1_ref, kept_in,
     out_ref, kept_out,
-    stack_ref, acc_ref,
+    stack_ref,
 ):
     size = north * upward
-
-    def start(i, carry):
-        for parity in range(2):
-            put_stack(grad_ref[2 * i + parity].astype(F32), upward, stack_ref, parity, i)
-        return carry
-
-    lax.fori_loop(0, east // 2 + 1, start, 0)
-    convolve(stack_ref, back1_ref, east // 2, size, acc_ref, False)
+    for plane in range(east + 2):
+        put_stack(grad_ref[plane].astype(F32), upward, stack_ref, plane % 2, plane // 2)
     for i in range(east // 2):
-        for parity in range(2):
+        for parity, value in enumerate(convolve(stack_ref, back1_ref, i, size)):
             plane = 2 * i + parity
-            value = acc_ref[i * size : (i + 1) * size, parity * LANES : (parity + 1) * LANES]
             mask = center_ref[plane, :, channels : channels + 1].astype(F32)
             out_ref[plane] = (mask * value)[:, 0:channels].astype(BF16)
 
@@ -481,31 +459,28 @@
         pltpu.with_memory_space_constraint(voxel_occupancy.transpose(0, 2, 1), pltpu.HBM),
         pltpu.with_memory_space_constraint(teacher.transpose(0, 1, 3, 2), pltpu.HBM),
     )
-    routes = [("east", pairs) for pairs, _, _ in easts] + [("north", pairs) for pairs, _, _ in norths]
-    routes += [(("east", "north"), jointly(a, b)) for a, _, _ in easts for b, _, _ in norths]
-    edges = [lax.ppermute(value, *route) for value, route in zip(edges, routes)]
+    stay = [list(range(lax.axis_size(axis))) for axis in ("east", "north")]
+    routes = [(partners, stay[1]) for partners, _, _ in easts] + [(stay[0], partners) for partners, _, _ in norths]
+    routes += [(a, b) for a, _, _ in easts for b, _, _ in norths]
+    edges = [exchange(value, *route) for value, route in zip(edges, routes)]
 
     unit = devices // 2 * 16
     packed = -(-21 * channels // unit) * unit
-    wide = (4, 2 * LANES, WIDE)
-    tall = (4, WIDE, 2 * LANES)
+    shapes = [(4 * WIDE, 2 * LANES)] * 4 + [(LANES, LANES)]
     ahead1, ahead2, back1, back2, head_wide = pl.pallas_call(
         functools.partial(weights_kernel, channels, classes),
-        out_shape=[jax.ShapeDtypeStruct(shape, BF16) for shape in (wide, wide, tall, tall, (LANES, LANES))],
-        in_specs=[far, far, vmem],
+        out_shape=[jax.ShapeDtypeStruct(shape, BF16) for shape in shapes],
+        in_specs=[far] * 3,
         out_specs=[vmem] * 5,
         scratch_shapes=[
             pltpu.VMEM(first_weights.shape, BF16),
             pltpu.VMEM(second_weights.shape, BF16),
-            pltpu.SemaphoreType.DMA((2,)),
+            pltpu.VMEM(head.shape, BF16),
+            pltpu.SemaphoreType.DMA((3,)),
         ],
-        compiler_params=pltpu.CompilerParams(vmem_limit_bytes=20 * 1024 * 1024),
+        compiler_params=pltpu.CompilerParams(vmem_limit_bytes=16 * 1024 * 1024),
         name="weights",
-    )(
-        pltpu.with_memory_space_constraint(first_weights, pltpu.HBM),
-        pltpu.with_memory_space_constraint(second_weights, pltpu.HBM),
-        head,
-    )
+    )(*[pltpu.with_memory_space_constraint(value, pltpu.HBM) for value in (first_weights, second_weights, head)])
     grad, kept, sent = pl.pallas_call(
         functools.partial(whole_kernel, channels, classes, east, north, upward, *counts),
         out_shape=(
@@ -522,10 +497,9 @@
             pltpu.VMEM((2, (planes - 4) // 2 * (rows - 6 * upward), WIDE), BF16),
             pltpu.VMEM((planes, rows, LANES), F32),
             pltpu.VMEM((planes - 2, rows, LANES), F32),
-            pltpu.VMEM(((planes - 2) // 2 * rows, 2 * LANES), F32),
             pltpu.VMEM((3 * channels, east * size), BF16),
         ],
-        compiler_params=pltpu.CompilerParams(vmem_limit_bytes=38 * 1024 * 1024),
+        compiler_params=pltpu.CompilerParams(vmem_limit_bytes=32 * 1024 * 1024),
         name="fields",
     )(flags, ahead1, ahead2, back2, head_wide, center, *edges)
 
@@ -541,11 +515,8 @@
             in_specs=[vmem] * 3 + [anywhere],
             out_specs=(vmem, anywhere),
             input_output_aliases={3: 1},
-            scratch_shapes=[
-                pltpu.VMEM((2, (east + 2) // 2 * size, WIDE), BF16),
-                pltpu.VMEM((east // 2 * size, 2 * LANES), F32),
-            ],
-            compiler_params=pltpu.CompilerParams(vmem_limit_bytes=24 * 1024 * 1024),
+            scratch_shapes=[pltpu.VMEM((2, (east + 2) // 2 * size, WIDE), BF16)],
+            compiler_params=pltpu.CompilerParams(vmem_limit_bytes=12 * 1024 * 1024),
             name="features",
         )(center, grad, back1, kept)
         features_out.append(out)

time: 81 us -> 72.6 us (0.90)
  Pallas kernels: 35.2 us -> 28.8 us
  starting transfers between devices: 24.5 us -> 23.4 us
    pallas_call x1, Pallas kernels: 23.2 us -> 17.2 us  [per_device(): pl.pallas_call(functools.partial(whole_kernel, channels, classes, east, n...]
    ppermute x19, starting transfers between devices: 24.5 us -> 23.4 us  [exchange(): return lax.ppermute(value, ('east', 'north'), pairs)]
    unnamed x7 -> x5, local copies, waits for them, and re-layouts: 3.15 us -> 2.47 us
  transfers between devices with their start and end apart: 19 -> 19, of which waited for: 12 -> 9; matrix products, arithmetic and copies ran while one was open for 0% -> 0% of each run, Pallas kernels for 8% -> 8%
where the time goes in v7:
time: 72.6 us; the launch traced here: 72.4 us
  Pallas kernels  28.8 us (40%)
  starting transfers between devices  23.4 us (32%)
  waiting for transfers between devices  16.3 us (22%)
  local copies, waits for them, and re-layouts  2.58 us (4%)
  between operations  0.95 us (1%)
    ppermute x19, starting transfers between devices, exchange(): return lax.ppermute(value, ('east', 'north'), pairs)  23.4 us
    pallas_call x1, Pallas kernels, per_device(): pl.pallas_call(functools.partial(whole_kernel, channels, classes, east, n...  17.2 us
    ppermute x19, waiting for transfers between devices, exchange(): return lax.ppermute(value, ('east', 'north'), pairs)  16.3 us
    pallas_call x1, Pallas kernels, per_device(): pl.pallas_call(functools.partial(prepare_kernel, channels, upward, edge,...  2.89 us
    unnamed x5, local copies, waits for them, and re-layouts  2.47 us
    pallas_call x2, Pallas kernels, unpack(): pl.pallas_call(functools.partial(unpack_kernel, channels, scale, bool(ali...  2.43 us
    pallas_call x1, Pallas kernels, per_device(): pl.pallas_call(functools.partial(weights_kernel, channels, classes), out_...  2.38 us
    pallas_call x1, Pallas kernels, beside(): pl.pallas_call(functools.partial(last_kernel, channels, east, north, upwa...  2.15 us
  transfers between devices with their start and end apart: 19, of which 9 were waited for; matrix products, arithmetic and copies ran while one was open for 0% of the time, Pallas kernels for 8%

profile of v7, /device:TPU:0, one launch (start us, length us, event | category | flops | bytes accessed | tf_op | source)
XLA Modules:
  0.0 72.4 jit_solution(16605932643686843660)
XLA Ops:
  1.5 2.9 %prepare.1 = (bf16[8,128,128]{2,1,0:T(8,128)(2,1)S(1)}, bf16[4,128,128]{2,1,0:T(8,128)(2,1)S(1)}, bf16[4,128,128]{2,1,0:T(8,128)(2,1)S(1)}, bf16[8,32,128]{2,1,0...) custom-call(s32[7]{0:T(128)S(1)} %stack.24.flags_ref, ...), custom_call_target="tpu_custom_call" | custom-call | tf_op jit(solution)/shard_map/prepare/pallas_call | solution.py:442
  4.9 2.6 %collective-permute-start.1 = (bf16[4,128,128]{2,1,0:T(8,128)(2,1)S(1)}, bf16[4,128,128]{2,1,0:T(8,128)(2,1)S(1)}, u32[]{:S(2)}, u32[]{:S(2)}) collective-permute-start(bf16[4,128,128]{2,1,0:T(8,128)(2,1)S(1)} %get-tuple-element.33), channel_id=1, source_target_pairs={{0,1},{1,0},{2,4},{3,5},{4,2},{5,3},{6,8},{7,9},{8,6},{9,7},{10,12... | collective-permute-start | bytes 393224 | tf_op jit(solution)/shard_map/ppermute | solution.py:41
  7.5 1.4 %collective-permute-start.3 = (bf16[4,32,128]{2,1,0:T(8,128)(2,1)S(1)}, bf16[4,32,128]{2,1,0:T(8,128)(2,1)S(1)}, u32[]{:S(2)}, u32[]{:S(2)}) collective-permute-start(bf16[4,32,128]{2,1,0:T(8,128)(2,1)S(1)} %get-tuple-element.35), channel_id=1, source_target_pairs={{0,3},{1,2},{2,1},{3,0},{4,7},{5,6},{6,5},{7,4},{8,11},{9,10},{10,... | collective-permute-start | bytes 98312 | tf_op jit(solution)/shard_map/ppermute | solution.py:41
  9.0 1.5 %collective-permute-start.4 = (bf16[4,32,128]{2,1,0:T(8,128)(2,1)S(1)}, bf16[4,32,128]{2,1,0:T(8,128)(2,1)S(1)}, u32[]{:S(2)}, u32[]{:S(2)}) collective-permute-start(bf16[4,32,128]{2,1,0:T(8,128)(2,1)S(1)} %get-tuple-element.36), channel_id=1, source_target_pairs={{0,1},{1,0},{2,5},{3,4},{4,3},{5,2},{6,9},{7,8},{8,7},{9,6},{10,13... | collective-permute-start | bytes 98312 | tf_op jit(solution)/shard_map/ppermute | solution.py:41
  10.4 2.4 %weights.1 = (bf16[4608,256]{1,0:T(8,128)(2,1)S(1)}, bf16[4608,256]{1,0:T(8,128)(2,1)S(1)}, bf16[4608,256]{1,0:T(8,128)(2,1)S(1)}, bf16[4608,256]{1,0:T(8,128)(2,1)S(1)}, bf16[128,128]{1,0:T(8,128)(2,1)S(1)}) custom-call(bf16[27,96,96]{2,1,0:T(8,128)(2,1)} %w1_in.1, bf16[27,96,96]{2,1,0:T(8,128)(2,1)} %w2_in.1, bf16[13,96]{1,0:T(8,128)(2,1)} %head_in.1), custom_call_target="tpu_custom_call" | custom-call | tf_op jit(solution)/shard_map/weights/pallas_call | solution.py:470
  12.9 17.2 %fields.1 = (bf16[10,144,128]{2,1,0:T(8,128)(2,1)S(1)}, bf16[2048,128]{1,0:T(8,128)(2,1)S(1)}, bf16[2048,128]{1,0:T(8,128)(2,1)}) custom-call(s32[7]{0:T(128)S(1)} %stack.24.flags_ref, bf16[4608,256]{1,0:T(8,128)(2,1)S(1)} %get-tuple-element.28.ahead1_ref, bf16[4608,256]{1,0:T(8,128)(2,1)S(1)} %get-tuple-element.29.ahead2_ref, ...), custom_call_target="tpu_custom_call" | custom-call | tf_op jit(solution)/shard_map/fields/pallas_call | solution.py:484
  31.9 1.9 %collective-permute-done.5.came_ref = bf16[2048,128]{1,0:T(8,128)(2,1)} collective-permute-done((bf16[2048,128]{1,0:T(8,128)(2,1)}, bf16[2048,128]{1,0:T(8,128)(2,1)}, u32[]{:S(2)}, u32[]{:S(2)}) %collective-permute-start.5) | collective-permute-done | bytes 524320 | tf_op jit(solution)/shard_map/ppermute | solution.py:41
  33.8 1.8 %parts.1 = (f32[512,128]{1,0:T(8,128)S(1)}, bf16[512,128]{1,0:T(8,128)(2,1)}, bf16[512,128]{1,0:T(8,128)(2,1)}, bf16[512,128]{1,0:T(8,128)(2,1)S(1)}) custom-call(s32[1]{0:T(128)} %bitcast.8.place_ref, bf16[2048,128]{1,0:T(8,128)(2,1)S(1)} %get-tuple-element.39.kept_ref, bf16[2048,128]{1,0:T(8,128)(2,1)} %collective-permute-done.5.came_ref), custom_call_target="tpu_custom_call" | custom-call | tf_op jit(solution)/shard_map/parts/pallas_call | solution.py:527
  35.6 1.7 %collective-permute-start.6 = (bf16[512,128]{1,0:T(8,128)(2,1)}, bf16[512,128]{1,0:T(8,128)(2,1)S(1)}, u32[]{:S(2)}, u32[]{:S(2)}) collective-permute-start(bf16[512,128]{1,0:T(8,128)(2,1)} %get-tuple-element.44), channel_id=1, source_target_pairs={{0,1},{1,0},{2,3},{3,2},{4,5},{5,4},{6,7},{7,6},{8,9},{9,8},{10,11... | collective-permute-start | bytes 393224 | tf_op jit(solution)/shard_map/ppermute | solution.py:41
  37.2 1.4 %collective-permute-start.7 = (bf16[512,128]{1,0:T(8,128)(2,1)}, bf16[512,128]{1,0:T(8,128)(2,1)S(1)}, u32[]{:S(2)}, u32[]{:S(2)}) collective-permute-start(bf16[512,128]{1,0:T(8,128)(2,1)} %get-tuple-element.45), channel_id=1, source_target_pairs={{0,4},{1,5},{2,6},{3,7},{4,0},{5,1},{6,2},{7,3},{8,12},{9,13},{10,... | collective-permute-start | bytes 393224 | tf_op jit(solution)/shard_map/ppermute | solution.py:41
  40.1 2.2 %features.1 = (bf16[8,128,96]{2,1,0:T(8,128)(2,1)}, f32[512,128]{1,0:T(8,128)S(1)}) custom-call(bf16[8,128,128]{2,1,0:T(8,128)(2,1)S(1)} %get-tuple-element.27.center_ref, bf16[10,144,128]{2,1,0:T(8,128)(2,1)S(1)} %copy-done.1, bf16[4608,256]{1,0:T(8,128)(2,1)S(1)} %get-tuple-element.38.back1_ref, ...), custom_call_target="tpu_custom_call", output_to_operand_aliasing={{1}: (3, {})} | custom-call | tf_op jit(solution)/shard_map/features/pallas_call | solution.py:509
  42.2 3.3 %collective-permute-done.7 = bf16[512,128]{1,0:T(8,128)(2,1)S(1)} collective-permute-done((bf16[512,128]{1,0:T(8,128)(2,1)}, bf16[512,128]{1,0:T(8,128)(2,1)S(1)}, u32[]{:S(2)}, u32[]{:S(2)}) %collective-permute-start.7) | collective-permute-done | bytes 131104 | tf_op jit(solution)/shard_map/ppermute | solution.py:41
  45.6 3.1 %collective-permute-start.10 = (bf16[128,128]{1,0:T(8,128)(2,1)S(1)}, bf16[128,128]{1,0:T(8,128)(2,1)S(1)}, u32[]{:S(2)}, u32[]{:S(2)}) collective-permute-start(bf16[128,128]{1,0:T(8,128)(2,1)S(1)} %get-tuple-element.57), channel_id=1, source_target_pairs={{0,16},{1,17},{2,18},{3,19},{4,20},{5,21},{6,22},{7,23},{8,24},{9,... | collective-permute-start | bytes 98312 | tf_op jit(solution)/shard_map/ppermute | solution.py:41
  48.7 1.3 %collective-permute-start.11 = (bf16[128,128]{1,0:T(8,128)(2,1)S(1)}, bf16[128,128]{1,0:T(8,128)(2,1)S(1)}, u32[]{:S(2)}, u32[]{:S(2)}) collective-permute-start(bf16[128,128]{1,0:T(8,128)(2,1)S(1)} %get-tuple-element.56), channel_id=1, source_target_pairs={{0,24},{1,25},{2,26},{3,27},{4,28},{5,29},{6,30},{7,31},{8,16},{9,... | collective-permute-start | bytes 98312 | tf_op jit(solution)/shard_map/ppermute | solution.py:41
  50.6 3.8 %collective-permute-done.11 = bf16[128,128]{1,0:T(8,128)(2,1)S(1)} collective-permute-done((bf16[128,128]{1,0:T(8,128)(2,1)S(1)}, bf16[128,128]{1,0:T(8,128)(2,1)S(1)}, u32[]{:S(2)}, u32[]{:S(2)}) %collective-permute-start.11) | collective-permute-done | bytes 32800 | tf_op jit(solution)/shard_map/ppermute | solution.py:41
  54.4 2.1 %collective-permute-start.12 = (bf16[128,128]{1,0:T(8,128)(2,1)S(1)}, bf16[128,128]{1,0:T(8,128)(2,1)S(1)}, u32[]{:S(2)}, u32[]{:S(2)}) collective-permute-start(bf16[128,128]{1,0:T(8,128)(2,1)S(1)} %add_convert_fusion), channel_id=1, source_target_pairs={{0,24},{1,25},{2,26},{3,27},{4,28},{5,29},{6,30},{7,31},{8,16},{9,... | collective-permute-start | bytes 98312 | tf_op jit(solution)/shard_map/ppermute | solution.py:41
  56.5 2.4 %collective-permute-start.14 = (bf16[128,128]{1,0:T(8,128)(2,1)S(1)}, bf16[128,128]{1,0:T(8,128)(2,1)S(1)}, u32[]{:S(2)}, u32[]{:S(2)}) collective-permute-start(bf16[128,128]{1,0:T(8,128)(2,1)S(1)} %add_convert_fusion), channel_id=1, source_target_pairs={{0,8},{1,9},{2,10},{3,11},{4,12},{5,13},{6,14},{7,15},{8,0},{9,1},... | collective-permute-start | bytes 98312 | tf_op jit(solution)/shard_map/ppermute | solution.py:41
  58.9 1.3 %collective-permute-done.12 = bf16[128,128]{1,0:T(8,128)(2,1)S(1)} collective-permute-done((bf16[128,128]{1,0:T(8,128)(2,1)S(1)}, bf16[128,128]{1,0:T(8,128)(2,1)S(1)}, u32[]{:S(2)}, u32[]{:S(2)}) %collective-permute-start.12) | collective-permute-done | bytes 32800 | tf_op jit(solution)/shard_map/ppermute | solution.py:41
  61.4 1.2 %collective-permute-start.15 = (bf16[512,128]{1,0:T(8,128)(2,1)S(1)}, bf16[512,128]{1,0:T(8,128)(2,1)S(1)}, u32[]{:S(2)}, u32[]{:S(2)}) collective-permute-start(bf16[512,128]{1,0:T(8,128)(2,1)S(1)} %pad_maximum_fusion.1), channel_id=1, source_target_pairs={{0,5},{1,4},{2,7},{3,6},{4,1},{5,0},{6,3},{7,2},{8,13},{9,12},{10,... | collective-permute-start | bytes 393224 | tf_op jit(solution)/shard_map/ppermute | solution.py:41
  63.6 1.3 %collective-permute-start.17 = (bf16[512,128]{1,0:T(8,128)(2,1)S(1)}, bf16[512,128]{1,0:T(8,128)(2,1)S(1)}, u32[]{:S(2)}, u32[]{:S(2)}) collective-permute-start(bf16[512,128]{1,0:T(8,128)(2,1)S(1)} %pad_maximum_fusion.1), channel_id=1, source_target_pairs={{0,1},{1,0},{2,3},{3,2},{4,5},{5,4},{6,7},{7,6},{8,9},{9,8},{10,11... | collective-permute-start | bytes 393224 | tf_op jit(solution)/shard_map/ppermute | solution.py:41
  65.0 2.5 %collective-permute-done.15 = bf16[512,128]{1,0:T(8,128)(2,1)S(1)} collective-permute-done((bf16[512,128]{1,0:T(8,128)(2,1)S(1)}, bf16[512,128]{1,0:T(8,128)(2,1)S(1)}, u32[]{:S(2)}, u32[]{:S(2)}) %collective-permute-start.15) | collective-permute-done | bytes 131104 | tf_op jit(solution)/shard_map/ppermute | solution.py:41
  67.4 1.3 %collective-permute-done.16 = bf16[512,128]{1,0:T(8,128)(2,1)S(1)} collective-permute-done((bf16[512,128]{1,0:T(8,128)(2,1)S(1)}, bf16[512,128]{1,0:T(8,128)(2,1)S(1)}, u32[]{:S(2)}, u32[]{:S(2)}) %collective-permute-start.16) | collective-permute-done | bytes 131104 | tf_op jit(solution)/shard_map/ppermute | solution.py:41
  69.1 1.2 %unpack.2 = (f32[27,96,96]{2,1,0:T(8,128)}, f32[27,96,96]{2,1,0:T(8,128)}) custom-call(s32[1]{0:T(128)} %bitcast.first_ref_flag, bf16[2048,128]{1,0:T(8,128)(2,1)S(1)} %pad_maximum_fusion.packed_ref), custom_call_target="tpu_custom_call" | custom-call | tf_op jit(solution)/shard_map/unpack/pallas_call | solution.py:544
  71.0 1.2 %unpack.3 = (f32[27,96,96]{2,1,0:T(8,128)}, f32[27,96,96]{2,1,0:T(8,128)}) custom-call(s32[1]{0:T(128)} %bitcast.11.first_ref_flag, bf16[2048,128]{1,0:T(8,128)(2,1)S(1)} %collective-permute-done.18.packed_ref, f32[27,96,96]{2,1,0:T(8,128)} %get-tuple-element.47.refs_0_, ...), custom_call_target="tpu_custom_call", output_to_operand_aliasing={{0}: (2, {}), {1}: (3, {})} | custom-call | tf_op jit(solution)/shard_map/unpack/pallas_call | solution.py:544
  (35 shorter events, 8.5 us)
Async XLA Ops:
  4.4 8.5 %collective-permute-start = (bf16[4,128,128]{2,1,0:T(8,128)(2,1)S(1)}, bf16[4,128,128]{2,1,0:T(8,128)(2,1)S(1)}, u32[]{:S(2)}, u32[]{:S(2)}) collective-permute-start(bf16[4,128,128]{2,1,0:T(8,128)(2,1)S(1)} %get-tuple-element.32), channel_id=1, source_target_pairs={{0,2},{1,3},{2,0},{3,1},{4,6},{5,7},{6,4},{7,5},{8,10},{9,11},{10,... | collective-permute-start | bytes 393224 | tf_op jit(solution)/shard_map/ppermute | solution.py:41
  4.9 8.0 %collective-permute-start.1 = (bf16[4,128,128]{2,1,0:T(8,128)(2,1)S(1)}, bf16[4,128,128]{2,1,0:T(8,128)(2,1)S(1)}, u32[]{:S(2)}, u32[]{:S(2)}) collective-permute-start(bf16[4,128,128]{2,1,0:T(8,128)(2,1)S(1)} %get-tuple-element.33), channel_id=1, source_target_pairs={{0,1},{1,0},{2,4},{3,5},{4,2},{5,3},{6,8},{7,9},{8,6},{9,7},{10,12... | collective-permute-start | bytes 393224 | tf_op jit(solution)/shard_map/ppermute | solution.py:41
  7.5 5.4 %collective-permute-start.2 = (bf16[8,32,128]{2,1,0:T(8,128)(2,1)S(1)}, bf16[8,32,128]{2,1,0:T(8,128)(2,1)S(1)}, u32[]{:S(2)}, u32[]{:S(2)}) collective-permute-start(bf16[8,32,128]{2,1,0:T(8,128)(2,1)S(1)} %get-tuple-element.34), channel_id=1, source_target_pairs={{0,1},{1,0},{2,3},{3,2},{4,5},{5,4},{6,7},{7,6},{8,9},{9,8},{10,11... | collective-permute-start | bytes 196616 | tf_op jit(solution)/shard_map/ppermute | solution.py:41
  7.5 5.3 %collective-permute-start.3 = (bf16[4,32,128]{2,1,0:T(8,128)(2,1)S(1)}, bf16[4,32,128]{2,1,0:T(8,128)(2,1)S(1)}, u32[]{:S(2)}, u32[]{:S(2)}) collective-permute-start(bf16[4,32,128]{2,1,0:T(8,128)(2,1)S(1)} %get-tuple-element.35), channel_id=1, source_target_pairs={{0,3},{1,2},{2,1},{3,0},{4,7},{5,6},{6,5},{7,4},{8,11},{9,10},{10,... | collective-permute-start | bytes 98312 | tf_op jit(solution)/shard_map/ppermute | solution.py:41
  9.0 3.9 %collective-permute-start.4 = (bf16[4,32,128]{2,1,0:T(8,128)(2,1)S(1)}, bf16[4,32,128]{2,1,0:T(8,128)(2,1)S(1)}, u32[]{:S(2)}, u32[]{:S(2)}) collective-permute-start(bf16[4,32,128]{2,1,0:T(8,128)(2,1)S(1)} %get-tuple-element.36), channel_id=1, source_target_pairs={{0,1},{1,0},{2,5},{3,4},{4,3},{5,2},{6,9},{7,8},{8,7},{9,6},{10,13... | collective-permute-start | bytes 98312 | tf_op jit(solution)/shard_map/ppermute | solution.py:41
  30.1 0.7 %copy-start = (bf16[10,144,128]{2,1,0:T(8,128)(2,1)}, bf16[10,144,128]{2,1,0:T(8,128)(2,1)S(1)}, u32[]{:S(2)}) copy-start(bf16[10,144,128]{2,1,0:T(8,128)(2,1)S(1)} %get-tuple-element.37.grad_ref) | copy-start | bytes 1105924
  30.8 2.9 %collective-permute-start.5 = (bf16[2048,128]{1,0:T(8,128)(2,1)}, bf16[2048,128]{1,0:T(8,128)(2,1)}, u32[]{:S(2)}, u32[]{:S(2)}) collective-permute-start(bf16[2048,128]{1,0:T(8,128)(2,1)} %get-tuple-element.40), channel_id=1, source_target_pairs={{0,2},{1,3},{2,0},{3,1},{4,6},{5,7},{6,4},{7,5},{8,10},{9,11},{10,... | collective-permute-start | bytes 1572872 | tf_op jit(solution)/shard_map/ppermute | solution.py:41
  35.6 6.6 %collective-permute-start.6 = (bf16[512,128]{1,0:T(8,128)(2,1)}, bf16[512,128]{1,0:T(8,128)(2,1)S(1)}, u32[]{:S(2)}, u32[]{:S(2)}) collective-permute-start(bf16[512,128]{1,0:T(8,128)(2,1)} %get-tuple-element.44), channel_id=1, source_target_pairs={{0,1},{1,0},{2,3},{3,2},{4,5},{5,4},{6,7},{7,6},{8,9},{9,8},{10,11... | collective-permute-start | bytes 393224 | tf_op jit(solution)/shard_map/ppermute | solution.py:41
  37.2 8.3 %collective-permute-start.7 = (bf16[512,128]{1,0:T(8,128)(2,1)}, bf16[512,128]{1,0:T(8,128)(2,1)S(1)}, u32[]{:S(2)}, u32[]{:S(2)}) collective-permute-start(bf16[512,128]{1,0:T(8,128)(2,1)} %get-tuple-element.45), channel_id=1, source_target_pairs={{0,4},{1,5},{2,6},{3,7},{4,0},{5,1},{6,2},{7,3},{8,12},{9,13},{10,... | collective-permute-start | bytes 393224 | tf_op jit(solution)/shard_map/ppermute | solution.py:41
  38.6 6.9 %collective-permute-start.8 = (bf16[512,128]{1,0:T(8,128)(2,1)S(1)}, bf16[512,128]{1,0:T(8,128)(2,1)S(1)}, u32[]{:S(2)}, u32[]{:S(2)}) collective-permute-start(bf16[512,128]{1,0:T(8,128)(2,1)S(1)} %get-tuple-element.46), channel_id=1, source_target_pairs={{0,5},{1,4},{2,7},{3,6},{4,1},{5,0},{6,3},{7,2},{8,13},{9,12},{10,... | collective-permute-start | bytes 393224 | tf_op jit(solution)/shard_map/ppermute | solution.py:41
  39.1 1.0 %copy-start.1 = (bf16[10,144,128]{2,1,0:T(8,128)(2,1)S(1)}, bf16[10,144,128]{2,1,0:T(8,128)(2,1)}, u32[]{:S(2)}) copy-start(bf16[10,144,128]{2,1,0:T(8,128)(2,1)} %copy-done) | copy-start | bytes 1105924
  45.6 5.0 %collective-permute-start.10 = (bf16[128,128]{1,0:T(8,128)(2,1)S(1)}, bf16[128,128]{1,0:T(8,128)(2,1)S(1)}, u32[]{:S(2)}, u32[]{:S(2)}) collective-permute-start(bf16[128,128]{1,0:T(8,128)(2,1)S(1)} %get-tuple-element.57), channel_id=1, source_target_pairs={{0,16},{1,17},{2,18},{3,19},{4,20},{5,21},{6,22},{7,23},{8,24},{9,... | collective-permute-start | bytes 98312 | tf_op jit(solution)/shard_map/ppermute | solution.py:41
  48.7 5.7 %collective-permute-start.11 = (bf16[128,128]{1,0:T(8,128)(2,1)S(1)}, bf16[128,128]{1,0:T(8,128)(2,1)S(1)}, u32[]{:S(2)}, u32[]{:S(2)}) collective-permute-start(bf16[128,128]{1,0:T(8,128)(2,1)S(1)} %get-tuple-element.56), channel_id=1, source_target_pairs={{0,24},{1,25},{2,26},{3,27},{4,28},{5,29},{6,30},{7,31},{8,16},{9,... | collective-permute-start | bytes 98312 | tf_op jit(solution)/shard_map/ppermute | solution.py:41
  50.0 4.4 %collective-permute-start.9 = (bf16[128,128]{1,0:T(8,128)(2,1)S(1)}, bf16[128,128]{1,0:T(8,128)(2,1)S(1)}, u32[]{:S(2)}, u32[]{:S(2)}) collective-permute-start(bf16[128,128]{1,0:T(8,128)(2,1)S(1)} %get-tuple-element.55), channel_id=1, source_target_pairs={{0,8},{1,9},{2,10},{3,11},{4,12},{5,13},{6,14},{7,15},{8,0},{9,1},... | collective-permute-start | bytes 98312 | tf_op jit(solution)/shard_map/ppermute | solution.py:41
  54.4 5.8 %collective-permute-start.12 = (bf16[128,128]{1,0:T(8,128)(2,1)S(1)}, bf16[128,128]{1,0:T(8,128)(2,1)S(1)}, u32[]{:S(2)}, u32[]{:S(2)}) collective-permute-start(bf16[128,128]{1,0:T(8,128)(2,1)S(1)} %add_convert_fusion), channel_id=1, source_target_pairs={{0,24},{1,25},{2,26},{3,27},{4,28},{5,29},{6,30},{7,31},{8,16},{9,... | collective-permute-start | bytes 98312 | tf_op jit(solution)/shard_map/ppermute | solution.py:41
  56.5 4.8 %collective-permute-start.13 = (bf16[128,128]{1,0:T(8,128)(2,1)S(1)}, bf16[128,128]{1,0:T(8,128)(2,1)S(1)}, u32[]{:S(2)}, u32[]{:S(2)}) collective-permute-start(bf16[128,128]{1,0:T(8,128)(2,1)S(1)} %add_convert_fusion), channel_id=1, source_target_pairs={{0,16},{1,17},{2,18},{3,19},{4,20},{5,21},{6,22},{7,23},{8,24},{9,... | collective-permute-start | bytes 98312 | tf_op jit(solution)/shard_map/ppermute | solution.py:41
  56.5 4.8 %collective-permute-start.14 = (bf16[128,128]{1,0:T(8,128)(2,1)S(1)}, bf16[128,128]{1,0:T(8,128)(2,1)S(1)}, u32[]{:S(2)}, u32[]{:S(2)}) collective-permute-start(bf16[128,128]{1,0:T(8,128)(2,1)S(1)} %add_convert_fusion), channel_id=1, source_target_pairs={{0,8},{1,9},{2,10},{3,11},{4,12},{5,13},{6,14},{7,15},{8,0},{9,1},... | collective-permute-start | bytes 98312 | tf_op jit(solution)/shard_map/ppermute | solution.py:41
  61.4 6.0 %collective-permute-start.15 = (bf16[512,128]{1,0:T(8,128)(2,1)S(1)}, bf16[512,128]{1,0:T(8,128)(2,1)S(1)}, u32[]{:S(2)}, u32[]{:S(2)}) collective-permute-start(bf16[512,128]{1,0:T(8,128)(2,1)S(1)} %pad_maximum_fusion.1), channel_id=1, source_target_pairs={{0,5},{1,4},{2,7},{3,6},{4,1},{5,0},{6,3},{7,2},{8,13},{9,12},{10,... | collective-permute-start | bytes 393224 | tf_op jit(solution)/shard_map/ppermute | solution.py:41
  62.6 6.1 %collective-permute-start.16 = (bf16[512,128]{1,0:T(8,128)(2,1)S(1)}, bf16[512,128]{1,0:T(8,128)(2,1)S(1)}, u32[]{:S(2)}, u32[]{:S(2)}) collective-permute-start(bf16[512,128]{1,0:T(8,128)(2,1)S(1)} %pad_maximum_fusion.1), channel_id=1, source_target_pairs={{0,4},{1,5},{2,6},{3,7},{4,0},{5,1},{6,2},{7,3},{8,12},{9,13},{10,... | collective-permute-start | bytes 393224 | tf_op jit(solution)/shard_map/ppermute | solution.py:41
  63.6 5.1 %collective-permute-start.17 = (bf16[512,128]{1,0:T(8,128)(2,1)S(1)}, bf16[512,128]{1,0:T(8,128)(2,1)S(1)}, u32[]{:S(2)}, u32[]{:S(2)}) collective-permute-start(bf16[512,128]{1,0:T(8,128)(2,1)S(1)} %pad_maximum_fusion.1), channel_id=1, source_target_pairs={{0,1},{1,0},{2,3},{3,2},{4,5},{5,4},{6,7},{7,6},{8,9},{9,8},{10,11... | collective-permute-start | bytes 393224 | tf_op jit(solution)/shard_map/ppermute | solution.py:41
  69.0 2.0 %collective-permute-start.18 = (bf16[2048,128]{1,0:T(8,128)(2,1)S(1)}, bf16[2048,128]{1,0:T(8,128)(2,1)S(1)}, u32[]{:S(2)}, u32[]{:S(2)}) collective-permute-start(bf16[2048,128]{1,0:T(8,128)(2,1)S(1)} %pad_maximum_fusion.packed_ref), channel_id=1, source_target_pairs={{0,2},{1,3},{2,0},{3,1},{4,6},{5,7},{6,4},{7,5},{8,10},{9,11},{10,... | collective-permute-start | bytes 1572872 | tf_op jit(solution)/shard_map/ppermute | solution.py:41

commit v8 on v7

--- a/solution.py
+++ b/solution.py
@@ -112,16 +112,35 @@
             stack_ref[parity, pl.ds(index * rows, rows), lane : lane + LANES] = shifted
 
 
-def convolve(stack_ref, weight_ref, pair, rows):
-    fields = [stack_ref[p % 2, (pair + p // 2) * rows : (pair + p // 2 + 1) * rows, :] for p in range(4)]
+def grouped(pairs, size):
+    count = max(1, pairs // size)
+    edges = [pairs * i // count for i in range(count + 1)]
+    return list(zip(edges, edges[1:]))
+
+
+def convolve(stack_ref, weight_ref, first, stop, rows):
+    fields = [stack_ref[p % 2, (first + p // 2) * rows : (stop + p // 2) * rows, :] for p in range(4)]
     both = jnp.dot(jnp.concatenate(fields, 1), weight_ref[...], preferred_element_type=F32)
-    return both[:, 0:LANES], both[:, LANES:]
+    return [
+        (pair, parity, both[(pair - first) * rows : (pair - first + 1) * rows, parity * LANES : (parity + 1) * LANES])
+        for pair in range(first, stop)
+        for parity in range(2)
+    ]
+
+
+def put_back(back_ref, w_ref, channels):
+    back_ref[...] = jnp.zeros_like(back_ref)
+    for d in range(3):
+        for j in range(OFFSETS):
+            for q in range(2):
+                start = ((2 - d + q) * OFFSETS + OFFSETS - 1 - j) * LANES
+                back_ref[start : start + channels, q * LANES : q * LANES + channels] = w_ref[d * OFFSETS + j]
 
 
 def weights_kernel(
     channels, classes,
     w1_in, w2_in, head_in,
-    ahead1_ref, ahead2_ref, back1_ref, back2_ref, head_out,
+    ahead1_ref, ahead2_ref, back2_ref, head_out,
     w1_ref, w2_ref, head_ref, arrived,
 ):
     copies = [
@@ -130,13 +149,13 @@
     ]
     for copy in copies:
         copy.start()
-    for ref in (ahead1_ref, ahead2_ref, back1_ref, back2_ref, head_out):
+    for ref in (ahead1_ref, ahead2_ref, head_out):
         ref[...] = jnp.zeros_like(ref)
     for copy in copies:
         copy.wait()
     row = lax.broadcasted_iota(jnp.int32, (channels, channels), 0)
     unit = (row == lax.broadcasted_iota(jnp.int32, (channels, channels), 1)).astype(BF16)
-    for w_ref, ahead_ref, back_ref in ((w1_ref, ahead1_ref, back1_ref), (w2_ref, ahead2_ref, back2_ref)):
+    for w_ref, ahead_ref in ((w1_ref, ahead1_ref), (w2_ref, ahead2_ref)):
         for d in range(3):
             for j in range(OFFSETS):
                 value = w_ref[d * OFFSETS + j]
@@ -145,8 +164,7 @@
                     side = slice(q * LANES, q * LANES + channels)
                     start = ((d + q) * OFFSETS + j) * LANES
                     ahead_ref[start : start + channels, side] = turned
-                    start = ((2 - d + q) * OFFSETS + OFFSETS - 1 - j) * LANES
-                    back_ref[start : start + channels, side] = value
+    put_back(back2_ref, w2_ref, channels)
     row = lax.broadcasted_iota(jnp.int32, (LANES, classes), 0)
     spread = (row == lax.broadcasted_iota(jnp.int32, (LANES, classes), 1) + channels + 1).astype(BF16)
     head_out[:, 0:channels] = jnp.dot(spread, head_ref[...], preferred_element_type=F32).astype(BF16)
@@ -162,19 +180,11 @@
 
 
 def kernel_sum(turned_ref, stack_ref, first, east, rows, low, size, channels):
-    total = None
-    for i in range(east // 2):
-        fields = []
-        for e in (2 * i, 2 * i + 1):
-            plane = e + first
-            start = (plane // 2) * rows + low
-            fields.append(stack_ref[plane % 2, start : start + size, :])
-        part = jnp.dot(
-            turned_ref[:, 2 * i * size : (2 * i + 2) * size],
-            jnp.concatenate(fields, 0),
-            preferred_element_type=F32,
-        )
-        total = part if total is None else total + part
+    fields = []
+    for e in range(first, first + east):
+        start = (e // 2) * rows + low
+        fields.append(stack_ref[e % 2, start : start + size, :])
+    total = jnp.dot(turned_ref[...], jnp.concatenate(fields, 0), preferred_element_type=F32)
     blocks = [
         total[d * channels : (d + 1) * channels, j * LANES : (j + 1) * LANES]
         for d in range(3)
@@ -218,14 +228,14 @@
     target = lax.broadcasted_iota(jnp.int32, (wide, LANES), 0) // upward + channels
     gather = (target == lax.broadcasted_iota(jnp.int32, (wide, LANES), 1)).astype(BF16)
     bricks = active_ref.shape
-    up = lax.broadcasted_iota(jnp.int32, (upward, north), 0) // (upward // bricks[2])
-    along = lax.broadcasted_iota(jnp.int32, (upward, north), 1) // (north // bricks[1])
+    up = lax.broadcasted_iota(jnp.int32, (upward, north), 0) // (upward // bricks[1])
+    along = lax.broadcasted_iota(jnp.int32, (upward, north), 1) // (north // bricks[2])
     for e in range(east):
         mask = jnp.zeros((upward, north), jnp.int32)
-        for b in range(bricks[1]):
-            for c in range(bricks[2]):
+        for b in range(bricks[2]):
+            for c in range(bricks[1]):
                 inside = (along == b) & (up == c)
-                mask = jnp.where(inside, active_ref[e // (east // bricks[0]), b, c], mask)
+                mask = jnp.where(inside, active_ref[e // (east // bricks[0]), c, b], mask)
         mask = (mask * occupied_ref[e]).astype(F32)
         field = jnp.concatenate([mask] + [teacher_ref[c, e].astype(F32) for c in range(classes)], 0).astype(BF16)
         everywhere = lax.dot_general(spread, field, (((1,), (1,)), ((), ())), preferred_element_type=F32)
@@ -297,8 +307,8 @@
         a0 = jnp.where((mask > 0) & (lane < channels), x, 0.0)
         put_stack(jnp.concatenate([border, a0, border], 0), upward, s0_ref, plane % 2, plane // 2)
 
-    for i in range((planes - 2) // 2):
-        for parity, value in enumerate(convolve(s0_ref, ahead1_ref, i, rows)):
+    for first, stop in grouped((planes - 2) // 2, 2):
+        for i, parity, value in convolve(s0_ref, ahead1_ref, first, stop, rows):
             plane = 2 * i + parity
             mask = mask_ref[plane + 1]
             p1 = mask * value
@@ -310,8 +320,8 @@
     class_lane = (lane[0:rows2] > channels) & (lane[0:rows2] <= channels + classes)
     here = slice(2 * upward, 2 * upward + rows2)
 
-    for i in range((planes - 4) // 2):
-        for parity, value in enumerate(convolve(s1_ref, ahead2_ref, i, rows2)):
+    for first, stop in grouped((planes - 4) // 2, 2):
+        for i, parity, value in convolve(s1_ref, ahead2_ref, first, stop, rows2):
             plane = 2 * i + parity
             mask = mask_ref[plane + 2, here]
             p2 = mask * value
@@ -333,8 +343,8 @@
         kept_ref[t * channels : (t + 1) * channels, :] = tile.astype(BF16)
 
     there = slice(2 * upward + upward, 2 * upward + upward + rows3)
-    for i in range((planes - 6) // 2):
-        for parity, value in enumerate(convolve(sg_ref, back2_ref, i, rows3)):
+    for first, stop in grouped((planes - 6) // 2, 2):
+        for i, parity, value in convolve(sg_ref, back2_ref, first, stop, rows3):
             plane = 2 * i + parity
             g_p1 = slope_ref[plane + 2, there] * value
             grad_ref[plane] = g_p1.astype(BF16)
@@ -354,15 +364,19 @@
 
 def last_kernel(
     channels, east, north, upward,
-    center_ref, grad_ref, back1_ref, kept_in,
+    center_ref, grad_ref, w1_in, kept_in,
     out_ref, kept_out,
-    stack_ref,
+    stack_ref, back1_ref, w1_ref, arrived,
 ):
     size = north * upward
+    copy = pltpu.make_async_copy(w1_in, w1_ref, arrived)
+    copy.start()
     for plane in range(east + 2):
         put_stack(grad_ref[plane].astype(F32), upward, stack_ref, plane % 2, plane // 2)
-    for i in range(east // 2):
-        for parity, value in enumerate(convolve(stack_ref, back1_ref, i, size)):
+    copy.wait()
+    put_back(back1_ref, w1_ref, channels)
+    for first, stop in grouped(east // 2, 2):
+        for i, parity, value in convolve(stack_ref, back1_ref, first, stop, size):
             plane = 2 * i + parity
             mask = center_ref[plane, :, channels : channels + 1].astype(F32)
             out_ref[plane] = (mask * value)[:, 0:channels].astype(BF16)
@@ -450,11 +464,11 @@
             pltpu.VMEM((classes, east, upward, north), BF16),
             pltpu.SemaphoreType.DMA((3,)),
         ],
-        compiler_params=pltpu.CompilerParams(vmem_limit_bytes=16 * 1024 * 1024),
+        compiler_params=pltpu.CompilerParams(vmem_limit_bytes=6 * 1024 * 1024),
         name="prepare",
     )(
         flags,
-        brick_active,
+        brick_active.transpose(0, 2, 1),
         pltpu.with_memory_space_constraint(features.transpose(1, 2, 3, 0).reshape(east, size, channels), pltpu.HBM),
         pltpu.with_memory_space_constraint(voxel_occupancy.transpose(0, 2, 1), pltpu.HBM),
         pltpu.with_memory_space_constraint(teacher.transpose(0, 1, 3, 2), pltpu.HBM),
@@ -466,19 +480,19 @@
 
     unit = devices // 2 * 16
     packed = -(-21 * channels // unit) * unit
-    shapes = [(4 * WIDE, 2 * LANES)] * 4 + [(LANES, LANES)]
-    ahead1, ahead2, back1, back2, head_wide = pl.pallas_call(
+    shapes = [(4 * WIDE, 2 * LANES)] * 3 + [(LANES, LANES)]
+    ahead1, ahead2, back2, head_wide = pl.pallas_call(
         functools.partial(weights_kernel, channels, classes),
         out_shape=[jax.ShapeDtypeStruct(shape, BF16) for shape in shapes],
         in_specs=[far] * 3,
-        out_specs=[vmem] * 5,
+        out_specs=[vmem] * 4,
         scratch_shapes=[
             pltpu.VMEM(first_weights.shape, BF16),
             pltpu.VMEM(second_weights.shape, BF16),
             pltpu.VMEM(head.shape, BF16),
             pltpu.SemaphoreType.DMA((3,)),
         ],
-        compiler_params=pltpu.CompilerParams(vmem_limit_bytes=16 * 1024 * 1024),
+        compiler_params=pltpu.CompilerParams(vmem_limit_bytes=12 * 1024 * 1024),
         name="weights",
     )(*[pltpu.with_memory_space_constraint(value, pltpu.HBM) for value in (first_weights, second_weights, head)])
     grad, kept, sent = pl.pallas_call(
@@ -499,7 +513,7 @@
             pltpu.VMEM((planes - 2, rows, LANES), F32),
             pltpu.VMEM((3 * channels, east * size), BF16),
         ],
-        compiler_params=pltpu.CompilerParams(vmem_limit_bytes=32 * 1024 * 1024),
+        compiler_params=pltpu.CompilerParams(vmem_limit_bytes=26 * 1024 * 1024),
         name="fields",
     )(flags, ahead1, ahead2, back2, head_wide, center, *edges)
 
@@ -512,13 +526,18 @@
                 jax.ShapeDtypeStruct((east, size, channels), BF16),
                 jax.ShapeDtypeStruct(kept.shape, F32),
             ),
-            in_specs=[vmem] * 3 + [anywhere],
+            in_specs=[vmem, vmem, far, anywhere],
             out_specs=(vmem, anywhere),
             input_output_aliases={3: 1},
-            scratch_shapes=[pltpu.VMEM((2, (east + 2) // 2 * size, WIDE), BF16)],
-            compiler_params=pltpu.CompilerParams(vmem_limit_bytes=12 * 1024 * 1024),
+            scratch_shapes=[
+                pltpu.VMEM((2, (east + 2) // 2 * size, WIDE), BF16),
+                pltpu.VMEM((4 * WIDE, 2 * LANES), BF16),
+                pltpu.VMEM(first_weights.shape, BF16),
+                pltpu.SemaphoreType.DMA(()),
+            ],
+            compiler_params=pltpu.CompilerParams(vmem_limit_bytes=10 * 1024 * 1024),
             name="features",
-        )(center, grad, back1, kept)
+        )(center, grad, pltpu.with_memory_space_constraint(first_weights, pltpu.HBM), kept)
         features_out.append(out)
         return kept
 
@@ -530,7 +549,7 @@
         + [jax.ShapeDtypeStruct((part, LANES), BF16)] * (ways - 1),
         in_specs=[smem] + [vmem] * 2,
         out_specs=[vmem] * ways,
-        compiler_params=pltpu.CompilerParams(vmem_limit_bytes=8 * 1024 * 1024),
+        compiler_params=pltpu.CompilerParams(vmem_limit_bytes=4 * 1024 * 1024),
         name="parts",
     )(place_in(groups[0]).reshape(1).astype(jnp.int32), kept, swap(sent, east_bits[:1], 1))
     total = beside(total)
@@ -551,7 +570,7 @@
             out_specs=(anywhere, anywhere),
             input_output_aliases={2: 0, 3: 1} if aliased else {},
             scratch_shapes=[pltpu.VMEM(first_weights.shape, F32), pltpu.SemaphoreType.DMA((7,))],
-            compiler_params=pltpu.CompilerParams(vmem_limit_bytes=12 * 1024 * 1024),
+            compiler_params=pltpu.CompilerParams(vmem_limit_bytes=5 * 1024 * 1024),
             name="unpack",
         )(is_first.reshape(1).astype(jnp.int32), value, *aliased)
 

time: 72.6 us -> 68.8 us (0.948)
  local copies, waits for them, and re-layouts: 2.58 us -> 0.77 us
  waiting for transfers between devices: 16.3 us -> 15.1 us
  Pallas kernels: 28.8 us -> 27.9 us
    unnamed x5 -> x2, local copies, waits for them, and re-layouts: 2.47 us -> 0.66 us
    pallas_call x1, Pallas kernels: 1.77 us -> 0.12 us  [per_device(): pl.pallas_call(parts_kernel, out_shape=[jax.ShapeDtypeStruct((part, LANES...]
    pallas_call x1, Pallas kernels: 2.15 us -> 3.55 us  [beside(): pl.pallas_call(functools.partial(last_kernel, channels, east, north, upwa...]
    ppermute x19, waiting for transfers between devices: 16.3 us -> 15.1 us  [exchange(): return lax.ppermute(value, ('east', 'north'), pairs)]
    pallas_call x1, Pallas kernels: 17.2 us -> 16.3 us  [per_device(): pl.pallas_call(functools.partial(whole_kernel, channels, classes, east, n...]
  transfers between devices with their start and end apart: 19 -> 19, of which waited for: 9 -> 10; matrix products, arithmetic and copies ran while one was open for 0% -> 0% of each run, Pallas kernels for 8% -> 11%
where the time goes in v8:
time: 68.8 us; the launch traced here: 68.6 us
  Pallas kernels  27.9 us (41%)
  starting transfers between devices  23.4 us (34%)
  waiting for transfers between devices  15.1 us (22%)
  between operations  1.01 us (1%)
  local copies, waits for them, and re-layouts  0.77 us (1%)
    ppermute x19, starting transfers between devices, exchange(): return lax.ppermute(value, ('east', 'north'), pairs)  23.4 us
    pallas_call x1, Pallas kernels, per_device(): pl.pallas_call(functools.partial(whole_kernel, channels, classes, east, n...  16.3 us
    ppermute x19, waiting for transfers between devices, exchange(): return lax.ppermute(value, ('east', 'north'), pairs)  15.1 us
    pallas_call x1, Pallas kernels, beside(): pl.pallas_call(functools.partial(last_kernel, channels, east, north, upwa...  3.55 us
    pallas_call x1, Pallas kernels, per_device(): pl.pallas_call(functools.partial(prepare_kernel, channels, upward, edge,...  2.87 us
    pallas_call x1, Pallas kernels, per_device(): pl.pallas_call(functools.partial(weights_kernel, channels, classes), out_...  2.67 us
    pallas_call x2, Pallas kernels, unpack(): pl.pallas_call(functools.partial(unpack_kernel, channels, scale, bool(ali...  2.43 us
  transfers between devices with their start and end apart: 19, of which 10 were waited for; matrix products, arithmetic and copies ran while one was open for 0% of the time, Pallas kernels for 11%

profile of v8, /device:TPU:0, one launch (start us, length us, event | category | flops | bytes accessed | tf_op | source)
XLA Modules:
  0.0 68.6 jit_solution(4869280252871288388)
XLA Ops:
  1.4 2.9 %prepare.1 = (bf16[8,128,128]{2,1,0:T(8,128)(2,1)S(1)}, bf16[4,128,128]{2,1,0:T(8,128)(2,1)S(1)}, bf16[4,128,128]{2,1,0:T(8,128)(2,1)S(1)}, bf16[8,32,128]{2,1,0...) custom-call(s32[7]{0:T(128)S(1)} %stack.24.flags_ref, s32[1,1,2]{2,1,0:T(1,128)S(1)} %bitcast.15, ...), custom_call_target="tpu_custom_call" | custom-call | tf_op jit(solution)/shard_map/prepare/pallas_call | solution.py:456
  4.8 2.6 %collective-permute-start.1 = (bf16[4,128,128]{2,1,0:T(8,128)(2,1)S(1)}, bf16[4,128,128]{2,1,0:T(8,128)(2,1)S(1)}, u32[]{:S(2)}, u32[]{:S(2)}) collective-permute-start(bf16[4,128,128]{2,1,0:T(8,128)(2,1)S(1)} %get-tuple-element.32), channel_id=1, source_target_pairs={{0,1},{1,0},{2,4},{3,5},{4,2},{5,3},{6,8},{7,9},{8,6},{9,7},{10,12... | collective-permute-start | bytes 393224 | tf_op jit(solution)/shard_map/ppermute | solution.py:41
  7.5 1.4 %collective-permute-start.3 = (bf16[4,32,128]{2,1,0:T(8,128)(2,1)S(1)}, bf16[4,32,128]{2,1,0:T(8,128)(2,1)S(1)}, u32[]{:S(2)}, u32[]{:S(2)}) collective-permute-start(bf16[4,32,128]{2,1,0:T(8,128)(2,1)S(1)} %get-tuple-element.34), channel_id=1, source_target_pairs={{0,3},{1,2},{2,1},{3,0},{4,7},{5,6},{6,5},{7,4},{8,11},{9,10},{10,... | collective-permute-start | bytes 98312 | tf_op jit(solution)/shard_map/ppermute | solution.py:41
  8.9 1.5 %collective-permute-start.4 = (bf16[4,32,128]{2,1,0:T(8,128)(2,1)S(1)}, bf16[4,32,128]{2,1,0:T(8,128)(2,1)S(1)}, u32[]{:S(2)}, u32[]{:S(2)}) collective-permute-start(bf16[4,32,128]{2,1,0:T(8,128)(2,1)S(1)} %get-tuple-element.35), channel_id=1, source_target_pairs={{0,1},{1,0},{2,5},{3,4},{4,3},{5,2},{6,9},{7,8},{8,7},{9,6},{10,13... | collective-permute-start | bytes 98312 | tf_op jit(solution)/shard_map/ppermute | solution.py:41
  10.4 2.7 %weights.1 = (bf16[4608,256]{1,0:T(8,128)(2,1)S(1)}, bf16[4608,256]{1,0:T(8,128)(2,1)S(1)}, bf16[4608,256]{1,0:T(8,128)(2,1)S(1)}, bf16[128,128]{1,0:T(8,128)(2,1)S(1)}) custom-call(bf16[27,96,96]{2,1,0:T(8,128)(2,1)} %w1_in.3, bf16[27,96,96]{2,1,0:T(8,128)(2,1)} %w2_in.1, bf16[13,96]{1,0:T(8,128)(2,1)} %head_in.1), custom_call_target="tpu_custom_call" | custom-call | tf_op jit(solution)/shard_map/weights/pallas_call | solution.py:484
  13.1 16.3 %fields.1 = (bf16[10,144,128]{2,1,0:T(8,128)(2,1)S(1)}, bf16[2048,128]{1,0:T(8,128)(2,1)S(1)}, bf16[2048,128]{1,0:T(8,128)(2,1)S(1)}) custom-call(s32[7]{0:T(128)S(1)} %stack.24.flags_ref, bf16[4608,256]{1,0:T(8,128)(2,1)S(1)} %get-tuple-element.27.ahead1_ref, bf16[4608,256]{1,0:T(8,128)(2,1)S(1)} %get-tuple-element.28.ahead2_ref, ...), custom_call_target="tpu_custom_call" | custom-call | tf_op jit(solution)/shard_map/fields/pallas_call | solution.py:498
  29.4 1.1 %collective-permute-start.5 = (bf16[2048,128]{1,0:T(8,128)(2,1)S(1)}, bf16[2048,128]{1,0:T(8,128)(2,1)S(1)}, u32[]{:S(2)}, u32[]{:S(2)}) collective-permute-start(bf16[2048,128]{1,0:T(8,128)(2,1)S(1)} %get-tuple-element.38), channel_id=1, source_target_pairs={{0,2},{1,3},{2,0},{3,1},{4,6},{5,7},{6,4},{7,5},{8,10},{9,11},{10,... | collective-permute-start | bytes 1572872 | tf_op jit(solution)/shard_map/ppermute | solution.py:41
  30.5 1.5 %collective-permute-done.5.came_ref = bf16[2048,128]{1,0:T(8,128)(2,1)S(1)} collective-permute-done((bf16[2048,128]{1,0:T(8,128)(2,1)S(1)}, bf16[2048,128]{1,0:T(8,128)(2,1)S(1)}, u32[]{:S(2)}, u32[]{:S(2)}) %collective-permute-start.5) | collective-permute-done | bytes 524320 | tf_op jit(solution)/shard_map/ppermute | solution.py:41
  32.2 1.4 %collective-permute-start.6 = (bf16[512,128]{1,0:T(8,128)(2,1)S(1)}, bf16[512,128]{1,0:T(8,128)(2,1)S(1)}, u32[]{:S(2)}, u32[]{:S(2)}) collective-permute-start(bf16[512,128]{1,0:T(8,128)(2,1)S(1)} %get-tuple-element.42), channel_id=1, source_target_pairs={{0,1},{1,0},{2,3},{3,2},{4,5},{5,4},{6,7},{7,6},{8,9},{9,8},{10,11... | collective-permute-start | bytes 393224 | tf_op jit(solution)/shard_map/ppermute | solution.py:41
  33.6 1.4 %collective-permute-start.7 = (bf16[512,128]{1,0:T(8,128)(2,1)S(1)}, bf16[512,128]{1,0:T(8,128)(2,1)S(1)}, u32[]{:S(2)}, u32[]{:S(2)}) collective-permute-start(bf16[512,128]{1,0:T(8,128)(2,1)S(1)} %get-tuple-element.43), channel_id=1, source_target_pairs={{0,4},{1,5},{2,6},{3,7},{4,0},{5,1},{6,2},{7,3},{8,12},{9,13},{10,... | collective-permute-start | bytes 393224 | tf_op jit(solution)/shard_map/ppermute | solution.py:41
  35.8 3.5 %features.1 = (bf16[8,128,96]{2,1,0:T(8,128)(2,1)}, f32[512,128]{1,0:T(8,128)S(1)}) custom-call(bf16[8,128,128]{2,1,0:T(8,128)(2,1)S(1)} %get-tuple-element.26.center_ref, bf16[10,144,128]{2,1,0:T(8,128)(2,1)S(1)} %get-tuple-element.36.grad_ref, bf16[27,96,96]{2,1,0:T(8,128)(2,1)} %w1_in.3, ...), custom_call_target="tpu_custom_call", output_to_operand_aliasing={{1}: (3, {})} | custom-call | tf_op jit(solution)/shard_map/features/pallas_call | solution.py:523
  39.3 1.4 %collective-permute-done.7 = bf16[512,128]{1,0:T(8,128)(2,1)S(1)} collective-permute-done((bf16[512,128]{1,0:T(8,128)(2,1)S(1)}, bf16[512,128]{1,0:T(8,128)(2,1)S(1)}, u32[]{:S(2)}, u32[]{:S(2)}) %collective-permute-start.7) | collective-permute-done | bytes 131104 | tf_op jit(solution)/shard_map/ppermute | solution.py:41
  41.9 3.0 %collective-permute-start.10 = (bf16[128,128]{1,0:T(8,128)(2,1)S(1)}, bf16[128,128]{1,0:T(8,128)(2,1)S(1)}, u32[]{:S(2)}, u32[]{:S(2)}) collective-permute-start(bf16[128,128]{1,0:T(8,128)(2,1)S(1)} %get-tuple-element.55), channel_id=1, source_target_pairs={{0,16},{1,17},{2,18},{3,19},{4,20},{5,21},{6,22},{7,23},{8,24},{9,... | collective-permute-start | bytes 98312 | tf_op jit(solution)/shard_map/ppermute | solution.py:41
  44.9 1.3 %collective-permute-start.11 = (bf16[128,128]{1,0:T(8,128)(2,1)S(1)}, bf16[128,128]{1,0:T(8,128)(2,1)S(1)}, u32[]{:S(2)}, u32[]{:S(2)}) collective-permute-start(bf16[128,128]{1,0:T(8,128)(2,1)S(1)} %get-tuple-element.54), channel_id=1, source_target_pairs={{0,24},{1,25},{2,26},{3,27},{4,28},{5,29},{6,30},{7,31},{8,16},{9,... | collective-permute-start | bytes 98312 | tf_op jit(solution)/shard_map/ppermute | solution.py:41
  47.0 3.6 %collective-permute-done.11 = bf16[128,128]{1,0:T(8,128)(2,1)S(1)} collective-permute-done((bf16[128,128]{1,0:T(8,128)(2,1)S(1)}, bf16[128,128]{1,0:T(8,128)(2,1)S(1)}, u32[]{:S(2)}, u32[]{:S(2)}) %collective-permute-start.11) | collective-permute-done | bytes 32800 | tf_op jit(solution)/shard_map/ppermute | solution.py:41
  50.6 2.1 %collective-permute-start.12 = (bf16[128,128]{1,0:T(8,128)(2,1)S(1)}, bf16[128,128]{1,0:T(8,128)(2,1)S(1)}, u32[]{:S(2)}, u32[]{:S(2)}) collective-permute-start(bf16[128,128]{1,0:T(8,128)(2,1)S(1)} %add_convert_fusion), channel_id=1, source_target_pairs={{0,24},{1,25},{2,26},{3,27},{4,28},{5,29},{6,30},{7,31},{8,16},{9,... | collective-permute-start | bytes 98312 | tf_op jit(solution)/shard_map/ppermute | solution.py:41
  52.7 2.4 %collective-permute-start.14 = (bf16[128,128]{1,0:T(8,128)(2,1)S(1)}, bf16[128,128]{1,0:T(8,128)(2,1)S(1)}, u32[]{:S(2)}, u32[]{:S(2)}) collective-permute-start(bf16[128,128]{1,0:T(8,128)(2,1)S(1)} %add_convert_fusion), channel_id=1, source_target_pairs={{0,8},{1,9},{2,10},{3,11},{4,12},{5,13},{6,14},{7,15},{8,0},{9,1},... | collective-permute-start | bytes 98312 | tf_op jit(solution)/shard_map/ppermute | solution.py:41
  55.1 1.3 %collective-permute-done.12 = bf16[128,128]{1,0:T(8,128)(2,1)S(1)} collective-permute-done((bf16[128,128]{1,0:T(8,128)(2,1)S(1)}, bf16[128,128]{1,0:T(8,128)(2,1)S(1)}, u32[]{:S(2)}, u32[]{:S(2)}) %collective-permute-start.12) | collective-permute-done | bytes 32800 | tf_op jit(solution)/shard_map/ppermute | solution.py:41
  57.6 1.5 %collective-permute-start.15 = (bf16[512,128]{1,0:T(8,128)(2,1)S(1)}, bf16[512,128]{1,0:T(8,128)(2,1)S(1)}, u32[]{:S(2)}, u32[]{:S(2)}) collective-permute-start(bf16[512,128]{1,0:T(8,128)(2,1)S(1)} %pad_maximum_fusion.1), channel_id=1, source_target_pairs={{0,5},{1,4},{2,7},{3,6},{4,1},{5,0},{6,3},{7,2},{8,13},{9,12},{10,... | collective-permute-start | bytes 393224 | tf_op jit(solution)/shard_map/ppermute | solution.py:41
  59.8 1.3 %collective-permute-start.17 = (bf16[512,128]{1,0:T(8,128)(2,1)S(1)}, bf16[512,128]{1,0:T(8,128)(2,1)S(1)}, u32[]{:S(2)}, u32[]{:S(2)}) collective-permute-start(bf16[512,128]{1,0:T(8,128)(2,1)S(1)} %pad_maximum_fusion.1), channel_id=1, source_target_pairs={{0,1},{1,0},{2,3},{3,2},{4,5},{5,4},{6,7},{7,6},{8,9},{9,8},{10,11... | collective-permute-start | bytes 393224 | tf_op jit(solution)/shard_map/ppermute | solution.py:41
  61.1 2.5 %collective-permute-done.15 = bf16[512,128]{1,0:T(8,128)(2,1)S(1)} collective-permute-done((bf16[512,128]{1,0:T(8,128)(2,1)S(1)}, bf16[512,128]{1,0:T(8,128)(2,1)S(1)}, u32[]{:S(2)}, u32[]{:S(2)}) %collective-permute-start.15) | collective-permute-done | bytes 131104 | tf_op jit(solution)/shard_map/ppermute | solution.py:41
  63.6 1.3 %collective-permute-done.16 = bf16[512,128]{1,0:T(8,128)(2,1)S(1)} collective-permute-done((bf16[512,128]{1,0:T(8,128)(2,1)S(1)}, bf16[512,128]{1,0:T(8,128)(2,1)S(1)}, u32[]{:S(2)}, u32[]{:S(2)}) %collective-permute-start.16) | collective-permute-done | bytes 131104 | tf_op jit(solution)/shard_map/ppermute | solution.py:41
  65.3 1.2 %unpack.2 = (f32[27,96,96]{2,1,0:T(8,128)}, f32[27,96,96]{2,1,0:T(8,128)}) custom-call(s32[1]{0:T(128)} %bitcast.first_ref_flag, bf16[2048,128]{1,0:T(8,128)(2,1)S(1)} %pad_maximum_fusion.packed_ref), custom_call_target="tpu_custom_call" | custom-call | tf_op jit(solution)/shard_map/unpack/pallas_call | solution.py:563
  67.2 1.2 %unpack.3 = (f32[27,96,96]{2,1,0:T(8,128)}, f32[27,96,96]{2,1,0:T(8,128)}) custom-call(s32[1]{0:T(128)} %bitcast.12.first_ref_flag, bf16[2048,128]{1,0:T(8,128)(2,1)S(1)} %collective-permute-done.18.packed_ref, f32[27,96,96]{2,1,0:T(8,128)} %get-tuple-element.45.refs_0_, ...), custom_call_target="tpu_custom_call", output_to_operand_aliasing={{0}: (2, {}), {1}: (3, {})} | custom-call | tf_op jit(solution)/shard_map/unpack/pallas_call | solution.py:563
  (32 shorter events, 7.1 us)
Async XLA Ops:
  0.8 0.7 copy-start
  4.3 8.8 %collective-permute-start = (bf16[4,128,128]{2,1,0:T(8,128)(2,1)S(1)}, bf16[4,128,128]{2,1,0:T(8,128)(2,1)S(1)}, u32[]{:S(2)}, u32[]{:S(2)}) collective-permute-start(bf16[4,128,128]{2,1,0:T(8,128)(2,1)S(1)} %get-tuple-element.31), channel_id=1, source_target_pairs={{0,2},{1,3},{2,0},{3,1},{4,6},{5,7},{6,4},{7,5},{8,10},{9,11},{10,... | collective-permute-start | bytes 393224 | tf_op jit(solution)/shard_map/ppermute | solution.py:41
  4.8 8.3 %collective-permute-start.1 = (bf16[4,128,128]{2,1,0:T(8,128)(2,1)S(1)}, bf16[4,128,128]{2,1,0:T(8,128)(2,1)S(1)}, u32[]{:S(2)}, u32[]{:S(2)}) collective-permute-start(bf16[4,128,128]{2,1,0:T(8,128)(2,1)S(1)} %get-tuple-element.32), channel_id=1, source_target_pairs={{0,1},{1,0},{2,4},{3,5},{4,2},{5,3},{6,8},{7,9},{8,6},{9,7},{10,12... | collective-permute-start | bytes 393224 | tf_op jit(solution)/shard_map/ppermute | solution.py:41
  7.4 5.7 %collective-permute-start.2 = (bf16[8,32,128]{2,1,0:T(8,128)(2,1)S(1)}, bf16[8,32,128]{2,1,0:T(8,128)(2,1)S(1)}, u32[]{:S(2)}, u32[]{:S(2)}) collective-permute-start(bf16[8,32,128]{2,1,0:T(8,128)(2,1)S(1)} %get-tuple-element.33), channel_id=1, source_target_pairs={{0,1},{1,0},{2,3},{3,2},{4,5},{5,4},{6,7},{7,6},{8,9},{9,8},{10,11... | collective-permute-start | bytes 196616 | tf_op jit(solution)/shard_map/ppermute | solution.py:41
  7.5 5.6 %collective-permute-start.3 = (bf16[4,32,128]{2,1,0:T(8,128)(2,1)S(1)}, bf16[4,32,128]{2,1,0:T(8,128)(2,1)S(1)}, u32[]{:S(2)}, u32[]{:S(2)}) collective-permute-start(bf16[4,32,128]{2,1,0:T(8,128)(2,1)S(1)} %get-tuple-element.34), channel_id=1, source_target_pairs={{0,3},{1,2},{2,1},{3,0},{4,7},{5,6},{6,5},{7,4},{8,11},{9,10},{10,... | collective-permute-start | bytes 98312 | tf_op jit(solution)/shard_map/ppermute | solution.py:41
  8.9 4.2 %collective-permute-start.4 = (bf16[4,32,128]{2,1,0:T(8,128)(2,1)S(1)}, bf16[4,32,128]{2,1,0:T(8,128)(2,1)S(1)}, u32[]{:S(2)}, u32[]{:S(2)}) collective-permute-start(bf16[4,32,128]{2,1,0:T(8,128)(2,1)S(1)} %get-tuple-element.35), channel_id=1, source_target_pairs={{0,1},{1,0},{2,5},{3,4},{4,3},{5,2},{6,9},{7,8},{8,7},{9,6},{10,13... | collective-permute-start | bytes 98312 | tf_op jit(solution)/shard_map/ppermute | solution.py:41
  29.4 2.7 %collective-permute-start.5 = (bf16[2048,128]{1,0:T(8,128)(2,1)S(1)}, bf16[2048,128]{1,0:T(8,128)(2,1)S(1)}, u32[]{:S(2)}, u32[]{:S(2)}) collective-permute-start(bf16[2048,128]{1,0:T(8,128)(2,1)S(1)} %get-tuple-element.38), channel_id=1, source_target_pairs={{0,2},{1,3},{2,0},{3,1},{4,6},{5,7},{6,4},{7,5},{8,10},{9,11},{10,... | collective-permute-start | bytes 1572872 | tf_op jit(solution)/shard_map/ppermute | solution.py:41
  32.2 7.1 %collective-permute-start.6 = (bf16[512,128]{1,0:T(8,128)(2,1)S(1)}, bf16[512,128]{1,0:T(8,128)(2,1)S(1)}, u32[]{:S(2)}, u32[]{:S(2)}) collective-permute-start(bf16[512,128]{1,0:T(8,128)(2,1)S(1)} %get-tuple-element.42), channel_id=1, source_target_pairs={{0,1},{1,0},{2,3},{3,2},{4,5},{5,4},{6,7},{7,6},{8,9},{9,8},{10,11... | collective-permute-start | bytes 393224 | tf_op jit(solution)/shard_map/ppermute | solution.py:41
  33.6 7.1 %collective-permute-start.7 = (bf16[512,128]{1,0:T(8,128)(2,1)S(1)}, bf16[512,128]{1,0:T(8,128)(2,1)S(1)}, u32[]{:S(2)}, u32[]{:S(2)}) collective-permute-start(bf16[512,128]{1,0:T(8,128)(2,1)S(1)} %get-tuple-element.43), channel_id=1, source_target_pairs={{0,4},{1,5},{2,6},{3,7},{4,0},{5,1},{6,2},{7,3},{8,12},{9,13},{10,... | collective-permute-start | bytes 393224 | tf_op jit(solution)/shard_map/ppermute | solution.py:41
  35.0 6.8 %collective-permute-start.8 = (bf16[512,128]{1,0:T(8,128)(2,1)S(1)}, bf16[512,128]{1,0:T(8,128)(2,1)S(1)}, u32[]{:S(2)}, u32[]{:S(2)}) collective-permute-start(bf16[512,128]{1,0:T(8,128)(2,1)S(1)} %get-tuple-element.44), channel_id=1, source_target_pairs={{0,5},{1,4},{2,7},{3,6},{4,1},{5,0},{6,3},{7,2},{8,13},{9,12},{10,... | collective-permute-start | bytes 393224 | tf_op jit(solution)/shard_map/ppermute | solution.py:41
  41.9 5.1 %collective-permute-start.10 = (bf16[128,128]{1,0:T(8,128)(2,1)S(1)}, bf16[128,128]{1,0:T(8,128)(2,1)S(1)}, u32[]{:S(2)}, u32[]{:S(2)}) collective-permute-start(bf16[128,128]{1,0:T(8,128)(2,1)S(1)} %get-tuple-element.55), channel_id=1, source_target_pairs={{0,16},{1,17},{2,18},{3,19},{4,20},{5,21},{6,22},{7,23},{8,24},{9,... | collective-permute-start | bytes 98312 | tf_op jit(solution)/shard_map/ppermute | solution.py:41
  44.9 5.7 %collective-permute-start.11 = (bf16[128,128]{1,0:T(8,128)(2,1)S(1)}, bf16[128,128]{1,0:T(8,128)(2,1)S(1)}, u32[]{:S(2)}, u32[]{:S(2)}) collective-permute-start(bf16[128,128]{1,0:T(8,128)(2,1)S(1)} %get-tuple-element.54), channel_id=1, source_target_pairs={{0,24},{1,25},{2,26},{3,27},{4,28},{5,29},{6,30},{7,31},{8,16},{9,... | collective-permute-start | bytes 98312 | tf_op jit(solution)/shard_map/ppermute | solution.py:41
  46.2 4.4 %collective-permute-start.9 = (bf16[128,128]{1,0:T(8,128)(2,1)S(1)}, bf16[128,128]{1,0:T(8,128)(2,1)S(1)}, u32[]{:S(2)}, u32[]{:S(2)}) collective-permute-start(bf16[128,128]{1,0:T(8,128)(2,1)S(1)} %get-tuple-element.53), channel_id=1, source_target_pairs={{0,8},{1,9},{2,10},{3,11},{4,12},{5,13},{6,14},{7,15},{8,0},{9,1},... | collective-permute-start | bytes 98312 | tf_op jit(solution)/shard_map/ppermute | solution.py:41
  50.6 5.8 %collective-permute-start.12 = (bf16[128,128]{1,0:T(8,128)(2,1)S(1)}, bf16[128,128]{1,0:T(8,128)(2,1)S(1)}, u32[]{:S(2)}, u32[]{:S(2)}) collective-permute-start(bf16[128,128]{1,0:T(8,128)(2,1)S(1)} %add_convert_fusion), channel_id=1, source_target_pairs={{0,24},{1,25},{2,26},{3,27},{4,28},{5,29},{6,30},{7,31},{8,16},{9,... | collective-permute-start | bytes 98312 | tf_op jit(solution)/shard_map/ppermute | solution.py:41
  52.7 4.8 %collective-permute-start.13 = (bf16[128,128]{1,0:T(8,128)(2,1)S(1)}, bf16[128,128]{1,0:T(8,128)(2,1)S(1)}, u32[]{:S(2)}, u32[]{:S(2)}) collective-permute-start(bf16[128,128]{1,0:T(8,128)(2,1)S(1)} %add_convert_fusion), channel_id=1, source_target_pairs={{0,16},{1,17},{2,18},{3,19},{4,20},{5,21},{6,22},{7,23},{8,24},{9,... | collective-permute-start | bytes 98312 | tf_op jit(solution)/shard_map/ppermute | solution.py:41
  52.7 4.8 %collective-permute-start.14 = (bf16[128,128]{1,0:T(8,128)(2,1)S(1)}, bf16[128,128]{1,0:T(8,128)(2,1)S(1)}, u32[]{:S(2)}, u32[]{:S(2)}) collective-permute-start(bf16[128,128]{1,0:T(8,128)(2,1)S(1)} %add_convert_fusion), channel_id=1, source_target_pairs={{0,8},{1,9},{2,10},{3,11},{4,12},{5,13},{6,14},{7,15},{8,0},{9,1},... | collective-permute-start | bytes 98312 | tf_op jit(solution)/shard_map/ppermute | solution.py:41
  57.6 6.0 %collective-permute-start.15 = (bf16[512,128]{1,0:T(8,128)(2,1)S(1)}, bf16[512,128]{1,0:T(8,128)(2,1)S(1)}, u32[]{:S(2)}, u32[]{:S(2)}) collective-permute-start(bf16[512,128]{1,0:T(8,128)(2,1)S(1)} %pad_maximum_fusion.1), channel_id=1, source_target_pairs={{0,5},{1,4},{2,7},{3,6},{4,1},{5,0},{6,3},{7,2},{8,13},{9,12},{10,... | collective-permute-start | bytes 393224 | tf_op jit(solution)/shard_map/ppermute | solution.py:41
  59.1 5.9 %collective-permute-start.16 = (bf16[512,128]{1,0:T(8,128)(2,1)S(1)}, bf16[512,128]{1,0:T(8,128)(2,1)S(1)}, u32[]{:S(2)}, u32[]{:S(2)}) collective-permute-start(bf16[512,128]{1,0:T(8,128)(2,1)S(1)} %pad_maximum_fusion.1), channel_id=1, source_target_pairs={{0,4},{1,5},{2,6},{3,7},{4,0},{5,1},{6,2},{7,3},{8,12},{9,13},{10,... | collective-permute-start | bytes 393224 | tf_op jit(solution)/shard_map/ppermute | solution.py:41
  59.8 5.1 %collective-permute-start.17 = (bf16[512,128]{1,0:T(8,128)(2,1)S(1)}, bf16[512,128]{1,0:T(8,128)(2,1)S(1)}, u32[]{:S(2)}, u32[]{:S(2)}) collective-permute-start(bf16[512,128]{1,0:T(8,128)(2,1)S(1)} %pad_maximum_fusion.1), channel_id=1, source_target_pairs={{0,1},{1,0},{2,3},{3,2},{4,5},{5,4},{6,7},{7,6},{8,9},{9,8},{10,11... | collective-permute-start | bytes 393224 | tf_op jit(solution)/shard_map/ppermute | solution.py:41
  65.2 2.0 %collective-permute-start.18 = (bf16[2048,128]{1,0:T(8,128)(2,1)S(1)}, bf16[2048,128]{1,0:T(8,128)(2,1)S(1)}, u32[]{:S(2)}, u32[]{:S(2)}) collective-permute-start(bf16[2048,128]{1,0:T(8,128)(2,1)S(1)} %pad_maximum_fusion.packed_ref), channel_id=1, source_target_pairs={{0,2},{1,3},{2,0},{3,1},{4,6},{5,7},{6,4},{7,5},{8,10},{9,11},{10,... | collective-permute-start | bytes 1572872 | tf_op jit(solution)/shard_map/ppermute | solution.py:41

commit v9 on v8

--- a/solution.py
+++ b/solution.py
@@ -63,33 +63,36 @@
     return exchange(value, *partners)
 
 
+def members_of(group):
+    count = lax.axis_size("north")
+    found = {}
+    for e in range(lax.axis_size("east")):
+        for n in range(count):
+            here = {"east": e, "north": n}
+            place = 0
+            for i, (axis, bit) in enumerate(group):
+                place |= (1 if here[axis] & bit else 0) << i
+                here[axis] &= ~bit
+            found.setdefault((here["east"], here["north"]), {})[place] = e * count + n
+    return [[places[i] for i in range(len(places))] for places in found.values()]
+
+
+def all_to_all(value, group):
+    ways = 1 << len(group)
+    parts = value.reshape(ways, value.shape[0] // ways, LANES)
+    return lax.all_to_all(parts, ("east", "north"), 0, 0, axis_index_groups=members_of(group))
+
+
 def scatter_sums(total, groups):
     for group in groups:
-        ways = 1 << len(group)
-        part = total.shape[0] // ways
-        place = place_in(group)
-        sent = [
-            lax.dynamic_slice_in_dim(total, (place ^ change) * part, part, 0).astype(BF16)
-            for change in range(1, ways)
-        ]
-        total = lax.dynamic_slice_in_dim(total, place * part, part, 0)
-        for change in range(1, ways):
-            total = total + swap(sent[change - 1], group, change).astype(F32)
+        total = all_to_all(total.astype(BF16), group).astype(F32).sum(0)
     return total
 
 
 def gather_parts(mine, groups):
     for group in reversed(groups):
         ways = 1 << len(group)
-        place = place_in(group)
-        parts = [mine] + [swap(mine, group, change) for change in range(1, ways)]
-        joined = []
-        for row in range(ways):
-            piece = parts[0]
-            for change in range(1, ways):
-                piece = jnp.where((place ^ row) == change, parts[change], piece)
-            joined.append(piece)
-        mine = jnp.concatenate(joined, 0)
+        mine = all_to_all(jnp.concatenate([mine] * ways, 0), group).reshape(-1, LANES)
     return mine
 
 
@@ -137,34 +140,30 @@
                 back_ref[start : start + channels, q * LANES : q * LANES + channels] = w_ref[d * OFFSETS + j]
 
 
-def weights_kernel(
-    channels, classes,
-    w1_in, w2_in, head_in,
-    ahead1_ref, ahead2_ref, back2_ref, head_out,
-    w1_ref, w2_ref, head_ref, arrived,
-):
+def put_ahead(ahead_ref, w_ref, channels):
+    ahead_ref[...] = jnp.zeros_like(ahead_ref)
+    row = lax.broadcasted_iota(jnp.int32, (channels, channels), 0)
+    unit = (row == lax.broadcasted_iota(jnp.int32, (channels, channels), 1)).astype(BF16)
+    for d in range(3):
+        for j in range(OFFSETS):
+            value = w_ref[d * OFFSETS + j]
+            turned = lax.dot_general(unit, value, (((1,), (1,)), ((), ())), preferred_element_type=F32).astype(BF16)
+            for q in range(2):
+                start = ((d + q) * OFFSETS + j) * LANES
+                ahead_ref[start : start + channels, q * LANES : q * LANES + channels] = turned
+
+
+def weights_kernel(channels, classes, w1_in, head_in, ahead1_ref, head_out, w1_ref, head_ref, arrived):
     copies = [
         pltpu.make_async_copy(source, target, arrived.at[i])
-        for i, (source, target) in enumerate(((w1_in, w1_ref), (w2_in, w2_ref), (head_in, head_ref)))
+        for i, (source, target) in enumerate(((w1_in, w1_ref), (head_in, head_ref)))
     ]
     for copy in copies:
         copy.start()
-    for ref in (ahead1_ref, ahead2_ref, head_out):
-        ref[...] = jnp.zeros_like(ref)
     for copy in copies:
         copy.wait()
-    row = lax.broadcasted_iota(jnp.int32, (channels, channels), 0)
-    unit = (row == lax.broadcasted_iota(jnp.int32, (channels, channels), 1)).astype(BF16)
-    for w_ref, ahead_ref in ((w1_ref, ahead1_ref), (w2_ref, ahead2_ref)):
-        for d in range(3):
-            for j in range(OFFSETS):
-                value = w_ref[d * OFFSETS + j]
-                turned = lax.dot_general(unit, value, (((1,), (1,)), ((), ())), preferred_element_type=F32).astype(BF16)
-                for q in range(2):
-                    side = slice(q * LANES, q * LANES + channels)
-                    start = ((d + q) * OFFSETS + j) * LANES
-                    ahead_ref[start : start + channels, side] = turned
-    put_back(back2_ref, w2_ref, channels)
+    put_ahead(ahead1_ref, w1_ref, channels)
+    head_out[...] = jnp.zeros_like(head_out)
     row = lax.broadcasted_iota(jnp.int32, (LANES, classes), 0)
     spread = (row == lax.broadcasted_iota(jnp.int32, (LANES, classes), 1) + channels + 1).astype(BF16)
     head_out[:, 0:channels] = jnp.dot(spread, head_ref[...], preferred_element_type=F32).astype(BF16)
@@ -202,15 +201,20 @@
 
 
 def prepare_kernel(
-    channels, upward, edge, east_rounds, north_rounds,
-    flags_ref, active_ref, features_in, occupied_in, teacher_in,
+    channels, upward, edge,
+    active_in, features_in, occupied_in, teacher_in,
     center_ref, *edge_refs,
 ):
-    *edge_refs, features_ref, occupied_ref, teacher_ref, arrived = edge_refs
+    *edge_refs, active_ref, features_ref, occupied_ref, teacher_ref, arrived = edge_refs
     copies = [
         pltpu.make_async_copy(source, target, arrived.at[i])
         for i, (source, target) in enumerate(
-            ((occupied_in, occupied_ref), (teacher_in, teacher_ref), (features_in, features_ref))
+            (
+                (active_in, active_ref),
+                (occupied_in, occupied_ref),
+                (teacher_in, teacher_ref),
+                (features_in, features_ref),
+            )
         )
     ]
     for copy in copies:
@@ -237,16 +241,15 @@
                 inside = (along == b) & (up == c)
                 mask = jnp.where(inside, active_ref[e // (east // bricks[0]), c, b], mask)
         mask = (mask * occupied_ref[e]).astype(F32)
-        field = jnp.concatenate([mask] + [teacher_ref[c, e].astype(F32) for c in range(classes)], 0).astype(BF16)
+        goal = teacher_ref[:, e].astype(F32).reshape(classes * upward, north)
+        field = jnp.concatenate([mask, goal], 0).astype(BF16)
         everywhere = lax.dot_general(spread, field, (((1,), (1,)), ((), ())), preferred_element_type=F32)
         own = jnp.where(same, everywhere, 0.0).astype(BF16)
         tail = jnp.dot(own, gather, preferred_element_type=F32).astype(BF16)
         center_ref[e, :, 0:channels] = features_ref[e]
         center_ref[e, :, channels:LANES] = tail[:, channels:LANES]
-    east_starts = [(1 - flags_ref[r]) * (east - HALO) for r in range(east_rounds)]
-    north_starts = [
-        pl.multiple_of((1 - flags_ref[2 * east_rounds + r]) * (size - edge), edge) for r in range(north_rounds)
-    ]
+    east_starts = [(1 - side) * (east - HALO) for _, side, _ in rounds_of("east")]
+    north_starts = [pl.multiple_of((1 - side) * (size - edge), edge) for _, side, _ in rounds_of("north")]
     edge_refs = iter(edge_refs)
     for e in east_starts:
         next(edge_refs)[...] = center_ref[pl.ds(e, HALO)]
@@ -257,18 +260,16 @@
             next(edge_refs)[...] = center_ref[pl.ds(e, HALO), pl.ds(n, edge), :]
 
 
-def place_edges(flags_ref, center_ref, edge_refs, east_rounds, north_rounds, edge, x_ref):
+def place_edges(center_ref, edge_refs, edge, x_ref):
     east, size, _ = center_ref.shape
     x_ref[...] = jnp.zeros_like(x_ref)
     x_ref[HALO : HALO + east, edge : edge + size, :] = center_ref[...]
     edge_refs = iter(edge_refs)
-    easts = [(flags_ref[r], flags_ref[east_rounds + r]) for r in range(east_rounds)]
-    base = 2 * east_rounds
-    norths = [(flags_ref[base + r], flags_ref[base + north_rounds + r]) for r in range(north_rounds)]
     middle_east, middle_north = pl.ds(HALO, east), pl.ds(edge, size)
-    east_places = [(pl.ds((1 - side) * (east + HALO), HALO), inside) for side, inside in easts]
+    east_places = [(pl.ds((1 - side) * (east + HALO), HALO), inside) for _, side, inside in rounds_of("east")]
     north_places = [
-        (pl.ds(pl.multiple_of((1 - side) * (size + edge), edge), edge), inside) for side, inside in norths
+        (pl.ds(pl.multiple_of((1 - side) * (size + edge), edge), edge), inside)
+        for _, side, inside in rounds_of("north")
     ]
     spots = [(e, middle_north, inside) for e, inside in east_places]
     spots += [(middle_east, n, inside) for n, inside in north_places]
@@ -282,14 +283,15 @@
 
 
 def whole_kernel(
-    channels, classes, east, north, upward, east_rounds, north_rounds,
-    flags_ref, ahead1_ref, ahead2_ref, back2_ref, head_ref, center_ref, *refs,
+    channels, classes, east, north, upward, edges,
+    ahead1_ref, w2_in, head_ref, center_ref, *refs,
 ):
-    edges = east_rounds + north_rounds + east_rounds * north_rounds
     (
         grad_ref, kept_ref, sent_ref,
-        x_ref, s0_ref, s1_ref, sg_ref, mask_ref, slope_ref, turned_ref,
+        x_ref, s0_ref, s1_ref, sg_ref, mask_ref, slope_ref, turned_ref, ahead2_ref, back2_ref, w2_ref, arrived,
     ) = refs[edges:]
+    copy = pltpu.make_async_copy(w2_in, w2_ref, arrived)
+    copy.start()
     rows = (north + 2 * HALO) * upward
     low, size = HALO * upward, north * upward
     planes = east + 2 * HALO
@@ -297,7 +299,7 @@
     rows1, rows2, rows3 = rows - 2 * upward, rows - 4 * upward, rows - 6 * upward
     low1, low2, low3 = low - upward, low - 2 * upward, low - 3 * upward
 
-    place_edges(flags_ref, center_ref, refs[:edges], east_rounds, north_rounds, low, x_ref)
+    place_edges(center_ref, refs[:edges], low, x_ref)
     border = jnp.zeros((upward, LANES), F32)
 
     for plane in range(planes):
@@ -307,6 +309,9 @@
         a0 = jnp.where((mask > 0) & (lane < channels), x, 0.0)
         put_stack(jnp.concatenate([border, a0, border], 0), upward, s0_ref, plane % 2, plane // 2)
 
+    copy.wait()
+    put_ahead(ahead2_ref, w2_ref, channels)
+    put_back(back2_ref, w2_ref, channels)
     for first, stop in grouped((planes - 2) // 2, 2):
         for i, parity, value in convolve(s0_ref, ahead1_ref, first, stop, rows):
             plane = 2 * i + parity
@@ -338,7 +343,7 @@
             put_stack(g_p2, upward, sg_ref, parity, i)
             put_turned(turned_ref, g_p2[low2 : low2 + size], plane - 2, east, channels)
 
-    upper = flags_ref[2 * (east_rounds + north_rounds)] == 1
+    upper = high_bit("east", 1) == 1
     for t, tile in enumerate(kernel_sum(turned_ref, s1_ref, 3, east, rows2, low2, size, channels)):
         kept_ref[t * channels : (t + 1) * channels, :] = tile.astype(BF16)
 
@@ -447,31 +452,33 @@
     upper = high_bit(*east_bits[0])
     easts, norths = rounds_of("east"), rounds_of("north")
     counts = (len(easts), len(norths))
-    flags = [side for _, side, _ in easts] + [inside for _, _, inside in easts]
-    flags += [side for _, side, _ in norths] + [inside for _, _, inside in norths] + [upper]
-    flags = jnp.stack(flags).astype(jnp.int32)
 
     shapes = [(HALO, size, LANES)] * counts[0] + [(east, edge, LANES)] * counts[1]
     shapes += [(HALO, edge, LANES)] * (counts[0] * counts[1])
     center, *edges = pl.pallas_call(
-        functools.partial(prepare_kernel, channels, upward, edge, *counts),
+        functools.partial(prepare_kernel, channels, upward, edge),
         out_shape=[jax.ShapeDtypeStruct(shape, BF16) for shape in [(east, size, LANES)] + shapes],
-        in_specs=[smem] * 2 + [far] * 3,
+        in_specs=[far] * 4,
         out_specs=[vmem] * (1 + len(shapes)),
         scratch_shapes=[
+            pltpu.SMEM((brick_active.shape[0], brick_active.shape[2], brick_active.shape[1]), jnp.int32),
             pltpu.VMEM((east, size, channels), BF16),
             pltpu.VMEM((east, upward, north), jnp.int32),
             pltpu.VMEM((classes, east, upward, north), BF16),
-            pltpu.SemaphoreType.DMA((3,)),
+            pltpu.SemaphoreType.DMA((4,)),
         ],
         compiler_params=pltpu.CompilerParams(vmem_limit_bytes=6 * 1024 * 1024),
         name="prepare",
     )(
-        flags,
-        brick_active.transpose(0, 2, 1),
-        pltpu.with_memory_space_constraint(features.transpose(1, 2, 3, 0).reshape(east, size, channels), pltpu.HBM),
-        pltpu.with_memory_space_constraint(voxel_occupancy.transpose(0, 2, 1), pltpu.HBM),
-        pltpu.with_memory_space_constraint(teacher.transpose(0, 1, 3, 2), pltpu.HBM),
+        *[
+            pltpu.with_memory_space_constraint(value, pltpu.HBM)
+            for value in (
+                brick_active.transpose(0, 2, 1),
+                features.transpose(1, 2, 3, 0).reshape(east, size, channels),
+                voxel_occupancy.transpose(0, 2, 1),
+                teacher.transpose(0, 1, 3, 2),
+            )
+        ]
     )
     stay = [list(range(lax.axis_size(axis))) for axis in ("east", "north")]
     routes = [(partners, stay[1]) for partners, _, _ in easts] + [(stay[0], partners) for partners, _, _ in norths]
@@ -480,29 +487,30 @@
 
     unit = devices // 2 * 16
     packed = -(-21 * channels // unit) * unit
-    shapes = [(4 * WIDE, 2 * LANES)] * 3 + [(LANES, LANES)]
-    ahead1, ahead2, back2, head_wide = pl.pallas_call(
+    first_far, second_far, head_far = [
+        pltpu.with_memory_space_constraint(value, pltpu.HBM) for value in (first_weights, second_weights, head)
+    ]
+    ahead1, head_wide = pl.pallas_call(
         functools.partial(weights_kernel, channels, classes),
-        out_shape=[jax.ShapeDtypeStruct(shape, BF16) for shape in shapes],
-        in_specs=[far] * 3,
-        out_specs=[vmem] * 4,
+        out_shape=[jax.ShapeDtypeStruct(shape, BF16) for shape in ((4 * WIDE, 2 * LANES), (LANES, LANES))],
+        in_specs=[far] * 2,
+        out_specs=[vmem] * 2,
         scratch_shapes=[
             pltpu.VMEM(first_weights.shape, BF16),
-            pltpu.VMEM(second_weights.shape, BF16),
             pltpu.VMEM(head.shape, BF16),
-            pltpu.SemaphoreType.DMA((3,)),
+            pltpu.SemaphoreType.DMA((2,)),
         ],
-        compiler_params=pltpu.CompilerParams(vmem_limit_bytes=12 * 1024 * 1024),
+        compiler_params=pltpu.CompilerParams(vmem_limit_bytes=6 * 1024 * 1024),
         name="weights",
-    )(*[pltpu.with_memory_space_constraint(value, pltpu.HBM) for value in (first_weights, second_weights, head)])
+    )(first_far, head_far)
     grad, kept, sent = pl.pallas_call(
-        functools.partial(whole_kernel, channels, classes, east, north, upward, *counts),
+        functools.partial(whole_kernel, channels, classes, east, north, upward, len(edges)),
         out_shape=(
             jax.ShapeDtypeStruct((east + 2, rows - 6 * upward, LANES), BF16),
             jax.ShapeDtypeStruct((packed, LANES), BF16),
             jax.ShapeDtypeStruct((packed, LANES), BF16),
         ),
-        in_specs=[smem] + [vmem] * (5 + len(edges)),
+        in_specs=[vmem, far] + [vmem] * (2 + len(edges)),
         out_specs=(vmem, vmem, vmem),
         scratch_shapes=[
             pltpu.VMEM((planes, rows, LANES), BF16),
@@ -512,10 +520,14 @@
             pltpu.VMEM((planes, rows, LANES), F32),
             pltpu.VMEM((planes - 2, rows, LANES), F32),
             pltpu.VMEM((3 * channels, east * size), BF16),
+            pltpu.VMEM((4 * WIDE, 2 * LANES), BF16),
+            pltpu.VMEM((4 * WIDE, 2 * LANES), BF16),
+            pltpu.VMEM(second_weights.shape, BF16),
+            pltpu.SemaphoreType.DMA(()),
         ],
-        compiler_params=pltpu.CompilerParams(vmem_limit_bytes=26 * 1024 * 1024),
+        compiler_params=pltpu.CompilerParams(vmem_limit_bytes=32 * 1024 * 1024),
         name="fields",
-    )(flags, ahead1, ahead2, back2, head_wide, center, *edges)
+    )(ahead1, second_far, head_wide, center, *edges)
 
     features_out = []
 
@@ -537,7 +549,7 @@
             ],
             compiler_params=pltpu.CompilerParams(vmem_limit_bytes=10 * 1024 * 1024),
             name="features",
-        )(center, grad, pltpu.with_memory_space_constraint(first_weights, pltpu.HBM), kept)
+        )(center, grad, first_far, kept)
         features_out.append(out)
         return kept
 

time: 68.8 us -> 72.2 us (1.049)
  blocking collectives: 0 us -> 29 us
  starting transfers between devices: 23.4 us -> 10.7 us
  waiting for transfers between devices: 15.1 us -> 5.87 us
  Pallas kernels: 27.9 us -> 25.4 us
  local copies, waits for them, and re-layouts: 0.77 us -> 0 us
    all_to_all x0 -> x3, blocking collectives: none -> 29 us  [all_to_all(): lax.all_to_all(parts, ('east', 'north'), 0, 0, axis_index_groups=members_...]
    ppermute x19 -> x10, starting transfers between devices: 23.4 us -> 10.7 us  [exchange(): return lax.ppermute(value, ('east', 'north'), pairs)]
    ppermute x19 -> x10, waiting for transfers between devices: 15.1 us -> 5.87 us  [exchange(): return lax.ppermute(value, ('east', 'north'), pairs)]
    pallas_call x1, Pallas kernels: 16.3 us -> 15.3 us  [per_device(): pl.pallas_call(functools.partial(whole_kernel, channels, classes, east, n...]
    pallas_call x1, Pallas kernels: 2.67 us -> 1.81 us  [per_device(): pl.pallas_call(functools.partial(weights_kernel, channels, classes), out_...]
  transfers between devices with their start and end apart: 19 -> 10, of which waited for: 10 -> 4; matrix products, arithmetic and copies ran while one was open for 0% -> 0% of each run, Pallas kernels for 11% -> 9%
where the time goes in v9:
time: 72.2 us; the launch traced here: 71.9 us
  blocking collectives  29 us (40%)
  Pallas kernels  25.4 us (35%)
  starting transfers between devices  10.7 us (15%)
  waiting for transfers between devices  5.87 us (8%)
  between operations  0.88 us (1%)
    all_to_all x3, blocking collectives, all_to_all(): lax.all_to_all(parts, ('east', 'north'), 0, 0, axis_index_groups=members_...  29 us
    pallas_call x1, Pallas kernels, per_device(): pl.pallas_call(functools.partial(whole_kernel, channels, classes, east, n...  15.3 us
    ppermute x10, starting transfers between devices, exchange(): return lax.ppermute(value, ('east', 'north'), pairs)  10.7 us
    ppermute x10, waiting for transfers between devices, exchange(): return lax.ppermute(value, ('east', 'north'), pairs)  5.87 us
    pallas_call x1, Pallas kernels, beside(): pl.pallas_call(functools.partial(last_kernel, channels, east, north, upwa...  3.31 us
    pallas_call x2, Pallas kernels, unpack(): pl.pallas_call(functools.partial(unpack_kernel, channels, scale, bool(ali...  2.43 us
    pallas_call x1, Pallas kernels, per_device(): pl.pallas_call(functools.partial(prepare_kernel, channels, upward, edge),...  2.37 us
    pallas_call x1, Pallas kernels, per_device(): pl.pallas_call(functools.partial(weights_kernel, channels, classes), out_...  1.81 us
  transfers between devices with their start and end apart: 10, of which 4 were waited for; matrix products, arithmetic and copies ran while one was open for 0% of the time, Pallas kernels for 9%

profile of v9, /device:TPU:0, one launch (start us, length us, event | category | flops | bytes accessed | tf_op | source)
XLA Modules:
  0.0 71.9 jit_solution(12729188214202050851)
XLA Ops:
  0.6 2.4 %prepare.1 = (bf16[8,128,128]{2,1,0:T(8,128)(2,1)S(1)}, bf16[4,128,128]{2,1,0:T(8,128)(2,1)S(1)}, bf16[4,128,128]{2,1,0:T(8,128)(2,1)S(1)}, bf16[8,32,128]{2,1,0...) custom-call(s32[1,1,2]{2,1,0:T(1,128)} %bitcast.26, bf16[8,128,96]{2,1,0:T(8,128)(2,1)} %bitcast.23, ...), custom_call_target="tpu_custom_call" | custom-call | tf_op jit(solution)/shard_map/prepare/pallas_call | solution.py:458
  3.0 0.5 collective-permute-start
  3.5 2.6 %collective-permute-start.1 = (bf16[4,128,128]{2,1,0:T(8,128)(2,1)S(1)}, bf16[4,128,128]{2,1,0:T(8,128)(2,1)S(1)}, u32[]{:S(2)}, u32[]{:S(2)}) collective-permute-start(bf16[4,128,128]{2,1,0:T(8,128)(2,1)S(1)} %get-tuple-element.28), channel_id=1, source_target_pairs={{0,1},{1,0},{2,4},{3,5},{4,2},{5,3},{6,8},{7,9},{8,6},{9,7},{10,12... | collective-permute-start | bytes 393224 | tf_op jit(solution)/shard_map/ppermute | solution.py:41
  6.1 0.1 collective-permute-start.2
  6.2 1.4 %collective-permute-start.3 = (bf16[4,32,128]{2,1,0:T(8,128)(2,1)S(1)}, bf16[4,32,128]{2,1,0:T(8,128)(2,1)S(1)}, u32[]{:S(2)}, u32[]{:S(2)}) collective-permute-start(bf16[4,32,128]{2,1,0:T(8,128)(2,1)S(1)} %get-tuple-element.30), channel_id=1, source_target_pairs={{0,3},{1,2},{2,1},{3,0},{4,7},{5,6},{6,5},{7,4},{8,11},{9,10},{10,... | collective-permute-start | bytes 98312 | tf_op jit(solution)/shard_map/ppermute | solution.py:41
  7.6 1.5 %collective-permute-start.4 = (bf16[4,32,128]{2,1,0:T(8,128)(2,1)S(1)}, bf16[4,32,128]{2,1,0:T(8,128)(2,1)S(1)}, u32[]{:S(2)}, u32[]{:S(2)}) collective-permute-start(bf16[4,32,128]{2,1,0:T(8,128)(2,1)S(1)} %get-tuple-element.31), channel_id=1, source_target_pairs={{0,1},{1,0},{2,5},{3,4},{4,3},{5,2},{6,9},{7,8},{8,7},{9,6},{10,13... | collective-permute-start | bytes 98312 | tf_op jit(solution)/shard_map/ppermute | solution.py:41
  9.1 1.8 %weights.1 = (bf16[4608,256]{1,0:T(8,128)(2,1)S(1)}, bf16[128,128]{1,0:T(8,128)(2,1)S(1)}) custom-call(bf16[27,96,96]{2,1,0:T(8,128)(2,1)} %w1_in.3, bf16[13,96]{1,0:T(8,128)(2,1)} %head_in.1), custom_call_target="tpu_custom_call" | custom-call | tf_op jit(solution)/shard_map/weights/pallas_call | solution.py:493
  10.9 0.6 collective-permute-done.4.refs_4_
  11.5 15.3 %fields.1 = (bf16[10,144,128]{2,1,0:T(8,128)(2,1)S(1)}, bf16[2048,128]{1,0:T(8,128)(2,1)S(1)}, bf16[2048,128]{1,0:T(8,128)(2,1)S(1)}) custom-call(bf16[4608,256]{1,0:T(8,128)(2,1)S(1)} %get-tuple-element.25.ahead1_ref, bf16[27,96,96]{2,1,0:T(8,128)(2,1)} %w2_in.1, bf16[128,128]{1,0:T(8,128)(2,1)S(1)} %get-tuple-element.26.head_ref, ...), custom_call_target="tpu_custom_call" | custom-call | tf_op jit(solution)/shard_map/fields/pallas_call | solution.py:506
  26.9 1.0 %collective-permute-start.5 = (bf16[2048,128]{1,0:T(8,128)(2,1)S(1)}, bf16[2048,128]{1,0:T(8,128)(2,1)S(1)}, u32[]{:S(2)}, u32[]{:S(2)}) collective-permute-start(bf16[2048,128]{1,0:T(8,128)(2,1)S(1)} %get-tuple-element.34), channel_id=1, source_target_pairs={{0,2},{1,3},{2,0},{3,1},{4,6},{5,7},{6,4},{7,5},{8,10},{9,11},{10,... | collective-permute-start | bytes 1572872 | tf_op jit(solution)/shard_map/ppermute | solution.py:41
  27.9 1.5 %collective-permute-done.5.came_ref = bf16[2048,128]{1,0:T(8,128)(2,1)S(1)} collective-permute-done((bf16[2048,128]{1,0:T(8,128)(2,1)S(1)}, bf16[2048,128]{1,0:T(8,128)(2,1)S(1)}, u32[]{:S(2)}, u32[]{:S(2)}) %collective-permute-start.5) | collective-permute-done | bytes 524320 | tf_op jit(solution)/shard_map/ppermute | solution.py:41
  29.4 0.1 parts.1
  29.6 1.8 %collective-permute-start.6 = (bf16[512,128]{1,0:T(8,128)(2,1)S(1)}, bf16[512,128]{1,0:T(8,128)(2,1)S(1)}, u32[]{:S(2)}, u32[]{:S(2)}) collective-permute-start(bf16[512,128]{1,0:T(8,128)(2,1)S(1)} %get-tuple-element.38), channel_id=1, source_target_pairs={{0,1},{1,0},{2,3},{3,2},{4,5},{5,4},{6,7},{7,6},{8,9},{9,8},{10,11... | collective-permute-start | bytes 393224 | tf_op jit(solution)/shard_map/ppermute | solution.py:41
  31.4 1.4 %collective-permute-start.7 = (bf16[512,128]{1,0:T(8,128)(2,1)S(1)}, bf16[512,128]{1,0:T(8,128)(2,1)S(1)}, u32[]{:S(2)}, u32[]{:S(2)}) collective-permute-start(bf16[512,128]{1,0:T(8,128)(2,1)S(1)} %get-tuple-element.39), channel_id=1, source_target_pairs={{0,4},{1,5},{2,6},{3,7},{4,0},{5,1},{6,2},{7,3},{8,12},{9,13},{10,... | collective-permute-start | bytes 393224 | tf_op jit(solution)/shard_map/ppermute | solution.py:41
  32.8 0.3 collective-permute-start.8
  33.1 3.3 %features.1 = (bf16[8,128,96]{2,1,0:T(8,128)(2,1)}, f32[512,128]{1,0:T(8,128)S(1)}) custom-call(bf16[8,128,128]{2,1,0:T(8,128)(2,1)S(1)} %get-tuple-element.24.center_ref, bf16[10,144,128]{2,1,0:T(8,128)(2,1)S(1)} %get-tuple-element.32.grad_ref, bf16[27,96,96]{2,1,0:T(8,128)(2,1)} %w1_in.3, ...), custom_call_target="tpu_custom_call", output_to_operand_aliasing={{1}: (3, {})} | custom-call | tf_op jit(solution)/shard_map/features/pallas_call | solution.py:535
  36.5 3.0 %collective-permute-done.7 = bf16[512,128]{1,0:T(8,128)(2,1)S(1)} collective-permute-done((bf16[512,128]{1,0:T(8,128)(2,1)S(1)}, bf16[512,128]{1,0:T(8,128)(2,1)S(1)}, u32[]{:S(2)}, u32[]{:S(2)}) %collective-permute-start.7) | collective-permute-done | bytes 131104 | tf_op jit(solution)/shard_map/ppermute | solution.py:41
  39.5 0.1 add_convert_fusion
  39.5 11.0 %all_to_all.15 = bf16[4,128,128]{2,1,0:T(8,128)(2,1)S(1)} all-to-all(bf16[4,128,128]{2,1,0:T(8,128)(2,1)S(1)} %bitcast.22), channel_id=1, replica_groups={{0,8,16,24},{1,9,17,25},{2,10,18,26},{3,11,19,27},{4,12,20,28},{5,13,21..., dimensions={0} | all-to-all | bytes 262144 | tf_op jit(solution)/shard_map/all_to_all | solution.py:83
  50.6 8.4 %all_to_all.16 = bf16[4,128,128]{2,1,0:T(8,128)(2,1)S(1)} all-to-all(bf16[4,128,128]{2,1,0:T(8,128)(2,1)S(1)} %bitcast.21), channel_id=1, replica_groups={{0,8,16,24},{1,9,17,25},{2,10,18,26},{3,11,19,27},{4,12,20,28},{5,13,21..., dimensions={0} | all-to-all | bytes 262144 | tf_op jit(solution)/shard_map/all_to_all | solution.py:83
  59.1 9.5 %all_to_all.17 = bf16[4,512,128]{2,1,0:T(8,128)(2,1)S(1)} all-to-all(bf16[4,512,128]{2,1,0:T(8,128)(2,1)S(1)} %bitcast.19), channel_id=1, replica_groups={{0,1,4,5},{2,3,6,7},{8,9,12,13},{10,11,14,15},{16,17,20,21},{18,19,22,2..., dimensions={0} | all-to-all | bytes 1048576 | tf_op jit(solution)/shard_map/all_to_all | solution.py:83
  68.6 1.2 %unpack.2 = (f32[27,96,96]{2,1,0:T(8,128)}, f32[27,96,96]{2,1,0:T(8,128)}) custom-call(s32[1]{0:T(128)} %bitcast.14.first_ref_flag, bf16[2048,128]{1,0:T(8,128)(2,1)S(1)} %bitcast.18), custom_call_target="tpu_custom_call" | custom-call | tf_op jit(solution)/shard_map/unpack/pallas_call | solution.py:575
  69.8 0.7 collective-permute-done.9.packed_ref
  70.5 1.2 %unpack.3 = (f32[27,96,96]{2,1,0:T(8,128)}, f32[27,96,96]{2,1,0:T(8,128)}) custom-call(s32[1]{0:T(128)} %bitcast.8.first_ref_flag, bf16[2048,128]{1,0:T(8,128)(2,1)S(1)} %collective-permute-done.9.packed_ref, f32[27,96,96]{2,1,0:T(8,128)} %get-tuple-element.41.refs_0_, ...), custom_call_target="tpu_custom_call", output_to_operand_aliasing={{0}: (2, {}), {1}: (3, {})} | custom-call | tf_op jit(solution)/shard_map/unpack/pallas_call | solution.py:575
  (10 shorter events, 0.1 us)
Async XLA Ops:
  3.0 8.5 %collective-permute-start = (bf16[4,128,128]{2,1,0:T(8,128)(2,1)S(1)}, bf16[4,128,128]{2,1,0:T(8,128)(2,1)S(1)}, u32[]{:S(2)}, u32[]{:S(2)}) collective-permute-start(bf16[4,128,128]{2,1,0:T(8,128)(2,1)S(1)} %get-tuple-element.27), channel_id=1, source_target_pairs={{0,2},{1,3},{2,0},{3,1},{4,6},{5,7},{6,4},{7,5},{8,10},{9,11},{10,... | collective-permute-start | bytes 393224 | tf_op jit(solution)/shard_map/ppermute | solution.py:41
  3.5 8.0 %collective-permute-start.1 = (bf16[4,128,128]{2,1,0:T(8,128)(2,1)S(1)}, bf16[4,128,128]{2,1,0:T(8,128)(2,1)S(1)}, u32[]{:S(2)}, u32[]{:S(2)}) collective-permute-start(bf16[4,128,128]{2,1,0:T(8,128)(2,1)S(1)} %get-tuple-element.28), channel_id=1, source_target_pairs={{0,1},{1,0},{2,4},{3,5},{4,2},{5,3},{6,8},{7,9},{8,6},{9,7},{10,12... | collective-permute-start | bytes 393224 | tf_op jit(solution)/shard_map/ppermute | solution.py:41
  6.1 5.4 %collective-permute-start.2 = (bf16[8,32,128]{2,1,0:T(8,128)(2,1)S(1)}, bf16[8,32,128]{2,1,0:T(8,128)(2,1)S(1)}, u32[]{:S(2)}, u32[]{:S(2)}) collective-permute-start(bf16[8,32,128]{2,1,0:T(8,128)(2,1)S(1)} %get-tuple-element.29), channel_id=1, source_target_pairs={{0,1},{1,0},{2,3},{3,2},{4,5},{5,4},{6,7},{7,6},{8,9},{9,8},{10,11... | collective-permute-start | bytes 196616 | tf_op jit(solution)/shard_map/ppermute | solution.py:41
  6.2 4.7 %collective-permute-start.3 = (bf16[4,32,128]{2,1,0:T(8,128)(2,1)S(1)}, bf16[4,32,128]{2,1,0:T(8,128)(2,1)S(1)}, u32[]{:S(2)}, u32[]{:S(2)}) collective-permute-start(bf16[4,32,128]{2,1,0:T(8,128)(2,1)S(1)} %get-tuple-element.30), channel_id=1, source_target_pairs={{0,3},{1,2},{2,1},{3,0},{4,7},{5,6},{6,5},{7,4},{8,11},{9,10},{10,... | collective-permute-start | bytes 98312 | tf_op jit(solution)/shard_map/ppermute | solution.py:41
  7.6 3.9 %collective-permute-start.4 = (bf16[4,32,128]{2,1,0:T(8,128)(2,1)S(1)}, bf16[4,32,128]{2,1,0:T(8,128)(2,1)S(1)}, u32[]{:S(2)}, u32[]{:S(2)}) collective-permute-start(bf16[4,32,128]{2,1,0:T(8,128)(2,1)S(1)} %get-tuple-element.31), channel_id=1, source_target_pairs={{0,1},{1,0},{2,5},{3,4},{4,3},{5,2},{6,9},{7,8},{8,7},{9,6},{10,13... | collective-permute-start | bytes 98312 | tf_op jit(solution)/shard_map/ppermute | solution.py:41
  26.9 2.6 %collective-permute-start.5 = (bf16[2048,128]{1,0:T(8,128)(2,1)S(1)}, bf16[2048,128]{1,0:T(8,128)(2,1)S(1)}, u32[]{:S(2)}, u32[]{:S(2)}) collective-permute-start(bf16[2048,128]{1,0:T(8,128)(2,1)S(1)} %get-tuple-element.34), channel_id=1, source_target_pairs={{0,2},{1,3},{2,0},{3,1},{4,6},{5,7},{6,4},{7,5},{8,10},{9,11},{10,... | collective-permute-start | bytes 1572872 | tf_op jit(solution)/shard_map/ppermute | solution.py:41
  29.6 6.9 %collective-permute-start.6 = (bf16[512,128]{1,0:T(8,128)(2,1)S(1)}, bf16[512,128]{1,0:T(8,128)(2,1)S(1)}, u32[]{:S(2)}, u32[]{:S(2)}) collective-permute-start(bf16[512,128]{1,0:T(8,128)(2,1)S(1)} %get-tuple-element.38), channel_id=1, source_target_pairs={{0,1},{1,0},{2,3},{3,2},{4,5},{5,4},{6,7},{7,6},{8,9},{9,8},{10,11... | collective-permute-start | bytes 393224 | tf_op jit(solution)/shard_map/ppermute | solution.py:41
  31.4 8.1 %collective-permute-start.7 = (bf16[512,128]{1,0:T(8,128)(2,1)S(1)}, bf16[512,128]{1,0:T(8,128)(2,1)S(1)}, u32[]{:S(2)}, u32[]{:S(2)}) collective-permute-start(bf16[512,128]{1,0:T(8,128)(2,1)S(1)} %get-tuple-element.39), channel_id=1, source_target_pairs={{0,4},{1,5},{2,6},{3,7},{4,0},{5,1},{6,2},{7,3},{8,12},{9,13},{10,... | collective-permute-start | bytes 393224 | tf_op jit(solution)/shard_map/ppermute | solution.py:41
  32.8 6.7 %collective-permute-start.8 = (bf16[512,128]{1,0:T(8,128)(2,1)S(1)}, bf16[512,128]{1,0:T(8,128)(2,1)S(1)}, u32[]{:S(2)}, u32[]{:S(2)}) collective-permute-start(bf16[512,128]{1,0:T(8,128)(2,1)S(1)} %get-tuple-element.40), channel_id=1, source_target_pairs={{0,5},{1,4},{2,7},{3,6},{4,1},{5,0},{6,3},{7,2},{8,13},{9,12},{10,... | collective-permute-start | bytes 393224 | tf_op jit(solution)/shard_map/ppermute | solution.py:41
  68.6 1.9 %collective-permute-start.9 = (bf16[2048,128]{1,0:T(8,128)(2,1)S(1)}, bf16[2048,128]{1,0:T(8,128)(2,1)S(1)}, u32[]{:S(2)}, u32[]{:S(2)}) collective-permute-start(bf16[2048,128]{1,0:T(8,128)(2,1)S(1)} %bitcast.17), channel_id=1, source_target_pairs={{0,2},{1,3},{2,0},{3,1},{4,6},{5,7},{6,4},{7,5},{8,10},{9,11},{10,... | collective-permute-start | bytes 1572872 | tf_op jit(solution)/shard_map/ppermute | solution.py:41

commit v10 on v9

--- a/solution.py
+++ b/solution.py
@@ -63,36 +63,33 @@
     return exchange(value, *partners)
 
 
-def members_of(group):
-    count = lax.axis_size("north")
-    found = {}
-    for e in range(lax.axis_size("east")):
-        for n in range(count):
-            here = {"east": e, "north": n}
-            place = 0
-            for i, (axis, bit) in enumerate(group):
-                place |= (1 if here[axis] & bit else 0) << i
-                here[axis] &= ~bit
-            found.setdefault((here["east"], here["north"]), {})[place] = e * count + n
-    return [[places[i] for i in range(len(places))] for places in found.values()]
-
-
-def all_to_all(value, group):
-    ways = 1 << len(group)
-    parts = value.reshape(ways, value.shape[0] // ways, LANES)
-    return lax.all_to_all(parts, ("east", "north"), 0, 0, axis_index_groups=members_of(group))
-
-
 def scatter_sums(total, groups):
     for group in groups:
-        total = all_to_all(total.astype(BF16), group).astype(F32).sum(0)
+        ways = 1 << len(group)
+        part = total.shape[0] // ways
+        place = place_in(group)
+        sent = [
+            lax.dynamic_slice_in_dim(total, (place ^ change) * part, part, 0).astype(BF16)
+            for change in range(1, ways)
+        ]
+        total = lax.dynamic_slice_in_dim(total, place * part, part, 0)
+        for change in range(1, ways):
+            total = total + swap(sent[change - 1], group, change).astype(F32)
     return total
 
 
 def gather_parts(mine, groups):
     for group in reversed(groups):
         ways = 1 << len(group)
-        mine = all_to_all(jnp.concatenate([mine] * ways, 0), group).reshape(-1, LANES)
+        place = place_in(group)
+        parts = [mine] + [swap(mine, group, change) for change in range(1, ways)]
+        joined = []
+        for row in range(ways):
+            piece = parts[0]
+            for change in range(1, ways):
+                piece = jnp.where((place ^ row) == change, parts[change], piece)
+            joined.append(piece)
+        mine = jnp.concatenate(joined, 0)
     return mine
 
 
@@ -100,7 +97,8 @@
     return lax.broadcasted_iota(jnp.int32, shape, len(shape) - 1)
 
 
-def put_stack(value, upward, stack_ref, parity, index):
+def put_stack(value, upward, stack, parity, index):
+    even_ref, odd_ref = stack
     total = value.shape[0]
     rows = total - 2 * upward
     cubes = value.reshape(total // upward, upward, LANES)
@@ -108,11 +106,27 @@
     below = jnp.where(level == 0, 0.0, pltpu.roll(cubes, 1, 1)).reshape(total, LANES)
     above = jnp.where(level == upward - 1, 0.0, pltpu.roll(cubes, upward - 1, 1)).reshape(total, LANES)
     for up, moved in enumerate((below, value, above)):
-        even = moved.astype(BF16)
-        shifts = (even[0:rows], moved[upward : upward + rows].astype(BF16), even[2 * upward :])
-        for north, shifted in enumerate(shifts):
-            lane = (north * 3 + up) * LANES
-            stack_ref[parity, pl.ds(index * rows, rows), lane : lane + LANES] = shifted
+        lanes = slice(up * LANES, (up + 1) * LANES)
+        even_ref[parity, index * total : (index + 1) * total, lanes] = moved.astype(BF16)
+        odd_ref[parity, index * rows : (index + 1) * rows, lanes] = moved[upward : upward + rows].astype(BF16)
+
+
+def shifts_of(stack, plane, rows, upward, start, size):
+    even_ref, odd_ref = stack
+    even = (plane // 2) * (rows + 2 * upward) + start
+    odd = (plane // 2) * rows + start
+    return jnp.concatenate(
+        [
+            even_ref[plane % 2, even : even + size, :],
+            odd_ref[plane % 2, odd : odd + size, :],
+            even_ref[plane % 2, even + 2 * upward : even + 2 * upward + size, :],
+        ],
+        1,
+    )
+
+
+def stack_shapes(planes, rows, upward):
+    return [pltpu.VMEM((2, planes // 2 * (rows + extra), 3 * LANES), BF16) for extra in (2 * upward, 0)]
 
 
 def grouped(pairs, size):
@@ -121,9 +135,12 @@
     return list(zip(edges, edges[1:]))
 
 
-def convolve(stack_ref, weight_ref, first, stop, rows):
-    fields = [stack_ref[p % 2, (first + p // 2) * rows : (stop + p // 2) * rows, :] for p in range(4)]
-    both = jnp.dot(jnp.concatenate(fields, 1), weight_ref[...], preferred_element_type=F32)
+def convolve(stack, weight_ref, first, stop, rows, upward):
+    fields = [
+        jnp.concatenate([shifts_of(stack, 2 * pair + p, rows, upward, 0, rows) for p in range(4)], 1)
+        for pair in range(first, stop)
+    ]
+    both = jnp.dot(jnp.concatenate(fields, 0), weight_ref[...], preferred_element_type=F32)
     return [
         (pair, parity, both[(pair - first) * rows : (pair - first + 1) * rows, parity * LANES : (parity + 1) * LANES])
         for pair in range(first, stop)
@@ -131,26 +148,41 @@
     ]
 
 
+def unit_of(channels):
+    row = lax.broadcasted_iota(jnp.int32, (channels, LANES), 0)
+    return (row == lax.broadcasted_iota(jnp.int32, (channels, LANES), 1)).astype(BF16)
+
+
 def put_back(back_ref, w_ref, channels):
-    back_ref[...] = jnp.zeros_like(back_ref)
+    unit = unit_of(channels)
+    border = jnp.zeros((LANES - channels, channels), BF16)
     for d in range(3):
         for j in range(OFFSETS):
+            wide = jnp.concatenate([w_ref[d * OFFSETS + j], border], 0)
+            block = jnp.dot(wide, unit, preferred_element_type=F32).astype(BF16)
             for q in range(2):
-                start = ((2 - d + q) * OFFSETS + OFFSETS - 1 - j) * LANES
-                back_ref[start : start + channels, q * LANES : q * LANES + channels] = w_ref[d * OFFSETS + j]
+                row = ((2 - d + q) * OFFSETS + OFFSETS - 1 - j) * LANES
+                back_ref[row : row + LANES, q * LANES : (q + 1) * LANES] = block
+    put_zeros(back_ref)
+
+
+def put_zeros(target_ref):
+    run = OFFSETS * LANES
+    target_ref[0:run, LANES : 2 * LANES] = jnp.zeros((run, LANES), BF16)
+    target_ref[3 * run : 4 * run, 0:LANES] = jnp.zeros((run, LANES), BF16)
 
 
 def put_ahead(ahead_ref, w_ref, channels):
-    ahead_ref[...] = jnp.zeros_like(ahead_ref)
-    row = lax.broadcasted_iota(jnp.int32, (channels, channels), 0)
-    unit = (row == lax.broadcasted_iota(jnp.int32, (channels, channels), 1)).astype(BF16)
+    unit = unit_of(channels)
+    border = jnp.zeros((LANES - channels, channels), BF16)
     for d in range(3):
         for j in range(OFFSETS):
-            value = w_ref[d * OFFSETS + j]
-            turned = lax.dot_general(unit, value, (((1,), (1,)), ((), ())), preferred_element_type=F32).astype(BF16)
+            wide = jnp.concatenate([w_ref[d * OFFSETS + j], border], 0)
+            turned = lax.dot_general(unit, wide, (((0,), (1,)), ((), ())), preferred_element_type=F32).astype(BF16)
             for q in range(2):
-                start = ((d + q) * OFFSETS + j) * LANES
-                ahead_ref[start : start + channels, q * LANES : q * LANES + channels] = turned
+                row = ((d + q) * OFFSETS + j) * LANES
+                ahead_ref[row : row + LANES, q * LANES : (q + 1) * LANES] = turned
+    put_zeros(ahead_ref)
 
 
 def weights_kernel(channels, classes, w1_in, head_in, ahead1_ref, head_out, w1_ref, head_ref, arrived):
@@ -170,7 +202,7 @@
 
 
 def put_turned(turned_ref, value, plane, east, channels):
-    turned = value.T[0:channels].astype(BF16)
+    turned = value.astype(BF16).T[0:channels]
     size = value.shape[0]
     for d in range(3):
         e = plane + d - 1
@@ -178,11 +210,8 @@
             turned_ref[d * channels : (d + 1) * channels, e * size : (e + 1) * size] = turned
 
 
-def kernel_sum(turned_ref, stack_ref, first, east, rows, low, size, channels):
-    fields = []
-    for e in range(first, first + east):
-        start = (e // 2) * rows + low
-        fields.append(stack_ref[e % 2, start : start + size, :])
+def kernel_sum(turned_ref, stack, first, east, rows, upward, low, size, channels):
+    fields = [shifts_of(stack, plane, rows, upward, low, size) for plane in range(first, first + east)]
     total = jnp.dot(turned_ref[...], jnp.concatenate(fields, 0), preferred_element_type=F32)
     blocks = [
         total[d * channels : (d + 1) * channels, j * LANES : (j + 1) * LANES]
@@ -219,7 +248,7 @@
     ]
     for copy in copies:
         copy.start()
-    for copy in copies:
+    for copy in copies[:-1]:
         copy.wait()
     east, size, _ = center_ref.shape
     north = size // upward
@@ -246,8 +275,9 @@
         everywhere = lax.dot_general(spread, field, (((1,), (1,)), ((), ())), preferred_element_type=F32)
         own = jnp.where(same, everywhere, 0.0).astype(BF16)
         tail = jnp.dot(own, gather, preferred_element_type=F32).astype(BF16)
-        center_ref[e, :, 0:channels] = features_ref[e]
         center_ref[e, :, channels:LANES] = tail[:, channels:LANES]
+    copies[-1].wait()
+    center_ref[:, :, 0:channels] = features_ref[...]
     east_starts = [(1 - side) * (east - HALO) for _, side, _ in rounds_of("east")]
     north_starts = [pl.multiple_of((1 - side) * (size - edge), edge) for _, side, _ in rounds_of("north")]
     edge_refs = iter(edge_refs)
@@ -288,8 +318,9 @@
 ):
     (
         grad_ref, kept_ref, sent_ref,
-        x_ref, s0_ref, s1_ref, sg_ref, mask_ref, slope_ref, turned_ref, ahead2_ref, back2_ref, w2_ref, arrived,
+        x_ref, even0, odd0, even1, odd1, even2, odd2, mask_ref, slope_ref, turned_ref, ahead2_ref, back2_ref, w2_ref, arrived,
     ) = refs[edges:]
+    stack0, stack1, stack2 = (even0, odd0), (even1, odd1), (even2, odd2)
     copy = pltpu.make_async_copy(w2_in, w2_ref, arrived)
     copy.start()
     rows = (north + 2 * HALO) * upward
@@ -307,30 +338,30 @@
         mask = jnp.broadcast_to(x[:, channels : channels + 1], (rows, LANES))
         mask_ref[plane] = mask
         a0 = jnp.where((mask > 0) & (lane < channels), x, 0.0)
-        put_stack(jnp.concatenate([border, a0, border], 0), upward, s0_ref, plane % 2, plane // 2)
+        put_stack(jnp.concatenate([border, a0, border], 0), upward, stack0, plane % 2, plane // 2)
 
     copy.wait()
     put_ahead(ahead2_ref, w2_ref, channels)
     put_back(back2_ref, w2_ref, channels)
     for first, stop in grouped((planes - 2) // 2, 2):
-        for i, parity, value in convolve(s0_ref, ahead1_ref, first, stop, rows):
+        for i, parity, value in convolve(stack0, ahead1_ref, first, stop, rows, upward):
             plane = 2 * i + parity
             mask = mask_ref[plane + 1]
             p1 = mask * value
-            sig = jax.nn.sigmoid(p1)
+            sig = 0.5 * jnp.tanh(0.5 * p1) + 0.5
             slope_ref[plane] = mask * (sig * (1.0 + p1 * (1.0 - sig)))
-            put_stack((p1 * sig)[upward : upward + rows1], upward, s1_ref, parity, i)
+            put_stack((p1 * sig)[upward : upward + rows1], upward, stack1, parity, i)
 
     head = head_ref[...]
     class_lane = (lane[0:rows2] > channels) & (lane[0:rows2] <= channels + classes)
     here = slice(2 * upward, 2 * upward + rows2)
 
     for first, stop in grouped((planes - 4) // 2, 2):
-        for i, parity, value in convolve(s1_ref, ahead2_ref, first, stop, rows2):
+        for i, parity, value in convolve(stack1, ahead2_ref, first, stop, rows2, upward):
             plane = 2 * i + parity
             mask = mask_ref[plane + 2, here]
             p2 = mask * value
-            sig = jax.nn.sigmoid(p2)
+            sig = 0.5 * jnp.tanh(0.5 * p2) + 0.5
             a2 = (p2 * sig).astype(BF16)
             logits = lax.dot_general(a2, head, (((1,), (1,)), ((), ())), preferred_element_type=F32)
             g_logits = jnp.where(class_lane, mask * (logits - x_ref[plane + 2, here].astype(F32)), 0.0)
@@ -340,22 +371,22 @@
                 jnp.concatenate([coarse, fine], 1), jnp.concatenate([head, head], 0), preferred_element_type=F32
             )
             g_p2 = mask * g_a2 * (sig * (1.0 + p2 * (1.0 - sig)))
-            put_stack(g_p2, upward, sg_ref, parity, i)
+            put_stack(g_p2, upward, stack2, parity, i)
             put_turned(turned_ref, g_p2[low2 : low2 + size], plane - 2, east, channels)
 
     upper = high_bit("east", 1) == 1
-    for t, tile in enumerate(kernel_sum(turned_ref, s1_ref, 3, east, rows2, low2, size, channels)):
+    for t, tile in enumerate(kernel_sum(turned_ref, stack1, 3, east, rows2, upward, low2, size, channels)):
         kept_ref[t * channels : (t + 1) * channels, :] = tile.astype(BF16)
 
     there = slice(2 * upward + upward, 2 * upward + upward + rows3)
     for first, stop in grouped((planes - 6) // 2, 2):
-        for i, parity, value in convolve(sg_ref, back2_ref, first, stop, rows3):
+        for i, parity, value in convolve(stack2, back2_ref, first, stop, rows3, upward):
             plane = 2 * i + parity
             g_p1 = slope_ref[plane + 2, there] * value
             grad_ref[plane] = g_p1.astype(BF16)
             put_turned(turned_ref, g_p1[low3 : low3 + size], plane - 1, east, channels)
 
-    tiles = kernel_sum(turned_ref, s0_ref, 4, east, rows, low, size, channels)
+    tiles = kernel_sum(turned_ref, stack0, 4, east, rows, upward, low, size, channels)
     for t, tile in enumerate(tiles):
         place = slice(t * channels, (t + 1) * channels)
         first, second = tile.astype(BF16), kept_ref[place, :]
@@ -371,17 +402,17 @@
     channels, east, north, upward,
     center_ref, grad_ref, w1_in, kept_in,
     out_ref, kept_out,
-    stack_ref, back1_ref, w1_ref, arrived,
+    even_ref, odd_ref, back1_ref, w1_ref, arrived,
 ):
     size = north * upward
     copy = pltpu.make_async_copy(w1_in, w1_ref, arrived)
     copy.start()
     for plane in range(east + 2):
-        put_stack(grad_ref[plane].astype(F32), upward, stack_ref, plane % 2, plane // 2)
+        put_stack(grad_ref[plane].astype(F32), upward, (even_ref, odd_ref), plane % 2, plane // 2)
     copy.wait()
     put_back(back1_ref, w1_ref, channels)
     for first, stop in grouped(east // 2, 2):
-        for i, parity, value in convolve(stack_ref, back1_ref, first, stop, size):
+        for i, parity, value in convolve((even_ref, odd_ref), back1_ref, first, stop, size, upward):
             plane = 2 * i + parity
             mask = center_ref[plane, :, channels : channels + 1].astype(F32)
             out_ref[plane] = (mask * value)[:, 0:channels].astype(BF16)
@@ -514,9 +545,9 @@
         out_specs=(vmem, vmem, vmem),
         scratch_shapes=[
             pltpu.VMEM((planes, rows, LANES), BF16),
-            pltpu.VMEM((2, planes // 2 * rows, WIDE), BF16),
-            pltpu.VMEM((2, (planes - 2) // 2 * (rows - 4 * upward), WIDE), BF16),
-            pltpu.VMEM((2, (planes - 4) // 2 * (rows - 6 * upward), WIDE), BF16),
+            *stack_shapes(planes, rows, upward),
+            *stack_shapes(planes - 2, rows - 4 * upward, upward),
+            *stack_shapes(planes - 4, rows - 6 * upward, upward),
             pltpu.VMEM((planes, rows, LANES), F32),
             pltpu.VMEM((planes - 2, rows, LANES), F32),
             pltpu.VMEM((3 * channels, east * size), BF16),
@@ -525,7 +556,7 @@
             pltpu.VMEM(second_weights.shape, BF16),
             pltpu.SemaphoreType.DMA(()),
         ],
-        compiler_params=pltpu.CompilerParams(vmem_limit_bytes=32 * 1024 * 1024),
+        compiler_params=pltpu.CompilerParams(vmem_limit_bytes=28 * 1024 * 1024),
         name="fields",
     )(ahead1, second_far, head_wide, center, *edges)
 
@@ -542,7 +573,7 @@
             out_specs=(vmem, anywhere),
             input_output_aliases={3: 1},
             scratch_shapes=[
-                pltpu.VMEM((2, (east + 2) // 2 * size, WIDE), BF16),
+                *stack_shapes(east + 2, size, upward),
                 pltpu.VMEM((4 * WIDE, 2 * LANES), BF16),
                 pltpu.VMEM(first_weights.shape, BF16),
                 pltpu.SemaphoreType.DMA(()),

time: 72.2 us -> 68.1 us (0.943)
  blocking collectives: 29 us -> 0 us
  starting transfers between devices: 10.7 us -> 23.4 us
  waiting for transfers between devices: 5.87 us -> 17.6 us
    all_to_all x3 -> x0, blocking collectives: 29 us -> none  [all_to_all(): lax.all_to_all(parts, ('east', 'north'), 0, 0, axis_index_groups=members_...]
    ppermute x10 -> x19, starting transfers between devices: 10.7 us -> 23.4 us  [exchange(): return lax.ppermute(value, ('east', 'north'), pairs)]
    ppermute x10 -> x19, waiting for transfers between devices: 5.87 us -> 17.6 us  [exchange(): return lax.ppermute(value, ('east', 'north'), pairs)]
  transfers between devices with their start and end apart: 10 -> 19, of which waited for: 4 -> 11; matrix products, arithmetic and copies ran while one was open for 0% -> 0% of each run, Pallas kernels for 9% -> 10%
where the time goes in v10:
time: 68.1 us; the launch traced here: 67.9 us
  Pallas kernels  25.6 us (38%)
  starting transfers between devices  23.4 us (34%)
  waiting for transfers between devices  17.6 us (26%)
  between operations  0.93 us (1%)
    ppermute x19, starting transfers between devices, exchange(): return lax.ppermute(value, ('east', 'north'), pairs)  23.4 us
    ppermute x19, waiting for transfers between devices, exchange(): return lax.ppermute(value, ('east', 'north'), pairs)  17.6 us
    pallas_call x1, Pallas kernels, per_device(): pl.pallas_call(functools.partial(whole_kernel, channels, classes, east, n...  15.1 us
    pallas_call x1, Pallas kernels, beside(): pl.pallas_call(functools.partial(last_kernel, channels, east, north, upwa...  3.86 us
    pallas_call x2, Pallas kernels, unpack(): pl.pallas_call(functools.partial(unpack_kernel, channels, scale, bool(ali...  2.43 us
    pallas_call x1, Pallas kernels, per_device(): pl.pallas_call(functools.partial(prepare_kernel, channels, upward, edge),...  2.28 us
    pallas_call x1, Pallas kernels, per_device(): pl.pallas_call(functools.partial(weights_kernel, channels, classes), out_...  1.81 us
  transfers between devices with their start and end apart: 19, of which 11 were waited for; matrix products, arithmetic and copies ran while one was open for 0% of the time, Pallas kernels for 10%

profile of v10, /device:TPU:0, one launch (start us, length us, event | category | flops | bytes accessed | tf_op | source)
XLA Modules:
  0.0 67.9 jit_solution(14185367619545014510)
XLA Ops:
  0.6 2.3 %prepare.1 = (bf16[8,128,128]{2,1,0:T(8,128)(2,1)S(1)}, bf16[4,128,128]{2,1,0:T(8,128)(2,1)S(1)}, bf16[4,128,128]{2,1,0:T(8,128)(2,1)S(1)}, bf16[8,32,128]{2,1,0...) custom-call(s32[1,1,2]{2,1,0:T(1,128)} %bitcast.15, bf16[8,128,96]{2,1,0:T(8,128)(2,1)} %bitcast.12, ...), custom_call_target="tpu_custom_call" | custom-call | tf_op jit(solution)/shard_map/prepare/pallas_call | solution.py:489
  3.4 2.6 %collective-permute-start.1 = (bf16[4,128,128]{2,1,0:T(8,128)(2,1)S(1)}, bf16[4,128,128]{2,1,0:T(8,128)(2,1)S(1)}, u32[]{:S(2)}, u32[]{:S(2)}) collective-permute-start(bf16[4,128,128]{2,1,0:T(8,128)(2,1)S(1)} %get-tuple-element.28), channel_id=1, source_target_pairs={{0,1},{1,0},{2,4},{3,5},{4,2},{5,3},{6,8},{7,9},{8,6},{9,7},{10,12... | collective-permute-start | bytes 393224 | tf_op jit(solution)/shard_map/ppermute | solution.py:41
  6.1 1.4 %collective-permute-start.3 = (bf16[4,32,128]{2,1,0:T(8,128)(2,1)S(1)}, bf16[4,32,128]{2,1,0:T(8,128)(2,1)S(1)}, u32[]{:S(2)}, u32[]{:S(2)}) collective-permute-start(bf16[4,32,128]{2,1,0:T(8,128)(2,1)S(1)} %get-tuple-element.30), channel_id=1, source_target_pairs={{0,3},{1,2},{2,1},{3,0},{4,7},{5,6},{6,5},{7,4},{8,11},{9,10},{10,... | collective-permute-start | bytes 98312 | tf_op jit(solution)/shard_map/ppermute | solution.py:41
  7.5 1.5 %collective-permute-start.4 = (bf16[4,32,128]{2,1,0:T(8,128)(2,1)S(1)}, bf16[4,32,128]{2,1,0:T(8,128)(2,1)S(1)}, u32[]{:S(2)}, u32[]{:S(2)}) collective-permute-start(bf16[4,32,128]{2,1,0:T(8,128)(2,1)S(1)} %get-tuple-element.31), channel_id=1, source_target_pairs={{0,1},{1,0},{2,5},{3,4},{4,3},{5,2},{6,9},{7,8},{8,7},{9,6},{10,13... | collective-permute-start | bytes 98312 | tf_op jit(solution)/shard_map/ppermute | solution.py:41
  9.0 1.8 %weights.1 = (bf16[4608,256]{1,0:T(8,128)(2,1)S(1)}, bf16[128,128]{1,0:T(8,128)(2,1)S(1)}) custom-call(bf16[27,96,96]{2,1,0:T(8,128)(2,1)} %w1_in.3, bf16[13,96]{1,0:T(8,128)(2,1)} %head_in.1), custom_call_target="tpu_custom_call" | custom-call | tf_op jit(solution)/shard_map/weights/pallas_call | solution.py:524
  11.4 15.1 %fields.1 = (bf16[10,144,128]{2,1,0:T(8,128)(2,1)S(1)}, bf16[2048,128]{1,0:T(8,128)(2,1)S(1)}, bf16[2048,128]{1,0:T(8,128)(2,1)S(1)}) custom-call(bf16[4608,256]{1,0:T(8,128)(2,1)S(1)} %get-tuple-element.25.ahead1_ref, bf16[27,96,96]{2,1,0:T(8,128)(2,1)} %w2_in.1, bf16[128,128]{1,0:T(8,128)(2,1)S(1)} %get-tuple-element.26.head_ref, ...), custom_call_target="tpu_custom_call" | custom-call | tf_op jit(solution)/shard_map/fields/pallas_call | solution.py:537
  27.5 1.5 %collective-permute-done.5.came_ref = bf16[2048,128]{1,0:T(8,128)(2,1)S(1)} collective-permute-done((bf16[2048,128]{1,0:T(8,128)(2,1)S(1)}, bf16[2048,128]{1,0:T(8,128)(2,1)S(1)}, u32[]{:S(2)}, u32[]{:S(2)}) %collective-permute-start.5) | collective-permute-done | bytes 524320 | tf_op jit(solution)/shard_map/ppermute | solution.py:41
  29.2 1.8 %collective-permute-start.6 = (bf16[512,128]{1,0:T(8,128)(2,1)S(1)}, bf16[512,128]{1,0:T(8,128)(2,1)S(1)}, u32[]{:S(2)}, u32[]{:S(2)}) collective-permute-start(bf16[512,128]{1,0:T(8,128)(2,1)S(1)} %get-tuple-element.38), channel_id=1, source_target_pairs={{0,1},{1,0},{2,3},{3,2},{4,5},{5,4},{6,7},{7,6},{8,9},{9,8},{10,11... | collective-permute-start | bytes 393224 | tf_op jit(solution)/shard_map/ppermute | solution.py:41
  31.0 1.4 %collective-permute-start.7 = (bf16[512,128]{1,0:T(8,128)(2,1)S(1)}, bf16[512,128]{1,0:T(8,128)(2,1)S(1)}, u32[]{:S(2)}, u32[]{:S(2)}) collective-permute-start(bf16[512,128]{1,0:T(8,128)(2,1)S(1)} %get-tuple-element.39), channel_id=1, source_target_pairs={{0,4},{1,5},{2,6},{3,7},{4,0},{5,1},{6,2},{7,3},{8,12},{9,13},{10,... | collective-permute-start | bytes 393224 | tf_op jit(solution)/shard_map/ppermute | solution.py:41
  32.8 3.9 %features.1 = (bf16[8,128,96]{2,1,0:T(8,128)(2,1)}, f32[512,128]{1,0:T(8,128)S(1)}) custom-call(bf16[8,128,128]{2,1,0:T(8,128)(2,1)S(1)} %get-tuple-element.24.center_ref, bf16[10,144,128]{2,1,0:T(8,128)(2,1)S(1)} %get-tuple-element.32.grad_ref, bf16[27,96,96]{2,1,0:T(8,128)(2,1)} %w1_in.3, ...), custom_call_target="tpu_custom_call", output_to_operand_aliasing={{1}: (3, {})} | custom-call | tf_op jit(solution)/shard_map/features/pallas_call | solution.py:566
  36.6 2.5 %collective-permute-done.7 = bf16[512,128]{1,0:T(8,128)(2,1)S(1)} collective-permute-done((bf16[512,128]{1,0:T(8,128)(2,1)S(1)}, bf16[512,128]{1,0:T(8,128)(2,1)S(1)}, u32[]{:S(2)}, u32[]{:S(2)}) %collective-permute-start.7) | collective-permute-done | bytes 131104 | tf_op jit(solution)/shard_map/ppermute | solution.py:41
  39.2 2.1 %collective-permute-start.9 = (bf16[128,128]{1,0:T(8,128)(2,1)S(1)}, bf16[128,128]{1,0:T(8,128)(2,1)S(1)}, u32[]{:S(2)}, u32[]{:S(2)}) collective-permute-start(bf16[128,128]{1,0:T(8,128)(2,1)S(1)} %get-tuple-element.49), channel_id=1, source_target_pairs={{0,8},{1,9},{2,10},{3,11},{4,12},{5,13},{6,14},{7,15},{8,0},{9,1},... | collective-permute-start | bytes 98312 | tf_op jit(solution)/shard_map/ppermute | solution.py:41
  41.3 2.5 %collective-permute-start.11 = (bf16[128,128]{1,0:T(8,128)(2,1)S(1)}, bf16[128,128]{1,0:T(8,128)(2,1)S(1)}, u32[]{:S(2)}, u32[]{:S(2)}) collective-permute-start(bf16[128,128]{1,0:T(8,128)(2,1)S(1)} %get-tuple-element.50), channel_id=1, source_target_pairs={{0,24},{1,25},{2,26},{3,27},{4,28},{5,29},{6,30},{7,31},{8,16},{9,... | collective-permute-start | bytes 98312 | tf_op jit(solution)/shard_map/ppermute | solution.py:41
  43.9 3.1 %collective-permute-done.11 = bf16[128,128]{1,0:T(8,128)(2,1)S(1)} collective-permute-done((bf16[128,128]{1,0:T(8,128)(2,1)S(1)}, bf16[128,128]{1,0:T(8,128)(2,1)S(1)}, u32[]{:S(2)}, u32[]{:S(2)}) %collective-permute-start.11) | collective-permute-done | bytes 32800 | tf_op jit(solution)/shard_map/ppermute | solution.py:41
  47.0 1.9 %collective-permute-done.10 = bf16[128,128]{1,0:T(8,128)(2,1)S(1)} collective-permute-done((bf16[128,128]{1,0:T(8,128)(2,1)S(1)}, bf16[128,128]{1,0:T(8,128)(2,1)S(1)}, u32[]{:S(2)}, u32[]{:S(2)}) %collective-permute-start.10) | collective-permute-done | bytes 32800 | tf_op jit(solution)/shard_map/ppermute | solution.py:41
  49.5 1.4 %collective-permute-start.13 = (bf16[128,128]{1,0:T(8,128)(2,1)S(1)}, bf16[128,128]{1,0:T(8,128)(2,1)S(1)}, u32[]{:S(2)}, u32[]{:S(2)}) collective-permute-start(bf16[128,128]{1,0:T(8,128)(2,1)S(1)} %add_convert_fusion), channel_id=1, source_target_pairs={{0,16},{1,17},{2,18},{3,19},{4,20},{5,21},{6,22},{7,23},{8,24},{9,... | collective-permute-start | bytes 98312 | tf_op jit(solution)/shard_map/ppermute | solution.py:41
  50.8 2.6 %collective-permute-start.12 = (bf16[128,128]{1,0:T(8,128)(2,1)S(1)}, bf16[128,128]{1,0:T(8,128)(2,1)S(1)}, u32[]{:S(2)}, u32[]{:S(2)}) collective-permute-start(bf16[128,128]{1,0:T(8,128)(2,1)S(1)} %add_convert_fusion), channel_id=1, source_target_pairs={{0,24},{1,25},{2,26},{3,27},{4,28},{5,29},{6,30},{7,31},{8,16},{9,... | collective-permute-start | bytes 98312 | tf_op jit(solution)/shard_map/ppermute | solution.py:41
  54.3 2.3 %collective-permute-done.12 = bf16[128,128]{1,0:T(8,128)(2,1)S(1)} collective-permute-done((bf16[128,128]{1,0:T(8,128)(2,1)S(1)}, bf16[128,128]{1,0:T(8,128)(2,1)S(1)}, u32[]{:S(2)}, u32[]{:S(2)}) %collective-permute-start.12) | collective-permute-done | bytes 32800 | tf_op jit(solution)/shard_map/ppermute | solution.py:41
  57.3 1.1 %collective-permute-start.16 = (bf16[512,128]{1,0:T(8,128)(2,1)S(1)}, bf16[512,128]{1,0:T(8,128)(2,1)S(1)}, u32[]{:S(2)}, u32[]{:S(2)}) collective-permute-start(bf16[512,128]{1,0:T(8,128)(2,1)S(1)} %pad_maximum_fusion.1), channel_id=1, source_target_pairs={{0,4},{1,5},{2,6},{3,7},{4,0},{5,1},{6,2},{7,3},{8,12},{9,13},{10,... | collective-permute-start | bytes 393224 | tf_op jit(solution)/shard_map/ppermute | solution.py:41
  58.4 1.8 %collective-permute-start.15 = (bf16[512,128]{1,0:T(8,128)(2,1)S(1)}, bf16[512,128]{1,0:T(8,128)(2,1)S(1)}, u32[]{:S(2)}, u32[]{:S(2)}) collective-permute-start(bf16[512,128]{1,0:T(8,128)(2,1)S(1)} %pad_maximum_fusion.1), channel_id=1, source_target_pairs={{0,5},{1,4},{2,7},{3,6},{4,1},{5,0},{6,3},{7,2},{8,13},{9,12},{10,... | collective-permute-start | bytes 393224 | tf_op jit(solution)/shard_map/ppermute | solution.py:41
  60.1 1.5 %collective-permute-done.17 = bf16[512,128]{1,0:T(8,128)(2,1)S(1)} collective-permute-done((bf16[512,128]{1,0:T(8,128)(2,1)S(1)}, bf16[512,128]{1,0:T(8,128)(2,1)S(1)}, u32[]{:S(2)}, u32[]{:S(2)}) %collective-permute-start.17) | collective-permute-done | bytes 131104 | tf_op jit(solution)/shard_map/ppermute | solution.py:41
  62.3 2.0 %collective-permute-done.15 = bf16[512,128]{1,0:T(8,128)(2,1)S(1)} collective-permute-done((bf16[512,128]{1,0:T(8,128)(2,1)S(1)}, bf16[512,128]{1,0:T(8,128)(2,1)S(1)}, u32[]{:S(2)}, u32[]{:S(2)}) %collective-permute-start.15) | collective-permute-done | bytes 131104 | tf_op jit(solution)/shard_map/ppermute | solution.py:41
  64.6 1.2 %unpack.2 = (f32[27,96,96]{2,1,0:T(8,128)}, f32[27,96,96]{2,1,0:T(8,128)}) custom-call(s32[1]{0:T(128)} %bitcast.9.first_ref_flag, bf16[2048,128]{1,0:T(8,128)(2,1)S(1)} %pad_maximum_fusion.packed_ref), custom_call_target="tpu_custom_call" | custom-call | tf_op jit(solution)/shard_map/unpack/pallas_call | solution.py:606
  66.5 1.2 %unpack.3 = (f32[27,96,96]{2,1,0:T(8,128)}, f32[27,96,96]{2,1,0:T(8,128)}) custom-call(s32[1]{0:T(128)} %bitcast.8.first_ref_flag, bf16[2048,128]{1,0:T(8,128)(2,1)S(1)} %collective-permute-done.18.packed_ref, f32[27,96,96]{2,1,0:T(8,128)} %get-tuple-element.41.refs_0_, ...), custom_call_target="tpu_custom_call", output_to_operand_aliasing={{0}: (2, {}), {1}: (3, {})} | custom-call | tf_op jit(solution)/shard_map/unpack/pallas_call | solution.py:606
  (29 shorter events, 6.7 us)
Async XLA Ops:
  2.9 8.5 %collective-permute-start = (bf16[4,128,128]{2,1,0:T(8,128)(2,1)S(1)}, bf16[4,128,128]{2,1,0:T(8,128)(2,1)S(1)}, u32[]{:S(2)}, u32[]{:S(2)}) collective-permute-start(bf16[4,128,128]{2,1,0:T(8,128)(2,1)S(1)} %get-tuple-element.27), channel_id=1, source_target_pairs={{0,2},{1,3},{2,0},{3,1},{4,6},{5,7},{6,4},{7,5},{8,10},{9,11},{10,... | collective-permute-start | bytes 393224 | tf_op jit(solution)/shard_map/ppermute | solution.py:41
  3.4 8.0 %collective-permute-start.1 = (bf16[4,128,128]{2,1,0:T(8,128)(2,1)S(1)}, bf16[4,128,128]{2,1,0:T(8,128)(2,1)S(1)}, u32[]{:S(2)}, u32[]{:S(2)}) collective-permute-start(bf16[4,128,128]{2,1,0:T(8,128)(2,1)S(1)} %get-tuple-element.28), channel_id=1, source_target_pairs={{0,1},{1,0},{2,4},{3,5},{4,2},{5,3},{6,8},{7,9},{8,6},{9,7},{10,12... | collective-permute-start | bytes 393224 | tf_op jit(solution)/shard_map/ppermute | solution.py:41
  6.0 5.4 %collective-permute-start.2 = (bf16[8,32,128]{2,1,0:T(8,128)(2,1)S(1)}, bf16[8,32,128]{2,1,0:T(8,128)(2,1)S(1)}, u32[]{:S(2)}, u32[]{:S(2)}) collective-permute-start(bf16[8,32,128]{2,1,0:T(8,128)(2,1)S(1)} %get-tuple-element.29), channel_id=1, source_target_pairs={{0,1},{1,0},{2,3},{3,2},{4,5},{5,4},{6,7},{7,6},{8,9},{9,8},{10,11... | collective-permute-start | bytes 196616 | tf_op jit(solution)/shard_map/ppermute | solution.py:41
  6.1 4.7 %collective-permute-start.3 = (bf16[4,32,128]{2,1,0:T(8,128)(2,1)S(1)}, bf16[4,32,128]{2,1,0:T(8,128)(2,1)S(1)}, u32[]{:S(2)}, u32[]{:S(2)}) collective-permute-start(bf16[4,32,128]{2,1,0:T(8,128)(2,1)S(1)} %get-tuple-element.30), channel_id=1, source_target_pairs={{0,3},{1,2},{2,1},{3,0},{4,7},{5,6},{6,5},{7,4},{8,11},{9,10},{10,... | collective-permute-start | bytes 98312 | tf_op jit(solution)/shard_map/ppermute | solution.py:41
  7.5 3.9 %collective-permute-start.4 = (bf16[4,32,128]{2,1,0:T(8,128)(2,1)S(1)}, bf16[4,32,128]{2,1,0:T(8,128)(2,1)S(1)}, u32[]{:S(2)}, u32[]{:S(2)}) collective-permute-start(bf16[4,32,128]{2,1,0:T(8,128)(2,1)S(1)} %get-tuple-element.31), channel_id=1, source_target_pairs={{0,1},{1,0},{2,5},{3,4},{4,3},{5,2},{6,9},{7,8},{8,7},{9,6},{10,13... | collective-permute-start | bytes 98312 | tf_op jit(solution)/shard_map/ppermute | solution.py:41
  26.5 2.6 %collective-permute-start.5 = (bf16[2048,128]{1,0:T(8,128)(2,1)S(1)}, bf16[2048,128]{1,0:T(8,128)(2,1)S(1)}, u32[]{:S(2)}, u32[]{:S(2)}) collective-permute-start(bf16[2048,128]{1,0:T(8,128)(2,1)S(1)} %get-tuple-element.34), channel_id=1, source_target_pairs={{0,2},{1,3},{2,0},{3,1},{4,6},{5,7},{6,4},{7,5},{8,10},{9,11},{10,... | collective-permute-start | bytes 1572872 | tf_op jit(solution)/shard_map/ppermute | solution.py:41
  29.2 7.4 %collective-permute-start.6 = (bf16[512,128]{1,0:T(8,128)(2,1)S(1)}, bf16[512,128]{1,0:T(8,128)(2,1)S(1)}, u32[]{:S(2)}, u32[]{:S(2)}) collective-permute-start(bf16[512,128]{1,0:T(8,128)(2,1)S(1)} %get-tuple-element.38), channel_id=1, source_target_pairs={{0,1},{1,0},{2,3},{3,2},{4,5},{5,4},{6,7},{7,6},{8,9},{9,8},{10,11... | collective-permute-start | bytes 393224 | tf_op jit(solution)/shard_map/ppermute | solution.py:41
  31.0 8.1 %collective-permute-start.7 = (bf16[512,128]{1,0:T(8,128)(2,1)S(1)}, bf16[512,128]{1,0:T(8,128)(2,1)S(1)}, u32[]{:S(2)}, u32[]{:S(2)}) collective-permute-start(bf16[512,128]{1,0:T(8,128)(2,1)S(1)} %get-tuple-element.39), channel_id=1, source_target_pairs={{0,4},{1,5},{2,6},{3,7},{4,0},{5,1},{6,2},{7,3},{8,12},{9,13},{10,... | collective-permute-start | bytes 393224 | tf_op jit(solution)/shard_map/ppermute | solution.py:41
  32.4 6.7 %collective-permute-start.8 = (bf16[512,128]{1,0:T(8,128)(2,1)S(1)}, bf16[512,128]{1,0:T(8,128)(2,1)S(1)}, u32[]{:S(2)}, u32[]{:S(2)}) collective-permute-start(bf16[512,128]{1,0:T(8,128)(2,1)S(1)} %get-tuple-element.40), channel_id=1, source_target_pairs={{0,5},{1,4},{2,7},{3,6},{4,1},{5,0},{6,3},{7,2},{8,13},{9,12},{10,... | collective-permute-start | bytes 393224 | tf_op jit(solution)/shard_map/ppermute | solution.py:41
  39.2 4.7 %collective-permute-start.9 = (bf16[128,128]{1,0:T(8,128)(2,1)S(1)}, bf16[128,128]{1,0:T(8,128)(2,1)S(1)}, u32[]{:S(2)}, u32[]{:S(2)}) collective-permute-start(bf16[128,128]{1,0:T(8,128)(2,1)S(1)} %get-tuple-element.49), channel_id=1, source_target_pairs={{0,8},{1,9},{2,10},{3,11},{4,12},{5,13},{6,14},{7,15},{8,0},{9,1},... | collective-permute-start | bytes 98312 | tf_op jit(solution)/shard_map/ppermute | solution.py:41
  41.3 5.7 %collective-permute-start.11 = (bf16[128,128]{1,0:T(8,128)(2,1)S(1)}, bf16[128,128]{1,0:T(8,128)(2,1)S(1)}, u32[]{:S(2)}, u32[]{:S(2)}) collective-permute-start(bf16[128,128]{1,0:T(8,128)(2,1)S(1)} %get-tuple-element.50), channel_id=1, source_target_pairs={{0,24},{1,25},{2,26},{3,27},{4,28},{5,29},{6,30},{7,31},{8,16},{9,... | collective-permute-start | bytes 98312 | tf_op jit(solution)/shard_map/ppermute | solution.py:41
  43.8 5.2 %collective-permute-start.10 = (bf16[128,128]{1,0:T(8,128)(2,1)S(1)}, bf16[128,128]{1,0:T(8,128)(2,1)S(1)}, u32[]{:S(2)}, u32[]{:S(2)}) collective-permute-start(bf16[128,128]{1,0:T(8,128)(2,1)S(1)} %get-tuple-element.51), channel_id=1, source_target_pairs={{0,16},{1,17},{2,18},{3,19},{4,20},{5,21},{6,22},{7,23},{8,24},{9,... | collective-permute-start | bytes 98312 | tf_op jit(solution)/shard_map/ppermute | solution.py:41
  49.0 4.5 %collective-permute-start.14 = (bf16[128,128]{1,0:T(8,128)(2,1)S(1)}, bf16[128,128]{1,0:T(8,128)(2,1)S(1)}, u32[]{:S(2)}, u32[]{:S(2)}) collective-permute-start(bf16[128,128]{1,0:T(8,128)(2,1)S(1)} %add_convert_fusion), channel_id=1, source_target_pairs={{0,8},{1,9},{2,10},{3,11},{4,12},{5,13},{6,14},{7,15},{8,0},{9,1},... | collective-permute-start | bytes 98312 | tf_op jit(solution)/shard_map/ppermute | solution.py:41
  49.5 4.8 %collective-permute-start.13 = (bf16[128,128]{1,0:T(8,128)(2,1)S(1)}, bf16[128,128]{1,0:T(8,128)(2,1)S(1)}, u32[]{:S(2)}, u32[]{:S(2)}) collective-permute-start(bf16[128,128]{1,0:T(8,128)(2,1)S(1)} %add_convert_fusion), channel_id=1, source_target_pairs={{0,16},{1,17},{2,18},{3,19},{4,20},{5,21},{6,22},{7,23},{8,24},{9,... | collective-permute-start | bytes 98312 | tf_op jit(solution)/shard_map/ppermute | solution.py:41
  50.8 5.7 %collective-permute-start.12 = (bf16[128,128]{1,0:T(8,128)(2,1)S(1)}, bf16[128,128]{1,0:T(8,128)(2,1)S(1)}, u32[]{:S(2)}, u32[]{:S(2)}) collective-permute-start(bf16[128,128]{1,0:T(8,128)(2,1)S(1)} %add_convert_fusion), channel_id=1, source_target_pairs={{0,24},{1,25},{2,26},{3,27},{4,28},{5,29},{6,30},{7,31},{8,16},{9,... | collective-permute-start | bytes 98312 | tf_op jit(solution)/shard_map/ppermute | solution.py:41
  56.6 5.0 %collective-permute-start.17 = (bf16[512,128]{1,0:T(8,128)(2,1)S(1)}, bf16[512,128]{1,0:T(8,128)(2,1)S(1)}, u32[]{:S(2)}, u32[]{:S(2)}) collective-permute-start(bf16[512,128]{1,0:T(8,128)(2,1)S(1)} %pad_maximum_fusion.1), channel_id=1, source_target_pairs={{0,1},{1,0},{2,3},{3,2},{4,5},{5,4},{6,7},{7,6},{8,9},{9,8},{10,11... | collective-permute-start | bytes 393224 | tf_op jit(solution)/shard_map/ppermute | solution.py:41
  57.3 5.0 %collective-permute-start.16 = (bf16[512,128]{1,0:T(8,128)(2,1)S(1)}, bf16[512,128]{1,0:T(8,128)(2,1)S(1)}, u32[]{:S(2)}, u32[]{:S(2)}) collective-permute-start(bf16[512,128]{1,0:T(8,128)(2,1)S(1)} %pad_maximum_fusion.1), channel_id=1, source_target_pairs={{0,4},{1,5},{2,6},{3,7},{4,0},{5,1},{6,2},{7,3},{8,12},{9,13},{10,... | collective-permute-start | bytes 393224 | tf_op jit(solution)/shard_map/ppermute | solution.py:41
  58.4 5.9 %collective-permute-start.15 = (bf16[512,128]{1,0:T(8,128)(2,1)S(1)}, bf16[512,128]{1,0:T(8,128)(2,1)S(1)}, u32[]{:S(2)}, u32[]{:S(2)}) collective-permute-start(bf16[512,128]{1,0:T(8,128)(2,1)S(1)} %pad_maximum_fusion.1), channel_id=1, source_target_pairs={{0,5},{1,4},{2,7},{3,6},{4,1},{5,0},{6,3},{7,2},{8,13},{9,12},{10,... | collective-permute-start | bytes 393224 | tf_op jit(solution)/shard_map/ppermute | solution.py:41
  64.5 2.0 %collective-permute-start.18 = (bf16[2048,128]{1,0:T(8,128)(2,1)S(1)}, bf16[2048,128]{1,0:T(8,128)(2,1)S(1)}, u32[]{:S(2)}, u32[]{:S(2)}) collective-permute-start(bf16[2048,128]{1,0:T(8,128)(2,1)S(1)} %pad_maximum_fusion.packed_ref), channel_id=1, source_target_pairs={{0,2},{1,3},{2,0},{3,1},{4,6},{5,7},{6,4},{7,5},{8,10},{9,11},{10,... | collective-permute-start | bytes 1572872 | tf_op jit(solution)/shard_map/ppermute | solution.py:41

commit v11 on v10

--- a/solution.py
+++ b/solution.py
@@ -63,18 +63,10 @@
     return exchange(value, *partners)
 
 
-def scatter_sums(total, groups):
-    for group in groups:
-        ways = 1 << len(group)
-        part = total.shape[0] // ways
-        place = place_in(group)
-        sent = [
-            lax.dynamic_slice_in_dim(total, (place ^ change) * part, part, 0).astype(BF16)
-            for change in range(1, ways)
-        ]
-        total = lax.dynamic_slice_in_dim(total, place * part, part, 0)
-        for change in range(1, ways):
-            total = total + swap(sent[change - 1], group, change).astype(F32)
+def share_sums(total, bits):
+    total = total.astype(BF16)
+    for bit in bits:
+        total = (total.astype(F32) + swap(total, [bit], 1).astype(F32)).astype(BF16)
     return total
 
 
@@ -343,7 +335,7 @@
     copy.wait()
     put_ahead(ahead2_ref, w2_ref, channels)
     put_back(back2_ref, w2_ref, channels)
-    for first, stop in grouped((planes - 2) // 2, 2):
+    for first, stop in grouped((planes - 2) // 2, 3):
         for i, parity, value in convolve(stack0, ahead1_ref, first, stop, rows, upward):
             plane = 2 * i + parity
             mask = mask_ref[plane + 1]
@@ -356,7 +348,7 @@
     class_lane = (lane[0:rows2] > channels) & (lane[0:rows2] <= channels + classes)
     here = slice(2 * upward, 2 * upward + rows2)
 
-    for first, stop in grouped((planes - 4) // 2, 2):
+    for first, stop in grouped((planes - 4) // 2, 3):
         for i, parity, value in convolve(stack1, ahead2_ref, first, stop, rows2, upward):
             plane = 2 * i + parity
             mask = mask_ref[plane + 2, here]
@@ -379,7 +371,7 @@
         kept_ref[t * channels : (t + 1) * channels, :] = tile.astype(BF16)
 
     there = slice(2 * upward + upward, 2 * upward + upward + rows3)
-    for first, stop in grouped((planes - 6) // 2, 2):
+    for first, stop in grouped((planes - 6) // 2, 3):
         for i, parity, value in convolve(stack2, back2_ref, first, stop, rows3, upward):
             plane = 2 * i + parity
             g_p1 = slope_ref[plane + 2, there] * value
@@ -411,7 +403,7 @@
         put_stack(grad_ref[plane].astype(F32), upward, (even_ref, odd_ref), plane % 2, plane // 2)
     copy.wait()
     put_back(back1_ref, w1_ref, channels)
-    for first, stop in grouped(east // 2, 2):
+    for first, stop in grouped(east // 2, 4):
         for i, parity, value in convolve((even_ref, odd_ref), back1_ref, first, stop, size, upward):
             plane = 2 * i + parity
             mask = center_ref[plane, :, channels : channels + 1].astype(F32)
@@ -479,7 +471,7 @@
 
     east_bits, north_bits = bits_of("east"), bits_of("north")
     rest = north_bits + east_bits[1:]
-    groups = [rest[i : i + 2] for i in range(0, len(rest), 2)]
+    near, others = rest[:2], rest[2:]
     upper = high_bit(*east_bits[0])
     easts, norths = rounds_of("east"), rounds_of("north")
     counts = (len(easts), len(norths))
@@ -584,7 +576,7 @@
         features_out.append(out)
         return kept
 
-    ways = 1 << len(groups[0])
+    ways = 1 << len(near)
     part = packed // ways
     total, *parts = pl.pallas_call(
         parts_kernel,
@@ -594,12 +586,11 @@
         out_specs=[vmem] * ways,
         compiler_params=pltpu.CompilerParams(vmem_limit_bytes=4 * 1024 * 1024),
         name="parts",
-    )(place_in(groups[0]).reshape(1).astype(jnp.int32), kept, swap(sent, east_bits[:1], 1))
+    )(place_in(near).reshape(1).astype(jnp.int32), kept, swap(sent, east_bits[:1], 1))
     total = beside(total)
     for change in range(1, ways):
-        total = total + swap(parts[change - 1], groups[0], change).astype(F32)
-    total = scatter_sums(total, groups[1:])
-    mine = gather_parts(total.astype(BF16), groups)
+        total = total + swap(parts[change - 1], near, change).astype(F32)
+    mine = gather_parts(share_sums(total, others), [near])
     other = swap(mine, east_bits[:1], 1)
 
     def unpack(is_first, value, *aliased):

time: 68.1 us -> 65.3 us (0.959)
  starting transfers between devices: 23.4 us -> 20.2 us
  Pallas kernels: 25.6 us -> 27.4 us
  waiting for transfers between devices: 17.6 us -> 16.5 us
    ppermute x19 -> x15, starting transfers between devices: 23.4 us -> 20.2 us  [exchange(): return lax.ppermute(value, ('east', 'north'), pairs)]
    pallas_call x1, Pallas kernels: 15.1 us -> 17.1 us  [per_device(): pl.pallas_call(functools.partial(whole_kernel, channels, classes, east, n...]
    ppermute x19 -> x15, waiting for transfers between devices: 17.6 us -> 16.5 us  [exchange(): return lax.ppermute(value, ('east', 'north'), pairs)]
  transfers between devices with their start and end apart: 19 -> 15, of which waited for: 11 -> 9; matrix products, arithmetic and copies ran while one was open for 0% -> 0% of each run, Pallas kernels for 10% -> 10%
where the time goes in v11:
time: 65.3 us; the launch traced here: 65.1 us
  Pallas kernels  27.4 us (42%)
  starting transfers between devices  20.2 us (31%)
  waiting for transfers between devices  16.5 us (25%)
  between operations  0.75 us (1%)
    ppermute x15, starting transfers between devices, exchange(): return lax.ppermute(value, ('east', 'north'), pairs)  20.2 us
    pallas_call x1, Pallas kernels, per_device(): pl.pallas_call(functools.partial(whole_kernel, channels, classes, east, n...  17.1 us
    ppermute x15, waiting for transfers between devices, exchange(): return lax.ppermute(value, ('east', 'north'), pairs)  16.5 us
    pallas_call x1, Pallas kernels, beside(): pl.pallas_call(functools.partial(last_kernel, channels, east, north, upwa...  3.62 us
    pallas_call x2, Pallas kernels, unpack(): pl.pallas_call(functools.partial(unpack_kernel, channels, scale, bool(ali...  2.43 us
    pallas_call x1, Pallas kernels, per_device(): pl.pallas_call(functools.partial(prepare_kernel, channels, upward, edge),...  2.28 us
    pallas_call x1, Pallas kernels, per_device(): pl.pallas_call(functools.partial(weights_kernel, channels, classes), out_...  1.81 us
  transfers between devices with their start and end apart: 15, of which 9 were waited for; matrix products, arithmetic and copies ran while one was open for 0% of the time, Pallas kernels for 10%

profile of v11, /device:TPU:0, one launch (start us, length us, event | category | flops | bytes accessed | tf_op | source)
XLA Modules:
  0.0 65.1 jit_solution(6679454655503900751)
XLA Ops:
  0.6 2.3 %prepare.1 = (bf16[8,128,128]{2,1,0:T(8,128)(2,1)S(1)}, bf16[4,128,128]{2,1,0:T(8,128)(2,1)S(1)}, bf16[4,128,128]{2,1,0:T(8,128)(2,1)S(1)}, bf16[8,32,128]{2,1,0...) custom-call(s32[1,1,2]{2,1,0:T(1,128)} %bitcast.15, bf16[8,128,96]{2,1,0:T(8,128)(2,1)} %bitcast.12, ...), custom_call_target="tpu_custom_call" | custom-call | tf_op jit(solution)/shard_map/prepare/pallas_call | solution.py:481
  3.4 2.6 %collective-permute-start.1 = (bf16[4,128,128]{2,1,0:T(8,128)(2,1)S(1)}, bf16[4,128,128]{2,1,0:T(8,128)(2,1)S(1)}, u32[]{:S(2)}, u32[]{:S(2)}) collective-permute-start(bf16[4,128,128]{2,1,0:T(8,128)(2,1)S(1)} %get-tuple-element.28), channel_id=1, source_target_pairs={{0,1},{1,0},{2,4},{3,5},{4,2},{5,3},{6,8},{7,9},{8,6},{9,7},{10,12... | collective-permute-start | bytes 393224 | tf_op jit(solution)/shard_map/ppermute | solution.py:41
  6.1 1.4 %collective-permute-start.3 = (bf16[4,32,128]{2,1,0:T(8,128)(2,1)S(1)}, bf16[4,32,128]{2,1,0:T(8,128)(2,1)S(1)}, u32[]{:S(2)}, u32[]{:S(2)}) collective-permute-start(bf16[4,32,128]{2,1,0:T(8,128)(2,1)S(1)} %get-tuple-element.30), channel_id=1, source_target_pairs={{0,3},{1,2},{2,1},{3,0},{4,7},{5,6},{6,5},{7,4},{8,11},{9,10},{10,... | collective-permute-start | bytes 98312 | tf_op jit(solution)/shard_map/ppermute | solution.py:41
  7.5 1.5 %collective-permute-start.4 = (bf16[4,32,128]{2,1,0:T(8,128)(2,1)S(1)}, bf16[4,32,128]{2,1,0:T(8,128)(2,1)S(1)}, u32[]{:S(2)}, u32[]{:S(2)}) collective-permute-start(bf16[4,32,128]{2,1,0:T(8,128)(2,1)S(1)} %get-tuple-element.31), channel_id=1, source_target_pairs={{0,1},{1,0},{2,5},{3,4},{4,3},{5,2},{6,9},{7,8},{8,7},{9,6},{10,13... | collective-permute-start | bytes 98312 | tf_op jit(solution)/shard_map/ppermute | solution.py:41
  9.0 1.8 %weights.1 = (bf16[4608,256]{1,0:T(8,128)(2,1)S(1)}, bf16[128,128]{1,0:T(8,128)(2,1)S(1)}) custom-call(bf16[27,96,96]{2,1,0:T(8,128)(2,1)} %w1_in.3, bf16[13,96]{1,0:T(8,128)(2,1)} %head_in.1), custom_call_target="tpu_custom_call" | custom-call | tf_op jit(solution)/shard_map/weights/pallas_call | solution.py:516
  11.4 17.1 %fields.1 = (bf16[10,144,128]{2,1,0:T(8,128)(2,1)S(1)}, bf16[2048,128]{1,0:T(8,128)(2,1)S(1)}, bf16[2048,128]{1,0:T(8,128)(2,1)S(1)}) custom-call(bf16[4608,256]{1,0:T(8,128)(2,1)S(1)} %get-tuple-element.25.ahead1_ref, bf16[27,96,96]{2,1,0:T(8,128)(2,1)} %w2_in.1, bf16[128,128]{1,0:T(8,128)(2,1)S(1)} %get-tuple-element.26.head_ref, ...), custom_call_target="tpu_custom_call" | custom-call | tf_op jit(solution)/shard_map/fields/pallas_call | solution.py:529
  28.6 1.0 %collective-permute-start.5 = (bf16[2048,128]{1,0:T(8,128)(2,1)S(1)}, bf16[2048,128]{1,0:T(8,128)(2,1)S(1)}, u32[]{:S(2)}, u32[]{:S(2)}) collective-permute-start(bf16[2048,128]{1,0:T(8,128)(2,1)S(1)} %get-tuple-element.34), channel_id=1, source_target_pairs={{0,2},{1,3},{2,0},{3,1},{4,6},{5,7},{6,4},{7,5},{8,10},{9,11},{10,... | collective-permute-start | bytes 1572872 | tf_op jit(solution)/shard_map/ppermute | solution.py:41
  29.6 1.5 %collective-permute-done.5.came_ref = bf16[2048,128]{1,0:T(8,128)(2,1)S(1)} collective-permute-done((bf16[2048,128]{1,0:T(8,128)(2,1)S(1)}, bf16[2048,128]{1,0:T(8,128)(2,1)S(1)}, u32[]{:S(2)}, u32[]{:S(2)}) %collective-permute-start.5) | collective-permute-done | bytes 524320 | tf_op jit(solution)/shard_map/ppermute | solution.py:41
  31.2 1.8 %collective-permute-start.6 = (bf16[512,128]{1,0:T(8,128)(2,1)S(1)}, bf16[512,128]{1,0:T(8,128)(2,1)S(1)}, u32[]{:S(2)}, u32[]{:S(2)}) collective-permute-start(bf16[512,128]{1,0:T(8,128)(2,1)S(1)} %get-tuple-element.38), channel_id=1, source_target_pairs={{0,1},{1,0},{2,3},{3,2},{4,5},{5,4},{6,7},{7,6},{8,9},{9,8},{10,11... | collective-permute-start | bytes 393224 | tf_op jit(solution)/shard_map/ppermute | solution.py:41
  33.1 1.4 %collective-permute-start.7 = (bf16[512,128]{1,0:T(8,128)(2,1)S(1)}, bf16[512,128]{1,0:T(8,128)(2,1)S(1)}, u32[]{:S(2)}, u32[]{:S(2)}) collective-permute-start(bf16[512,128]{1,0:T(8,128)(2,1)S(1)} %get-tuple-element.39), channel_id=1, source_target_pairs={{0,4},{1,5},{2,6},{3,7},{4,0},{5,1},{6,2},{7,3},{8,12},{9,13},{10,... | collective-permute-start | bytes 393224 | tf_op jit(solution)/shard_map/ppermute | solution.py:41
  34.8 3.6 %features.1 = (bf16[8,128,96]{2,1,0:T(8,128)(2,1)}, f32[512,128]{1,0:T(8,128)S(1)}) custom-call(bf16[8,128,128]{2,1,0:T(8,128)(2,1)S(1)} %get-tuple-element.24.center_ref, bf16[10,144,128]{2,1,0:T(8,128)(2,1)S(1)} %get-tuple-element.32.grad_ref, bf16[27,96,96]{2,1,0:T(8,128)(2,1)} %w1_in.3, ...), custom_call_target="tpu_custom_call", output_to_operand_aliasing={{1}: (3, {})} | custom-call | tf_op jit(solution)/shard_map/features/pallas_call | solution.py:558
  38.5 2.7 %collective-permute-done.7 = bf16[512,128]{1,0:T(8,128)(2,1)S(1)} collective-permute-done((bf16[512,128]{1,0:T(8,128)(2,1)S(1)}, bf16[512,128]{1,0:T(8,128)(2,1)S(1)}, u32[]{:S(2)}, u32[]{:S(2)}) %collective-permute-start.7) | collective-permute-done | bytes 131104 | tf_op jit(solution)/shard_map/ppermute | solution.py:41
  41.2 2.1 %collective-permute-start.9 = (bf16[512,128]{1,0:T(8,128)(2,1)S(1)}, bf16[512,128]{1,0:T(8,128)(2,1)S(1)}, u32[]{:S(2)}, u32[]{:S(2)}) collective-permute-start(bf16[512,128]{1,0:T(8,128)(2,1)S(1)} %add_convert_fusion.2), channel_id=1, source_target_pairs={{0,8},{1,9},{2,10},{3,11},{4,12},{5,13},{6,14},{7,15},{8,0},{9,1},... | collective-permute-start | bytes 393224 | tf_op jit(solution)/shard_map/ppermute | solution.py:41
  43.3 2.9 %collective-permute-done.9 = bf16[512,128]{1,0:T(8,128)(2,1)S(1)} collective-permute-done((bf16[512,128]{1,0:T(8,128)(2,1)S(1)}, bf16[512,128]{1,0:T(8,128)(2,1)S(1)}, u32[]{:S(2)}, u32[]{:S(2)}) %collective-permute-start.9) | collective-permute-done | bytes 131104 | tf_op jit(solution)/shard_map/ppermute | solution.py:41
  46.3 3.1 %collective-permute-start.10 = (bf16[512,128]{1,0:T(8,128)(2,1)S(1)}, bf16[512,128]{1,0:T(8,128)(2,1)S(1)}, u32[]{:S(2)}, u32[]{:S(2)}) collective-permute-start(bf16[512,128]{1,0:T(8,128)(2,1)S(1)} %add_convert_fusion.1), channel_id=1, source_target_pairs={{0,16},{1,17},{2,18},{3,19},{4,20},{5,21},{6,22},{7,23},{8,24},{9,... | collective-permute-start | bytes 393224 | tf_op jit(solution)/shard_map/ppermute | solution.py:41
  49.4 3.0 %collective-permute-done.10 = bf16[512,128]{1,0:T(8,128)(2,1)S(1)} collective-permute-done((bf16[512,128]{1,0:T(8,128)(2,1)S(1)}, bf16[512,128]{1,0:T(8,128)(2,1)S(1)}, u32[]{:S(2)}, u32[]{:S(2)}) %collective-permute-start.10) | collective-permute-done | bytes 131104 | tf_op jit(solution)/shard_map/ppermute | solution.py:41
  52.4 2.7 %collective-permute-start.13 = (bf16[512,128]{1,0:T(8,128)(2,1)S(1)}, bf16[512,128]{1,0:T(8,128)(2,1)S(1)}, u32[]{:S(2)}, u32[]{:S(2)}) collective-permute-start(bf16[512,128]{1,0:T(8,128)(2,1)S(1)} %add_convert_fusion), channel_id=1, source_target_pairs={{0,1},{1,0},{2,3},{3,2},{4,5},{5,4},{6,7},{7,6},{8,9},{9,8},{10,11... | collective-permute-start | bytes 393224 | tf_op jit(solution)/shard_map/ppermute | solution.py:41
  55.1 0.8 %collective-permute-start.12 = (bf16[512,128]{1,0:T(8,128)(2,1)S(1)}, bf16[512,128]{1,0:T(8,128)(2,1)S(1)}, u32[]{:S(2)}, u32[]{:S(2)}) collective-permute-start(bf16[512,128]{1,0:T(8,128)(2,1)S(1)} %add_convert_fusion), channel_id=1, source_target_pairs={{0,4},{1,5},{2,6},{3,7},{4,0},{5,1},{6,2},{7,3},{8,12},{9,13},{10,... | collective-permute-start | bytes 393224 | tf_op jit(solution)/shard_map/ppermute | solution.py:41
  55.9 0.8 %collective-permute-start.11 = (bf16[512,128]{1,0:T(8,128)(2,1)S(1)}, bf16[512,128]{1,0:T(8,128)(2,1)S(1)}, u32[]{:S(2)}, u32[]{:S(2)}) collective-permute-start(bf16[512,128]{1,0:T(8,128)(2,1)S(1)} %add_convert_fusion), channel_id=1, source_target_pairs={{0,5},{1,4},{2,7},{3,6},{4,1},{5,0},{6,3},{7,2},{8,13},{9,12},{10,... | collective-permute-start | bytes 393224 | tf_op jit(solution)/shard_map/ppermute | solution.py:41
  56.7 2.1 %collective-permute-done.13 = bf16[512,128]{1,0:T(8,128)(2,1)S(1)} collective-permute-done((bf16[512,128]{1,0:T(8,128)(2,1)S(1)}, bf16[512,128]{1,0:T(8,128)(2,1)S(1)}, u32[]{:S(2)}, u32[]{:S(2)}) %collective-permute-start.13) | collective-permute-done | bytes 131104 | tf_op jit(solution)/shard_map/ppermute | solution.py:41
  58.8 1.3 %collective-permute-done.12 = bf16[512,128]{1,0:T(8,128)(2,1)S(1)} collective-permute-done((bf16[512,128]{1,0:T(8,128)(2,1)S(1)}, bf16[512,128]{1,0:T(8,128)(2,1)S(1)}, u32[]{:S(2)}, u32[]{:S(2)}) %collective-permute-start.12) | collective-permute-done | bytes 131104 | tf_op jit(solution)/shard_map/ppermute | solution.py:41
  60.1 1.7 %collective-permute-done.11 = bf16[512,128]{1,0:T(8,128)(2,1)S(1)} collective-permute-done((bf16[512,128]{1,0:T(8,128)(2,1)S(1)}, bf16[512,128]{1,0:T(8,128)(2,1)S(1)}, u32[]{:S(2)}, u32[]{:S(2)}) %collective-permute-start.11) | collective-permute-done | bytes 131104 | tf_op jit(solution)/shard_map/ppermute | solution.py:41
  62.0 1.2 %unpack.2 = (f32[27,96,96]{2,1,0:T(8,128)}, f32[27,96,96]{2,1,0:T(8,128)}) custom-call(s32[1]{0:T(128)} %bitcast.9.first_ref_flag, bf16[2048,128]{1,0:T(8,128)(2,1)S(1)} %pad_maximum_fusion.packed_ref), custom_call_target="tpu_custom_call" | custom-call | tf_op jit(solution)/shard_map/unpack/pallas_call | solution.py:597
  63.9 1.2 %unpack.3 = (f32[27,96,96]{2,1,0:T(8,128)}, f32[27,96,96]{2,1,0:T(8,128)}) custom-call(s32[1]{0:T(128)} %bitcast.8.first_ref_flag, bf16[2048,128]{1,0:T(8,128)(2,1)S(1)} %collective-permute-done.14.packed_ref, f32[27,96,96]{2,1,0:T(8,128)} %get-tuple-element.41.refs_0_, ...), custom_call_target="tpu_custom_call", output_to_operand_aliasing={{0}: (2, {}), {1}: (3, {})} | custom-call | tf_op jit(solution)/shard_map/unpack/pallas_call | solution.py:597
  (18 shorter events, 2.7 us)
Async XLA Ops:
  2.9 8.5 %collective-permute-start = (bf16[4,128,128]{2,1,0:T(8,128)(2,1)S(1)}, bf16[4,128,128]{2,1,0:T(8,128)(2,1)S(1)}, u32[]{:S(2)}, u32[]{:S(2)}) collective-permute-start(bf16[4,128,128]{2,1,0:T(8,128)(2,1)S(1)} %get-tuple-element.27), channel_id=1, source_target_pairs={{0,2},{1,3},{2,0},{3,1},{4,6},{5,7},{6,4},{7,5},{8,10},{9,11},{10,... | collective-permute-start | bytes 393224 | tf_op jit(solution)/shard_map/ppermute | solution.py:41
  3.4 8.0 %collective-permute-start.1 = (bf16[4,128,128]{2,1,0:T(8,128)(2,1)S(1)}, bf16[4,128,128]{2,1,0:T(8,128)(2,1)S(1)}, u32[]{:S(2)}, u32[]{:S(2)}) collective-permute-start(bf16[4,128,128]{2,1,0:T(8,128)(2,1)S(1)} %get-tuple-element.28), channel_id=1, source_target_pairs={{0,1},{1,0},{2,4},{3,5},{4,2},{5,3},{6,8},{7,9},{8,6},{9,7},{10,12... | collective-permute-start | bytes 393224 | tf_op jit(solution)/shard_map/ppermute | solution.py:41
  6.0 5.4 %collective-permute-start.2 = (bf16[8,32,128]{2,1,0:T(8,128)(2,1)S(1)}, bf16[8,32,128]{2,1,0:T(8,128)(2,1)S(1)}, u32[]{:S(2)}, u32[]{:S(2)}) collective-permute-start(bf16[8,32,128]{2,1,0:T(8,128)(2,1)S(1)} %get-tuple-element.29), channel_id=1, source_target_pairs={{0,1},{1,0},{2,3},{3,2},{4,5},{5,4},{6,7},{7,6},{8,9},{9,8},{10,11... | collective-permute-start | bytes 196616 | tf_op jit(solution)/shard_map/ppermute | solution.py:41
  6.1 4.7 %collective-permute-start.3 = (bf16[4,32,128]{2,1,0:T(8,128)(2,1)S(1)}, bf16[4,32,128]{2,1,0:T(8,128)(2,1)S(1)}, u32[]{:S(2)}, u32[]{:S(2)}) collective-permute-start(bf16[4,32,128]{2,1,0:T(8,128)(2,1)S(1)} %get-tuple-element.30), channel_id=1, source_target_pairs={{0,3},{1,2},{2,1},{3,0},{4,7},{5,6},{6,5},{7,4},{8,11},{9,10},{10,... | collective-permute-start | bytes 98312 | tf_op jit(solution)/shard_map/ppermute | solution.py:41
  7.5 3.9 %collective-permute-start.4 = (bf16[4,32,128]{2,1,0:T(8,128)(2,1)S(1)}, bf16[4,32,128]{2,1,0:T(8,128)(2,1)S(1)}, u32[]{:S(2)}, u32[]{:S(2)}) collective-permute-start(bf16[4,32,128]{2,1,0:T(8,128)(2,1)S(1)} %get-tuple-element.31), channel_id=1, source_target_pairs={{0,1},{1,0},{2,5},{3,4},{4,3},{5,2},{6,9},{7,8},{8,7},{9,6},{10,13... | collective-permute-start | bytes 98312 | tf_op jit(solution)/shard_map/ppermute | solution.py:41
  28.6 2.6 %collective-permute-start.5 = (bf16[2048,128]{1,0:T(8,128)(2,1)S(1)}, bf16[2048,128]{1,0:T(8,128)(2,1)S(1)}, u32[]{:S(2)}, u32[]{:S(2)}) collective-permute-start(bf16[2048,128]{1,0:T(8,128)(2,1)S(1)} %get-tuple-element.34), channel_id=1, source_target_pairs={{0,2},{1,3},{2,0},{3,1},{4,6},{5,7},{6,4},{7,5},{8,10},{9,11},{10,... | collective-permute-start | bytes 1572872 | tf_op jit(solution)/shard_map/ppermute | solution.py:41
  31.2 7.2 %collective-permute-start.6 = (bf16[512,128]{1,0:T(8,128)(2,1)S(1)}, bf16[512,128]{1,0:T(8,128)(2,1)S(1)}, u32[]{:S(2)}, u32[]{:S(2)}) collective-permute-start(bf16[512,128]{1,0:T(8,128)(2,1)S(1)} %get-tuple-element.38), channel_id=1, source_target_pairs={{0,1},{1,0},{2,3},{3,2},{4,5},{5,4},{6,7},{7,6},{8,9},{9,8},{10,11... | collective-permute-start | bytes 393224 | tf_op jit(solution)/shard_map/ppermute | solution.py:41
  33.1 8.1 %collective-permute-start.7 = (bf16[512,128]{1,0:T(8,128)(2,1)S(1)}, bf16[512,128]{1,0:T(8,128)(2,1)S(1)}, u32[]{:S(2)}, u32[]{:S(2)}) collective-permute-start(bf16[512,128]{1,0:T(8,128)(2,1)S(1)} %get-tuple-element.39), channel_id=1, source_target_pairs={{0,4},{1,5},{2,6},{3,7},{4,0},{5,1},{6,2},{7,3},{8,12},{9,13},{10,... | collective-permute-start | bytes 393224 | tf_op jit(solution)/shard_map/ppermute | solution.py:41
  34.5 6.7 %collective-permute-start.8 = (bf16[512,128]{1,0:T(8,128)(2,1)S(1)}, bf16[512,128]{1,0:T(8,128)(2,1)S(1)}, u32[]{:S(2)}, u32[]{:S(2)}) collective-permute-start(bf16[512,128]{1,0:T(8,128)(2,1)S(1)} %get-tuple-element.40), channel_id=1, source_target_pairs={{0,5},{1,4},{2,7},{3,6},{4,1},{5,0},{6,3},{7,2},{8,13},{9,12},{10,... | collective-permute-start | bytes 393224 | tf_op jit(solution)/shard_map/ppermute | solution.py:41
  41.2 5.0 %collective-permute-start.9 = (bf16[512,128]{1,0:T(8,128)(2,1)S(1)}, bf16[512,128]{1,0:T(8,128)(2,1)S(1)}, u32[]{:S(2)}, u32[]{:S(2)}) collective-permute-start(bf16[512,128]{1,0:T(8,128)(2,1)S(1)} %add_convert_fusion.2), channel_id=1, source_target_pairs={{0,8},{1,9},{2,10},{3,11},{4,12},{5,13},{6,14},{7,15},{8,0},{9,1},... | collective-permute-start | bytes 393224 | tf_op jit(solution)/shard_map/ppermute | solution.py:41
  46.3 6.0 %collective-permute-start.10 = (bf16[512,128]{1,0:T(8,128)(2,1)S(1)}, bf16[512,128]{1,0:T(8,128)(2,1)S(1)}, u32[]{:S(2)}, u32[]{:S(2)}) collective-permute-start(bf16[512,128]{1,0:T(8,128)(2,1)S(1)} %add_convert_fusion.1), channel_id=1, source_target_pairs={{0,16},{1,17},{2,18},{3,19},{4,20},{5,21},{6,22},{7,23},{8,24},{9,... | collective-permute-start | bytes 393224 | tf_op jit(solution)/shard_map/ppermute | solution.py:41
  52.4 6.4 %collective-permute-start.13 = (bf16[512,128]{1,0:T(8,128)(2,1)S(1)}, bf16[512,128]{1,0:T(8,128)(2,1)S(1)}, u32[]{:S(2)}, u32[]{:S(2)}) collective-permute-start(bf16[512,128]{1,0:T(8,128)(2,1)S(1)} %add_convert_fusion), channel_id=1, source_target_pairs={{0,1},{1,0},{2,3},{3,2},{4,5},{5,4},{6,7},{7,6},{8,9},{9,8},{10,11... | collective-permute-start | bytes 393224 | tf_op jit(solution)/shard_map/ppermute | solution.py:41
  55.1 5.0 %collective-permute-start.12 = (bf16[512,128]{1,0:T(8,128)(2,1)S(1)}, bf16[512,128]{1,0:T(8,128)(2,1)S(1)}, u32[]{:S(2)}, u32[]{:S(2)}) collective-permute-start(bf16[512,128]{1,0:T(8,128)(2,1)S(1)} %add_convert_fusion), channel_id=1, source_target_pairs={{0,4},{1,5},{2,6},{3,7},{4,0},{5,1},{6,2},{7,3},{8,12},{9,13},{10,... | collective-permute-start | bytes 393224 | tf_op jit(solution)/shard_map/ppermute | solution.py:41
  55.9 5.9 %collective-permute-start.11 = (bf16[512,128]{1,0:T(8,128)(2,1)S(1)}, bf16[512,128]{1,0:T(8,128)(2,1)S(1)}, u32[]{:S(2)}, u32[]{:S(2)}) collective-permute-start(bf16[512,128]{1,0:T(8,128)(2,1)S(1)} %add_convert_fusion), channel_id=1, source_target_pairs={{0,5},{1,4},{2,7},{3,6},{4,1},{5,0},{6,3},{7,2},{8,13},{9,12},{10,... | collective-permute-start | bytes 393224 | tf_op jit(solution)/shard_map/ppermute | solution.py:41
  61.9 2.0 %collective-permute-start.14 = (bf16[2048,128]{1,0:T(8,128)(2,1)S(1)}, bf16[2048,128]{1,0:T(8,128)(2,1)S(1)}, u32[]{:S(2)}, u32[]{:S(2)}) collective-permute-start(bf16[2048,128]{1,0:T(8,128)(2,1)S(1)} %pad_maximum_fusion.packed_ref), channel_id=1, source_target_pairs={{0,2},{1,3},{2,0},{3,1},{4,6},{5,7},{6,4},{7,5},{8,10},{9,11},{10,... | collective-permute-start | bytes 1572872 | tf_op jit(solution)/shard_map/ppermute | solution.py:41

commit v12 on v11

--- a/solution.py
+++ b/solution.py
@@ -335,7 +335,7 @@
     copy.wait()
     put_ahead(ahead2_ref, w2_ref, channels)
     put_back(back2_ref, w2_ref, channels)
-    for first, stop in grouped((planes - 2) // 2, 3):
+    for first, stop in grouped((planes - 2) // 2, 1):
         for i, parity, value in convolve(stack0, ahead1_ref, first, stop, rows, upward):
             plane = 2 * i + parity
             mask = mask_ref[plane + 1]
@@ -348,7 +348,7 @@
     class_lane = (lane[0:rows2] > channels) & (lane[0:rows2] <= channels + classes)
     here = slice(2 * upward, 2 * upward + rows2)
 
-    for first, stop in grouped((planes - 4) // 2, 3):
+    for first, stop in grouped((planes - 4) // 2, 1):
         for i, parity, value in convolve(stack1, ahead2_ref, first, stop, rows2, upward):
             plane = 2 * i + parity
             mask = mask_ref[plane + 2, here]
@@ -371,7 +371,7 @@
         kept_ref[t * channels : (t + 1) * channels, :] = tile.astype(BF16)
 
     there = slice(2 * upward + upward, 2 * upward + upward + rows3)
-    for first, stop in grouped((planes - 6) // 2, 3):
+    for first, stop in grouped((planes - 6) // 2, 1):
         for i, parity, value in convolve(stack2, back2_ref, first, stop, rows3, upward):
             plane = 2 * i + parity
             g_p1 = slope_ref[plane + 2, there] * value

time: 65.3 us -> 64.7 us (level)
  Pallas kernels: 27.4 us -> 26.6 us
    pallas_call x1, Pallas kernels: 17.1 us -> 16.4 us  [per_device(): pl.pallas_call(functools.partial(whole_kernel, channels, classes, east, n...]
where the time goes in v12:
time: 64.7 us; the launch traced here: 64.5 us
  Pallas kernels  26.6 us (41%)
  starting transfers between devices  20.2 us (31%)
  waiting for transfers between devices  16.5 us (26%)
  between operations  0.91 us (1%)
    ppermute x15, starting transfers between devices, exchange(): return lax.ppermute(value, ('east', 'north'), pairs)  20.2 us
    ppermute x15, waiting for transfers between devices, exchange(): return lax.ppermute(value, ('east', 'north'), pairs)  16.5 us
    pallas_call x1, Pallas kernels, per_device(): pl.pallas_call(functools.partial(whole_kernel, channels, classes, east, n...  16.4 us
    pallas_call x1, Pallas kernels, beside(): pl.pallas_call(functools.partial(last_kernel, channels, east, north, upwa...  3.62 us
    pallas_call x2, Pallas kernels, unpack(): pl.pallas_call(functools.partial(unpack_kernel, channels, scale, bool(ali...  2.43 us
    pallas_call x1, Pallas kernels, per_device(): pl.pallas_call(functools.partial(prepare_kernel, channels, upward, edge),...  2.28 us
    pallas_call x1, Pallas kernels, per_device(): pl.pallas_call(functools.partial(weights_kernel, channels, classes), out_...  1.81 us
  transfers between devices with their start and end apart: 15, of which 9 were waited for; matrix products, arithmetic and copies ran while one was open for 0% of the time, Pallas kernels for 10%

profile of v12, /device:TPU:0, one launch (start us, length us, event | category | flops | bytes accessed | tf_op | source)
XLA Modules:
  0.0 64.5 jit_solution(8203395133170233025)
XLA Ops:
  0.6 2.3 %prepare.1 = (bf16[8,128,128]{2,1,0:T(8,128)(2,1)S(1)}, bf16[4,128,128]{2,1,0:T(8,128)(2,1)S(1)}, bf16[4,128,128]{2,1,0:T(8,128)(2,1)S(1)}, bf16[8,32,128]{2,1,0...) custom-call(s32[1,1,2]{2,1,0:T(1,128)} %bitcast.15, bf16[8,128,96]{2,1,0:T(8,128)(2,1)} %bitcast.12, ...), custom_call_target="tpu_custom_call" | custom-call | tf_op jit(solution)/shard_map/prepare/pallas_call | solution.py:481
  3.4 2.6 %collective-permute-start.1 = (bf16[4,128,128]{2,1,0:T(8,128)(2,1)S(1)}, bf16[4,128,128]{2,1,0:T(8,128)(2,1)S(1)}, u32[]{:S(2)}, u32[]{:S(2)}) collective-permute-start(bf16[4,128,128]{2,1,0:T(8,128)(2,1)S(1)} %get-tuple-element.28), channel_id=1, source_target_pairs={{0,1},{1,0},{2,4},{3,5},{4,2},{5,3},{6,8},{7,9},{8,6},{9,7},{10,12... | collective-permute-start | bytes 393224 | tf_op jit(solution)/shard_map/ppermute | solution.py:41
  6.1 1.4 %collective-permute-start.3 = (bf16[4,32,128]{2,1,0:T(8,128)(2,1)S(1)}, bf16[4,32,128]{2,1,0:T(8,128)(2,1)S(1)}, u32[]{:S(2)}, u32[]{:S(2)}) collective-permute-start(bf16[4,32,128]{2,1,0:T(8,128)(2,1)S(1)} %get-tuple-element.30), channel_id=1, source_target_pairs={{0,3},{1,2},{2,1},{3,0},{4,7},{5,6},{6,5},{7,4},{8,11},{9,10},{10,... | collective-permute-start | bytes 98312 | tf_op jit(solution)/shard_map/ppermute | solution.py:41
  7.5 1.5 %collective-permute-start.4 = (bf16[4,32,128]{2,1,0:T(8,128)(2,1)S(1)}, bf16[4,32,128]{2,1,0:T(8,128)(2,1)S(1)}, u32[]{:S(2)}, u32[]{:S(2)}) collective-permute-start(bf16[4,32,128]{2,1,0:T(8,128)(2,1)S(1)} %get-tuple-element.31), channel_id=1, source_target_pairs={{0,1},{1,0},{2,5},{3,4},{4,3},{5,2},{6,9},{7,8},{8,7},{9,6},{10,13... | collective-permute-start | bytes 98312 | tf_op jit(solution)/shard_map/ppermute | solution.py:41
  9.0 1.8 %weights.1 = (bf16[4608,256]{1,0:T(8,128)(2,1)S(1)}, bf16[128,128]{1,0:T(8,128)(2,1)S(1)}) custom-call(bf16[27,96,96]{2,1,0:T(8,128)(2,1)} %w1_in.3, bf16[13,96]{1,0:T(8,128)(2,1)} %head_in.1), custom_call_target="tpu_custom_call" | custom-call | tf_op jit(solution)/shard_map/weights/pallas_call | solution.py:516
  11.4 16.4 %fields.1 = (bf16[10,144,128]{2,1,0:T(8,128)(2,1)S(1)}, bf16[2048,128]{1,0:T(8,128)(2,1)S(1)}, bf16[2048,128]{1,0:T(8,128)(2,1)S(1)}) custom-call(bf16[4608,256]{1,0:T(8,128)(2,1)S(1)} %get-tuple-element.25.ahead1_ref, bf16[27,96,96]{2,1,0:T(8,128)(2,1)} %w2_in.1, bf16[128,128]{1,0:T(8,128)(2,1)S(1)} %get-tuple-element.26.head_ref, ...), custom_call_target="tpu_custom_call" | custom-call | tf_op jit(solution)/shard_map/fields/pallas_call | solution.py:529
  27.8 1.0 %collective-permute-start.5 = (bf16[2048,128]{1,0:T(8,128)(2,1)S(1)}, bf16[2048,128]{1,0:T(8,128)(2,1)S(1)}, u32[]{:S(2)}, u32[]{:S(2)}) collective-permute-start(bf16[2048,128]{1,0:T(8,128)(2,1)S(1)} %get-tuple-element.34), channel_id=1, source_target_pairs={{0,2},{1,3},{2,0},{3,1},{4,6},{5,7},{6,4},{7,5},{8,10},{9,11},{10,... | collective-permute-start | bytes 1572872 | tf_op jit(solution)/shard_map/ppermute | solution.py:41
  28.8 1.5 %collective-permute-done.5.came_ref = bf16[2048,128]{1,0:T(8,128)(2,1)S(1)} collective-permute-done((bf16[2048,128]{1,0:T(8,128)(2,1)S(1)}, bf16[2048,128]{1,0:T(8,128)(2,1)S(1)}, u32[]{:S(2)}, u32[]{:S(2)}) %collective-permute-start.5) | collective-permute-done | bytes 524320 | tf_op jit(solution)/shard_map/ppermute | solution.py:41
  30.5 1.8 %collective-permute-start.6 = (bf16[512,128]{1,0:T(8,128)(2,1)S(1)}, bf16[512,128]{1,0:T(8,128)(2,1)S(1)}, u32[]{:S(2)}, u32[]{:S(2)}) collective-permute-start(bf16[512,128]{1,0:T(8,128)(2,1)S(1)} %get-tuple-element.38), channel_id=1, source_target_pairs={{0,1},{1,0},{2,3},{3,2},{4,5},{5,4},{6,7},{7,6},{8,9},{9,8},{10,11... | collective-permute-start | bytes 393224 | tf_op jit(solution)/shard_map/ppermute | solution.py:41
  32.4 1.4 %collective-permute-start.7 = (bf16[512,128]{1,0:T(8,128)(2,1)S(1)}, bf16[512,128]{1,0:T(8,128)(2,1)S(1)}, u32[]{:S(2)}, u32[]{:S(2)}) collective-permute-start(bf16[512,128]{1,0:T(8,128)(2,1)S(1)} %get-tuple-element.39), channel_id=1, source_target_pairs={{0,4},{1,5},{2,6},{3,7},{4,0},{5,1},{6,2},{7,3},{8,12},{9,13},{10,... | collective-permute-start | bytes 393224 | tf_op jit(solution)/shard_map/ppermute | solution.py:41
  34.1 3.6 %features.1 = (bf16[8,128,96]{2,1,0:T(8,128)(2,1)}, f32[512,128]{1,0:T(8,128)S(1)}) custom-call(bf16[8,128,128]{2,1,0:T(8,128)(2,1)S(1)} %get-tuple-element.24.center_ref, bf16[10,144,128]{2,1,0:T(8,128)(2,1)S(1)} %get-tuple-element.32.grad_ref, bf16[27,96,96]{2,1,0:T(8,128)(2,1)} %w1_in.3, ...), custom_call_target="tpu_custom_call", output_to_operand_aliasing={{1}: (3, {})} | custom-call | tf_op jit(solution)/shard_map/features/pallas_call | solution.py:558
  37.7 2.7 %collective-permute-done.7 = bf16[512,128]{1,0:T(8,128)(2,1)S(1)} collective-permute-done((bf16[512,128]{1,0:T(8,128)(2,1)S(1)}, bf16[512,128]{1,0:T(8,128)(2,1)S(1)}, u32[]{:S(2)}, u32[]{:S(2)}) %collective-permute-start.7) | collective-permute-done | bytes 131104 | tf_op jit(solution)/shard_map/ppermute | solution.py:41
  40.5 2.1 %collective-permute-start.9 = (bf16[512,128]{1,0:T(8,128)(2,1)S(1)}, bf16[512,128]{1,0:T(8,128)(2,1)S(1)}, u32[]{:S(2)}, u32[]{:S(2)}) collective-permute-start(bf16[512,128]{1,0:T(8,128)(2,1)S(1)} %add_convert_fusion.2), channel_id=1, source_target_pairs={{0,8},{1,9},{2,10},{3,11},{4,12},{5,13},{6,14},{7,15},{8,0},{9,1},... | collective-permute-start | bytes 393224 | tf_op jit(solution)/shard_map/ppermute | solution.py:41
  42.6 2.9 %collective-permute-done.9 = bf16[512,128]{1,0:T(8,128)(2,1)S(1)} collective-permute-done((bf16[512,128]{1,0:T(8,128)(2,1)S(1)}, bf16[512,128]{1,0:T(8,128)(2,1)S(1)}, u32[]{:S(2)}, u32[]{:S(2)}) %collective-permute-start.9) | collective-permute-done | bytes 131104 | tf_op jit(solution)/shard_map/ppermute | solution.py:41
  45.6 3.1 %collective-permute-start.10 = (bf16[512,128]{1,0:T(8,128)(2,1)S(1)}, bf16[512,128]{1,0:T(8,128)(2,1)S(1)}, u32[]{:S(2)}, u32[]{:S(2)}) collective-permute-start(bf16[512,128]{1,0:T(8,128)(2,1)S(1)} %add_convert_fusion.1), channel_id=1, source_target_pairs={{0,16},{1,17},{2,18},{3,19},{4,20},{5,21},{6,22},{7,23},{8,24},{9,... | collective-permute-start | bytes 393224 | tf_op jit(solution)/shard_map/ppermute | solution.py:41
  48.7 3.0 %collective-permute-done.10 = bf16[512,128]{1,0:T(8,128)(2,1)S(1)} collective-permute-done((bf16[512,128]{1,0:T(8,128)(2,1)S(1)}, bf16[512,128]{1,0:T(8,128)(2,1)S(1)}, u32[]{:S(2)}, u32[]{:S(2)}) %collective-permute-start.10) | collective-permute-done | bytes 131104 | tf_op jit(solution)/shard_map/ppermute | solution.py:41
  51.7 2.7 %collective-permute-start.13 = (bf16[512,128]{1,0:T(8,128)(2,1)S(1)}, bf16[512,128]{1,0:T(8,128)(2,1)S(1)}, u32[]{:S(2)}, u32[]{:S(2)}) collective-permute-start(bf16[512,128]{1,0:T(8,128)(2,1)S(1)} %add_convert_fusion), channel_id=1, source_target_pairs={{0,1},{1,0},{2,3},{3,2},{4,5},{5,4},{6,7},{7,6},{8,9},{9,8},{10,11... | collective-permute-start | bytes 393224 | tf_op jit(solution)/shard_map/ppermute | solution.py:41
  54.4 0.8 %collective-permute-start.12 = (bf16[512,128]{1,0:T(8,128)(2,1)S(1)}, bf16[512,128]{1,0:T(8,128)(2,1)S(1)}, u32[]{:S(2)}, u32[]{:S(2)}) collective-permute-start(bf16[512,128]{1,0:T(8,128)(2,1)S(1)} %add_convert_fusion), channel_id=1, source_target_pairs={{0,4},{1,5},{2,6},{3,7},{4,0},{5,1},{6,2},{7,3},{8,12},{9,13},{10,... | collective-permute-start | bytes 393224 | tf_op jit(solution)/shard_map/ppermute | solution.py:41
  55.2 0.8 %collective-permute-start.11 = (bf16[512,128]{1,0:T(8,128)(2,1)S(1)}, bf16[512,128]{1,0:T(8,128)(2,1)S(1)}, u32[]{:S(2)}, u32[]{:S(2)}) collective-permute-start(bf16[512,128]{1,0:T(8,128)(2,1)S(1)} %add_convert_fusion), channel_id=1, source_target_pairs={{0,5},{1,4},{2,7},{3,6},{4,1},{5,0},{6,3},{7,2},{8,13},{9,12},{10,... | collective-permute-start | bytes 393224 | tf_op jit(solution)/shard_map/ppermute | solution.py:41
  56.0 2.0 %collective-permute-done.13 = bf16[512,128]{1,0:T(8,128)(2,1)S(1)} collective-permute-done((bf16[512,128]{1,0:T(8,128)(2,1)S(1)}, bf16[512,128]{1,0:T(8,128)(2,1)S(1)}, u32[]{:S(2)}, u32[]{:S(2)}) %collective-permute-start.13) | collective-permute-done | bytes 131104 | tf_op jit(solution)/shard_map/ppermute | solution.py:41
  58.0 1.3 %collective-permute-done.12 = bf16[512,128]{1,0:T(8,128)(2,1)S(1)} collective-permute-done((bf16[512,128]{1,0:T(8,128)(2,1)S(1)}, bf16[512,128]{1,0:T(8,128)(2,1)S(1)}, u32[]{:S(2)}, u32[]{:S(2)}) %collective-permute-start.12) | collective-permute-done | bytes 131104 | tf_op jit(solution)/shard_map/ppermute | solution.py:41
  59.3 1.7 %collective-permute-done.11 = bf16[512,128]{1,0:T(8,128)(2,1)S(1)} collective-permute-done((bf16[512,128]{1,0:T(8,128)(2,1)S(1)}, bf16[512,128]{1,0:T(8,128)(2,1)S(1)}, u32[]{:S(2)}, u32[]{:S(2)}) %collective-permute-start.11) | collective-permute-done | bytes 131104 | tf_op jit(solution)/shard_map/ppermute | solution.py:41
  61.2 1.2 %unpack.2 = (f32[27,96,96]{2,1,0:T(8,128)}, f32[27,96,96]{2,1,0:T(8,128)}) custom-call(s32[1]{0:T(128)} %bitcast.9.first_ref_flag, bf16[2048,128]{1,0:T(8,128)(2,1)S(1)} %pad_maximum_fusion.packed_ref), custom_call_target="tpu_custom_call" | custom-call | tf_op jit(solution)/shard_map/unpack/pallas_call | solution.py:597
  63.1 1.2 %unpack.3 = (f32[27,96,96]{2,1,0:T(8,128)}, f32[27,96,96]{2,1,0:T(8,128)}) custom-call(s32[1]{0:T(128)} %bitcast.8.first_ref_flag, bf16[2048,128]{1,0:T(8,128)(2,1)S(1)} %collective-permute-done.14.packed_ref, f32[27,96,96]{2,1,0:T(8,128)} %get-tuple-element.41.refs_0_, ...), custom_call_target="tpu_custom_call", output_to_operand_aliasing={{0}: (2, {}), {1}: (3, {})} | custom-call | tf_op jit(solution)/shard_map/unpack/pallas_call | solution.py:597
  (18 shorter events, 2.7 us)
Async XLA Ops:
  2.9 8.5 %collective-permute-start = (bf16[4,128,128]{2,1,0:T(8,128)(2,1)S(1)}, bf16[4,128,128]{2,1,0:T(8,128)(2,1)S(1)}, u32[]{:S(2)}, u32[]{:S(2)}) collective-permute-start(bf16[4,128,128]{2,1,0:T(8,128)(2,1)S(1)} %get-tuple-element.27), channel_id=1, source_target_pairs={{0,2},{1,3},{2,0},{3,1},{4,6},{5,7},{6,4},{7,5},{8,10},{9,11},{10,... | collective-permute-start | bytes 393224 | tf_op jit(solution)/shard_map/ppermute | solution.py:41
  3.4 8.0 %collective-permute-start.1 = (bf16[4,128,128]{2,1,0:T(8,128)(2,1)S(1)}, bf16[4,128,128]{2,1,0:T(8,128)(2,1)S(1)}, u32[]{:S(2)}, u32[]{:S(2)}) collective-permute-start(bf16[4,128,128]{2,1,0:T(8,128)(2,1)S(1)} %get-tuple-element.28), channel_id=1, source_target_pairs={{0,1},{1,0},{2,4},{3,5},{4,2},{5,3},{6,8},{7,9},{8,6},{9,7},{10,12... | collective-permute-start | bytes 393224 | tf_op jit(solution)/shard_map/ppermute | solution.py:41
  6.0 5.4 %collective-permute-start.2 = (bf16[8,32,128]{2,1,0:T(8,128)(2,1)S(1)}, bf16[8,32,128]{2,1,0:T(8,128)(2,1)S(1)}, u32[]{:S(2)}, u32[]{:S(2)}) collective-permute-start(bf16[8,32,128]{2,1,0:T(8,128)(2,1)S(1)} %get-tuple-element.29), channel_id=1, source_target_pairs={{0,1},{1,0},{2,3},{3,2},{4,5},{5,4},{6,7},{7,6},{8,9},{9,8},{10,11... | collective-permute-start | bytes 196616 | tf_op jit(solution)/shard_map/ppermute | solution.py:41
  6.1 4.7 %collective-permute-start.3 = (bf16[4,32,128]{2,1,0:T(8,128)(2,1)S(1)}, bf16[4,32,128]{2,1,0:T(8,128)(2,1)S(1)}, u32[]{:S(2)}, u32[]{:S(2)}) collective-permute-start(bf16[4,32,128]{2,1,0:T(8,128)(2,1)S(1)} %get-tuple-element.30), channel_id=1, source_target_pairs={{0,3},{1,2},{2,1},{3,0},{4,7},{5,6},{6,5},{7,4},{8,11},{9,10},{10,... | collective-permute-start | bytes 98312 | tf_op jit(solution)/shard_map/ppermute | solution.py:41
  7.5 3.9 %collective-permute-start.4 = (bf16[4,32,128]{2,1,0:T(8,128)(2,1)S(1)}, bf16[4,32,128]{2,1,0:T(8,128)(2,1)S(1)}, u32[]{:S(2)}, u32[]{:S(2)}) collective-permute-start(bf16[4,32,128]{2,1,0:T(8,128)(2,1)S(1)} %get-tuple-element.31), channel_id=1, source_target_pairs={{0,1},{1,0},{2,5},{3,4},{4,3},{5,2},{6,9},{7,8},{8,7},{9,6},{10,13... | collective-permute-start | bytes 98312 | tf_op jit(solution)/shard_map/ppermute | solution.py:41
  27.8 2.6 %collective-permute-start.5 = (bf16[2048,128]{1,0:T(8,128)(2,1)S(1)}, bf16[2048,128]{1,0:T(8,128)(2,1)S(1)}, u32[]{:S(2)}, u32[]{:S(2)}) collective-permute-start(bf16[2048,128]{1,0:T(8,128)(2,1)S(1)} %get-tuple-element.34), channel_id=1, source_target_pairs={{0,2},{1,3},{2,0},{3,1},{4,6},{5,7},{6,4},{7,5},{8,10},{9,11},{10,... | collective-permute-start | bytes 1572872 | tf_op jit(solution)/shard_map/ppermute | solution.py:41
  30.5 7.2 %collective-permute-start.6 = (bf16[512,128]{1,0:T(8,128)(2,1)S(1)}, bf16[512,128]{1,0:T(8,128)(2,1)S(1)}, u32[]{:S(2)}, u32[]{:S(2)}) collective-permute-start(bf16[512,128]{1,0:T(8,128)(2,1)S(1)} %get-tuple-element.38), channel_id=1, source_target_pairs={{0,1},{1,0},{2,3},{3,2},{4,5},{5,4},{6,7},{7,6},{8,9},{9,8},{10,11... | collective-permute-start | bytes 393224 | tf_op jit(solution)/shard_map/ppermute | solution.py:41
  32.4 8.1 %collective-permute-start.7 = (bf16[512,128]{1,0:T(8,128)(2,1)S(1)}, bf16[512,128]{1,0:T(8,128)(2,1)S(1)}, u32[]{:S(2)}, u32[]{:S(2)}) collective-permute-start(bf16[512,128]{1,0:T(8,128)(2,1)S(1)} %get-tuple-element.39), channel_id=1, source_target_pairs={{0,4},{1,5},{2,6},{3,7},{4,0},{5,1},{6,2},{7,3},{8,12},{9,13},{10,... | collective-permute-start | bytes 393224 | tf_op jit(solution)/shard_map/ppermute | solution.py:41
  33.7 6.7 %collective-permute-start.8 = (bf16[512,128]{1,0:T(8,128)(2,1)S(1)}, bf16[512,128]{1,0:T(8,128)(2,1)S(1)}, u32[]{:S(2)}, u32[]{:S(2)}) collective-permute-start(bf16[512,128]{1,0:T(8,128)(2,1)S(1)} %get-tuple-element.40), channel_id=1, source_target_pairs={{0,5},{1,4},{2,7},{3,6},{4,1},{5,0},{6,3},{7,2},{8,13},{9,12},{10,... | collective-permute-start | bytes 393224 | tf_op jit(solution)/shard_map/ppermute | solution.py:41
  40.5 5.0 %collective-permute-start.9 = (bf16[512,128]{1,0:T(8,128)(2,1)S(1)}, bf16[512,128]{1,0:T(8,128)(2,1)S(1)}, u32[]{:S(2)}, u32[]{:S(2)}) collective-permute-start(bf16[512,128]{1,0:T(8,128)(2,1)S(1)} %add_convert_fusion.2), channel_id=1, source_target_pairs={{0,8},{1,9},{2,10},{3,11},{4,12},{5,13},{6,14},{7,15},{8,0},{9,1},... | collective-permute-start | bytes 393224 | tf_op jit(solution)/shard_map/ppermute | solution.py:41
  45.6 6.1 %collective-permute-start.10 = (bf16[512,128]{1,0:T(8,128)(2,1)S(1)}, bf16[512,128]{1,0:T(8,128)(2,1)S(1)}, u32[]{:S(2)}, u32[]{:S(2)}) collective-permute-start(bf16[512,128]{1,0:T(8,128)(2,1)S(1)} %add_convert_fusion.1), channel_id=1, source_target_pairs={{0,16},{1,17},{2,18},{3,19},{4,20},{5,21},{6,22},{7,23},{8,24},{9,... | collective-permute-start | bytes 393224 | tf_op jit(solution)/shard_map/ppermute | solution.py:41
  51.7 6.3 %collective-permute-start.13 = (bf16[512,128]{1,0:T(8,128)(2,1)S(1)}, bf16[512,128]{1,0:T(8,128)(2,1)S(1)}, u32[]{:S(2)}, u32[]{:S(2)}) collective-permute-start(bf16[512,128]{1,0:T(8,128)(2,1)S(1)} %add_convert_fusion), channel_id=1, source_target_pairs={{0,1},{1,0},{2,3},{3,2},{4,5},{5,4},{6,7},{7,6},{8,9},{9,8},{10,11... | collective-permute-start | bytes 393224 | tf_op jit(solution)/shard_map/ppermute | solution.py:41
  54.4 5.0 %collective-permute-start.12 = (bf16[512,128]{1,0:T(8,128)(2,1)S(1)}, bf16[512,128]{1,0:T(8,128)(2,1)S(1)}, u32[]{:S(2)}, u32[]{:S(2)}) collective-permute-start(bf16[512,128]{1,0:T(8,128)(2,1)S(1)} %add_convert_fusion), channel_id=1, source_target_pairs={{0,4},{1,5},{2,6},{3,7},{4,0},{5,1},{6,2},{7,3},{8,12},{9,13},{10,... | collective-permute-start | bytes 393224 | tf_op jit(solution)/shard_map/ppermute | solution.py:41
  55.2 5.9 %collective-permute-start.11 = (bf16[512,128]{1,0:T(8,128)(2,1)S(1)}, bf16[512,128]{1,0:T(8,128)(2,1)S(1)}, u32[]{:S(2)}, u32[]{:S(2)}) collective-permute-start(bf16[512,128]{1,0:T(8,128)(2,1)S(1)} %add_convert_fusion), channel_id=1, source_target_pairs={{0,5},{1,4},{2,7},{3,6},{4,1},{5,0},{6,3},{7,2},{8,13},{9,12},{10,... | collective-permute-start | bytes 393224 | tf_op jit(solution)/shard_map/ppermute | solution.py:41
  61.1 2.0 %collective-permute-start.14 = (bf16[2048,128]{1,0:T(8,128)(2,1)S(1)}, bf16[2048,128]{1,0:T(8,128)(2,1)S(1)}, u32[]{:S(2)}, u32[]{:S(2)}) collective-permute-start(bf16[2048,128]{1,0:T(8,128)(2,1)S(1)} %pad_maximum_fusion.packed_ref), channel_id=1, source_target_pairs={{0,2},{1,3},{2,0},{3,1},{4,6},{5,7},{6,4},{7,5},{8,10},{9,11},{10,... | collective-permute-start | bytes 1572872 | tf_op jit(solution)/shard_map/ppermute | solution.py:41

commit v13 on v12

--- a/solution.py
+++ b/solution.py
@@ -177,16 +177,22 @@
     put_zeros(ahead_ref)
 
 
-def weights_kernel(channels, classes, w1_in, head_in, ahead1_ref, head_out, w1_ref, head_ref, arrived):
+def weights_kernel(
+    channels, classes,
+    w1_in, w2_in, head_in,
+    ahead1_ref, back2_ref, head_out,
+    w1_ref, w2_ref, head_ref, arrived,
+):
     copies = [
         pltpu.make_async_copy(source, target, arrived.at[i])
-        for i, (source, target) in enumerate(((w1_in, w1_ref), (head_in, head_ref)))
+        for i, (source, target) in enumerate(((w1_in, w1_ref), (w2_in, w2_ref), (head_in, head_ref)))
     ]
     for copy in copies:
         copy.start()
     for copy in copies:
         copy.wait()
     put_ahead(ahead1_ref, w1_ref, channels)
+    put_back(back2_ref, w2_ref, channels)
     head_out[...] = jnp.zeros_like(head_out)
     row = lax.broadcasted_iota(jnp.int32, (LANES, classes), 0)
     spread = (row == lax.broadcasted_iota(jnp.int32, (LANES, classes), 1) + channels + 1).astype(BF16)
@@ -306,11 +312,11 @@
 
 def whole_kernel(
     channels, classes, east, north, upward, edges,
-    ahead1_ref, w2_in, head_ref, center_ref, *refs,
+    ahead1_ref, w2_in, back2_ref, head_ref, center_ref, *refs,
 ):
     (
         grad_ref, kept_ref, sent_ref,
-        x_ref, even0, odd0, even1, odd1, even2, odd2, mask_ref, slope_ref, turned_ref, ahead2_ref, back2_ref, w2_ref, arrived,
+        x_ref, even0, odd0, even1, odd1, even2, odd2, mask_ref, slope_ref, turned_ref, ahead2_ref, w2_ref, arrived,
     ) = refs[edges:]
     stack0, stack1, stack2 = (even0, odd0), (even1, odd1), (even2, odd2)
     copy = pltpu.make_async_copy(w2_in, w2_ref, arrived)
@@ -334,8 +340,7 @@
 
     copy.wait()
     put_ahead(ahead2_ref, w2_ref, channels)
-    put_back(back2_ref, w2_ref, channels)
-    for first, stop in grouped((planes - 2) // 2, 1):
+    for first, stop in grouped((planes - 2) // 2, 2):
         for i, parity, value in convolve(stack0, ahead1_ref, first, stop, rows, upward):
             plane = 2 * i + parity
             mask = mask_ref[plane + 1]
@@ -348,7 +353,7 @@
     class_lane = (lane[0:rows2] > channels) & (lane[0:rows2] <= channels + classes)
     here = slice(2 * upward, 2 * upward + rows2)
 
-    for first, stop in grouped((planes - 4) // 2, 1):
+    for first, stop in grouped((planes - 4) // 2, 2):
         for i, parity, value in convolve(stack1, ahead2_ref, first, stop, rows2, upward):
             plane = 2 * i + parity
             mask = mask_ref[plane + 2, here]
@@ -371,7 +376,7 @@
         kept_ref[t * channels : (t + 1) * channels, :] = tile.astype(BF16)
 
     there = slice(2 * upward + upward, 2 * upward + upward + rows3)
-    for first, stop in grouped((planes - 6) // 2, 1):
+    for first, stop in grouped((planes - 6) // 2, 2):
         for i, parity, value in convolve(stack2, back2_ref, first, stop, rows3, upward):
             plane = 2 * i + parity
             g_p1 = slope_ref[plane + 2, there] * value
@@ -513,19 +518,20 @@
     first_far, second_far, head_far = [
         pltpu.with_memory_space_constraint(value, pltpu.HBM) for value in (first_weights, second_weights, head)
     ]
-    ahead1, head_wide = pl.pallas_call(
+    ahead1, back2, head_wide = pl.pallas_call(
         functools.partial(weights_kernel, channels, classes),
-        out_shape=[jax.ShapeDtypeStruct(shape, BF16) for shape in ((4 * WIDE, 2 * LANES), (LANES, LANES))],
-        in_specs=[far] * 2,
-        out_specs=[vmem] * 2,
+        out_shape=[jax.ShapeDtypeStruct(shape, BF16) for shape in ((4 * WIDE, 2 * LANES), (4 * WIDE, 2 * LANES), (LANES, LANES))],
+        in_specs=[far] * 3,
+        out_specs=[vmem] * 3,
         scratch_shapes=[
             pltpu.VMEM(first_weights.shape, BF16),
+            pltpu.VMEM(second_weights.shape, BF16),
             pltpu.VMEM(head.shape, BF16),
-            pltpu.SemaphoreType.DMA((2,)),
+            pltpu.SemaphoreType.DMA((3,)),
         ],
-        compiler_params=pltpu.CompilerParams(vmem_limit_bytes=6 * 1024 * 1024),
+        compiler_params=pltpu.CompilerParams(vmem_limit_bytes=10 * 1024 * 1024),
         name="weights",
-    )(first_far, head_far)
+    )(first_far, second_far, head_far)
     grad, kept, sent = pl.pallas_call(
         functools.partial(whole_kernel, channels, classes, east, north, upward, len(edges)),
         out_shape=(
@@ -533,7 +539,7 @@
             jax.ShapeDtypeStruct((packed, LANES), BF16),
             jax.ShapeDtypeStruct((packed, LANES), BF16),
         ),
-        in_specs=[vmem, far] + [vmem] * (2 + len(edges)),
+        in_specs=[vmem, far] + [vmem] * (3 + len(edges)),
         out_specs=(vmem, vmem, vmem),
         scratch_shapes=[
             pltpu.VMEM((planes, rows, LANES), BF16),
@@ -544,13 +550,12 @@
             pltpu.VMEM((planes - 2, rows, LANES), F32),
             pltpu.VMEM((3 * channels, east * size), BF16),
             pltpu.VMEM((4 * WIDE, 2 * LANES), BF16),
-            pltpu.VMEM((4 * WIDE, 2 * LANES), BF16),
             pltpu.VMEM(second_weights.shape, BF16),
             pltpu.SemaphoreType.DMA(()),
         ],
         compiler_params=pltpu.CompilerParams(vmem_limit_bytes=28 * 1024 * 1024),
         name="fields",
-    )(ahead1, second_far, head_wide, center, *edges)
+    )(ahead1, second_far, back2, head_wide, center, *edges)
 
     features_out = []
 
@@ -588,7 +593,7 @@
         name="parts",
     )(place_in(near).reshape(1).astype(jnp.int32), kept, swap(sent, east_bits[:1], 1))
     total = beside(total)
-    for change in range(1, ways):
+    for change in range(ways - 1, 0, -1):
         total = total + swap(parts[change - 1], near, change).astype(F32)
     mine = gather_parts(share_sums(total, others), [near])
     other = swap(mine, east_bits[:1], 1)

time: 64.7 us -> 62.6 us (0.968)
  Pallas kernels: 26.6 us -> 25.5 us
  waiting for transfers between devices: 16.5 us -> 15.7 us
    pallas_call x1, Pallas kernels: 16.4 us -> 14.7 us  [per_device(): pl.pallas_call(functools.partial(whole_kernel, channels, classes, east, n...]
    ppermute x15, waiting for transfers between devices: 16.5 us -> 15.7 us  [exchange(): return lax.ppermute(value, ('east', 'north'), pairs)]
  transfers between devices with their start and end apart: 15 -> 15, of which waited for: 9 -> 9; matrix products, arithmetic and copies ran while one was open for 0% -> 0% of each run, Pallas kernels for 10% -> 12%
where the time goes in v13:
time: 62.6 us; the launch traced here: 62.4 us
  Pallas kernels  25.5 us (41%)
  starting transfers between devices  20.2 us (32%)
  waiting for transfers between devices  15.7 us (25%)
  between operations  0.75 us (1%)
    ppermute x15, starting transfers between devices, exchange(): return lax.ppermute(value, ('east', 'north'), pairs)  20.2 us
    ppermute x15, waiting for transfers between devices, exchange(): return lax.ppermute(value, ('east', 'north'), pairs)  15.7 us
    pallas_call x1, Pallas kernels, per_device(): pl.pallas_call(functools.partial(whole_kernel, channels, classes, east, n...  14.7 us
    pallas_call x1, Pallas kernels, beside(): pl.pallas_call(functools.partial(last_kernel, channels, east, north, upwa...  3.63 us
    pallas_call x2, Pallas kernels, unpack(): pl.pallas_call(functools.partial(unpack_kernel, channels, scale, bool(ali...  2.43 us
    pallas_call x1, Pallas kernels, per_device(): pl.pallas_call(functools.partial(weights_kernel, channels, classes), out_...  2.37 us
    pallas_call x1, Pallas kernels, per_device(): pl.pallas_call(functools.partial(prepare_kernel, channels, upward, edge),...  2.28 us
  transfers between devices with their start and end apart: 15, of which 9 were waited for; matrix products, arithmetic and copies ran while one was open for 0% of the time, Pallas kernels for 12%

profile of v13, /device:TPU:0, one launch (start us, length us, event | category | flops | bytes accessed | tf_op | source)
XLA Modules:
  0.0 62.4 jit_solution(17931289484461107370)
XLA Ops:
  0.6 2.3 %prepare.1 = (bf16[8,128,128]{2,1,0:T(8,128)(2,1)S(1)}, bf16[4,128,128]{2,1,0:T(8,128)(2,1)S(1)}, bf16[4,128,128]{2,1,0:T(8,128)(2,1)S(1)}, bf16[8,32,128]{2,1,0...) custom-call(s32[1,1,2]{2,1,0:T(1,128)} %bitcast.15, bf16[8,128,96]{2,1,0:T(8,128)(2,1)} %bitcast.12, ...), custom_call_target="tpu_custom_call" | custom-call | tf_op jit(solution)/shard_map/prepare/pallas_call | solution.py:486
  3.4 2.6 %collective-permute-start.1 = (bf16[4,128,128]{2,1,0:T(8,128)(2,1)S(1)}, bf16[4,128,128]{2,1,0:T(8,128)(2,1)S(1)}, u32[]{:S(2)}, u32[]{:S(2)}) collective-permute-start(bf16[4,128,128]{2,1,0:T(8,128)(2,1)S(1)} %get-tuple-element.30), channel_id=1, source_target_pairs={{0,1},{1,0},{2,4},{3,5},{4,2},{5,3},{6,8},{7,9},{8,6},{9,7},{10,12... | collective-permute-start | bytes 393224 | tf_op jit(solution)/shard_map/ppermute | solution.py:41
  6.1 1.4 %collective-permute-start.3 = (bf16[4,32,128]{2,1,0:T(8,128)(2,1)S(1)}, bf16[4,32,128]{2,1,0:T(8,128)(2,1)S(1)}, u32[]{:S(2)}, u32[]{:S(2)}) collective-permute-start(bf16[4,32,128]{2,1,0:T(8,128)(2,1)S(1)} %get-tuple-element.32), channel_id=1, source_target_pairs={{0,3},{1,2},{2,1},{3,0},{4,7},{5,6},{6,5},{7,4},{8,11},{9,10},{10,... | collective-permute-start | bytes 98312 | tf_op jit(solution)/shard_map/ppermute | solution.py:41
  7.5 1.5 %collective-permute-start.4 = (bf16[4,32,128]{2,1,0:T(8,128)(2,1)S(1)}, bf16[4,32,128]{2,1,0:T(8,128)(2,1)S(1)}, u32[]{:S(2)}, u32[]{:S(2)}) collective-permute-start(bf16[4,32,128]{2,1,0:T(8,128)(2,1)S(1)} %get-tuple-element.33), channel_id=1, source_target_pairs={{0,1},{1,0},{2,5},{3,4},{4,3},{5,2},{6,9},{7,8},{8,7},{9,6},{10,13... | collective-permute-start | bytes 98312 | tf_op jit(solution)/shard_map/ppermute | solution.py:41
  9.0 2.4 %weights.1 = (bf16[4608,256]{1,0:T(8,128)(2,1)S(1)}, bf16[4608,256]{1,0:T(8,128)(2,1)S(1)}, bf16[128,128]{1,0:T(8,128)(2,1)S(1)}) custom-call(bf16[27,96,96]{2,1,0:T(8,128)(2,1)} %w1_in.3, bf16[27,96,96]{2,1,0:T(8,128)(2,1)} %w2_in.3, bf16[13,96]{1,0:T(8,128)(2,1)} %head_in.1), custom_call_target="tpu_custom_call" | custom-call | tf_op jit(solution)/shard_map/weights/pallas_call | solution.py:521
  11.4 14.7 %fields.1 = (bf16[10,144,128]{2,1,0:T(8,128)(2,1)S(1)}, bf16[2048,128]{1,0:T(8,128)(2,1)S(1)}, bf16[2048,128]{1,0:T(8,128)(2,1)S(1)}) custom-call(bf16[4608,256]{1,0:T(8,128)(2,1)S(1)} %get-tuple-element.26.ahead1_ref, bf16[27,96,96]{2,1,0:T(8,128)(2,1)} %w2_in.3, bf16[4608,256]{1,0:T(8,128)(2,1)S(1)} %get-tuple-element.27.back2_ref, ...), custom_call_target="tpu_custom_call" | custom-call | tf_op jit(solution)/shard_map/fields/pallas_call | solution.py:535
  26.1 1.1 %collective-permute-start.5 = (bf16[2048,128]{1,0:T(8,128)(2,1)S(1)}, bf16[2048,128]{1,0:T(8,128)(2,1)S(1)}, u32[]{:S(2)}, u32[]{:S(2)}) collective-permute-start(bf16[2048,128]{1,0:T(8,128)(2,1)S(1)} %get-tuple-element.36), channel_id=1, source_target_pairs={{0,2},{1,3},{2,0},{3,1},{4,6},{5,7},{6,4},{7,5},{8,10},{9,11},{10,... | collective-permute-start | bytes 1572872 | tf_op jit(solution)/shard_map/ppermute | solution.py:41
  27.2 1.5 %collective-permute-done.5.came_ref = bf16[2048,128]{1,0:T(8,128)(2,1)S(1)} collective-permute-done((bf16[2048,128]{1,0:T(8,128)(2,1)S(1)}, bf16[2048,128]{1,0:T(8,128)(2,1)S(1)}, u32[]{:S(2)}, u32[]{:S(2)}) %collective-permute-start.5) | collective-permute-done | bytes 524320 | tf_op jit(solution)/shard_map/ppermute | solution.py:41
  28.9 1.8 %collective-permute-start.8 = (bf16[512,128]{1,0:T(8,128)(2,1)S(1)}, bf16[512,128]{1,0:T(8,128)(2,1)S(1)}, u32[]{:S(2)}, u32[]{:S(2)}) collective-permute-start(bf16[512,128]{1,0:T(8,128)(2,1)S(1)} %get-tuple-element.42), channel_id=1, source_target_pairs={{0,1},{1,0},{2,3},{3,2},{4,5},{5,4},{6,7},{7,6},{8,9},{9,8},{10,11... | collective-permute-start | bytes 393224 | tf_op jit(solution)/shard_map/ppermute | solution.py:41
  30.7 1.4 %collective-permute-start.7 = (bf16[512,128]{1,0:T(8,128)(2,1)S(1)}, bf16[512,128]{1,0:T(8,128)(2,1)S(1)}, u32[]{:S(2)}, u32[]{:S(2)}) collective-permute-start(bf16[512,128]{1,0:T(8,128)(2,1)S(1)} %get-tuple-element.41), channel_id=1, source_target_pairs={{0,4},{1,5},{2,6},{3,7},{4,0},{5,1},{6,2},{7,3},{8,12},{9,13},{10,... | collective-permute-start | bytes 393224 | tf_op jit(solution)/shard_map/ppermute | solution.py:41
  32.4 3.6 %features.1 = (bf16[8,128,96]{2,1,0:T(8,128)(2,1)}, f32[512,128]{1,0:T(8,128)S(1)}) custom-call(bf16[8,128,128]{2,1,0:T(8,128)(2,1)S(1)} %get-tuple-element.25.center_ref, bf16[10,144,128]{2,1,0:T(8,128)(2,1)S(1)} %get-tuple-element.34.grad_ref, bf16[27,96,96]{2,1,0:T(8,128)(2,1)} %w1_in.3, ...), custom_call_target="tpu_custom_call", output_to_operand_aliasing={{1}: (3, {})} | custom-call | tf_op jit(solution)/shard_map/features/pallas_call | solution.py:563
  36.1 2.7 %collective-permute-done.7 = bf16[512,128]{1,0:T(8,128)(2,1)S(1)} collective-permute-done((bf16[512,128]{1,0:T(8,128)(2,1)S(1)}, bf16[512,128]{1,0:T(8,128)(2,1)S(1)}, u32[]{:S(2)}, u32[]{:S(2)}) %collective-permute-start.7) | collective-permute-done | bytes 131104 | tf_op jit(solution)/shard_map/ppermute | solution.py:41
  38.8 2.0 %collective-permute-start.9 = (bf16[512,128]{1,0:T(8,128)(2,1)S(1)}, bf16[512,128]{1,0:T(8,128)(2,1)S(1)}, u32[]{:S(2)}, u32[]{:S(2)}) collective-permute-start(bf16[512,128]{1,0:T(8,128)(2,1)S(1)} %add_convert_fusion.2), channel_id=1, source_target_pairs={{0,8},{1,9},{2,10},{3,11},{4,12},{5,13},{6,14},{7,15},{8,0},{9,1},... | collective-permute-start | bytes 393224 | tf_op jit(solution)/shard_map/ppermute | solution.py:41
  40.9 3.0 %collective-permute-done.9 = bf16[512,128]{1,0:T(8,128)(2,1)S(1)} collective-permute-done((bf16[512,128]{1,0:T(8,128)(2,1)S(1)}, bf16[512,128]{1,0:T(8,128)(2,1)S(1)}, u32[]{:S(2)}, u32[]{:S(2)}) %collective-permute-start.9) | collective-permute-done | bytes 131104 | tf_op jit(solution)/shard_map/ppermute | solution.py:41
  43.9 3.1 %collective-permute-start.10 = (bf16[512,128]{1,0:T(8,128)(2,1)S(1)}, bf16[512,128]{1,0:T(8,128)(2,1)S(1)}, u32[]{:S(2)}, u32[]{:S(2)}) collective-permute-start(bf16[512,128]{1,0:T(8,128)(2,1)S(1)} %add_convert_fusion.1), channel_id=1, source_target_pairs={{0,16},{1,17},{2,18},{3,19},{4,20},{5,21},{6,22},{7,23},{8,24},{9,... | collective-permute-start | bytes 393224 | tf_op jit(solution)/shard_map/ppermute | solution.py:41
  47.0 3.0 %collective-permute-done.10 = bf16[512,128]{1,0:T(8,128)(2,1)S(1)} collective-permute-done((bf16[512,128]{1,0:T(8,128)(2,1)S(1)}, bf16[512,128]{1,0:T(8,128)(2,1)S(1)}, u32[]{:S(2)}, u32[]{:S(2)}) %collective-permute-start.10) | collective-permute-done | bytes 131104 | tf_op jit(solution)/shard_map/ppermute | solution.py:41
  50.0 2.9 %collective-permute-start.11 = (bf16[512,128]{1,0:T(8,128)(2,1)S(1)}, bf16[512,128]{1,0:T(8,128)(2,1)S(1)}, u32[]{:S(2)}, u32[]{:S(2)}) collective-permute-start(bf16[512,128]{1,0:T(8,128)(2,1)S(1)} %add_convert_fusion), channel_id=1, source_target_pairs={{0,5},{1,4},{2,7},{3,6},{4,1},{5,0},{6,3},{7,2},{8,13},{9,12},{10,... | collective-permute-start | bytes 393224 | tf_op jit(solution)/shard_map/ppermute | solution.py:41
  52.9 1.2 %collective-permute-start.12 = (bf16[512,128]{1,0:T(8,128)(2,1)S(1)}, bf16[512,128]{1,0:T(8,128)(2,1)S(1)}, u32[]{:S(2)}, u32[]{:S(2)}) collective-permute-start(bf16[512,128]{1,0:T(8,128)(2,1)S(1)} %add_convert_fusion), channel_id=1, source_target_pairs={{0,4},{1,5},{2,6},{3,7},{4,0},{5,1},{6,2},{7,3},{8,12},{9,13},{10,... | collective-permute-start | bytes 393224 | tf_op jit(solution)/shard_map/ppermute | solution.py:41
  54.2 2.0 %collective-permute-done.11 = bf16[512,128]{1,0:T(8,128)(2,1)S(1)} collective-permute-done((bf16[512,128]{1,0:T(8,128)(2,1)S(1)}, bf16[512,128]{1,0:T(8,128)(2,1)S(1)}, u32[]{:S(2)}, u32[]{:S(2)}) %collective-permute-start.11) | collective-permute-done | bytes 131104 | tf_op jit(solution)/shard_map/ppermute | solution.py:41
  56.2 1.7 %collective-permute-done.12 = bf16[512,128]{1,0:T(8,128)(2,1)S(1)} collective-permute-done((bf16[512,128]{1,0:T(8,128)(2,1)S(1)}, bf16[512,128]{1,0:T(8,128)(2,1)S(1)}, u32[]{:S(2)}, u32[]{:S(2)}) %collective-permute-start.12) | collective-permute-done | bytes 131104 | tf_op jit(solution)/shard_map/ppermute | solution.py:41
  57.9 1.2 %collective-permute-done.13 = bf16[512,128]{1,0:T(8,128)(2,1)S(1)} collective-permute-done((bf16[512,128]{1,0:T(8,128)(2,1)S(1)}, bf16[512,128]{1,0:T(8,128)(2,1)S(1)}, u32[]{:S(2)}, u32[]{:S(2)}) %collective-permute-start.13) | collective-permute-done | bytes 131104 | tf_op jit(solution)/shard_map/ppermute | solution.py:41
  59.3 1.2 %unpack.2 = (f32[27,96,96]{2,1,0:T(8,128)}, f32[27,96,96]{2,1,0:T(8,128)}) custom-call(s32[1]{0:T(128)} %bitcast.9.first_ref_flag, bf16[2048,128]{1,0:T(8,128)(2,1)S(1)} %pad_maximum_fusion.packed_ref), custom_call_target="tpu_custom_call" | custom-call | tf_op jit(solution)/shard_map/unpack/pallas_call | solution.py:602
  60.5 0.7 %collective-permute-done.14.packed_ref = bf16[2048,128]{1,0:T(8,128)(2,1)S(1)} collective-permute-done((bf16[2048,128]{1,0:T(8,128)(2,1)S(1)}, bf16[2048,128]{1,0:T(8,128)(2,1)S(1)}, u32[]{:S(2)}, u32[]{:S(2)}) %collective-permute-start.14) | collective-permute-done | bytes 524320 | tf_op jit(solution)/shard_map/ppermute | solution.py:41
  61.2 1.2 %unpack.3 = (f32[27,96,96]{2,1,0:T(8,128)}, f32[27,96,96]{2,1,0:T(8,128)}) custom-call(s32[1]{0:T(128)} %bitcast.8.first_ref_flag, bf16[2048,128]{1,0:T(8,128)(2,1)S(1)} %collective-permute-done.14.packed_ref, f32[27,96,96]{2,1,0:T(8,128)} %get-tuple-element.43.refs_0_, ...), custom_call_target="tpu_custom_call", output_to_operand_aliasing={{0}: (2, {}), {1}: (3, {})} | custom-call | tf_op jit(solution)/shard_map/unpack/pallas_call | solution.py:602
  (18 shorter events, 1.6 us)
Async XLA Ops:
  2.9 8.5 %collective-permute-start = (bf16[4,128,128]{2,1,0:T(8,128)(2,1)S(1)}, bf16[4,128,128]{2,1,0:T(8,128)(2,1)S(1)}, u32[]{:S(2)}, u32[]{:S(2)}) collective-permute-start(bf16[4,128,128]{2,1,0:T(8,128)(2,1)S(1)} %get-tuple-element.29), channel_id=1, source_target_pairs={{0,2},{1,3},{2,0},{3,1},{4,6},{5,7},{6,4},{7,5},{8,10},{9,11},{10,... | collective-permute-start | bytes 393224 | tf_op jit(solution)/shard_map/ppermute | solution.py:41
  3.4 8.0 %collective-permute-start.1 = (bf16[4,128,128]{2,1,0:T(8,128)(2,1)S(1)}, bf16[4,128,128]{2,1,0:T(8,128)(2,1)S(1)}, u32[]{:S(2)}, u32[]{:S(2)}) collective-permute-start(bf16[4,128,128]{2,1,0:T(8,128)(2,1)S(1)} %get-tuple-element.30), channel_id=1, source_target_pairs={{0,1},{1,0},{2,4},{3,5},{4,2},{5,3},{6,8},{7,9},{8,6},{9,7},{10,12... | collective-permute-start | bytes 393224 | tf_op jit(solution)/shard_map/ppermute | solution.py:41
  6.0 5.4 %collective-permute-start.2 = (bf16[8,32,128]{2,1,0:T(8,128)(2,1)S(1)}, bf16[8,32,128]{2,1,0:T(8,128)(2,1)S(1)}, u32[]{:S(2)}, u32[]{:S(2)}) collective-permute-start(bf16[8,32,128]{2,1,0:T(8,128)(2,1)S(1)} %get-tuple-element.31), channel_id=1, source_target_pairs={{0,1},{1,0},{2,3},{3,2},{4,5},{5,4},{6,7},{7,6},{8,9},{9,8},{10,11... | collective-permute-start | bytes 196616 | tf_op jit(solution)/shard_map/ppermute | solution.py:41
  6.1 5.3 %collective-permute-start.3 = (bf16[4,32,128]{2,1,0:T(8,128)(2,1)S(1)}, bf16[4,32,128]{2,1,0:T(8,128)(2,1)S(1)}, u32[]{:S(2)}, u32[]{:S(2)}) collective-permute-start(bf16[4,32,128]{2,1,0:T(8,128)(2,1)S(1)} %get-tuple-element.32), channel_id=1, source_target_pairs={{0,3},{1,2},{2,1},{3,0},{4,7},{5,6},{6,5},{7,4},{8,11},{9,10},{10,... | collective-permute-start | bytes 98312 | tf_op jit(solution)/shard_map/ppermute | solution.py:41
  7.5 3.9 %collective-permute-start.4 = (bf16[4,32,128]{2,1,0:T(8,128)(2,1)S(1)}, bf16[4,32,128]{2,1,0:T(8,128)(2,1)S(1)}, u32[]{:S(2)}, u32[]{:S(2)}) collective-permute-start(bf16[4,32,128]{2,1,0:T(8,128)(2,1)S(1)} %get-tuple-element.33), channel_id=1, source_target_pairs={{0,1},{1,0},{2,5},{3,4},{4,3},{5,2},{6,9},{7,8},{8,7},{9,6},{10,13... | collective-permute-start | bytes 98312 | tf_op jit(solution)/shard_map/ppermute | solution.py:41
  26.1 2.6 %collective-permute-start.5 = (bf16[2048,128]{1,0:T(8,128)(2,1)S(1)}, bf16[2048,128]{1,0:T(8,128)(2,1)S(1)}, u32[]{:S(2)}, u32[]{:S(2)}) collective-permute-start(bf16[2048,128]{1,0:T(8,128)(2,1)S(1)} %get-tuple-element.36), channel_id=1, source_target_pairs={{0,2},{1,3},{2,0},{3,1},{4,6},{5,7},{6,4},{7,5},{8,10},{9,11},{10,... | collective-permute-start | bytes 1572872 | tf_op jit(solution)/shard_map/ppermute | solution.py:41
  28.9 7.2 %collective-permute-start.8 = (bf16[512,128]{1,0:T(8,128)(2,1)S(1)}, bf16[512,128]{1,0:T(8,128)(2,1)S(1)}, u32[]{:S(2)}, u32[]{:S(2)}) collective-permute-start(bf16[512,128]{1,0:T(8,128)(2,1)S(1)} %get-tuple-element.42), channel_id=1, source_target_pairs={{0,1},{1,0},{2,3},{3,2},{4,5},{5,4},{6,7},{7,6},{8,9},{9,8},{10,11... | collective-permute-start | bytes 393224 | tf_op jit(solution)/shard_map/ppermute | solution.py:41
  30.7 8.1 %collective-permute-start.7 = (bf16[512,128]{1,0:T(8,128)(2,1)S(1)}, bf16[512,128]{1,0:T(8,128)(2,1)S(1)}, u32[]{:S(2)}, u32[]{:S(2)}) collective-permute-start(bf16[512,128]{1,0:T(8,128)(2,1)S(1)} %get-tuple-element.41), channel_id=1, source_target_pairs={{0,4},{1,5},{2,6},{3,7},{4,0},{5,1},{6,2},{7,3},{8,12},{9,13},{10,... | collective-permute-start | bytes 393224 | tf_op jit(solution)/shard_map/ppermute | solution.py:41
  32.0 6.7 %collective-permute-start.6 = (bf16[512,128]{1,0:T(8,128)(2,1)S(1)}, bf16[512,128]{1,0:T(8,128)(2,1)S(1)}, u32[]{:S(2)}, u32[]{:S(2)}) collective-permute-start(bf16[512,128]{1,0:T(8,128)(2,1)S(1)} %get-tuple-element.40), channel_id=1, source_target_pairs={{0,5},{1,4},{2,7},{3,6},{4,1},{5,0},{6,3},{7,2},{8,13},{9,12},{10,... | collective-permute-start | bytes 393224 | tf_op jit(solution)/shard_map/ppermute | solution.py:41
  38.8 5.0 %collective-permute-start.9 = (bf16[512,128]{1,0:T(8,128)(2,1)S(1)}, bf16[512,128]{1,0:T(8,128)(2,1)S(1)}, u32[]{:S(2)}, u32[]{:S(2)}) collective-permute-start(bf16[512,128]{1,0:T(8,128)(2,1)S(1)} %add_convert_fusion.2), channel_id=1, source_target_pairs={{0,8},{1,9},{2,10},{3,11},{4,12},{5,13},{6,14},{7,15},{8,0},{9,1},... | collective-permute-start | bytes 393224 | tf_op jit(solution)/shard_map/ppermute | solution.py:41
  43.9 6.0 %collective-permute-start.10 = (bf16[512,128]{1,0:T(8,128)(2,1)S(1)}, bf16[512,128]{1,0:T(8,128)(2,1)S(1)}, u32[]{:S(2)}, u32[]{:S(2)}) collective-permute-start(bf16[512,128]{1,0:T(8,128)(2,1)S(1)} %add_convert_fusion.1), channel_id=1, source_target_pairs={{0,16},{1,17},{2,18},{3,19},{4,20},{5,21},{6,22},{7,23},{8,24},{9,... | collective-permute-start | bytes 393224 | tf_op jit(solution)/shard_map/ppermute | solution.py:41
  50.0 6.2 %collective-permute-start.11 = (bf16[512,128]{1,0:T(8,128)(2,1)S(1)}, bf16[512,128]{1,0:T(8,128)(2,1)S(1)}, u32[]{:S(2)}, u32[]{:S(2)}) collective-permute-start(bf16[512,128]{1,0:T(8,128)(2,1)S(1)} %add_convert_fusion), channel_id=1, source_target_pairs={{0,5},{1,4},{2,7},{3,6},{4,1},{5,0},{6,3},{7,2},{8,13},{9,12},{10,... | collective-permute-start | bytes 393224 | tf_op jit(solution)/shard_map/ppermute | solution.py:41
  52.9 5.0 %collective-permute-start.12 = (bf16[512,128]{1,0:T(8,128)(2,1)S(1)}, bf16[512,128]{1,0:T(8,128)(2,1)S(1)}, u32[]{:S(2)}, u32[]{:S(2)}) collective-permute-start(bf16[512,128]{1,0:T(8,128)(2,1)S(1)} %add_convert_fusion), channel_id=1, source_target_pairs={{0,4},{1,5},{2,6},{3,7},{4,0},{5,1},{6,2},{7,3},{8,12},{9,13},{10,... | collective-permute-start | bytes 393224 | tf_op jit(solution)/shard_map/ppermute | solution.py:41
  54.1 5.0 %collective-permute-start.13 = (bf16[512,128]{1,0:T(8,128)(2,1)S(1)}, bf16[512,128]{1,0:T(8,128)(2,1)S(1)}, u32[]{:S(2)}, u32[]{:S(2)}) collective-permute-start(bf16[512,128]{1,0:T(8,128)(2,1)S(1)} %add_convert_fusion), channel_id=1, source_target_pairs={{0,1},{1,0},{2,3},{3,2},{4,5},{5,4},{6,7},{7,6},{8,9},{9,8},{10,11... | collective-permute-start | bytes 393224 | tf_op jit(solution)/shard_map/ppermute | solution.py:41
  59.2 2.0 %collective-permute-start.14 = (bf16[2048,128]{1,0:T(8,128)(2,1)S(1)}, bf16[2048,128]{1,0:T(8,128)(2,1)S(1)}, u32[]{:S(2)}, u32[]{:S(2)}) collective-permute-start(bf16[2048,128]{1,0:T(8,128)(2,1)S(1)} %pad_maximum_fusion.packed_ref), channel_id=1, source_target_pairs={{0,2},{1,3},{2,0},{3,1},{4,6},{5,7},{6,4},{7,5},{8,10},{9,11},{10,... | collective-permute-start | bytes 1572872 | tf_op jit(solution)/shard_map/ppermute | solution.py:41

commit v14 on v13

--- a/solution.py
+++ b/solution.py
@@ -122,9 +122,7 @@
 
 
 def grouped(pairs, size):
-    count = max(1, pairs // size)
-    edges = [pairs * i // count for i in range(count + 1)]
-    return list(zip(edges, edges[1:]))
+    return [(first, min(first + size, pairs)) for first in range(0, pairs, size)]
 
 
 def convolve(stack, weight_ref, first, stop, rows, upward):
@@ -511,7 +509,8 @@
     stay = [list(range(lax.axis_size(axis))) for axis in ("east", "north")]
     routes = [(partners, stay[1]) for partners, _, _ in easts] + [(stay[0], partners) for partners, _, _ in norths]
     routes += [(a, b) for a, _, _ in easts for b, _, _ in norths]
-    edges = [exchange(value, *route) for value, route in zip(edges, routes)]
+    came = {i: exchange(edges[i], *routes[i]) for i in [*range(1, len(edges)), 0]}
+    edges = [came[i] for i in range(len(edges))]
 
     unit = devices // 2 * 16
     packed = -(-21 * channels // unit) * unit

time: 62.6 us -> 63.5 us (1.014)
  Pallas kernels: 25.5 us -> 26.3 us
    pallas_call x1, Pallas kernels: 14.7 us -> 15.5 us  [per_device(): pl.pallas_call(functools.partial(whole_kernel, channels, classes, east, n...]
  transfers between devices with their start and end apart: 15 -> 15, of which waited for: 9 -> 9; matrix products, arithmetic and copies ran while one was open for 0% -> 0% of each run, Pallas kernels for 12% -> 11%
where the time goes in v14:
time: 63.5 us; the launch traced here: 63.2 us
  Pallas kernels  26.3 us (41%)
  starting transfers between devices  20.2 us (32%)
  waiting for transfers between devices  15.7 us (25%)
  between operations  0.75 us (1%)
    ppermute x15, starting transfers between devices, exchange(): return lax.ppermute(value, ('east', 'north'), pairs)  20.2 us
    ppermute x15, waiting for transfers between devices, exchange(): return lax.ppermute(value, ('east', 'north'), pairs)  15.7 us
    pallas_call x1, Pallas kernels, per_device(): pl.pallas_call(functools.partial(whole_kernel, channels, classes, east, n...  15.5 us
    pallas_call x1, Pallas kernels, beside(): pl.pallas_call(functools.partial(last_kernel, channels, east, north, upwa...  3.63 us
    pallas_call x2, Pallas kernels, unpack(): pl.pallas_call(functools.partial(unpack_kernel, channels, scale, bool(ali...  2.43 us
    pallas_call x1, Pallas kernels, per_device(): pl.pallas_call(functools.partial(weights_kernel, channels, classes), out_...  2.37 us
    pallas_call x1, Pallas kernels, per_device(): pl.pallas_call(functools.partial(prepare_kernel, channels, upward, edge),...  2.28 us
  transfers between devices with their start and end apart: 15, of which 9 were waited for; matrix products, arithmetic and copies ran while one was open for 0% of the time, Pallas kernels for 11%

profile of v14, /device:TPU:0, one launch (start us, length us, event | category | flops | bytes accessed | tf_op | source)
XLA Modules:
  0.0 63.2 jit_solution(4789081118039051189)
XLA Ops:
  0.6 2.3 %prepare.1 = (bf16[8,128,128]{2,1,0:T(8,128)(2,1)S(1)}, bf16[4,128,128]{2,1,0:T(8,128)(2,1)S(1)}, bf16[4,128,128]{2,1,0:T(8,128)(2,1)S(1)}, bf16[8,32,128]{2,1,0...) custom-call(s32[1,1,2]{2,1,0:T(1,128)} %bitcast.15, bf16[8,128,96]{2,1,0:T(8,128)(2,1)} %bitcast.12, ...), custom_call_target="tpu_custom_call" | custom-call | tf_op jit(solution)/shard_map/prepare/pallas_call | solution.py:484
  3.4 2.6 %collective-permute-start.1 = (bf16[4,128,128]{2,1,0:T(8,128)(2,1)S(1)}, bf16[4,128,128]{2,1,0:T(8,128)(2,1)S(1)}, u32[]{:S(2)}, u32[]{:S(2)}) collective-permute-start(bf16[4,128,128]{2,1,0:T(8,128)(2,1)S(1)} %get-tuple-element.30), channel_id=1, source_target_pairs={{0,1},{1,0},{2,4},{3,5},{4,2},{5,3},{6,8},{7,9},{8,6},{9,7},{10,12... | collective-permute-start | bytes 393224 | tf_op jit(solution)/shard_map/ppermute | solution.py:41
  6.1 1.4 %collective-permute-start.3 = (bf16[4,32,128]{2,1,0:T(8,128)(2,1)S(1)}, bf16[4,32,128]{2,1,0:T(8,128)(2,1)S(1)}, u32[]{:S(2)}, u32[]{:S(2)}) collective-permute-start(bf16[4,32,128]{2,1,0:T(8,128)(2,1)S(1)} %get-tuple-element.32), channel_id=1, source_target_pairs={{0,3},{1,2},{2,1},{3,0},{4,7},{5,6},{6,5},{7,4},{8,11},{9,10},{10,... | collective-permute-start | bytes 98312 | tf_op jit(solution)/shard_map/ppermute | solution.py:41
  7.5 1.5 %collective-permute-start.4 = (bf16[4,32,128]{2,1,0:T(8,128)(2,1)S(1)}, bf16[4,32,128]{2,1,0:T(8,128)(2,1)S(1)}, u32[]{:S(2)}, u32[]{:S(2)}) collective-permute-start(bf16[4,32,128]{2,1,0:T(8,128)(2,1)S(1)} %get-tuple-element.33), channel_id=1, source_target_pairs={{0,1},{1,0},{2,5},{3,4},{4,3},{5,2},{6,9},{7,8},{8,7},{9,6},{10,13... | collective-permute-start | bytes 98312 | tf_op jit(solution)/shard_map/ppermute | solution.py:41
  9.0 2.4 %weights.1 = (bf16[4608,256]{1,0:T(8,128)(2,1)S(1)}, bf16[4608,256]{1,0:T(8,128)(2,1)S(1)}, bf16[128,128]{1,0:T(8,128)(2,1)S(1)}) custom-call(bf16[27,96,96]{2,1,0:T(8,128)(2,1)} %w1_in.3, bf16[27,96,96]{2,1,0:T(8,128)(2,1)} %w2_in.3, bf16[13,96]{1,0:T(8,128)(2,1)} %head_in.1), custom_call_target="tpu_custom_call" | custom-call | tf_op jit(solution)/shard_map/weights/pallas_call | solution.py:520
  11.4 15.5 %fields.1 = (bf16[10,144,128]{2,1,0:T(8,128)(2,1)S(1)}, bf16[2048,128]{1,0:T(8,128)(2,1)S(1)}, bf16[2048,128]{1,0:T(8,128)(2,1)S(1)}) custom-call(bf16[4608,256]{1,0:T(8,128)(2,1)S(1)} %get-tuple-element.26.ahead1_ref, bf16[27,96,96]{2,1,0:T(8,128)(2,1)} %w2_in.3, bf16[4608,256]{1,0:T(8,128)(2,1)S(1)} %get-tuple-element.27.back2_ref, ...), custom_call_target="tpu_custom_call" | custom-call | tf_op jit(solution)/shard_map/fields/pallas_call | solution.py:534
  26.9 1.1 %collective-permute-start.5 = (bf16[2048,128]{1,0:T(8,128)(2,1)S(1)}, bf16[2048,128]{1,0:T(8,128)(2,1)S(1)}, u32[]{:S(2)}, u32[]{:S(2)}) collective-permute-start(bf16[2048,128]{1,0:T(8,128)(2,1)S(1)} %get-tuple-element.36), channel_id=1, source_target_pairs={{0,2},{1,3},{2,0},{3,1},{4,6},{5,7},{6,4},{7,5},{8,10},{9,11},{10,... | collective-permute-start | bytes 1572872 | tf_op jit(solution)/shard_map/ppermute | solution.py:41
  28.0 1.5 %collective-permute-done.5.came_ref = bf16[2048,128]{1,0:T(8,128)(2,1)S(1)} collective-permute-done((bf16[2048,128]{1,0:T(8,128)(2,1)S(1)}, bf16[2048,128]{1,0:T(8,128)(2,1)S(1)}, u32[]{:S(2)}, u32[]{:S(2)}) %collective-permute-start.5) | collective-permute-done | bytes 524320 | tf_op jit(solution)/shard_map/ppermute | solution.py:41
  29.7 1.8 %collective-permute-start.8 = (bf16[512,128]{1,0:T(8,128)(2,1)S(1)}, bf16[512,128]{1,0:T(8,128)(2,1)S(1)}, u32[]{:S(2)}, u32[]{:S(2)}) collective-permute-start(bf16[512,128]{1,0:T(8,128)(2,1)S(1)} %get-tuple-element.42), channel_id=1, source_target_pairs={{0,1},{1,0},{2,3},{3,2},{4,5},{5,4},{6,7},{7,6},{8,9},{9,8},{10,11... | collective-permute-start | bytes 393224 | tf_op jit(solution)/shard_map/ppermute | solution.py:41
  31.5 1.4 %collective-permute-start.7 = (bf16[512,128]{1,0:T(8,128)(2,1)S(1)}, bf16[512,128]{1,0:T(8,128)(2,1)S(1)}, u32[]{:S(2)}, u32[]{:S(2)}) collective-permute-start(bf16[512,128]{1,0:T(8,128)(2,1)S(1)} %get-tuple-element.41), channel_id=1, source_target_pairs={{0,4},{1,5},{2,6},{3,7},{4,0},{5,1},{6,2},{7,3},{8,12},{9,13},{10,... | collective-permute-start | bytes 393224 | tf_op jit(solution)/shard_map/ppermute | solution.py:41
  33.2 3.6 %features.1 = (bf16[8,128,96]{2,1,0:T(8,128)(2,1)}, f32[512,128]{1,0:T(8,128)S(1)}) custom-call(bf16[8,128,128]{2,1,0:T(8,128)(2,1)S(1)} %get-tuple-element.25.center_ref, bf16[10,144,128]{2,1,0:T(8,128)(2,1)S(1)} %get-tuple-element.34.grad_ref, bf16[27,96,96]{2,1,0:T(8,128)(2,1)} %w1_in.3, ...), custom_call_target="tpu_custom_call", output_to_operand_aliasing={{1}: (3, {})} | custom-call | tf_op jit(solution)/shard_map/features/pallas_call | solution.py:562
  36.9 2.7 %collective-permute-done.7 = bf16[512,128]{1,0:T(8,128)(2,1)S(1)} collective-permute-done((bf16[512,128]{1,0:T(8,128)(2,1)S(1)}, bf16[512,128]{1,0:T(8,128)(2,1)S(1)}, u32[]{:S(2)}, u32[]{:S(2)}) %collective-permute-start.7) | collective-permute-done | bytes 131104 | tf_op jit(solution)/shard_map/ppermute | solution.py:41
  39.6 2.0 %collective-permute-start.9 = (bf16[512,128]{1,0:T(8,128)(2,1)S(1)}, bf16[512,128]{1,0:T(8,128)(2,1)S(1)}, u32[]{:S(2)}, u32[]{:S(2)}) collective-permute-start(bf16[512,128]{1,0:T(8,128)(2,1)S(1)} %add_convert_fusion.2), channel_id=1, source_target_pairs={{0,8},{1,9},{2,10},{3,11},{4,12},{5,13},{6,14},{7,15},{8,0},{9,1},... | collective-permute-start | bytes 393224 | tf_op jit(solution)/shard_map/ppermute | solution.py:41
  41.7 3.0 %collective-permute-done.9 = bf16[512,128]{1,0:T(8,128)(2,1)S(1)} collective-permute-done((bf16[512,128]{1,0:T(8,128)(2,1)S(1)}, bf16[512,128]{1,0:T(8,128)(2,1)S(1)}, u32[]{:S(2)}, u32[]{:S(2)}) %collective-permute-start.9) | collective-permute-done | bytes 131104 | tf_op jit(solution)/shard_map/ppermute | solution.py:41
  44.7 3.1 %collective-permute-start.10 = (bf16[512,128]{1,0:T(8,128)(2,1)S(1)}, bf16[512,128]{1,0:T(8,128)(2,1)S(1)}, u32[]{:S(2)}, u32[]{:S(2)}) collective-permute-start(bf16[512,128]{1,0:T(8,128)(2,1)S(1)} %add_convert_fusion.1), channel_id=1, source_target_pairs={{0,16},{1,17},{2,18},{3,19},{4,20},{5,21},{6,22},{7,23},{8,24},{9,... | collective-permute-start | bytes 393224 | tf_op jit(solution)/shard_map/ppermute | solution.py:41
  47.8 3.0 %collective-permute-done.10 = bf16[512,128]{1,0:T(8,128)(2,1)S(1)} collective-permute-done((bf16[512,128]{1,0:T(8,128)(2,1)S(1)}, bf16[512,128]{1,0:T(8,128)(2,1)S(1)}, u32[]{:S(2)}, u32[]{:S(2)}) %collective-permute-start.10) | collective-permute-done | bytes 131104 | tf_op jit(solution)/shard_map/ppermute | solution.py:41
  50.8 2.9 %collective-permute-start.11 = (bf16[512,128]{1,0:T(8,128)(2,1)S(1)}, bf16[512,128]{1,0:T(8,128)(2,1)S(1)}, u32[]{:S(2)}, u32[]{:S(2)}) collective-permute-start(bf16[512,128]{1,0:T(8,128)(2,1)S(1)} %add_convert_fusion), channel_id=1, source_target_pairs={{0,5},{1,4},{2,7},{3,6},{4,1},{5,0},{6,3},{7,2},{8,13},{9,12},{10,... | collective-permute-start | bytes 393224 | tf_op jit(solution)/shard_map/ppermute | solution.py:41
  53.7 1.2 %collective-permute-start.12 = (bf16[512,128]{1,0:T(8,128)(2,1)S(1)}, bf16[512,128]{1,0:T(8,128)(2,1)S(1)}, u32[]{:S(2)}, u32[]{:S(2)}) collective-permute-start(bf16[512,128]{1,0:T(8,128)(2,1)S(1)} %add_convert_fusion), channel_id=1, source_target_pairs={{0,4},{1,5},{2,6},{3,7},{4,0},{5,1},{6,2},{7,3},{8,12},{9,13},{10,... | collective-permute-start | bytes 393224 | tf_op jit(solution)/shard_map/ppermute | solution.py:41
  55.1 2.0 %collective-permute-done.11 = bf16[512,128]{1,0:T(8,128)(2,1)S(1)} collective-permute-done((bf16[512,128]{1,0:T(8,128)(2,1)S(1)}, bf16[512,128]{1,0:T(8,128)(2,1)S(1)}, u32[]{:S(2)}, u32[]{:S(2)}) %collective-permute-start.11) | collective-permute-done | bytes 131104 | tf_op jit(solution)/shard_map/ppermute | solution.py:41
  57.0 1.7 %collective-permute-done.12 = bf16[512,128]{1,0:T(8,128)(2,1)S(1)} collective-permute-done((bf16[512,128]{1,0:T(8,128)(2,1)S(1)}, bf16[512,128]{1,0:T(8,128)(2,1)S(1)}, u32[]{:S(2)}, u32[]{:S(2)}) %collective-permute-start.12) | collective-permute-done | bytes 131104 | tf_op jit(solution)/shard_map/ppermute | solution.py:41
  58.7 1.2 %collective-permute-done.13 = bf16[512,128]{1,0:T(8,128)(2,1)S(1)} collective-permute-done((bf16[512,128]{1,0:T(8,128)(2,1)S(1)}, bf16[512,128]{1,0:T(8,128)(2,1)S(1)}, u32[]{:S(2)}, u32[]{:S(2)}) %collective-permute-start.13) | collective-permute-done | bytes 131104 | tf_op jit(solution)/shard_map/ppermute | solution.py:41
  60.1 1.2 %unpack.2 = (f32[27,96,96]{2,1,0:T(8,128)}, f32[27,96,96]{2,1,0:T(8,128)}) custom-call(s32[1]{0:T(128)} %bitcast.9.first_ref_flag, bf16[2048,128]{1,0:T(8,128)(2,1)S(1)} %pad_maximum_fusion.packed_ref), custom_call_target="tpu_custom_call" | custom-call | tf_op jit(solution)/shard_map/unpack/pallas_call | solution.py:601
  61.3 0.7 %collective-permute-done.14.packed_ref = bf16[2048,128]{1,0:T(8,128)(2,1)S(1)} collective-permute-done((bf16[2048,128]{1,0:T(8,128)(2,1)S(1)}, bf16[2048,128]{1,0:T(8,128)(2,1)S(1)}, u32[]{:S(2)}, u32[]{:S(2)}) %collective-permute-start.14) | collective-permute-done | bytes 524320 | tf_op jit(solution)/shard_map/ppermute | solution.py:41
  62.0 1.2 %unpack.3 = (f32[27,96,96]{2,1,0:T(8,128)}, f32[27,96,96]{2,1,0:T(8,128)}) custom-call(s32[1]{0:T(128)} %bitcast.8.first_ref_flag, bf16[2048,128]{1,0:T(8,128)(2,1)S(1)} %collective-permute-done.14.packed_ref, f32[27,96,96]{2,1,0:T(8,128)} %get-tuple-element.43.refs_0_, ...), custom_call_target="tpu_custom_call", output_to_operand_aliasing={{0}: (2, {}), {1}: (3, {})} | custom-call | tf_op jit(solution)/shard_map/unpack/pallas_call | solution.py:601
  (18 shorter events, 1.6 us)
Async XLA Ops:
  2.9 8.5 %collective-permute-start = (bf16[4,128,128]{2,1,0:T(8,128)(2,1)S(1)}, bf16[4,128,128]{2,1,0:T(8,128)(2,1)S(1)}, u32[]{:S(2)}, u32[]{:S(2)}) collective-permute-start(bf16[4,128,128]{2,1,0:T(8,128)(2,1)S(1)} %get-tuple-element.29), channel_id=1, source_target_pairs={{0,2},{1,3},{2,0},{3,1},{4,6},{5,7},{6,4},{7,5},{8,10},{9,11},{10,... | collective-permute-start | bytes 393224 | tf_op jit(solution)/shard_map/ppermute | solution.py:41
  3.4 8.0 %collective-permute-start.1 = (bf16[4,128,128]{2,1,0:T(8,128)(2,1)S(1)}, bf16[4,128,128]{2,1,0:T(8,128)(2,1)S(1)}, u32[]{:S(2)}, u32[]{:S(2)}) collective-permute-start(bf16[4,128,128]{2,1,0:T(8,128)(2,1)S(1)} %get-tuple-element.30), channel_id=1, source_target_pairs={{0,1},{1,0},{2,4},{3,5},{4,2},{5,3},{6,8},{7,9},{8,6},{9,7},{10,12... | collective-permute-start | bytes 393224 | tf_op jit(solution)/shard_map/ppermute | solution.py:41
  6.0 5.4 %collective-permute-start.2 = (bf16[8,32,128]{2,1,0:T(8,128)(2,1)S(1)}, bf16[8,32,128]{2,1,0:T(8,128)(2,1)S(1)}, u32[]{:S(2)}, u32[]{:S(2)}) collective-permute-start(bf16[8,32,128]{2,1,0:T(8,128)(2,1)S(1)} %get-tuple-element.31), channel_id=1, source_target_pairs={{0,1},{1,0},{2,3},{3,2},{4,5},{5,4},{6,7},{7,6},{8,9},{9,8},{10,11... | collective-permute-start | bytes 196616 | tf_op jit(solution)/shard_map/ppermute | solution.py:41
  6.1 5.3 %collective-permute-start.3 = (bf16[4,32,128]{2,1,0:T(8,128)(2,1)S(1)}, bf16[4,32,128]{2,1,0:T(8,128)(2,1)S(1)}, u32[]{:S(2)}, u32[]{:S(2)}) collective-permute-start(bf16[4,32,128]{2,1,0:T(8,128)(2,1)S(1)} %get-tuple-element.32), channel_id=1, source_target_pairs={{0,3},{1,2},{2,1},{3,0},{4,7},{5,6},{6,5},{7,4},{8,11},{9,10},{10,... | collective-permute-start | bytes 98312 | tf_op jit(solution)/shard_map/ppermute | solution.py:41
  7.5 3.9 %collective-permute-start.4 = (bf16[4,32,128]{2,1,0:T(8,128)(2,1)S(1)}, bf16[4,32,128]{2,1,0:T(8,128)(2,1)S(1)}, u32[]{:S(2)}, u32[]{:S(2)}) collective-permute-start(bf16[4,32,128]{2,1,0:T(8,128)(2,1)S(1)} %get-tuple-element.33), channel_id=1, source_target_pairs={{0,1},{1,0},{2,5},{3,4},{4,3},{5,2},{6,9},{7,8},{8,7},{9,6},{10,13... | collective-permute-start | bytes 98312 | tf_op jit(solution)/shard_map/ppermute | solution.py:41
  26.9 2.6 %collective-permute-start.5 = (bf16[2048,128]{1,0:T(8,128)(2,1)S(1)}, bf16[2048,128]{1,0:T(8,128)(2,1)S(1)}, u32[]{:S(2)}, u32[]{:S(2)}) collective-permute-start(bf16[2048,128]{1,0:T(8,128)(2,1)S(1)} %get-tuple-element.36), channel_id=1, source_target_pairs={{0,2},{1,3},{2,0},{3,1},{4,6},{5,7},{6,4},{7,5},{8,10},{9,11},{10,... | collective-permute-start | bytes 1572872 | tf_op jit(solution)/shard_map/ppermute | solution.py:41
  29.7 7.2 %collective-permute-start.8 = (bf16[512,128]{1,0:T(8,128)(2,1)S(1)}, bf16[512,128]{1,0:T(8,128)(2,1)S(1)}, u32[]{:S(2)}, u32[]{:S(2)}) collective-permute-start(bf16[512,128]{1,0:T(8,128)(2,1)S(1)} %get-tuple-element.42), channel_id=1, source_target_pairs={{0,1},{1,0},{2,3},{3,2},{4,5},{5,4},{6,7},{7,6},{8,9},{9,8},{10,11... | collective-permute-start | bytes 393224 | tf_op jit(solution)/shard_map/ppermute | solution.py:41
  31.5 8.1 %collective-permute-start.7 = (bf16[512,128]{1,0:T(8,128)(2,1)S(1)}, bf16[512,128]{1,0:T(8,128)(2,1)S(1)}, u32[]{:S(2)}, u32[]{:S(2)}) collective-permute-start(bf16[512,128]{1,0:T(8,128)(2,1)S(1)} %get-tuple-element.41), channel_id=1, source_target_pairs={{0,4},{1,5},{2,6},{3,7},{4,0},{5,1},{6,2},{7,3},{8,12},{9,13},{10,... | collective-permute-start | bytes 393224 | tf_op jit(solution)/shard_map/ppermute | solution.py:41
  32.9 6.7 %collective-permute-start.6 = (bf16[512,128]{1,0:T(8,128)(2,1)S(1)}, bf16[512,128]{1,0:T(8,128)(2,1)S(1)}, u32[]{:S(2)}, u32[]{:S(2)}) collective-permute-start(bf16[512,128]{1,0:T(8,128)(2,1)S(1)} %get-tuple-element.40), channel_id=1, source_target_pairs={{0,5},{1,4},{2,7},{3,6},{4,1},{5,0},{6,3},{7,2},{8,13},{9,12},{10,... | collective-permute-start | bytes 393224 | tf_op jit(solution)/shard_map/ppermute | solution.py:41
  39.6 5.0 %collective-permute-start.9 = (bf16[512,128]{1,0:T(8,128)(2,1)S(1)}, bf16[512,128]{1,0:T(8,128)(2,1)S(1)}, u32[]{:S(2)}, u32[]{:S(2)}) collective-permute-start(bf16[512,128]{1,0:T(8,128)(2,1)S(1)} %add_convert_fusion.2), channel_id=1, source_target_pairs={{0,8},{1,9},{2,10},{3,11},{4,12},{5,13},{6,14},{7,15},{8,0},{9,1},... | collective-permute-start | bytes 393224 | tf_op jit(solution)/shard_map/ppermute | solution.py:41
  44.7 6.0 %collective-permute-start.10 = (bf16[512,128]{1,0:T(8,128)(2,1)S(1)}, bf16[512,128]{1,0:T(8,128)(2,1)S(1)}, u32[]{:S(2)}, u32[]{:S(2)}) collective-permute-start(bf16[512,128]{1,0:T(8,128)(2,1)S(1)} %add_convert_fusion.1), channel_id=1, source_target_pairs={{0,16},{1,17},{2,18},{3,19},{4,20},{5,21},{6,22},{7,23},{8,24},{9,... | collective-permute-start | bytes 393224 | tf_op jit(solution)/shard_map/ppermute | solution.py:41
  50.8 6.2 %collective-permute-start.11 = (bf16[512,128]{1,0:T(8,128)(2,1)S(1)}, bf16[512,128]{1,0:T(8,128)(2,1)S(1)}, u32[]{:S(2)}, u32[]{:S(2)}) collective-permute-start(bf16[512,128]{1,0:T(8,128)(2,1)S(1)} %add_convert_fusion), channel_id=1, source_target_pairs={{0,5},{1,4},{2,7},{3,6},{4,1},{5,0},{6,3},{7,2},{8,13},{9,12},{10,... | collective-permute-start | bytes 393224 | tf_op jit(solution)/shard_map/ppermute | solution.py:41
  53.7 5.0 %collective-permute-start.12 = (bf16[512,128]{1,0:T(8,128)(2,1)S(1)}, bf16[512,128]{1,0:T(8,128)(2,1)S(1)}, u32[]{:S(2)}, u32[]{:S(2)}) collective-permute-start(bf16[512,128]{1,0:T(8,128)(2,1)S(1)} %add_convert_fusion), channel_id=1, source_target_pairs={{0,4},{1,5},{2,6},{3,7},{4,0},{5,1},{6,2},{7,3},{8,12},{9,13},{10,... | collective-permute-start | bytes 393224 | tf_op jit(solution)/shard_map/ppermute | solution.py:41
  54.9 5.0 %collective-permute-start.13 = (bf16[512,128]{1,0:T(8,128)(2,1)S(1)}, bf16[512,128]{1,0:T(8,128)(2,1)S(1)}, u32[]{:S(2)}, u32[]{:S(2)}) collective-permute-start(bf16[512,128]{1,0:T(8,128)(2,1)S(1)} %add_convert_fusion), channel_id=1, source_target_pairs={{0,1},{1,0},{2,3},{3,2},{4,5},{5,4},{6,7},{7,6},{8,9},{9,8},{10,11... | collective-permute-start | bytes 393224 | tf_op jit(solution)/shard_map/ppermute | solution.py:41
  60.0 2.0 %collective-permute-start.14 = (bf16[2048,128]{1,0:T(8,128)(2,1)S(1)}, bf16[2048,128]{1,0:T(8,128)(2,1)S(1)}, u32[]{:S(2)}, u32[]{:S(2)}) collective-permute-start(bf16[2048,128]{1,0:T(8,128)(2,1)S(1)} %pad_maximum_fusion.packed_ref), channel_id=1, source_target_pairs={{0,2},{1,3},{2,0},{3,1},{4,6},{5,7},{6,4},{7,5},{8,10},{9,11},{10,... | collective-permute-start | bytes 1572872 | tf_op jit(solution)/shard_map/ppermute | solution.py:41

commit v15 on v13

--- a/solution.py
+++ b/solution.py
@@ -138,6 +138,15 @@
         for pair in range(first, stop)
         for parity in range(2)
     ]
+
+
+def ahead_of(runs, product):
+    held = product(*runs[0])
+    for run in runs[1:]:
+        coming = product(*run)
+        yield from held
+        held = coming
+    yield from held
 
 
 def unit_of(channels):
@@ -340,48 +349,48 @@
 
     copy.wait()
     put_ahead(ahead2_ref, w2_ref, channels)
-    for first, stop in grouped((planes - 2) // 2, 2):
-        for i, parity, value in convolve(stack0, ahead1_ref, first, stop, rows, upward):
-            plane = 2 * i + parity
-            mask = mask_ref[plane + 1]
-            p1 = mask * value
-            sig = 0.5 * jnp.tanh(0.5 * p1) + 0.5
-            slope_ref[plane] = mask * (sig * (1.0 + p1 * (1.0 - sig)))
-            put_stack((p1 * sig)[upward : upward + rows1], upward, stack1, parity, i)
+    product = functools.partial(convolve, stack0, ahead1_ref, rows=rows, upward=upward)
+    for i, parity, value in ahead_of(grouped((planes - 2) // 2, 2), product):
+        plane = 2 * i + parity
+        mask = mask_ref[plane + 1]
+        p1 = mask * value
+        sig = 0.5 * jnp.tanh(0.5 * p1) + 0.5
+        slope_ref[plane] = mask * (sig * (1.0 + p1 * (1.0 - sig)))
+        put_stack((p1 * sig)[upward : upward + rows1], upward, stack1, parity, i)
 
     head = head_ref[...]
     class_lane = (lane[0:rows2] > channels) & (lane[0:rows2] <= channels + classes)
     here = slice(2 * upward, 2 * upward + rows2)
 
-    for first, stop in grouped((planes - 4) // 2, 2):
-        for i, parity, value in convolve(stack1, ahead2_ref, first, stop, rows2, upward):
-            plane = 2 * i + parity
-            mask = mask_ref[plane + 2, here]
-            p2 = mask * value
-            sig = 0.5 * jnp.tanh(0.5 * p2) + 0.5
-            a2 = (p2 * sig).astype(BF16)
-            logits = lax.dot_general(a2, head, (((1,), (1,)), ((), ())), preferred_element_type=F32)
-            g_logits = jnp.where(class_lane, mask * (logits - x_ref[plane + 2, here].astype(F32)), 0.0)
-            coarse = g_logits.astype(BF16)
-            fine = (g_logits - coarse.astype(F32)).astype(BF16)
-            g_a2 = jnp.dot(
-                jnp.concatenate([coarse, fine], 1), jnp.concatenate([head, head], 0), preferred_element_type=F32
-            )
-            g_p2 = mask * g_a2 * (sig * (1.0 + p2 * (1.0 - sig)))
-            put_stack(g_p2, upward, stack2, parity, i)
-            put_turned(turned_ref, g_p2[low2 : low2 + size], plane - 2, east, channels)
+    product = functools.partial(convolve, stack1, ahead2_ref, rows=rows2, upward=upward)
+    for i, parity, value in ahead_of(grouped((planes - 4) // 2, 2), product):
+        plane = 2 * i + parity
+        mask = mask_ref[plane + 2, here]
+        p2 = mask * value
+        sig = 0.5 * jnp.tanh(0.5 * p2) + 0.5
+        a2 = (p2 * sig).astype(BF16)
+        logits = lax.dot_general(a2, head, (((1,), (1,)), ((), ())), preferred_element_type=F32)
+        g_logits = jnp.where(class_lane, mask * (logits - x_ref[plane + 2, here].astype(F32)), 0.0)
+        coarse = g_logits.astype(BF16)
+        fine = (g_logits - coarse.astype(F32)).astype(BF16)
+        g_a2 = jnp.dot(
+            jnp.concatenate([coarse, fine], 1), jnp.concatenate([head, head], 0), preferred_element_type=F32
+        )
+        g_p2 = mask * g_a2 * (sig * (1.0 + p2 * (1.0 - sig)))
+        put_stack(g_p2, upward, stack2, parity, i)
+        put_turned(turned_ref, g_p2[low2 : low2 + size], plane - 2, east, channels)
 
     upper = high_bit("east", 1) == 1
     for t, tile in enumerate(kernel_sum(turned_ref, stack1, 3, east, rows2, upward, low2, size, channels)):
         kept_ref[t * channels : (t + 1) * channels, :] = tile.astype(BF16)
 
     there = slice(2 * upward + upward, 2 * upward + upward + rows3)
-    for first, stop in grouped((planes - 6) // 2, 2):
-        for i, parity, value in convolve(stack2, back2_ref, first, stop, rows3, upward):
-            plane = 2 * i + parity
-            g_p1 = slope_ref[plane + 2, there] * value
-            grad_ref[plane] = g_p1.astype(BF16)
-            put_turned(turned_ref, g_p1[low3 : low3 + size], plane - 1, east, channels)
+    product = functools.partial(convolve, stack2, back2_ref, rows=rows3, upward=upward)
+    for i, parity, value in ahead_of(grouped((planes - 6) // 2, 2), product):
+        plane = 2 * i + parity
+        g_p1 = slope_ref[plane + 2, there] * value
+        grad_ref[plane] = g_p1.astype(BF16)
+        put_turned(turned_ref, g_p1[low3 : low3 + size], plane - 1, east, channels)
 
     tiles = kernel_sum(turned_ref, stack0, 4, east, rows, upward, low, size, channels)
     for t, tile in enumerate(tiles):

time: 62.6 us -> 61.7 us (0.986)
  Pallas kernels: 25.5 us -> 24.5 us
    pallas_call x1, Pallas kernels: 14.7 us -> 13.7 us  [per_device(): pl.pallas_call(functools.partial(whole_kernel, channels, classes, east, n...]
where the time goes in v15:
time: 61.7 us; the launch traced here: 61.4 us
  Pallas kernels  24.5 us (40%)
  starting transfers between devices  20.2 us (33%)
  waiting for transfers between devices  15.7 us (25%)
  between operations  0.75 us (1%)
    ppermute x15, starting transfers between devices, exchange(): return lax.ppermute(value, ('east', 'north'), pairs)  20.2 us
    ppermute x15, waiting for transfers between devices, exchange(): return lax.ppermute(value, ('east', 'north'), pairs)  15.7 us
    pallas_call x1, Pallas kernels, per_device(): pl.pallas_call(functools.partial(whole_kernel, channels, classes, east, n...  13.7 us
    pallas_call x1, Pallas kernels, beside(): pl.pallas_call(functools.partial(last_kernel, channels, east, north, upwa...  3.63 us
    pallas_call x2, Pallas kernels, unpack(): pl.pallas_call(functools.partial(unpack_kernel, channels, scale, bool(ali...  2.43 us
    pallas_call x1, Pallas kernels, per_device(): pl.pallas_call(functools.partial(weights_kernel, channels, classes), out_...  2.37 us
    pallas_call x1, Pallas kernels, per_device(): pl.pallas_call(functools.partial(prepare_kernel, channels, upward, edge),...  2.28 us
  transfers between devices with their start and end apart: 15, of which 9 were waited for; matrix products, arithmetic and copies ran while one was open for 0% of the time, Pallas kernels for 12%

profile of v15, /device:TPU:0, one launch (start us, length us, event | category | flops | bytes accessed | tf_op | source)
XLA Modules:
  0.0 61.4 jit_solution(7818554976835534139)
XLA Ops:
  0.6 2.3 %prepare.1 = (bf16[8,128,128]{2,1,0:T(8,128)(2,1)S(1)}, bf16[4,128,128]{2,1,0:T(8,128)(2,1)S(1)}, bf16[4,128,128]{2,1,0:T(8,128)(2,1)S(1)}, bf16[8,32,128]{2,1,0...) custom-call(s32[1,1,2]{2,1,0:T(1,128)} %bitcast.15, bf16[8,128,96]{2,1,0:T(8,128)(2,1)} %bitcast.12, ...), custom_call_target="tpu_custom_call" | custom-call | tf_op jit(solution)/shard_map/prepare/pallas_call | solution.py:495
  3.4 2.6 %collective-permute-start.1 = (bf16[4,128,128]{2,1,0:T(8,128)(2,1)S(1)}, bf16[4,128,128]{2,1,0:T(8,128)(2,1)S(1)}, u32[]{:S(2)}, u32[]{:S(2)}) collective-permute-start(bf16[4,128,128]{2,1,0:T(8,128)(2,1)S(1)} %get-tuple-element.30), channel_id=1, source_target_pairs={{0,1},{1,0},{2,4},{3,5},{4,2},{5,3},{6,8},{7,9},{8,6},{9,7},{10,12... | collective-permute-start | bytes 393224 | tf_op jit(solution)/shard_map/ppermute | solution.py:41
  6.1 1.4 %collective-permute-start.3 = (bf16[4,32,128]{2,1,0:T(8,128)(2,1)S(1)}, bf16[4,32,128]{2,1,0:T(8,128)(2,1)S(1)}, u32[]{:S(2)}, u32[]{:S(2)}) collective-permute-start(bf16[4,32,128]{2,1,0:T(8,128)(2,1)S(1)} %get-tuple-element.32), channel_id=1, source_target_pairs={{0,3},{1,2},{2,1},{3,0},{4,7},{5,6},{6,5},{7,4},{8,11},{9,10},{10,... | collective-permute-start | bytes 98312 | tf_op jit(solution)/shard_map/ppermute | solution.py:41
  7.5 1.5 %collective-permute-start.4 = (bf16[4,32,128]{2,1,0:T(8,128)(2,1)S(1)}, bf16[4,32,128]{2,1,0:T(8,128)(2,1)S(1)}, u32[]{:S(2)}, u32[]{:S(2)}) collective-permute-start(bf16[4,32,128]{2,1,0:T(8,128)(2,1)S(1)} %get-tuple-element.33), channel_id=1, source_target_pairs={{0,1},{1,0},{2,5},{3,4},{4,3},{5,2},{6,9},{7,8},{8,7},{9,6},{10,13... | collective-permute-start | bytes 98312 | tf_op jit(solution)/shard_map/ppermute | solution.py:41
  9.0 2.4 %weights.1 = (bf16[4608,256]{1,0:T(8,128)(2,1)S(1)}, bf16[4608,256]{1,0:T(8,128)(2,1)S(1)}, bf16[128,128]{1,0:T(8,128)(2,1)S(1)}) custom-call(bf16[27,96,96]{2,1,0:T(8,128)(2,1)} %w1_in.3, bf16[27,96,96]{2,1,0:T(8,128)(2,1)} %w2_in.3, bf16[13,96]{1,0:T(8,128)(2,1)} %head_in.1), custom_call_target="tpu_custom_call" | custom-call | tf_op jit(solution)/shard_map/weights/pallas_call | solution.py:530
  11.4 13.7 %fields.1 = (bf16[10,144,128]{2,1,0:T(8,128)(2,1)S(1)}, bf16[2048,128]{1,0:T(8,128)(2,1)S(1)}, bf16[2048,128]{1,0:T(8,128)(2,1)S(1)}) custom-call(bf16[4608,256]{1,0:T(8,128)(2,1)S(1)} %get-tuple-element.26.ahead1_ref, bf16[27,96,96]{2,1,0:T(8,128)(2,1)} %w2_in.3, bf16[4608,256]{1,0:T(8,128)(2,1)S(1)} %get-tuple-element.27.back2_ref, ...), custom_call_target="tpu_custom_call" | custom-call | tf_op jit(solution)/shard_map/fields/pallas_call | solution.py:544
  25.1 1.1 %collective-permute-start.5 = (bf16[2048,128]{1,0:T(8,128)(2,1)S(1)}, bf16[2048,128]{1,0:T(8,128)(2,1)S(1)}, u32[]{:S(2)}, u32[]{:S(2)}) collective-permute-start(bf16[2048,128]{1,0:T(8,128)(2,1)S(1)} %get-tuple-element.36), channel_id=1, source_target_pairs={{0,2},{1,3},{2,0},{3,1},{4,6},{5,7},{6,4},{7,5},{8,10},{9,11},{10,... | collective-permute-start | bytes 1572872 | tf_op jit(solution)/shard_map/ppermute | solution.py:41
  26.2 1.5 %collective-permute-done.5.came_ref = bf16[2048,128]{1,0:T(8,128)(2,1)S(1)} collective-permute-done((bf16[2048,128]{1,0:T(8,128)(2,1)S(1)}, bf16[2048,128]{1,0:T(8,128)(2,1)S(1)}, u32[]{:S(2)}, u32[]{:S(2)}) %collective-permute-start.5) | collective-permute-done | bytes 524320 | tf_op jit(solution)/shard_map/ppermute | solution.py:41
  27.9 1.8 %collective-permute-start.8 = (bf16[512,128]{1,0:T(8,128)(2,1)S(1)}, bf16[512,128]{1,0:T(8,128)(2,1)S(1)}, u32[]{:S(2)}, u32[]{:S(2)}) collective-permute-start(bf16[512,128]{1,0:T(8,128)(2,1)S(1)} %get-tuple-element.42), channel_id=1, source_target_pairs={{0,1},{1,0},{2,3},{3,2},{4,5},{5,4},{6,7},{7,6},{8,9},{9,8},{10,11... | collective-permute-start | bytes 393224 | tf_op jit(solution)/shard_map/ppermute | solution.py:41
  29.7 1.4 %collective-permute-start.7 = (bf16[512,128]{1,0:T(8,128)(2,1)S(1)}, bf16[512,128]{1,0:T(8,128)(2,1)S(1)}, u32[]{:S(2)}, u32[]{:S(2)}) collective-permute-start(bf16[512,128]{1,0:T(8,128)(2,1)S(1)} %get-tuple-element.41), channel_id=1, source_target_pairs={{0,4},{1,5},{2,6},{3,7},{4,0},{5,1},{6,2},{7,3},{8,12},{9,13},{10,... | collective-permute-start | bytes 393224 | tf_op jit(solution)/shard_map/ppermute | solution.py:41
  31.4 3.6 %features.1 = (bf16[8,128,96]{2,1,0:T(8,128)(2,1)}, f32[512,128]{1,0:T(8,128)S(1)}) custom-call(bf16[8,128,128]{2,1,0:T(8,128)(2,1)S(1)} %get-tuple-element.25.center_ref, bf16[10,144,128]{2,1,0:T(8,128)(2,1)S(1)} %get-tuple-element.34.grad_ref, bf16[27,96,96]{2,1,0:T(8,128)(2,1)} %w1_in.3, ...), custom_call_target="tpu_custom_call", output_to_operand_aliasing={{1}: (3, {})} | custom-call | tf_op jit(solution)/shard_map/features/pallas_call | solution.py:572
  35.1 2.7 %collective-permute-done.7 = bf16[512,128]{1,0:T(8,128)(2,1)S(1)} collective-permute-done((bf16[512,128]{1,0:T(8,128)(2,1)S(1)}, bf16[512,128]{1,0:T(8,128)(2,1)S(1)}, u32[]{:S(2)}, u32[]{:S(2)}) %collective-permute-start.7) | collective-permute-done | bytes 131104 | tf_op jit(solution)/shard_map/ppermute | solution.py:41
  37.8 2.0 %collective-permute-start.9 = (bf16[512,128]{1,0:T(8,128)(2,1)S(1)}, bf16[512,128]{1,0:T(8,128)(2,1)S(1)}, u32[]{:S(2)}, u32[]{:S(2)}) collective-permute-start(bf16[512,128]{1,0:T(8,128)(2,1)S(1)} %add_convert_fusion.2), channel_id=1, source_target_pairs={{0,8},{1,9},{2,10},{3,11},{4,12},{5,13},{6,14},{7,15},{8,0},{9,1},... | collective-permute-start | bytes 393224 | tf_op jit(solution)/shard_map/ppermute | solution.py:41
  39.9 3.0 %collective-permute-done.9 = bf16[512,128]{1,0:T(8,128)(2,1)S(1)} collective-permute-done((bf16[512,128]{1,0:T(8,128)(2,1)S(1)}, bf16[512,128]{1,0:T(8,128)(2,1)S(1)}, u32[]{:S(2)}, u32[]{:S(2)}) %collective-permute-start.9) | collective-permute-done | bytes 131104 | tf_op jit(solution)/shard_map/ppermute | solution.py:41
  42.9 3.1 %collective-permute-start.10 = (bf16[512,128]{1,0:T(8,128)(2,1)S(1)}, bf16[512,128]{1,0:T(8,128)(2,1)S(1)}, u32[]{:S(2)}, u32[]{:S(2)}) collective-permute-start(bf16[512,128]{1,0:T(8,128)(2,1)S(1)} %add_convert_fusion.1), channel_id=1, source_target_pairs={{0,16},{1,17},{2,18},{3,19},{4,20},{5,21},{6,22},{7,23},{8,24},{9,... | collective-permute-start | bytes 393224 | tf_op jit(solution)/shard_map/ppermute | solution.py:41
  46.0 3.0 %collective-permute-done.10 = bf16[512,128]{1,0:T(8,128)(2,1)S(1)} collective-permute-done((bf16[512,128]{1,0:T(8,128)(2,1)S(1)}, bf16[512,128]{1,0:T(8,128)(2,1)S(1)}, u32[]{:S(2)}, u32[]{:S(2)}) %collective-permute-start.10) | collective-permute-done | bytes 131104 | tf_op jit(solution)/shard_map/ppermute | solution.py:41
  49.0 2.9 %collective-permute-start.11 = (bf16[512,128]{1,0:T(8,128)(2,1)S(1)}, bf16[512,128]{1,0:T(8,128)(2,1)S(1)}, u32[]{:S(2)}, u32[]{:S(2)}) collective-permute-start(bf16[512,128]{1,0:T(8,128)(2,1)S(1)} %add_convert_fusion), channel_id=1, source_target_pairs={{0,5},{1,4},{2,7},{3,6},{4,1},{5,0},{6,3},{7,2},{8,13},{9,12},{10,... | collective-permute-start | bytes 393224 | tf_op jit(solution)/shard_map/ppermute | solution.py:41
  51.9 1.2 %collective-permute-start.12 = (bf16[512,128]{1,0:T(8,128)(2,1)S(1)}, bf16[512,128]{1,0:T(8,128)(2,1)S(1)}, u32[]{:S(2)}, u32[]{:S(2)}) collective-permute-start(bf16[512,128]{1,0:T(8,128)(2,1)S(1)} %add_convert_fusion), channel_id=1, source_target_pairs={{0,4},{1,5},{2,6},{3,7},{4,0},{5,1},{6,2},{7,3},{8,12},{9,13},{10,... | collective-permute-start | bytes 393224 | tf_op jit(solution)/shard_map/ppermute | solution.py:41
  53.3 2.0 %collective-permute-done.11 = bf16[512,128]{1,0:T(8,128)(2,1)S(1)} collective-permute-done((bf16[512,128]{1,0:T(8,128)(2,1)S(1)}, bf16[512,128]{1,0:T(8,128)(2,1)S(1)}, u32[]{:S(2)}, u32[]{:S(2)}) %collective-permute-start.11) | collective-permute-done | bytes 131104 | tf_op jit(solution)/shard_map/ppermute | solution.py:41
  55.2 1.7 %collective-permute-done.12 = bf16[512,128]{1,0:T(8,128)(2,1)S(1)} collective-permute-done((bf16[512,128]{1,0:T(8,128)(2,1)S(1)}, bf16[512,128]{1,0:T(8,128)(2,1)S(1)}, u32[]{:S(2)}, u32[]{:S(2)}) %collective-permute-start.12) | collective-permute-done | bytes 131104 | tf_op jit(solution)/shard_map/ppermute | solution.py:41
  56.9 1.2 %collective-permute-done.13 = bf16[512,128]{1,0:T(8,128)(2,1)S(1)} collective-permute-done((bf16[512,128]{1,0:T(8,128)(2,1)S(1)}, bf16[512,128]{1,0:T(8,128)(2,1)S(1)}, u32[]{:S(2)}, u32[]{:S(2)}) %collective-permute-start.13) | collective-permute-done | bytes 131104 | tf_op jit(solution)/shard_map/ppermute | solution.py:41
  58.3 1.2 %unpack.2 = (f32[27,96,96]{2,1,0:T(8,128)}, f32[27,96,96]{2,1,0:T(8,128)}) custom-call(s32[1]{0:T(128)} %bitcast.9.first_ref_flag, bf16[2048,128]{1,0:T(8,128)(2,1)S(1)} %pad_maximum_fusion.packed_ref), custom_call_target="tpu_custom_call" | custom-call | tf_op jit(solution)/shard_map/unpack/pallas_call | solution.py:611
  59.5 0.7 %collective-permute-done.14.packed_ref = bf16[2048,128]{1,0:T(8,128)(2,1)S(1)} collective-permute-done((bf16[2048,128]{1,0:T(8,128)(2,1)S(1)}, bf16[2048,128]{1,0:T(8,128)(2,1)S(1)}, u32[]{:S(2)}, u32[]{:S(2)}) %collective-permute-start.14) | collective-permute-done | bytes 524320 | tf_op jit(solution)/shard_map/ppermute | solution.py:41
  60.2 1.2 %unpack.3 = (f32[27,96,96]{2,1,0:T(8,128)}, f32[27,96,96]{2,1,0:T(8,128)}) custom-call(s32[1]{0:T(128)} %bitcast.8.first_ref_flag, bf16[2048,128]{1,0:T(8,128)(2,1)S(1)} %collective-permute-done.14.packed_ref, f32[27,96,96]{2,1,0:T(8,128)} %get-tuple-element.43.refs_0_, ...), custom_call_target="tpu_custom_call", output_to_operand_aliasing={{0}: (2, {}), {1}: (3, {})} | custom-call | tf_op jit(solution)/shard_map/unpack/pallas_call | solution.py:611
  (18 shorter events, 1.6 us)
Async XLA Ops:
  2.9 8.5 %collective-permute-start = (bf16[4,128,128]{2,1,0:T(8,128)(2,1)S(1)}, bf16[4,128,128]{2,1,0:T(8,128)(2,1)S(1)}, u32[]{:S(2)}, u32[]{:S(2)}) collective-permute-start(bf16[4,128,128]{2,1,0:T(8,128)(2,1)S(1)} %get-tuple-element.29), channel_id=1, source_target_pairs={{0,2},{1,3},{2,0},{3,1},{4,6},{5,7},{6,4},{7,5},{8,10},{9,11},{10,... | collective-permute-start | bytes 393224 | tf_op jit(solution)/shard_map/ppermute | solution.py:41
  3.4 8.0 %collective-permute-start.1 = (bf16[4,128,128]{2,1,0:T(8,128)(2,1)S(1)}, bf16[4,128,128]{2,1,0:T(8,128)(2,1)S(1)}, u32[]{:S(2)}, u32[]{:S(2)}) collective-permute-start(bf16[4,128,128]{2,1,0:T(8,128)(2,1)S(1)} %get-tuple-element.30), channel_id=1, source_target_pairs={{0,1},{1,0},{2,4},{3,5},{4,2},{5,3},{6,8},{7,9},{8,6},{9,7},{10,12... | collective-permute-start | bytes 393224 | tf_op jit(solution)/shard_map/ppermute | solution.py:41
  6.0 5.4 %collective-permute-start.2 = (bf16[8,32,128]{2,1,0:T(8,128)(2,1)S(1)}, bf16[8,32,128]{2,1,0:T(8,128)(2,1)S(1)}, u32[]{:S(2)}, u32[]{:S(2)}) collective-permute-start(bf16[8,32,128]{2,1,0:T(8,128)(2,1)S(1)} %get-tuple-element.31), channel_id=1, source_target_pairs={{0,1},{1,0},{2,3},{3,2},{4,5},{5,4},{6,7},{7,6},{8,9},{9,8},{10,11... | collective-permute-start | bytes 196616 | tf_op jit(solution)/shard_map/ppermute | solution.py:41
  6.1 5.3 %collective-permute-start.3 = (bf16[4,32,128]{2,1,0:T(8,128)(2,1)S(1)}, bf16[4,32,128]{2,1,0:T(8,128)(2,1)S(1)}, u32[]{:S(2)}, u32[]{:S(2)}) collective-permute-start(bf16[4,32,128]{2,1,0:T(8,128)(2,1)S(1)} %get-tuple-element.32), channel_id=1, source_target_pairs={{0,3},{1,2},{2,1},{3,0},{4,7},{5,6},{6,5},{7,4},{8,11},{9,10},{10,... | collective-permute-start | bytes 98312 | tf_op jit(solution)/shard_map/ppermute | solution.py:41
  7.5 3.9 %collective-permute-start.4 = (bf16[4,32,128]{2,1,0:T(8,128)(2,1)S(1)}, bf16[4,32,128]{2,1,0:T(8,128)(2,1)S(1)}, u32[]{:S(2)}, u32[]{:S(2)}) collective-permute-start(bf16[4,32,128]{2,1,0:T(8,128)(2,1)S(1)} %get-tuple-element.33), channel_id=1, source_target_pairs={{0,1},{1,0},{2,5},{3,4},{4,3},{5,2},{6,9},{7,8},{8,7},{9,6},{10,13... | collective-permute-start | bytes 98312 | tf_op jit(solution)/shard_map/ppermute | solution.py:41
  25.1 2.6 %collective-permute-start.5 = (bf16[2048,128]{1,0:T(8,128)(2,1)S(1)}, bf16[2048,128]{1,0:T(8,128)(2,1)S(1)}, u32[]{:S(2)}, u32[]{:S(2)}) collective-permute-start(bf16[2048,128]{1,0:T(8,128)(2,1)S(1)} %get-tuple-element.36), channel_id=1, source_target_pairs={{0,2},{1,3},{2,0},{3,1},{4,6},{5,7},{6,4},{7,5},{8,10},{9,11},{10,... | collective-permute-start | bytes 1572872 | tf_op jit(solution)/shard_map/ppermute | solution.py:41
  27.9 7.2 %collective-permute-start.8 = (bf16[512,128]{1,0:T(8,128)(2,1)S(1)}, bf16[512,128]{1,0:T(8,128)(2,1)S(1)}, u32[]{:S(2)}, u32[]{:S(2)}) collective-permute-start(bf16[512,128]{1,0:T(8,128)(2,1)S(1)} %get-tuple-element.42), channel_id=1, source_target_pairs={{0,1},{1,0},{2,3},{3,2},{4,5},{5,4},{6,7},{7,6},{8,9},{9,8},{10,11... | collective-permute-start | bytes 393224 | tf_op jit(solution)/shard_map/ppermute | solution.py:41
  29.7 8.1 %collective-permute-start.7 = (bf16[512,128]{1,0:T(8,128)(2,1)S(1)}, bf16[512,128]{1,0:T(8,128)(2,1)S(1)}, u32[]{:S(2)}, u32[]{:S(2)}) collective-permute-start(bf16[512,128]{1,0:T(8,128)(2,1)S(1)} %get-tuple-element.41), channel_id=1, source_target_pairs={{0,4},{1,5},{2,6},{3,7},{4,0},{5,1},{6,2},{7,3},{8,12},{9,13},{10,... | collective-permute-start | bytes 393224 | tf_op jit(solution)/shard_map/ppermute | solution.py:41
  31.1 6.7 %collective-permute-start.6 = (bf16[512,128]{1,0:T(8,128)(2,1)S(1)}, bf16[512,128]{1,0:T(8,128)(2,1)S(1)}, u32[]{:S(2)}, u32[]{:S(2)}) collective-permute-start(bf16[512,128]{1,0:T(8,128)(2,1)S(1)} %get-tuple-element.40), channel_id=1, source_target_pairs={{0,5},{1,4},{2,7},{3,6},{4,1},{5,0},{6,3},{7,2},{8,13},{9,12},{10,... | collective-permute-start | bytes 393224 | tf_op jit(solution)/shard_map/ppermute | solution.py:41
  37.8 5.0 %collective-permute-start.9 = (bf16[512,128]{1,0:T(8,128)(2,1)S(1)}, bf16[512,128]{1,0:T(8,128)(2,1)S(1)}, u32[]{:S(2)}, u32[]{:S(2)}) collective-permute-start(bf16[512,128]{1,0:T(8,128)(2,1)S(1)} %add_convert_fusion.2), channel_id=1, source_target_pairs={{0,8},{1,9},{2,10},{3,11},{4,12},{5,13},{6,14},{7,15},{8,0},{9,1},... | collective-permute-start | bytes 393224 | tf_op jit(solution)/shard_map/ppermute | solution.py:41
  42.9 6.1 %collective-permute-start.10 = (bf16[512,128]{1,0:T(8,128)(2,1)S(1)}, bf16[512,128]{1,0:T(8,128)(2,1)S(1)}, u32[]{:S(2)}, u32[]{:S(2)}) collective-permute-start(bf16[512,128]{1,0:T(8,128)(2,1)S(1)} %add_convert_fusion.1), channel_id=1, source_target_pairs={{0,16},{1,17},{2,18},{3,19},{4,20},{5,21},{6,22},{7,23},{8,24},{9,... | collective-permute-start | bytes 393224 | tf_op jit(solution)/shard_map/ppermute | solution.py:41
  49.0 6.2 %collective-permute-start.11 = (bf16[512,128]{1,0:T(8,128)(2,1)S(1)}, bf16[512,128]{1,0:T(8,128)(2,1)S(1)}, u32[]{:S(2)}, u32[]{:S(2)}) collective-permute-start(bf16[512,128]{1,0:T(8,128)(2,1)S(1)} %add_convert_fusion), channel_id=1, source_target_pairs={{0,5},{1,4},{2,7},{3,6},{4,1},{5,0},{6,3},{7,2},{8,13},{9,12},{10,... | collective-permute-start | bytes 393224 | tf_op jit(solution)/shard_map/ppermute | solution.py:41
  51.9 5.0 %collective-permute-start.12 = (bf16[512,128]{1,0:T(8,128)(2,1)S(1)}, bf16[512,128]{1,0:T(8,128)(2,1)S(1)}, u32[]{:S(2)}, u32[]{:S(2)}) collective-permute-start(bf16[512,128]{1,0:T(8,128)(2,1)S(1)} %add_convert_fusion), channel_id=1, source_target_pairs={{0,4},{1,5},{2,6},{3,7},{4,0},{5,1},{6,2},{7,3},{8,12},{9,13},{10,... | collective-permute-start | bytes 393224 | tf_op jit(solution)/shard_map/ppermute | solution.py:41
  53.1 5.0 %collective-permute-start.13 = (bf16[512,128]{1,0:T(8,128)(2,1)S(1)}, bf16[512,128]{1,0:T(8,128)(2,1)S(1)}, u32[]{:S(2)}, u32[]{:S(2)}) collective-permute-start(bf16[512,128]{1,0:T(8,128)(2,1)S(1)} %add_convert_fusion), channel_id=1, source_target_pairs={{0,1},{1,0},{2,3},{3,2},{4,5},{5,4},{6,7},{7,6},{8,9},{9,8},{10,11... | collective-permute-start | bytes 393224 | tf_op jit(solution)/shard_map/ppermute | solution.py:41
  58.2 2.0 %collective-permute-start.14 = (bf16[2048,128]{1,0:T(8,128)(2,1)S(1)}, bf16[2048,128]{1,0:T(8,128)(2,1)S(1)}, u32[]{:S(2)}, u32[]{:S(2)}) collective-permute-start(bf16[2048,128]{1,0:T(8,128)(2,1)S(1)} %pad_maximum_fusion.packed_ref), channel_id=1, source_target_pairs={{0,2},{1,3},{2,0},{3,1},{4,6},{5,7},{6,4},{7,5},{8,10},{9,11},{10,... | collective-permute-start | bytes 1572872 | tf_op jit(solution)/shard_map/ppermute | solution.py:41

commit v16 on v13

--- a/solution.py
+++ b/solution.py
@@ -138,6 +138,26 @@
         for pair in range(first, stop)
         for parity in range(2)
     ]
+
+
+def staged(stages):
+    held, done = None, [0] * len(stages)
+
+    def finish():
+        number, last, outcome = held
+        stages[number][2](outcome, last)
+        done[number] += len(outcome)
+
+    for number, (runs, product, _) in enumerate(stages):
+        for run in runs:
+            if number > 0 and done[number - 1] < 2 * run[1] + 2:
+                finish()
+                held = None
+            coming = (number, run == runs[-1], product(*run))
+            if held is not None:
+                finish()
+            held = coming
+    finish()
 
 
 def unit_of(channels):
@@ -338,10 +358,16 @@
         a0 = jnp.where((mask > 0) & (lane < channels), x, 0.0)
         put_stack(jnp.concatenate([border, a0, border], 0), upward, stack0, plane % 2, plane // 2)
 
-    copy.wait()
-    put_ahead(ahead2_ref, w2_ref, channels)
-    for first, stop in grouped((planes - 2) // 2, 2):
-        for i, parity, value in convolve(stack0, ahead1_ref, first, stop, rows, upward):
+    head = head_ref[...]
+    class_lane = (lane[0:rows2] > channels) & (lane[0:rows2] <= channels + classes)
+    here = slice(2 * upward, 2 * upward + rows2)
+    there = slice(2 * upward + upward, 2 * upward + upward + rows3)
+
+    def first_forward(outcome, last):
+        if outcome[0][0] == 0:
+            copy.wait()
+            put_ahead(ahead2_ref, w2_ref, channels)
+        for i, parity, value in outcome:
             plane = 2 * i + parity
             mask = mask_ref[plane + 1]
             p1 = mask * value
@@ -349,40 +375,56 @@
             slope_ref[plane] = mask * (sig * (1.0 + p1 * (1.0 - sig)))
             put_stack((p1 * sig)[upward : upward + rows1], upward, stack1, parity, i)
 
-    head = head_ref[...]
-    class_lane = (lane[0:rows2] > channels) & (lane[0:rows2] <= channels + classes)
-    here = slice(2 * upward, 2 * upward + rows2)
-
-    for first, stop in grouped((planes - 4) // 2, 2):
-        for i, parity, value in convolve(stack1, ahead2_ref, first, stop, rows2, upward):
-            plane = 2 * i + parity
-            mask = mask_ref[plane + 2, here]
+    def second_forward(outcome, last):
+        a2, slopes, errors = [], [], []
+        for i, parity, value in outcome:
+            mask = mask_ref[2 * i + parity + 2, here]
             p2 = mask * value
             sig = 0.5 * jnp.tanh(0.5 * p2) + 0.5
-            a2 = (p2 * sig).astype(BF16)
-            logits = lax.dot_general(a2, head, (((1,), (1,)), ((), ())), preferred_element_type=F32)
-            g_logits = jnp.where(class_lane, mask * (logits - x_ref[plane + 2, here].astype(F32)), 0.0)
-            coarse = g_logits.astype(BF16)
-            fine = (g_logits - coarse.astype(F32)).astype(BF16)
-            g_a2 = jnp.dot(
-                jnp.concatenate([coarse, fine], 1), jnp.concatenate([head, head], 0), preferred_element_type=F32
-            )
-            g_p2 = mask * g_a2 * (sig * (1.0 + p2 * (1.0 - sig)))
+            a2.append((p2 * sig).astype(BF16))
+            slopes.append(mask * (sig * (1.0 + p2 * (1.0 - sig))))
+        logits = lax.dot_general(
+            jnp.concatenate(a2, 0), head, (((1,), (1,)), ((), ())), preferred_element_type=F32
+        )
+        for number, (i, parity, _) in enumerate(outcome):
+            plane = 2 * i + parity + 2
+            own = logits[number * rows2 : (number + 1) * rows2]
+            error = jnp.where(class_lane, mask_ref[plane, here] * (own - x_ref[plane, here].astype(F32)), 0.0)
+            coarse = error.astype(BF16)
+            fine = (error - coarse.astype(F32)).astype(BF16)
+            errors.append(jnp.concatenate([coarse, fine], 1))
+        g_a2 = jnp.dot(jnp.concatenate(errors, 0), jnp.concatenate([head, head], 0), preferred_element_type=F32)
+        for number, (i, parity, _) in enumerate(outcome):
+            g_p2 = g_a2[number * rows2 : (number + 1) * rows2] * slopes[number]
             put_stack(g_p2, upward, stack2, parity, i)
-            put_turned(turned_ref, g_p2[low2 : low2 + size], plane - 2, east, channels)
-
-    upper = high_bit("east", 1) == 1
-    for t, tile in enumerate(kernel_sum(turned_ref, stack1, 3, east, rows2, upward, low2, size, channels)):
-        kept_ref[t * channels : (t + 1) * channels, :] = tile.astype(BF16)
-
-    there = slice(2 * upward + upward, 2 * upward + upward + rows3)
-    for first, stop in grouped((planes - 6) // 2, 2):
-        for i, parity, value in convolve(stack2, back2_ref, first, stop, rows3, upward):
+            put_turned(turned_ref, g_p2[low2 : low2 + size], 2 * i + parity - 2, east, channels)
+        if last:
+            for t, tile in enumerate(kernel_sum(turned_ref, stack1, 3, east, rows2, upward, low2, size, channels)):
+                kept_ref[t * channels : (t + 1) * channels, :] = tile.astype(BF16)
+
+    def second_backward(outcome, last):
+        for i, parity, value in outcome:
             plane = 2 * i + parity
             g_p1 = slope_ref[plane + 2, there] * value
             grad_ref[plane] = g_p1.astype(BF16)
             put_turned(turned_ref, g_p1[low3 : low3 + size], plane - 1, east, channels)
 
+    steps = (
+        (2, stack0, ahead1_ref, rows, first_forward),
+        (4, stack1, ahead2_ref, rows2, second_forward),
+        (6, stack2, back2_ref, rows3, second_backward),
+    )
+    staged(
+        [
+            (
+                grouped((planes - margin) // 2, 2),
+                functools.partial(convolve, stack, weight_ref, rows=height, upward=upward),
+                handler,
+            )
+            for margin, stack, weight_ref, height, handler in steps
+        ]
+    )
+    upper = high_bit("east", 1) == 1
     tiles = kernel_sum(turned_ref, stack0, 4, east, rows, upward, low, size, channels)
     for t, tile in enumerate(tiles):
         place = slice(t * channels, (t + 1) * channels)

time: 62.6 us -> 60.7 us (0.970)
  Pallas kernels: 25.5 us -> 23.6 us
    pallas_call x1, Pallas kernels: 14.7 us -> 12.8 us  [per_device(): pl.pallas_call(functools.partial(whole_kernel, channels, classes, east, n...]
where the time goes in v16:
time: 60.7 us; the launch traced here: 60.5 us
  Pallas kernels  23.6 us (39%)
  starting transfers between devices  20.3 us (33%)
  waiting for transfers between devices  15.6 us (26%)
  between operations  0.75 us (1%)
    ppermute x15, starting transfers between devices, exchange(): return lax.ppermute(value, ('east', 'north'), pairs)  20.3 us
    ppermute x15, waiting for transfers between devices, exchange(): return lax.ppermute(value, ('east', 'north'), pairs)  15.6 us
    pallas_call x1, Pallas kernels, per_device(): pl.pallas_call(functools.partial(whole_kernel, channels, classes, east, n...  12.8 us
    pallas_call x1, Pallas kernels, beside(): pl.pallas_call(functools.partial(last_kernel, channels, east, north, upwa...  3.63 us
    pallas_call x2, Pallas kernels, unpack(): pl.pallas_call(functools.partial(unpack_kernel, channels, scale, bool(ali...  2.43 us
    pallas_call x1, Pallas kernels, per_device(): pl.pallas_call(functools.partial(weights_kernel, channels, classes), out_...  2.37 us
    pallas_call x1, Pallas kernels, per_device(): pl.pallas_call(functools.partial(prepare_kernel, channels, upward, edge),...  2.28 us
  transfers between devices with their start and end apart: 15, of which 9 were waited for; matrix products, arithmetic and copies ran while one was open for 0% of the time, Pallas kernels for 12%

profile of v16, /device:TPU:0, one launch (start us, length us, event | category | flops | bytes accessed | tf_op | source)
XLA Modules:
  0.0 60.5 jit_solution(3640235241187867822)
XLA Ops:
  0.6 2.3 %prepare.1 = (bf16[8,128,128]{2,1,0:T(8,128)(2,1)S(1)}, bf16[4,128,128]{2,1,0:T(8,128)(2,1)S(1)}, bf16[4,128,128]{2,1,0:T(8,128)(2,1)S(1)}, bf16[8,32,128]{2,1,0...) custom-call(s32[1,1,2]{2,1,0:T(1,128)} %bitcast.15, bf16[8,128,96]{2,1,0:T(8,128)(2,1)} %bitcast.12, ...), custom_call_target="tpu_custom_call" | custom-call | tf_op jit(solution)/shard_map/prepare/pallas_call | solution.py:528
  3.4 2.6 %collective-permute-start.1 = (bf16[4,128,128]{2,1,0:T(8,128)(2,1)S(1)}, bf16[4,128,128]{2,1,0:T(8,128)(2,1)S(1)}, u32[]{:S(2)}, u32[]{:S(2)}) collective-permute-start(bf16[4,128,128]{2,1,0:T(8,128)(2,1)S(1)} %get-tuple-element.30), channel_id=1, source_target_pairs={{0,1},{1,0},{2,4},{3,5},{4,2},{5,3},{6,8},{7,9},{8,6},{9,7},{10,12... | collective-permute-start | bytes 393224 | tf_op jit(solution)/shard_map/ppermute | solution.py:41
  6.1 1.4 %collective-permute-start.3 = (bf16[4,32,128]{2,1,0:T(8,128)(2,1)S(1)}, bf16[4,32,128]{2,1,0:T(8,128)(2,1)S(1)}, u32[]{:S(2)}, u32[]{:S(2)}) collective-permute-start(bf16[4,32,128]{2,1,0:T(8,128)(2,1)S(1)} %get-tuple-element.32), channel_id=1, source_target_pairs={{0,3},{1,2},{2,1},{3,0},{4,7},{5,6},{6,5},{7,4},{8,11},{9,10},{10,... | collective-permute-start | bytes 98312 | tf_op jit(solution)/shard_map/ppermute | solution.py:41
  7.5 1.5 %collective-permute-start.4 = (bf16[4,32,128]{2,1,0:T(8,128)(2,1)S(1)}, bf16[4,32,128]{2,1,0:T(8,128)(2,1)S(1)}, u32[]{:S(2)}, u32[]{:S(2)}) collective-permute-start(bf16[4,32,128]{2,1,0:T(8,128)(2,1)S(1)} %get-tuple-element.33), channel_id=1, source_target_pairs={{0,1},{1,0},{2,5},{3,4},{4,3},{5,2},{6,9},{7,8},{8,7},{9,6},{10,13... | collective-permute-start | bytes 98312 | tf_op jit(solution)/shard_map/ppermute | solution.py:41
  9.0 2.4 %weights.1 = (bf16[4608,256]{1,0:T(8,128)(2,1)S(1)}, bf16[4608,256]{1,0:T(8,128)(2,1)S(1)}, bf16[128,128]{1,0:T(8,128)(2,1)S(1)}) custom-call(bf16[27,96,96]{2,1,0:T(8,128)(2,1)} %w1_in.3, bf16[27,96,96]{2,1,0:T(8,128)(2,1)} %w2_in.3, bf16[13,96]{1,0:T(8,128)(2,1)} %head_in.1), custom_call_target="tpu_custom_call" | custom-call | tf_op jit(solution)/shard_map/weights/pallas_call | solution.py:563
  11.4 12.8 %fields.1 = (bf16[10,144,128]{2,1,0:T(8,128)(2,1)S(1)}, bf16[2048,128]{1,0:T(8,128)(2,1)S(1)}, bf16[2048,128]{1,0:T(8,128)(2,1)S(1)}) custom-call(bf16[4608,256]{1,0:T(8,128)(2,1)S(1)} %get-tuple-element.26.ahead1_ref, bf16[27,96,96]{2,1,0:T(8,128)(2,1)} %w2_in.3, bf16[4608,256]{1,0:T(8,128)(2,1)S(1)} %get-tuple-element.27.back2_ref, ...), custom_call_target="tpu_custom_call" | custom-call | tf_op jit(solution)/shard_map/fields/pallas_call | solution.py:577
  24.2 1.1 %collective-permute-start.5 = (bf16[2048,128]{1,0:T(8,128)(2,1)S(1)}, bf16[2048,128]{1,0:T(8,128)(2,1)S(1)}, u32[]{:S(2)}, u32[]{:S(2)}) collective-permute-start(bf16[2048,128]{1,0:T(8,128)(2,1)S(1)} %get-tuple-element.36), channel_id=1, source_target_pairs={{0,2},{1,3},{2,0},{3,1},{4,6},{5,7},{6,4},{7,5},{8,10},{9,11},{10,... | collective-permute-start | bytes 1572872 | tf_op jit(solution)/shard_map/ppermute | solution.py:41
  25.3 1.5 %collective-permute-done.5.came_ref = bf16[2048,128]{1,0:T(8,128)(2,1)S(1)} collective-permute-done((bf16[2048,128]{1,0:T(8,128)(2,1)S(1)}, bf16[2048,128]{1,0:T(8,128)(2,1)S(1)}, u32[]{:S(2)}, u32[]{:S(2)}) %collective-permute-start.5) | collective-permute-done | bytes 524320 | tf_op jit(solution)/shard_map/ppermute | solution.py:41
  27.0 1.8 %collective-permute-start.8 = (bf16[512,128]{1,0:T(8,128)(2,1)S(1)}, bf16[512,128]{1,0:T(8,128)(2,1)S(1)}, u32[]{:S(2)}, u32[]{:S(2)}) collective-permute-start(bf16[512,128]{1,0:T(8,128)(2,1)S(1)} %get-tuple-element.42), channel_id=1, source_target_pairs={{0,1},{1,0},{2,3},{3,2},{4,5},{5,4},{6,7},{7,6},{8,9},{9,8},{10,11... | collective-permute-start | bytes 393224 | tf_op jit(solution)/shard_map/ppermute | solution.py:41
  28.7 1.4 %collective-permute-start.7 = (bf16[512,128]{1,0:T(8,128)(2,1)S(1)}, bf16[512,128]{1,0:T(8,128)(2,1)S(1)}, u32[]{:S(2)}, u32[]{:S(2)}) collective-permute-start(bf16[512,128]{1,0:T(8,128)(2,1)S(1)} %get-tuple-element.41), channel_id=1, source_target_pairs={{0,4},{1,5},{2,6},{3,7},{4,0},{5,1},{6,2},{7,3},{8,12},{9,13},{10,... | collective-permute-start | bytes 393224 | tf_op jit(solution)/shard_map/ppermute | solution.py:41
  30.5 3.6 %features.1 = (bf16[8,128,96]{2,1,0:T(8,128)(2,1)}, f32[512,128]{1,0:T(8,128)S(1)}) custom-call(bf16[8,128,128]{2,1,0:T(8,128)(2,1)S(1)} %get-tuple-element.25.center_ref, bf16[10,144,128]{2,1,0:T(8,128)(2,1)S(1)} %get-tuple-element.34.grad_ref, bf16[27,96,96]{2,1,0:T(8,128)(2,1)} %w1_in.3, ...), custom_call_target="tpu_custom_call", output_to_operand_aliasing={{1}: (3, {})} | custom-call | tf_op jit(solution)/shard_map/features/pallas_call | solution.py:605
  34.2 2.6 %collective-permute-done.7 = bf16[512,128]{1,0:T(8,128)(2,1)S(1)} collective-permute-done((bf16[512,128]{1,0:T(8,128)(2,1)S(1)}, bf16[512,128]{1,0:T(8,128)(2,1)S(1)}, u32[]{:S(2)}, u32[]{:S(2)}) %collective-permute-start.7) | collective-permute-done | bytes 131104 | tf_op jit(solution)/shard_map/ppermute | solution.py:41
  36.9 2.1 %collective-permute-start.9 = (bf16[512,128]{1,0:T(8,128)(2,1)S(1)}, bf16[512,128]{1,0:T(8,128)(2,1)S(1)}, u32[]{:S(2)}, u32[]{:S(2)}) collective-permute-start(bf16[512,128]{1,0:T(8,128)(2,1)S(1)} %add_convert_fusion.2), channel_id=1, source_target_pairs={{0,8},{1,9},{2,10},{3,11},{4,12},{5,13},{6,14},{7,15},{8,0},{9,1},... | collective-permute-start | bytes 393224 | tf_op jit(solution)/shard_map/ppermute | solution.py:41
  39.0 2.9 %collective-permute-done.9 = bf16[512,128]{1,0:T(8,128)(2,1)S(1)} collective-permute-done((bf16[512,128]{1,0:T(8,128)(2,1)S(1)}, bf16[512,128]{1,0:T(8,128)(2,1)S(1)}, u32[]{:S(2)}, u32[]{:S(2)}) %collective-permute-start.9) | collective-permute-done | bytes 131104 | tf_op jit(solution)/shard_map/ppermute | solution.py:41
  42.0 3.1 %collective-permute-start.10 = (bf16[512,128]{1,0:T(8,128)(2,1)S(1)}, bf16[512,128]{1,0:T(8,128)(2,1)S(1)}, u32[]{:S(2)}, u32[]{:S(2)}) collective-permute-start(bf16[512,128]{1,0:T(8,128)(2,1)S(1)} %add_convert_fusion.1), channel_id=1, source_target_pairs={{0,16},{1,17},{2,18},{3,19},{4,20},{5,21},{6,22},{7,23},{8,24},{9,... | collective-permute-start | bytes 393224 | tf_op jit(solution)/shard_map/ppermute | solution.py:41
  45.0 3.0 %collective-permute-done.10 = bf16[512,128]{1,0:T(8,128)(2,1)S(1)} collective-permute-done((bf16[512,128]{1,0:T(8,128)(2,1)S(1)}, bf16[512,128]{1,0:T(8,128)(2,1)S(1)}, u32[]{:S(2)}, u32[]{:S(2)}) %collective-permute-start.10) | collective-permute-done | bytes 131104 | tf_op jit(solution)/shard_map/ppermute | solution.py:41
  48.1 2.9 %collective-permute-start.11 = (bf16[512,128]{1,0:T(8,128)(2,1)S(1)}, bf16[512,128]{1,0:T(8,128)(2,1)S(1)}, u32[]{:S(2)}, u32[]{:S(2)}) collective-permute-start(bf16[512,128]{1,0:T(8,128)(2,1)S(1)} %add_convert_fusion), channel_id=1, source_target_pairs={{0,5},{1,4},{2,7},{3,6},{4,1},{5,0},{6,3},{7,2},{8,13},{9,12},{10,... | collective-permute-start | bytes 393224 | tf_op jit(solution)/shard_map/ppermute | solution.py:41
  51.0 1.2 %collective-permute-start.12 = (bf16[512,128]{1,0:T(8,128)(2,1)S(1)}, bf16[512,128]{1,0:T(8,128)(2,1)S(1)}, u32[]{:S(2)}, u32[]{:S(2)}) collective-permute-start(bf16[512,128]{1,0:T(8,128)(2,1)S(1)} %add_convert_fusion), channel_id=1, source_target_pairs={{0,4},{1,5},{2,6},{3,7},{4,0},{5,1},{6,2},{7,3},{8,12},{9,13},{10,... | collective-permute-start | bytes 393224 | tf_op jit(solution)/shard_map/ppermute | solution.py:41
  52.4 1.9 %collective-permute-done.11 = bf16[512,128]{1,0:T(8,128)(2,1)S(1)} collective-permute-done((bf16[512,128]{1,0:T(8,128)(2,1)S(1)}, bf16[512,128]{1,0:T(8,128)(2,1)S(1)}, u32[]{:S(2)}, u32[]{:S(2)}) %collective-permute-start.11) | collective-permute-done | bytes 131104 | tf_op jit(solution)/shard_map/ppermute | solution.py:41
  54.3 1.7 %collective-permute-done.12 = bf16[512,128]{1,0:T(8,128)(2,1)S(1)} collective-permute-done((bf16[512,128]{1,0:T(8,128)(2,1)S(1)}, bf16[512,128]{1,0:T(8,128)(2,1)S(1)}, u32[]{:S(2)}, u32[]{:S(2)}) %collective-permute-start.12) | collective-permute-done | bytes 131104 | tf_op jit(solution)/shard_map/ppermute | solution.py:41
  55.9 1.2 %collective-permute-done.13 = bf16[512,128]{1,0:T(8,128)(2,1)S(1)} collective-permute-done((bf16[512,128]{1,0:T(8,128)(2,1)S(1)}, bf16[512,128]{1,0:T(8,128)(2,1)S(1)}, u32[]{:S(2)}, u32[]{:S(2)}) %collective-permute-start.13) | collective-permute-done | bytes 131104 | tf_op jit(solution)/shard_map/ppermute | solution.py:41
  57.4 1.2 %unpack.2 = (f32[27,96,96]{2,1,0:T(8,128)}, f32[27,96,96]{2,1,0:T(8,128)}) custom-call(s32[1]{0:T(128)} %bitcast.9.first_ref_flag, bf16[2048,128]{1,0:T(8,128)(2,1)S(1)} %pad_maximum_fusion.packed_ref), custom_call_target="tpu_custom_call" | custom-call | tf_op jit(solution)/shard_map/unpack/pallas_call | solution.py:644
  58.6 0.7 %collective-permute-done.14.packed_ref = bf16[2048,128]{1,0:T(8,128)(2,1)S(1)} collective-permute-done((bf16[2048,128]{1,0:T(8,128)(2,1)S(1)}, bf16[2048,128]{1,0:T(8,128)(2,1)S(1)}, u32[]{:S(2)}, u32[]{:S(2)}) %collective-permute-start.14) | collective-permute-done | bytes 524320 | tf_op jit(solution)/shard_map/ppermute | solution.py:41
  59.3 1.2 %unpack.3 = (f32[27,96,96]{2,1,0:T(8,128)}, f32[27,96,96]{2,1,0:T(8,128)}) custom-call(s32[1]{0:T(128)} %bitcast.8.first_ref_flag, bf16[2048,128]{1,0:T(8,128)(2,1)S(1)} %collective-permute-done.14.packed_ref, f32[27,96,96]{2,1,0:T(8,128)} %get-tuple-element.43.refs_0_, ...), custom_call_target="tpu_custom_call", output_to_operand_aliasing={{0}: (2, {}), {1}: (3, {})} | custom-call | tf_op jit(solution)/shard_map/unpack/pallas_call | solution.py:644
  (18 shorter events, 1.7 us)
Async XLA Ops:
  2.9 8.5 %collective-permute-start = (bf16[4,128,128]{2,1,0:T(8,128)(2,1)S(1)}, bf16[4,128,128]{2,1,0:T(8,128)(2,1)S(1)}, u32[]{:S(2)}, u32[]{:S(2)}) collective-permute-start(bf16[4,128,128]{2,1,0:T(8,128)(2,1)S(1)} %get-tuple-element.29), channel_id=1, source_target_pairs={{0,2},{1,3},{2,0},{3,1},{4,6},{5,7},{6,4},{7,5},{8,10},{9,11},{10,... | collective-permute-start | bytes 393224 | tf_op jit(solution)/shard_map/ppermute | solution.py:41
  3.4 8.0 %collective-permute-start.1 = (bf16[4,128,128]{2,1,0:T(8,128)(2,1)S(1)}, bf16[4,128,128]{2,1,0:T(8,128)(2,1)S(1)}, u32[]{:S(2)}, u32[]{:S(2)}) collective-permute-start(bf16[4,128,128]{2,1,0:T(8,128)(2,1)S(1)} %get-tuple-element.30), channel_id=1, source_target_pairs={{0,1},{1,0},{2,4},{3,5},{4,2},{5,3},{6,8},{7,9},{8,6},{9,7},{10,12... | collective-permute-start | bytes 393224 | tf_op jit(solution)/shard_map/ppermute | solution.py:41
  6.0 5.4 %collective-permute-start.2 = (bf16[8,32,128]{2,1,0:T(8,128)(2,1)S(1)}, bf16[8,32,128]{2,1,0:T(8,128)(2,1)S(1)}, u32[]{:S(2)}, u32[]{:S(2)}) collective-permute-start(bf16[8,32,128]{2,1,0:T(8,128)(2,1)S(1)} %get-tuple-element.31), channel_id=1, source_target_pairs={{0,1},{1,0},{2,3},{3,2},{4,5},{5,4},{6,7},{7,6},{8,9},{9,8},{10,11... | collective-permute-start | bytes 196616 | tf_op jit(solution)/shard_map/ppermute | solution.py:41
  6.1 5.3 %collective-permute-start.3 = (bf16[4,32,128]{2,1,0:T(8,128)(2,1)S(1)}, bf16[4,32,128]{2,1,0:T(8,128)(2,1)S(1)}, u32[]{:S(2)}, u32[]{:S(2)}) collective-permute-start(bf16[4,32,128]{2,1,0:T(8,128)(2,1)S(1)} %get-tuple-element.32), channel_id=1, source_target_pairs={{0,3},{1,2},{2,1},{3,0},{4,7},{5,6},{6,5},{7,4},{8,11},{9,10},{10,... | collective-permute-start | bytes 98312 | tf_op jit(solution)/shard_map/ppermute | solution.py:41
  7.5 3.9 %collective-permute-start.4 = (bf16[4,32,128]{2,1,0:T(8,128)(2,1)S(1)}, bf16[4,32,128]{2,1,0:T(8,128)(2,1)S(1)}, u32[]{:S(2)}, u32[]{:S(2)}) collective-permute-start(bf16[4,32,128]{2,1,0:T(8,128)(2,1)S(1)} %get-tuple-element.33), channel_id=1, source_target_pairs={{0,1},{1,0},{2,5},{3,4},{4,3},{5,2},{6,9},{7,8},{8,7},{9,6},{10,13... | collective-permute-start | bytes 98312 | tf_op jit(solution)/shard_map/ppermute | solution.py:41
  24.2 2.6 %collective-permute-start.5 = (bf16[2048,128]{1,0:T(8,128)(2,1)S(1)}, bf16[2048,128]{1,0:T(8,128)(2,1)S(1)}, u32[]{:S(2)}, u32[]{:S(2)}) collective-permute-start(bf16[2048,128]{1,0:T(8,128)(2,1)S(1)} %get-tuple-element.36), channel_id=1, source_target_pairs={{0,2},{1,3},{2,0},{3,1},{4,6},{5,7},{6,4},{7,5},{8,10},{9,11},{10,... | collective-permute-start | bytes 1572872 | tf_op jit(solution)/shard_map/ppermute | solution.py:41
  27.0 7.2 %collective-permute-start.8 = (bf16[512,128]{1,0:T(8,128)(2,1)S(1)}, bf16[512,128]{1,0:T(8,128)(2,1)S(1)}, u32[]{:S(2)}, u32[]{:S(2)}) collective-permute-start(bf16[512,128]{1,0:T(8,128)(2,1)S(1)} %get-tuple-element.42), channel_id=1, source_target_pairs={{0,1},{1,0},{2,3},{3,2},{4,5},{5,4},{6,7},{7,6},{8,9},{9,8},{10,11... | collective-permute-start | bytes 393224 | tf_op jit(solution)/shard_map/ppermute | solution.py:41
  28.7 8.1 %collective-permute-start.7 = (bf16[512,128]{1,0:T(8,128)(2,1)S(1)}, bf16[512,128]{1,0:T(8,128)(2,1)S(1)}, u32[]{:S(2)}, u32[]{:S(2)}) collective-permute-start(bf16[512,128]{1,0:T(8,128)(2,1)S(1)} %get-tuple-element.41), channel_id=1, source_target_pairs={{0,4},{1,5},{2,6},{3,7},{4,0},{5,1},{6,2},{7,3},{8,12},{9,13},{10,... | collective-permute-start | bytes 393224 | tf_op jit(solution)/shard_map/ppermute | solution.py:41
  30.1 6.7 %collective-permute-start.6 = (bf16[512,128]{1,0:T(8,128)(2,1)S(1)}, bf16[512,128]{1,0:T(8,128)(2,1)S(1)}, u32[]{:S(2)}, u32[]{:S(2)}) collective-permute-start(bf16[512,128]{1,0:T(8,128)(2,1)S(1)} %get-tuple-element.40), channel_id=1, source_target_pairs={{0,5},{1,4},{2,7},{3,6},{4,1},{5,0},{6,3},{7,2},{8,13},{9,12},{10,... | collective-permute-start | bytes 393224 | tf_op jit(solution)/shard_map/ppermute | solution.py:41
  36.9 5.0 %collective-permute-start.9 = (bf16[512,128]{1,0:T(8,128)(2,1)S(1)}, bf16[512,128]{1,0:T(8,128)(2,1)S(1)}, u32[]{:S(2)}, u32[]{:S(2)}) collective-permute-start(bf16[512,128]{1,0:T(8,128)(2,1)S(1)} %add_convert_fusion.2), channel_id=1, source_target_pairs={{0,8},{1,9},{2,10},{3,11},{4,12},{5,13},{6,14},{7,15},{8,0},{9,1},... | collective-permute-start | bytes 393224 | tf_op jit(solution)/shard_map/ppermute | solution.py:41
  42.0 6.0 %collective-permute-start.10 = (bf16[512,128]{1,0:T(8,128)(2,1)S(1)}, bf16[512,128]{1,0:T(8,128)(2,1)S(1)}, u32[]{:S(2)}, u32[]{:S(2)}) collective-permute-start(bf16[512,128]{1,0:T(8,128)(2,1)S(1)} %add_convert_fusion.1), channel_id=1, source_target_pairs={{0,16},{1,17},{2,18},{3,19},{4,20},{5,21},{6,22},{7,23},{8,24},{9,... | collective-permute-start | bytes 393224 | tf_op jit(solution)/shard_map/ppermute | solution.py:41
  48.1 6.2 %collective-permute-start.11 = (bf16[512,128]{1,0:T(8,128)(2,1)S(1)}, bf16[512,128]{1,0:T(8,128)(2,1)S(1)}, u32[]{:S(2)}, u32[]{:S(2)}) collective-permute-start(bf16[512,128]{1,0:T(8,128)(2,1)S(1)} %add_convert_fusion), channel_id=1, source_target_pairs={{0,5},{1,4},{2,7},{3,6},{4,1},{5,0},{6,3},{7,2},{8,13},{9,12},{10,... | collective-permute-start | bytes 393224 | tf_op jit(solution)/shard_map/ppermute | solution.py:41
  51.0 5.0 %collective-permute-start.12 = (bf16[512,128]{1,0:T(8,128)(2,1)S(1)}, bf16[512,128]{1,0:T(8,128)(2,1)S(1)}, u32[]{:S(2)}, u32[]{:S(2)}) collective-permute-start(bf16[512,128]{1,0:T(8,128)(2,1)S(1)} %add_convert_fusion), channel_id=1, source_target_pairs={{0,4},{1,5},{2,6},{3,7},{4,0},{5,1},{6,2},{7,3},{8,12},{9,13},{10,... | collective-permute-start | bytes 393224 | tf_op jit(solution)/shard_map/ppermute | solution.py:41
  52.2 5.0 %collective-permute-start.13 = (bf16[512,128]{1,0:T(8,128)(2,1)S(1)}, bf16[512,128]{1,0:T(8,128)(2,1)S(1)}, u32[]{:S(2)}, u32[]{:S(2)}) collective-permute-start(bf16[512,128]{1,0:T(8,128)(2,1)S(1)} %add_convert_fusion), channel_id=1, source_target_pairs={{0,1},{1,0},{2,3},{3,2},{4,5},{5,4},{6,7},{7,6},{8,9},{9,8},{10,11... | collective-permute-start | bytes 393224 | tf_op jit(solution)/shard_map/ppermute | solution.py:41
  57.3 2.0 %collective-permute-start.14 = (bf16[2048,128]{1,0:T(8,128)(2,1)S(1)}, bf16[2048,128]{1,0:T(8,128)(2,1)S(1)}, u32[]{:S(2)}, u32[]{:S(2)}) collective-permute-start(bf16[2048,128]{1,0:T(8,128)(2,1)S(1)} %pad_maximum_fusion.packed_ref), channel_id=1, source_target_pairs={{0,2},{1,3},{2,0},{3,1},{4,6},{5,7},{6,4},{7,5},{8,10},{9,11},{10,... | collective-permute-start | bytes 1572872 | tf_op jit(solution)/shard_map/ppermute | solution.py:41

commit v17 on v16

--- a/solution.py
+++ b/solution.py
@@ -351,12 +351,20 @@
     place_edges(center_ref, refs[:edges], low, x_ref)
     border = jnp.zeros((upward, LANES), F32)
 
-    for plane in range(planes):
+    built = []
+
+    def build(plane):
         x = x_ref[plane].astype(F32)
         mask = jnp.broadcast_to(x[:, channels : channels + 1], (rows, LANES))
         mask_ref[plane] = mask
         a0 = jnp.where((mask > 0) & (lane < channels), x, 0.0)
         put_stack(jnp.concatenate([border, a0, border], 0), upward, stack0, plane % 2, plane // 2)
+        built.append(plane)
+
+    def first_product(first, stop):
+        while len(built) < 2 * stop + 2:
+            build(len(built))
+        return convolve(stack0, ahead1_ref, first, stop, rows, upward)
 
     head = head_ref[...]
     class_lane = (lane[0:rows2] > channels) & (lane[0:rows2] <= channels + classes)
@@ -409,19 +417,19 @@
             grad_ref[plane] = g_p1.astype(BF16)
             put_turned(turned_ref, g_p1[low3 : low3 + size], plane - 1, east, channels)
 
-    steps = (
-        (2, stack0, ahead1_ref, rows, first_forward),
-        (4, stack1, ahead2_ref, rows2, second_forward),
-        (6, stack2, back2_ref, rows3, second_backward),
-    )
     staged(
         [
+            (grouped((planes - 2) // 2, 2), first_product, first_forward),
             (
-                grouped((planes - margin) // 2, 2),
-                functools.partial(convolve, stack, weight_ref, rows=height, upward=upward),
-                handler,
-            )
-            for margin, stack, weight_ref, height, handler in steps
+                grouped((planes - 4) // 2, 2),
+                functools.partial(convolve, stack1, ahead2_ref, rows=rows2, upward=upward),
+                second_forward,
+            ),
+            (
+                grouped((planes - 6) // 2, 2),
+                functools.partial(convolve, stack2, back2_ref, rows=rows3, upward=upward),
+                second_backward,
+            ),
         ]
     )
     upper = high_bit("east", 1) == 1

time: 60.7 us -> 60.7 us (level)
  no operation moved by 1% of the time
where the time goes in v17:
time: 60.7 us; the launch traced here: 60.5 us
  Pallas kernels  23.6 us (39%)
  starting transfers between devices  20.3 us (33%)
  waiting for transfers between devices  15.6 us (26%)
  between operations  0.75 us (1%)
    ppermute x15, starting transfers between devices, exchange(): return lax.ppermute(value, ('east', 'north'), pairs)  20.3 us
    ppermute x15, waiting for transfers between devices, exchange(): return lax.ppermute(value, ('east', 'north'), pairs)  15.6 us
    pallas_call x1, Pallas kernels, per_device(): pl.pallas_call(functools.partial(whole_kernel, channels, classes, east, n...  12.8 us
    pallas_call x1, Pallas kernels, beside(): pl.pallas_call(functools.partial(last_kernel, channels, east, north, upwa...  3.63 us
    pallas_call x2, Pallas kernels, unpack(): pl.pallas_call(functools.partial(unpack_kernel, channels, scale, bool(ali...  2.43 us
    pallas_call x1, Pallas kernels, per_device(): pl.pallas_call(functools.partial(weights_kernel, channels, classes), out_...  2.37 us
    pallas_call x1, Pallas kernels, per_device(): pl.pallas_call(functools.partial(prepare_kernel, channels, upward, edge),...  2.28 us
  transfers between devices with their start and end apart: 15, of which 9 were waited for; matrix products, arithmetic and copies ran while one was open for 0% of the time, Pallas kernels for 12%

profile of v17, /device:TPU:0, one launch (start us, length us, event | category | flops | bytes accessed | tf_op | source)
XLA Modules:
  0.0 60.5 jit_solution(14841973895146370293)
XLA Ops:
  0.6 2.3 %prepare.1 = (bf16[8,128,128]{2,1,0:T(8,128)(2,1)S(1)}, bf16[4,128,128]{2,1,0:T(8,128)(2,1)S(1)}, bf16[4,128,128]{2,1,0:T(8,128)(2,1)S(1)}, bf16[8,32,128]{2,1,0...) custom-call(s32[1,1,2]{2,1,0:T(1,128)} %bitcast.15, bf16[8,128,96]{2,1,0:T(8,128)(2,1)} %bitcast.12, ...), custom_call_target="tpu_custom_call" | custom-call | tf_op jit(solution)/shard_map/prepare/pallas_call | solution.py:536
  3.4 2.6 %collective-permute-start.1 = (bf16[4,128,128]{2,1,0:T(8,128)(2,1)S(1)}, bf16[4,128,128]{2,1,0:T(8,128)(2,1)S(1)}, u32[]{:S(2)}, u32[]{:S(2)}) collective-permute-start(bf16[4,128,128]{2,1,0:T(8,128)(2,1)S(1)} %get-tuple-element.30), channel_id=1, source_target_pairs={{0,1},{1,0},{2,4},{3,5},{4,2},{5,3},{6,8},{7,9},{8,6},{9,7},{10,12... | collective-permute-start | bytes 393224 | tf_op jit(solution)/shard_map/ppermute | solution.py:41
  6.1 1.4 %collective-permute-start.3 = (bf16[4,32,128]{2,1,0:T(8,128)(2,1)S(1)}, bf16[4,32,128]{2,1,0:T(8,128)(2,1)S(1)}, u32[]{:S(2)}, u32[]{:S(2)}) collective-permute-start(bf16[4,32,128]{2,1,0:T(8,128)(2,1)S(1)} %get-tuple-element.32), channel_id=1, source_target_pairs={{0,3},{1,2},{2,1},{3,0},{4,7},{5,6},{6,5},{7,4},{8,11},{9,10},{10,... | collective-permute-start | bytes 98312 | tf_op jit(solution)/shard_map/ppermute | solution.py:41
  7.5 1.5 %collective-permute-start.4 = (bf16[4,32,128]{2,1,0:T(8,128)(2,1)S(1)}, bf16[4,32,128]{2,1,0:T(8,128)(2,1)S(1)}, u32[]{:S(2)}, u32[]{:S(2)}) collective-permute-start(bf16[4,32,128]{2,1,0:T(8,128)(2,1)S(1)} %get-tuple-element.33), channel_id=1, source_target_pairs={{0,1},{1,0},{2,5},{3,4},{4,3},{5,2},{6,9},{7,8},{8,7},{9,6},{10,13... | collective-permute-start | bytes 98312 | tf_op jit(solution)/shard_map/ppermute | solution.py:41
  9.0 2.4 %weights.1 = (bf16[4608,256]{1,0:T(8,128)(2,1)S(1)}, bf16[4608,256]{1,0:T(8,128)(2,1)S(1)}, bf16[128,128]{1,0:T(8,128)(2,1)S(1)}) custom-call(bf16[27,96,96]{2,1,0:T(8,128)(2,1)} %w1_in.3, bf16[27,96,96]{2,1,0:T(8,128)(2,1)} %w2_in.3, bf16[13,96]{1,0:T(8,128)(2,1)} %head_in.1), custom_call_target="tpu_custom_call" | custom-call | tf_op jit(solution)/shard_map/weights/pallas_call | solution.py:571
  11.4 12.8 %fields.1 = (bf16[10,144,128]{2,1,0:T(8,128)(2,1)S(1)}, bf16[2048,128]{1,0:T(8,128)(2,1)S(1)}, bf16[2048,128]{1,0:T(8,128)(2,1)S(1)}) custom-call(bf16[4608,256]{1,0:T(8,128)(2,1)S(1)} %get-tuple-element.26.ahead1_ref, bf16[27,96,96]{2,1,0:T(8,128)(2,1)} %w2_in.3, bf16[4608,256]{1,0:T(8,128)(2,1)S(1)} %get-tuple-element.27.back2_ref, ...), custom_call_target="tpu_custom_call" | custom-call | tf_op jit(solution)/shard_map/fields/pallas_call | solution.py:585
  24.2 1.1 %collective-permute-start.5 = (bf16[2048,128]{1,0:T(8,128)(2,1)S(1)}, bf16[2048,128]{1,0:T(8,128)(2,1)S(1)}, u32[]{:S(2)}, u32[]{:S(2)}) collective-permute-start(bf16[2048,128]{1,0:T(8,128)(2,1)S(1)} %get-tuple-element.36), channel_id=1, source_target_pairs={{0,2},{1,3},{2,0},{3,1},{4,6},{5,7},{6,4},{7,5},{8,10},{9,11},{10,... | collective-permute-start | bytes 1572872 | tf_op jit(solution)/shard_map/ppermute | solution.py:41
  25.3 1.5 %collective-permute-done.5.came_ref = bf16[2048,128]{1,0:T(8,128)(2,1)S(1)} collective-permute-done((bf16[2048,128]{1,0:T(8,128)(2,1)S(1)}, bf16[2048,128]{1,0:T(8,128)(2,1)S(1)}, u32[]{:S(2)}, u32[]{:S(2)}) %collective-permute-start.5) | collective-permute-done | bytes 524320 | tf_op jit(solution)/shard_map/ppermute | solution.py:41
  27.0 1.7 %collective-permute-start.8 = (bf16[512,128]{1,0:T(8,128)(2,1)S(1)}, bf16[512,128]{1,0:T(8,128)(2,1)S(1)}, u32[]{:S(2)}, u32[]{:S(2)}) collective-permute-start(bf16[512,128]{1,0:T(8,128)(2,1)S(1)} %get-tuple-element.42), channel_id=1, source_target_pairs={{0,1},{1,0},{2,3},{3,2},{4,5},{5,4},{6,7},{7,6},{8,9},{9,8},{10,11... | collective-permute-start | bytes 393224 | tf_op jit(solution)/shard_map/ppermute | solution.py:41
  28.7 1.4 %collective-permute-start.7 = (bf16[512,128]{1,0:T(8,128)(2,1)S(1)}, bf16[512,128]{1,0:T(8,128)(2,1)S(1)}, u32[]{:S(2)}, u32[]{:S(2)}) collective-permute-start(bf16[512,128]{1,0:T(8,128)(2,1)S(1)} %get-tuple-element.41), channel_id=1, source_target_pairs={{0,4},{1,5},{2,6},{3,7},{4,0},{5,1},{6,2},{7,3},{8,12},{9,13},{10,... | collective-permute-start | bytes 393224 | tf_op jit(solution)/shard_map/ppermute | solution.py:41
  30.6 3.6 %features.1 = (bf16[8,128,96]{2,1,0:T(8,128)(2,1)}, f32[512,128]{1,0:T(8,128)S(1)}) custom-call(bf16[8,128,128]{2,1,0:T(8,128)(2,1)S(1)} %get-tuple-element.25.center_ref, bf16[10,144,128]{2,1,0:T(8,128)(2,1)S(1)} %get-tuple-element.34.grad_ref, bf16[27,96,96]{2,1,0:T(8,128)(2,1)} %w1_in.3, ...), custom_call_target="tpu_custom_call", output_to_operand_aliasing={{1}: (3, {})} | custom-call | tf_op jit(solution)/shard_map/features/pallas_call | solution.py:613
  34.2 2.6 %collective-permute-done.7 = bf16[512,128]{1,0:T(8,128)(2,1)S(1)} collective-permute-done((bf16[512,128]{1,0:T(8,128)(2,1)S(1)}, bf16[512,128]{1,0:T(8,128)(2,1)S(1)}, u32[]{:S(2)}, u32[]{:S(2)}) %collective-permute-start.7) | collective-permute-done | bytes 131104 | tf_op jit(solution)/shard_map/ppermute | solution.py:41
  36.9 2.1 %collective-permute-start.9 = (bf16[512,128]{1,0:T(8,128)(2,1)S(1)}, bf16[512,128]{1,0:T(8,128)(2,1)S(1)}, u32[]{:S(2)}, u32[]{:S(2)}) collective-permute-start(bf16[512,128]{1,0:T(8,128)(2,1)S(1)} %add_convert_fusion.2), channel_id=1, source_target_pairs={{0,8},{1,9},{2,10},{3,11},{4,12},{5,13},{6,14},{7,15},{8,0},{9,1},... | collective-permute-start | bytes 393224 | tf_op jit(solution)/shard_map/ppermute | solution.py:41
  39.0 3.0 %collective-permute-done.9 = bf16[512,128]{1,0:T(8,128)(2,1)S(1)} collective-permute-done((bf16[512,128]{1,0:T(8,128)(2,1)S(1)}, bf16[512,128]{1,0:T(8,128)(2,1)S(1)}, u32[]{:S(2)}, u32[]{:S(2)}) %collective-permute-start.9) | collective-permute-done | bytes 131104 | tf_op jit(solution)/shard_map/ppermute | solution.py:41
  42.0 3.1 %collective-permute-start.10 = (bf16[512,128]{1,0:T(8,128)(2,1)S(1)}, bf16[512,128]{1,0:T(8,128)(2,1)S(1)}, u32[]{:S(2)}, u32[]{:S(2)}) collective-permute-start(bf16[512,128]{1,0:T(8,128)(2,1)S(1)} %add_convert_fusion.1), channel_id=1, source_target_pairs={{0,16},{1,17},{2,18},{3,19},{4,20},{5,21},{6,22},{7,23},{8,24},{9,... | collective-permute-start | bytes 393224 | tf_op jit(solution)/shard_map/ppermute | solution.py:41
  45.1 3.0 %collective-permute-done.10 = bf16[512,128]{1,0:T(8,128)(2,1)S(1)} collective-permute-done((bf16[512,128]{1,0:T(8,128)(2,1)S(1)}, bf16[512,128]{1,0:T(8,128)(2,1)S(1)}, u32[]{:S(2)}, u32[]{:S(2)}) %collective-permute-start.10) | collective-permute-done | bytes 131104 | tf_op jit(solution)/shard_map/ppermute | solution.py:41
  48.1 2.9 %collective-permute-start.11 = (bf16[512,128]{1,0:T(8,128)(2,1)S(1)}, bf16[512,128]{1,0:T(8,128)(2,1)S(1)}, u32[]{:S(2)}, u32[]{:S(2)}) collective-permute-start(bf16[512,128]{1,0:T(8,128)(2,1)S(1)} %add_convert_fusion), channel_id=1, source_target_pairs={{0,5},{1,4},{2,7},{3,6},{4,1},{5,0},{6,3},{7,2},{8,13},{9,12},{10,... | collective-permute-start | bytes 393224 | tf_op jit(solution)/shard_map/ppermute | solution.py:41
  51.0 1.2 %collective-permute-start.12 = (bf16[512,128]{1,0:T(8,128)(2,1)S(1)}, bf16[512,128]{1,0:T(8,128)(2,1)S(1)}, u32[]{:S(2)}, u32[]{:S(2)}) collective-permute-start(bf16[512,128]{1,0:T(8,128)(2,1)S(1)} %add_convert_fusion), channel_id=1, source_target_pairs={{0,4},{1,5},{2,6},{3,7},{4,0},{5,1},{6,2},{7,3},{8,12},{9,13},{10,... | collective-permute-start | bytes 393224 | tf_op jit(solution)/shard_map/ppermute | solution.py:41
  52.4 1.9 %collective-permute-done.11 = bf16[512,128]{1,0:T(8,128)(2,1)S(1)} collective-permute-done((bf16[512,128]{1,0:T(8,128)(2,1)S(1)}, bf16[512,128]{1,0:T(8,128)(2,1)S(1)}, u32[]{:S(2)}, u32[]{:S(2)}) %collective-permute-start.11) | collective-permute-done | bytes 131104 | tf_op jit(solution)/shard_map/ppermute | solution.py:41
  54.3 1.7 %collective-permute-done.12 = bf16[512,128]{1,0:T(8,128)(2,1)S(1)} collective-permute-done((bf16[512,128]{1,0:T(8,128)(2,1)S(1)}, bf16[512,128]{1,0:T(8,128)(2,1)S(1)}, u32[]{:S(2)}, u32[]{:S(2)}) %collective-permute-start.12) | collective-permute-done | bytes 131104 | tf_op jit(solution)/shard_map/ppermute | solution.py:41
  56.0 1.2 %collective-permute-done.13 = bf16[512,128]{1,0:T(8,128)(2,1)S(1)} collective-permute-done((bf16[512,128]{1,0:T(8,128)(2,1)S(1)}, bf16[512,128]{1,0:T(8,128)(2,1)S(1)}, u32[]{:S(2)}, u32[]{:S(2)}) %collective-permute-start.13) | collective-permute-done | bytes 131104 | tf_op jit(solution)/shard_map/ppermute | solution.py:41
  57.4 1.2 %unpack.2 = (f32[27,96,96]{2,1,0:T(8,128)}, f32[27,96,96]{2,1,0:T(8,128)}) custom-call(s32[1]{0:T(128)} %bitcast.9.first_ref_flag, bf16[2048,128]{1,0:T(8,128)(2,1)S(1)} %pad_maximum_fusion.packed_ref), custom_call_target="tpu_custom_call" | custom-call | tf_op jit(solution)/shard_map/unpack/pallas_call | solution.py:652
  58.6 0.7 %collective-permute-done.14.packed_ref = bf16[2048,128]{1,0:T(8,128)(2,1)S(1)} collective-permute-done((bf16[2048,128]{1,0:T(8,128)(2,1)S(1)}, bf16[2048,128]{1,0:T(8,128)(2,1)S(1)}, u32[]{:S(2)}, u32[]{:S(2)}) %collective-permute-start.14) | collective-permute-done | bytes 524320 | tf_op jit(solution)/shard_map/ppermute | solution.py:41
  59.3 1.2 %unpack.3 = (f32[27,96,96]{2,1,0:T(8,128)}, f32[27,96,96]{2,1,0:T(8,128)}) custom-call(s32[1]{0:T(128)} %bitcast.8.first_ref_flag, bf16[2048,128]{1,0:T(8,128)(2,1)S(1)} %collective-permute-done.14.packed_ref, f32[27,96,96]{2,1,0:T(8,128)} %get-tuple-element.43.refs_0_, ...), custom_call_target="tpu_custom_call", output_to_operand_aliasing={{0}: (2, {}), {1}: (3, {})} | custom-call | tf_op jit(solution)/shard_map/unpack/pallas_call | solution.py:652
  (18 shorter events, 1.7 us)
Async XLA Ops:
  2.9 8.5 %collective-permute-start = (bf16[4,128,128]{2,1,0:T(8,128)(2,1)S(1)}, bf16[4,128,128]{2,1,0:T(8,128)(2,1)S(1)}, u32[]{:S(2)}, u32[]{:S(2)}) collective-permute-start(bf16[4,128,128]{2,1,0:T(8,128)(2,1)S(1)} %get-tuple-element.29), channel_id=1, source_target_pairs={{0,2},{1,3},{2,0},{3,1},{4,6},{5,7},{6,4},{7,5},{8,10},{9,11},{10,... | collective-permute-start | bytes 393224 | tf_op jit(solution)/shard_map/ppermute | solution.py:41
  3.4 8.0 %collective-permute-start.1 = (bf16[4,128,128]{2,1,0:T(8,128)(2,1)S(1)}, bf16[4,128,128]{2,1,0:T(8,128)(2,1)S(1)}, u32[]{:S(2)}, u32[]{:S(2)}) collective-permute-start(bf16[4,128,128]{2,1,0:T(8,128)(2,1)S(1)} %get-tuple-element.30), channel_id=1, source_target_pairs={{0,1},{1,0},{2,4},{3,5},{4,2},{5,3},{6,8},{7,9},{8,6},{9,7},{10,12... | collective-permute-start | bytes 393224 | tf_op jit(solution)/shard_map/ppermute | solution.py:41
  6.0 5.4 %collective-permute-start.2 = (bf16[8,32,128]{2,1,0:T(8,128)(2,1)S(1)}, bf16[8,32,128]{2,1,0:T(8,128)(2,1)S(1)}, u32[]{:S(2)}, u32[]{:S(2)}) collective-permute-start(bf16[8,32,128]{2,1,0:T(8,128)(2,1)S(1)} %get-tuple-element.31), channel_id=1, source_target_pairs={{0,1},{1,0},{2,3},{3,2},{4,5},{5,4},{6,7},{7,6},{8,9},{9,8},{10,11... | collective-permute-start | bytes 196616 | tf_op jit(solution)/shard_map/ppermute | solution.py:41
  6.1 5.3 %collective-permute-start.3 = (bf16[4,32,128]{2,1,0:T(8,128)(2,1)S(1)}, bf16[4,32,128]{2,1,0:T(8,128)(2,1)S(1)}, u32[]{:S(2)}, u32[]{:S(2)}) collective-permute-start(bf16[4,32,128]{2,1,0:T(8,128)(2,1)S(1)} %get-tuple-element.32), channel_id=1, source_target_pairs={{0,3},{1,2},{2,1},{3,0},{4,7},{5,6},{6,5},{7,4},{8,11},{9,10},{10,... | collective-permute-start | bytes 98312 | tf_op jit(solution)/shard_map/ppermute | solution.py:41
  7.5 3.9 %collective-permute-start.4 = (bf16[4,32,128]{2,1,0:T(8,128)(2,1)S(1)}, bf16[4,32,128]{2,1,0:T(8,128)(2,1)S(1)}, u32[]{:S(2)}, u32[]{:S(2)}) collective-permute-start(bf16[4,32,128]{2,1,0:T(8,128)(2,1)S(1)} %get-tuple-element.33), channel_id=1, source_target_pairs={{0,1},{1,0},{2,5},{3,4},{4,3},{5,2},{6,9},{7,8},{8,7},{9,6},{10,13... | collective-permute-start | bytes 98312 | tf_op jit(solution)/shard_map/ppermute | solution.py:41
  24.2 2.6 %collective-permute-start.5 = (bf16[2048,128]{1,0:T(8,128)(2,1)S(1)}, bf16[2048,128]{1,0:T(8,128)(2,1)S(1)}, u32[]{:S(2)}, u32[]{:S(2)}) collective-permute-start(bf16[2048,128]{1,0:T(8,128)(2,1)S(1)} %get-tuple-element.36), channel_id=1, source_target_pairs={{0,2},{1,3},{2,0},{3,1},{4,6},{5,7},{6,4},{7,5},{8,10},{9,11},{10,... | collective-permute-start | bytes 1572872 | tf_op jit(solution)/shard_map/ppermute | solution.py:41
  27.0 7.2 %collective-permute-start.8 = (bf16[512,128]{1,0:T(8,128)(2,1)S(1)}, bf16[512,128]{1,0:T(8,128)(2,1)S(1)}, u32[]{:S(2)}, u32[]{:S(2)}) collective-permute-start(bf16[512,128]{1,0:T(8,128)(2,1)S(1)} %get-tuple-element.42), channel_id=1, source_target_pairs={{0,1},{1,0},{2,3},{3,2},{4,5},{5,4},{6,7},{7,6},{8,9},{9,8},{10,11... | collective-permute-start | bytes 393224 | tf_op jit(solution)/shard_map/ppermute | solution.py:41
  28.7 8.1 %collective-permute-start.7 = (bf16[512,128]{1,0:T(8,128)(2,1)S(1)}, bf16[512,128]{1,0:T(8,128)(2,1)S(1)}, u32[]{:S(2)}, u32[]{:S(2)}) collective-permute-start(bf16[512,128]{1,0:T(8,128)(2,1)S(1)} %get-tuple-element.41), channel_id=1, source_target_pairs={{0,4},{1,5},{2,6},{3,7},{4,0},{5,1},{6,2},{7,3},{8,12},{9,13},{10,... | collective-permute-start | bytes 393224 | tf_op jit(solution)/shard_map/ppermute | solution.py:41
  30.1 6.7 %collective-permute-start.6 = (bf16[512,128]{1,0:T(8,128)(2,1)S(1)}, bf16[512,128]{1,0:T(8,128)(2,1)S(1)}, u32[]{:S(2)}, u32[]{:S(2)}) collective-permute-start(bf16[512,128]{1,0:T(8,128)(2,1)S(1)} %get-tuple-element.40), channel_id=1, source_target_pairs={{0,5},{1,4},{2,7},{3,6},{4,1},{5,0},{6,3},{7,2},{8,13},{9,12},{10,... | collective-permute-start | bytes 393224 | tf_op jit(solution)/shard_map/ppermute | solution.py:41
  36.9 5.0 %collective-permute-start.9 = (bf16[512,128]{1,0:T(8,128)(2,1)S(1)}, bf16[512,128]{1,0:T(8,128)(2,1)S(1)}, u32[]{:S(2)}, u32[]{:S(2)}) collective-permute-start(bf16[512,128]{1,0:T(8,128)(2,1)S(1)} %add_convert_fusion.2), channel_id=1, source_target_pairs={{0,8},{1,9},{2,10},{3,11},{4,12},{5,13},{6,14},{7,15},{8,0},{9,1},... | collective-permute-start | bytes 393224 | tf_op jit(solution)/shard_map/ppermute | solution.py:41
  42.0 6.1 %collective-permute-start.10 = (bf16[512,128]{1,0:T(8,128)(2,1)S(1)}, bf16[512,128]{1,0:T(8,128)(2,1)S(1)}, u32[]{:S(2)}, u32[]{:S(2)}) collective-permute-start(bf16[512,128]{1,0:T(8,128)(2,1)S(1)} %add_convert_fusion.1), channel_id=1, source_target_pairs={{0,16},{1,17},{2,18},{3,19},{4,20},{5,21},{6,22},{7,23},{8,24},{9,... | collective-permute-start | bytes 393224 | tf_op jit(solution)/shard_map/ppermute | solution.py:41
  48.1 6.2 %collective-permute-start.11 = (bf16[512,128]{1,0:T(8,128)(2,1)S(1)}, bf16[512,128]{1,0:T(8,128)(2,1)S(1)}, u32[]{:S(2)}, u32[]{:S(2)}) collective-permute-start(bf16[512,128]{1,0:T(8,128)(2,1)S(1)} %add_convert_fusion), channel_id=1, source_target_pairs={{0,5},{1,4},{2,7},{3,6},{4,1},{5,0},{6,3},{7,2},{8,13},{9,12},{10,... | collective-permute-start | bytes 393224 | tf_op jit(solution)/shard_map/ppermute | solution.py:41
  51.0 5.0 %collective-permute-start.12 = (bf16[512,128]{1,0:T(8,128)(2,1)S(1)}, bf16[512,128]{1,0:T(8,128)(2,1)S(1)}, u32[]{:S(2)}, u32[]{:S(2)}) collective-permute-start(bf16[512,128]{1,0:T(8,128)(2,1)S(1)} %add_convert_fusion), channel_id=1, source_target_pairs={{0,4},{1,5},{2,6},{3,7},{4,0},{5,1},{6,2},{7,3},{8,12},{9,13},{10,... | collective-permute-start | bytes 393224 | tf_op jit(solution)/shard_map/ppermute | solution.py:41
  52.2 5.0 %collective-permute-start.13 = (bf16[512,128]{1,0:T(8,128)(2,1)S(1)}, bf16[512,128]{1,0:T(8,128)(2,1)S(1)}, u32[]{:S(2)}, u32[]{:S(2)}) collective-permute-start(bf16[512,128]{1,0:T(8,128)(2,1)S(1)} %add_convert_fusion), channel_id=1, source_target_pairs={{0,1},{1,0},{2,3},{3,2},{4,5},{5,4},{6,7},{7,6},{8,9},{9,8},{10,11... | collective-permute-start | bytes 393224 | tf_op jit(solution)/shard_map/ppermute | solution.py:41
  57.3 2.0 %collective-permute-start.14 = (bf16[2048,128]{1,0:T(8,128)(2,1)S(1)}, bf16[2048,128]{1,0:T(8,128)(2,1)S(1)}, u32[]{:S(2)}, u32[]{:S(2)}) collective-permute-start(bf16[2048,128]{1,0:T(8,128)(2,1)S(1)} %pad_maximum_fusion.packed_ref), channel_id=1, source_target_pairs={{0,2},{1,3},{2,0},{3,1},{4,6},{5,7},{6,4},{7,5},{8,10},{9,11},{10,... | collective-permute-start | bytes 1572872 | tf_op jit(solution)/shard_map/ppermute | solution.py:41

commit v18 on v17

--- a/solution.py
+++ b/solution.py
@@ -421,7 +421,7 @@
         [
             (grouped((planes - 2) // 2, 2), first_product, first_forward),
             (
-                grouped((planes - 4) // 2, 2),
+                grouped((planes - 4) // 2, 3),
                 functools.partial(convolve, stack1, ahead2_ref, rows=rows2, upward=upward),
                 second_forward,
             ),

time: 60.7 us -> 61.2 us (level)
  no operation moved by 1% of the time
where the time goes in v18:
time: 61.2 us; the launch traced here: 61 us
  Pallas kernels  24.1 us (39%)
  starting transfers between devices  20.3 us (33%)
  waiting for transfers between devices  15.6 us (25%)
  between operations  0.75 us (1%)
    ppermute x15, starting transfers between devices, exchange(): return lax.ppermute(value, ('east', 'north'), pairs)  20.3 us
    ppermute x15, waiting for transfers between devices, exchange(): return lax.ppermute(value, ('east', 'north'), pairs)  15.6 us
    pallas_call x1, Pallas kernels, per_device(): pl.pallas_call(functools.partial(whole_kernel, channels, classes, east, n...  13.3 us
    pallas_call x1, Pallas kernels, beside(): pl.pallas_call(functools.partial(last_kernel, channels, east, north, upwa...  3.63 us
    pallas_call x2, Pallas kernels, unpack(): pl.pallas_call(functools.partial(unpack_kernel, channels, scale, bool(ali...  2.43 us
    pallas_call x1, Pallas kernels, per_device(): pl.pallas_call(functools.partial(weights_kernel, channels, classes), out_...  2.37 us
    pallas_call x1, Pallas kernels, per_device(): pl.pallas_call(functools.partial(prepare_kernel, channels, upward, edge),...  2.28 us
  transfers between devices with their start and end apart: 15, of which 9 were waited for; matrix products, arithmetic and copies ran while one was open for 0% of the time, Pallas kernels for 12%

profile of v18, /device:TPU:0, one launch (start us, length us, event | category | flops | bytes accessed | tf_op | source)
XLA Modules:
  0.0 61.0 jit_solution(4880249621116344870)
XLA Ops:
  0.6 2.3 %prepare.1 = (bf16[8,128,128]{2,1,0:T(8,128)(2,1)S(1)}, bf16[4,128,128]{2,1,0:T(8,128)(2,1)S(1)}, bf16[4,128,128]{2,1,0:T(8,128)(2,1)S(1)}, bf16[8,32,128]{2,1,0...) custom-call(s32[1,1,2]{2,1,0:T(1,128)} %bitcast.15, bf16[8,128,96]{2,1,0:T(8,128)(2,1)} %bitcast.12, ...), custom_call_target="tpu_custom_call" | custom-call | tf_op jit(solution)/shard_map/prepare/pallas_call | solution.py:536
  3.4 2.6 %collective-permute-start.1 = (bf16[4,128,128]{2,1,0:T(8,128)(2,1)S(1)}, bf16[4,128,128]{2,1,0:T(8,128)(2,1)S(1)}, u32[]{:S(2)}, u32[]{:S(2)}) collective-permute-start(bf16[4,128,128]{2,1,0:T(8,128)(2,1)S(1)} %get-tuple-element.30), channel_id=1, source_target_pairs={{0,1},{1,0},{2,4},{3,5},{4,2},{5,3},{6,8},{7,9},{8,6},{9,7},{10,12... | collective-permute-start | bytes 393224 | tf_op jit(solution)/shard_map/ppermute | solution.py:41
  6.1 1.4 %collective-permute-start.3 = (bf16[4,32,128]{2,1,0:T(8,128)(2,1)S(1)}, bf16[4,32,128]{2,1,0:T(8,128)(2,1)S(1)}, u32[]{:S(2)}, u32[]{:S(2)}) collective-permute-start(bf16[4,32,128]{2,1,0:T(8,128)(2,1)S(1)} %get-tuple-element.32), channel_id=1, source_target_pairs={{0,3},{1,2},{2,1},{3,0},{4,7},{5,6},{6,5},{7,4},{8,11},{9,10},{10,... | collective-permute-start | bytes 98312 | tf_op jit(solution)/shard_map/ppermute | solution.py:41
  7.5 1.5 %collective-permute-start.4 = (bf16[4,32,128]{2,1,0:T(8,128)(2,1)S(1)}, bf16[4,32,128]{2,1,0:T(8,128)(2,1)S(1)}, u32[]{:S(2)}, u32[]{:S(2)}) collective-permute-start(bf16[4,32,128]{2,1,0:T(8,128)(2,1)S(1)} %get-tuple-element.33), channel_id=1, source_target_pairs={{0,1},{1,0},{2,5},{3,4},{4,3},{5,2},{6,9},{7,8},{8,7},{9,6},{10,13... | collective-permute-start | bytes 98312 | tf_op jit(solution)/shard_map/ppermute | solution.py:41
  9.0 2.4 %weights.1 = (bf16[4608,256]{1,0:T(8,128)(2,1)S(1)}, bf16[4608,256]{1,0:T(8,128)(2,1)S(1)}, bf16[128,128]{1,0:T(8,128)(2,1)S(1)}) custom-call(bf16[27,96,96]{2,1,0:T(8,128)(2,1)} %w1_in.3, bf16[27,96,96]{2,1,0:T(8,128)(2,1)} %w2_in.3, bf16[13,96]{1,0:T(8,128)(2,1)} %head_in.1), custom_call_target="tpu_custom_call" | custom-call | tf_op jit(solution)/shard_map/weights/pallas_call | solution.py:571
  11.4 13.3 %fields.1 = (bf16[10,144,128]{2,1,0:T(8,128)(2,1)S(1)}, bf16[2048,128]{1,0:T(8,128)(2,1)S(1)}, bf16[2048,128]{1,0:T(8,128)(2,1)S(1)}) custom-call(bf16[4608,256]{1,0:T(8,128)(2,1)S(1)} %get-tuple-element.26.ahead1_ref, bf16[27,96,96]{2,1,0:T(8,128)(2,1)} %w2_in.3, bf16[4608,256]{1,0:T(8,128)(2,1)S(1)} %get-tuple-element.27.back2_ref, ...), custom_call_target="tpu_custom_call" | custom-call | tf_op jit(solution)/shard_map/fields/pallas_call | solution.py:585
  24.8 1.1 %collective-permute-start.5 = (bf16[2048,128]{1,0:T(8,128)(2,1)S(1)}, bf16[2048,128]{1,0:T(8,128)(2,1)S(1)}, u32[]{:S(2)}, u32[]{:S(2)}) collective-permute-start(bf16[2048,128]{1,0:T(8,128)(2,1)S(1)} %get-tuple-element.36), channel_id=1, source_target_pairs={{0,2},{1,3},{2,0},{3,1},{4,6},{5,7},{6,4},{7,5},{8,10},{9,11},{10,... | collective-permute-start | bytes 1572872 | tf_op jit(solution)/shard_map/ppermute | solution.py:41
  25.9 1.5 %collective-permute-done.5.came_ref = bf16[2048,128]{1,0:T(8,128)(2,1)S(1)} collective-permute-done((bf16[2048,128]{1,0:T(8,128)(2,1)S(1)}, bf16[2048,128]{1,0:T(8,128)(2,1)S(1)}, u32[]{:S(2)}, u32[]{:S(2)}) %collective-permute-start.5) | collective-permute-done | bytes 524320 | tf_op jit(solution)/shard_map/ppermute | solution.py:41
  27.5 1.8 %collective-permute-start.8 = (bf16[512,128]{1,0:T(8,128)(2,1)S(1)}, bf16[512,128]{1,0:T(8,128)(2,1)S(1)}, u32[]{:S(2)}, u32[]{:S(2)}) collective-permute-start(bf16[512,128]{1,0:T(8,128)(2,1)S(1)} %get-tuple-element.42), channel_id=1, source_target_pairs={{0,1},{1,0},{2,3},{3,2},{4,5},{5,4},{6,7},{7,6},{8,9},{9,8},{10,11... | collective-permute-start | bytes 393224 | tf_op jit(solution)/shard_map/ppermute | solution.py:41
  29.3 1.4 %collective-permute-start.7 = (bf16[512,128]{1,0:T(8,128)(2,1)S(1)}, bf16[512,128]{1,0:T(8,128)(2,1)S(1)}, u32[]{:S(2)}, u32[]{:S(2)}) collective-permute-start(bf16[512,128]{1,0:T(8,128)(2,1)S(1)} %get-tuple-element.41), channel_id=1, source_target_pairs={{0,4},{1,5},{2,6},{3,7},{4,0},{5,1},{6,2},{7,3},{8,12},{9,13},{10,... | collective-permute-start | bytes 393224 | tf_op jit(solution)/shard_map/ppermute | solution.py:41
  31.1 3.6 %features.1 = (bf16[8,128,96]{2,1,0:T(8,128)(2,1)}, f32[512,128]{1,0:T(8,128)S(1)}) custom-call(bf16[8,128,128]{2,1,0:T(8,128)(2,1)S(1)} %get-tuple-element.25.center_ref, bf16[10,144,128]{2,1,0:T(8,128)(2,1)S(1)} %get-tuple-element.34.grad_ref, bf16[27,96,96]{2,1,0:T(8,128)(2,1)} %w1_in.3, ...), custom_call_target="tpu_custom_call", output_to_operand_aliasing={{1}: (3, {})} | custom-call | tf_op jit(solution)/shard_map/features/pallas_call | solution.py:613
  34.7 2.6 %collective-permute-done.7 = bf16[512,128]{1,0:T(8,128)(2,1)S(1)} collective-permute-done((bf16[512,128]{1,0:T(8,128)(2,1)S(1)}, bf16[512,128]{1,0:T(8,128)(2,1)S(1)}, u32[]{:S(2)}, u32[]{:S(2)}) %collective-permute-start.7) | collective-permute-done | bytes 131104 | tf_op jit(solution)/shard_map/ppermute | solution.py:41
  37.4 2.1 %collective-permute-start.9 = (bf16[512,128]{1,0:T(8,128)(2,1)S(1)}, bf16[512,128]{1,0:T(8,128)(2,1)S(1)}, u32[]{:S(2)}, u32[]{:S(2)}) collective-permute-start(bf16[512,128]{1,0:T(8,128)(2,1)S(1)} %add_convert_fusion.2), channel_id=1, source_target_pairs={{0,8},{1,9},{2,10},{3,11},{4,12},{5,13},{6,14},{7,15},{8,0},{9,1},... | collective-permute-start | bytes 393224 | tf_op jit(solution)/shard_map/ppermute | solution.py:41
  39.5 3.0 %collective-permute-done.9 = bf16[512,128]{1,0:T(8,128)(2,1)S(1)} collective-permute-done((bf16[512,128]{1,0:T(8,128)(2,1)S(1)}, bf16[512,128]{1,0:T(8,128)(2,1)S(1)}, u32[]{:S(2)}, u32[]{:S(2)}) %collective-permute-start.9) | collective-permute-done | bytes 131104 | tf_op jit(solution)/shard_map/ppermute | solution.py:41
  42.5 3.1 %collective-permute-start.10 = (bf16[512,128]{1,0:T(8,128)(2,1)S(1)}, bf16[512,128]{1,0:T(8,128)(2,1)S(1)}, u32[]{:S(2)}, u32[]{:S(2)}) collective-permute-start(bf16[512,128]{1,0:T(8,128)(2,1)S(1)} %add_convert_fusion.1), channel_id=1, source_target_pairs={{0,16},{1,17},{2,18},{3,19},{4,20},{5,21},{6,22},{7,23},{8,24},{9,... | collective-permute-start | bytes 393224 | tf_op jit(solution)/shard_map/ppermute | solution.py:41
  45.6 3.0 %collective-permute-done.10 = bf16[512,128]{1,0:T(8,128)(2,1)S(1)} collective-permute-done((bf16[512,128]{1,0:T(8,128)(2,1)S(1)}, bf16[512,128]{1,0:T(8,128)(2,1)S(1)}, u32[]{:S(2)}, u32[]{:S(2)}) %collective-permute-start.10) | collective-permute-done | bytes 131104 | tf_op jit(solution)/shard_map/ppermute | solution.py:41
  48.6 2.9 %collective-permute-start.11 = (bf16[512,128]{1,0:T(8,128)(2,1)S(1)}, bf16[512,128]{1,0:T(8,128)(2,1)S(1)}, u32[]{:S(2)}, u32[]{:S(2)}) collective-permute-start(bf16[512,128]{1,0:T(8,128)(2,1)S(1)} %add_convert_fusion), channel_id=1, source_target_pairs={{0,5},{1,4},{2,7},{3,6},{4,1},{5,0},{6,3},{7,2},{8,13},{9,12},{10,... | collective-permute-start | bytes 393224 | tf_op jit(solution)/shard_map/ppermute | solution.py:41
  51.5 1.2 %collective-permute-start.12 = (bf16[512,128]{1,0:T(8,128)(2,1)S(1)}, bf16[512,128]{1,0:T(8,128)(2,1)S(1)}, u32[]{:S(2)}, u32[]{:S(2)}) collective-permute-start(bf16[512,128]{1,0:T(8,128)(2,1)S(1)} %add_convert_fusion), channel_id=1, source_target_pairs={{0,4},{1,5},{2,6},{3,7},{4,0},{5,1},{6,2},{7,3},{8,12},{9,13},{10,... | collective-permute-start | bytes 393224 | tf_op jit(solution)/shard_map/ppermute | solution.py:41
  52.9 1.9 %collective-permute-done.11 = bf16[512,128]{1,0:T(8,128)(2,1)S(1)} collective-permute-done((bf16[512,128]{1,0:T(8,128)(2,1)S(1)}, bf16[512,128]{1,0:T(8,128)(2,1)S(1)}, u32[]{:S(2)}, u32[]{:S(2)}) %collective-permute-start.11) | collective-permute-done | bytes 131104 | tf_op jit(solution)/shard_map/ppermute | solution.py:41
  54.8 1.7 %collective-permute-done.12 = bf16[512,128]{1,0:T(8,128)(2,1)S(1)} collective-permute-done((bf16[512,128]{1,0:T(8,128)(2,1)S(1)}, bf16[512,128]{1,0:T(8,128)(2,1)S(1)}, u32[]{:S(2)}, u32[]{:S(2)}) %collective-permute-start.12) | collective-permute-done | bytes 131104 | tf_op jit(solution)/shard_map/ppermute | solution.py:41
  56.5 1.2 %collective-permute-done.13 = bf16[512,128]{1,0:T(8,128)(2,1)S(1)} collective-permute-done((bf16[512,128]{1,0:T(8,128)(2,1)S(1)}, bf16[512,128]{1,0:T(8,128)(2,1)S(1)}, u32[]{:S(2)}, u32[]{:S(2)}) %collective-permute-start.13) | collective-permute-done | bytes 131104 | tf_op jit(solution)/shard_map/ppermute | solution.py:41
  57.9 1.2 %unpack.2 = (f32[27,96,96]{2,1,0:T(8,128)}, f32[27,96,96]{2,1,0:T(8,128)}) custom-call(s32[1]{0:T(128)} %bitcast.9.first_ref_flag, bf16[2048,128]{1,0:T(8,128)(2,1)S(1)} %pad_maximum_fusion.packed_ref), custom_call_target="tpu_custom_call" | custom-call | tf_op jit(solution)/shard_map/unpack/pallas_call | solution.py:652
  59.1 0.7 %collective-permute-done.14.packed_ref = bf16[2048,128]{1,0:T(8,128)(2,1)S(1)} collective-permute-done((bf16[2048,128]{1,0:T(8,128)(2,1)S(1)}, bf16[2048,128]{1,0:T(8,128)(2,1)S(1)}, u32[]{:S(2)}, u32[]{:S(2)}) %collective-permute-start.14) | collective-permute-done | bytes 524320 | tf_op jit(solution)/shard_map/ppermute | solution.py:41
  59.8 1.2 %unpack.3 = (f32[27,96,96]{2,1,0:T(8,128)}, f32[27,96,96]{2,1,0:T(8,128)}) custom-call(s32[1]{0:T(128)} %bitcast.8.first_ref_flag, bf16[2048,128]{1,0:T(8,128)(2,1)S(1)} %collective-permute-done.14.packed_ref, f32[27,96,96]{2,1,0:T(8,128)} %get-tuple-element.43.refs_0_, ...), custom_call_target="tpu_custom_call", output_to_operand_aliasing={{0}: (2, {}), {1}: (3, {})} | custom-call | tf_op jit(solution)/shard_map/unpack/pallas_call | solution.py:652
  (18 shorter events, 1.7 us)
Async XLA Ops:
  2.9 8.5 %collective-permute-start = (bf16[4,128,128]{2,1,0:T(8,128)(2,1)S(1)}, bf16[4,128,128]{2,1,0:T(8,128)(2,1)S(1)}, u32[]{:S(2)}, u32[]{:S(2)}) collective-permute-start(bf16[4,128,128]{2,1,0:T(8,128)(2,1)S(1)} %get-tuple-element.29), channel_id=1, source_target_pairs={{0,2},{1,3},{2,0},{3,1},{4,6},{5,7},{6,4},{7,5},{8,10},{9,11},{10,... | collective-permute-start | bytes 393224 | tf_op jit(solution)/shard_map/ppermute | solution.py:41
  3.4 8.0 %collective-permute-start.1 = (bf16[4,128,128]{2,1,0:T(8,128)(2,1)S(1)}, bf16[4,128,128]{2,1,0:T(8,128)(2,1)S(1)}, u32[]{:S(2)}, u32[]{:S(2)}) collective-permute-start(bf16[4,128,128]{2,1,0:T(8,128)(2,1)S(1)} %get-tuple-element.30), channel_id=1, source_target_pairs={{0,1},{1,0},{2,4},{3,5},{4,2},{5,3},{6,8},{7,9},{8,6},{9,7},{10,12... | collective-permute-start | bytes 393224 | tf_op jit(solution)/shard_map/ppermute | solution.py:41
  6.0 5.4 %collective-permute-start.2 = (bf16[8,32,128]{2,1,0:T(8,128)(2,1)S(1)}, bf16[8,32,128]{2,1,0:T(8,128)(2,1)S(1)}, u32[]{:S(2)}, u32[]{:S(2)}) collective-permute-start(bf16[8,32,128]{2,1,0:T(8,128)(2,1)S(1)} %get-tuple-element.31), channel_id=1, source_target_pairs={{0,1},{1,0},{2,3},{3,2},{4,5},{5,4},{6,7},{7,6},{8,9},{9,8},{10,11... | collective-permute-start | bytes 196616 | tf_op jit(solution)/shard_map/ppermute | solution.py:41
  6.1 5.3 %collective-permute-start.3 = (bf16[4,32,128]{2,1,0:T(8,128)(2,1)S(1)}, bf16[4,32,128]{2,1,0:T(8,128)(2,1)S(1)}, u32[]{:S(2)}, u32[]{:S(2)}) collective-permute-start(bf16[4,32,128]{2,1,0:T(8,128)(2,1)S(1)} %get-tuple-element.32), channel_id=1, source_target_pairs={{0,3},{1,2},{2,1},{3,0},{4,7},{5,6},{6,5},{7,4},{8,11},{9,10},{10,... | collective-permute-start | bytes 98312 | tf_op jit(solution)/shard_map/ppermute | solution.py:41
  7.5 3.9 %collective-permute-start.4 = (bf16[4,32,128]{2,1,0:T(8,128)(2,1)S(1)}, bf16[4,32,128]{2,1,0:T(8,128)(2,1)S(1)}, u32[]{:S(2)}, u32[]{:S(2)}) collective-permute-start(bf16[4,32,128]{2,1,0:T(8,128)(2,1)S(1)} %get-tuple-element.33), channel_id=1, source_target_pairs={{0,1},{1,0},{2,5},{3,4},{4,3},{5,2},{6,9},{7,8},{8,7},{9,6},{10,13... | collective-permute-start | bytes 98312 | tf_op jit(solution)/shard_map/ppermute | solution.py:41
  24.8 2.6 %collective-permute-start.5 = (bf16[2048,128]{1,0:T(8,128)(2,1)S(1)}, bf16[2048,128]{1,0:T(8,128)(2,1)S(1)}, u32[]{:S(2)}, u32[]{:S(2)}) collective-permute-start(bf16[2048,128]{1,0:T(8,128)(2,1)S(1)} %get-tuple-element.36), channel_id=1, source_target_pairs={{0,2},{1,3},{2,0},{3,1},{4,6},{5,7},{6,4},{7,5},{8,10},{9,11},{10,... | collective-permute-start | bytes 1572872 | tf_op jit(solution)/shard_map/ppermute | solution.py:41
  27.5 7.2 %collective-permute-start.8 = (bf16[512,128]{1,0:T(8,128)(2,1)S(1)}, bf16[512,128]{1,0:T(8,128)(2,1)S(1)}, u32[]{:S(2)}, u32[]{:S(2)}) collective-permute-start(bf16[512,128]{1,0:T(8,128)(2,1)S(1)} %get-tuple-element.42), channel_id=1, source_target_pairs={{0,1},{1,0},{2,3},{3,2},{4,5},{5,4},{6,7},{7,6},{8,9},{9,8},{10,11... | collective-permute-start | bytes 393224 | tf_op jit(solution)/shard_map/ppermute | solution.py:41
  29.3 8.1 %collective-permute-start.7 = (bf16[512,128]{1,0:T(8,128)(2,1)S(1)}, bf16[512,128]{1,0:T(8,128)(2,1)S(1)}, u32[]{:S(2)}, u32[]{:S(2)}) collective-permute-start(bf16[512,128]{1,0:T(8,128)(2,1)S(1)} %get-tuple-element.41), channel_id=1, source_target_pairs={{0,4},{1,5},{2,6},{3,7},{4,0},{5,1},{6,2},{7,3},{8,12},{9,13},{10,... | collective-permute-start | bytes 393224 | tf_op jit(solution)/shard_map/ppermute | solution.py:41
  30.7 6.7 %collective-permute-start.6 = (bf16[512,128]{1,0:T(8,128)(2,1)S(1)}, bf16[512,128]{1,0:T(8,128)(2,1)S(1)}, u32[]{:S(2)}, u32[]{:S(2)}) collective-permute-start(bf16[512,128]{1,0:T(8,128)(2,1)S(1)} %get-tuple-element.40), channel_id=1, source_target_pairs={{0,5},{1,4},{2,7},{3,6},{4,1},{5,0},{6,3},{7,2},{8,13},{9,12},{10,... | collective-permute-start | bytes 393224 | tf_op jit(solution)/shard_map/ppermute | solution.py:41
  37.4 5.0 %collective-permute-start.9 = (bf16[512,128]{1,0:T(8,128)(2,1)S(1)}, bf16[512,128]{1,0:T(8,128)(2,1)S(1)}, u32[]{:S(2)}, u32[]{:S(2)}) collective-permute-start(bf16[512,128]{1,0:T(8,128)(2,1)S(1)} %add_convert_fusion.2), channel_id=1, source_target_pairs={{0,8},{1,9},{2,10},{3,11},{4,12},{5,13},{6,14},{7,15},{8,0},{9,1},... | collective-permute-start | bytes 393224 | tf_op jit(solution)/shard_map/ppermute | solution.py:41
  42.5 6.1 %collective-permute-start.10 = (bf16[512,128]{1,0:T(8,128)(2,1)S(1)}, bf16[512,128]{1,0:T(8,128)(2,1)S(1)}, u32[]{:S(2)}, u32[]{:S(2)}) collective-permute-start(bf16[512,128]{1,0:T(8,128)(2,1)S(1)} %add_convert_fusion.1), channel_id=1, source_target_pairs={{0,16},{1,17},{2,18},{3,19},{4,20},{5,21},{6,22},{7,23},{8,24},{9,... | collective-permute-start | bytes 393224 | tf_op jit(solution)/shard_map/ppermute | solution.py:41
  48.6 6.2 %collective-permute-start.11 = (bf16[512,128]{1,0:T(8,128)(2,1)S(1)}, bf16[512,128]{1,0:T(8,128)(2,1)S(1)}, u32[]{:S(2)}, u32[]{:S(2)}) collective-permute-start(bf16[512,128]{1,0:T(8,128)(2,1)S(1)} %add_convert_fusion), channel_id=1, source_target_pairs={{0,5},{1,4},{2,7},{3,6},{4,1},{5,0},{6,3},{7,2},{8,13},{9,12},{10,... | collective-permute-start | bytes 393224 | tf_op jit(solution)/shard_map/ppermute | solution.py:41
  51.5 5.0 %collective-permute-start.12 = (bf16[512,128]{1,0:T(8,128)(2,1)S(1)}, bf16[512,128]{1,0:T(8,128)(2,1)S(1)}, u32[]{:S(2)}, u32[]{:S(2)}) collective-permute-start(bf16[512,128]{1,0:T(8,128)(2,1)S(1)} %add_convert_fusion), channel_id=1, source_target_pairs={{0,4},{1,5},{2,6},{3,7},{4,0},{5,1},{6,2},{7,3},{8,12},{9,13},{10,... | collective-permute-start | bytes 393224 | tf_op jit(solution)/shard_map/ppermute | solution.py:41
  52.7 5.0 %collective-permute-start.13 = (bf16[512,128]{1,0:T(8,128)(2,1)S(1)}, bf16[512,128]{1,0:T(8,128)(2,1)S(1)}, u32[]{:S(2)}, u32[]{:S(2)}) collective-permute-start(bf16[512,128]{1,0:T(8,128)(2,1)S(1)} %add_convert_fusion), channel_id=1, source_target_pairs={{0,1},{1,0},{2,3},{3,2},{4,5},{5,4},{6,7},{7,6},{8,9},{9,8},{10,11... | collective-permute-start | bytes 393224 | tf_op jit(solution)/shard_map/ppermute | solution.py:41
  57.8 2.0 %collective-permute-start.14 = (bf16[2048,128]{1,0:T(8,128)(2,1)S(1)}, bf16[2048,128]{1,0:T(8,128)(2,1)S(1)}, u32[]{:S(2)}, u32[]{:S(2)}) collective-permute-start(bf16[2048,128]{1,0:T(8,128)(2,1)S(1)} %pad_maximum_fusion.packed_ref), channel_id=1, source_target_pairs={{0,2},{1,3},{2,0},{3,1},{4,6},{5,7},{6,4},{7,5},{8,10},{9,11},{10,... | collective-permute-start | bytes 1572872 | tf_op jit(solution)/shard_map/ppermute | solution.py:41
